TPU v7x, 128 devices: a whole 4x4x4 slice. The times are simulated.
128 devices in a mesh: section: 2 (over z_hi), dp: 8 (over z_lo, x), tensor: 8 (over y, core).
Axes of the slice: x: 4, y: 4, z: 4 (z_hi: 2, z_lo: 2; z = z_hi * 2 + z_lo), core: 2. Of those that a mesh axis runs over, the one named last changes fastest.
Arguments:
- act: bfloat16 [512, 8192], P(('section', 'dp', 'tensor')), may hold values from -6 to 6
- gain: float32 [8192], replicated, may hold values from 0.5 to 1.5
- shift: float32 [8192], replicated, may hold values from -3 to 3
- w_in: bfloat16 [8192, 32768], P(('section', 'tensor'), 'dp'), may hold values from -0.0625 to 0.0625
- w_out: bfloat16 [32768, 8192], P('dp', ('section', 'tensor')), may hold values from -0.03125 to 0.03125
- cotangent: bfloat16 [512, 8192], P(None, ('section', 'tensor')), may hold values from -6 to 6
Outputs:
- grad_in: float32 [8192, 32768], P(('section', 'tensor'), 'dp')
- grad_out: float32 [32768, 8192], P('dp', ('section', 'tensor'))
- grad_act: float32 [512, 8192], P(('section', 'dp', 'tensor'))
All inputs are finite; a program needn't handle non-finite values.
Results may differ from a plain program's by a relative error of at most 0.0047.
Values may be sent and summed in bfloat16 or wider, within the bound.
No kernel may reach another device: no remote copies, remote signals or barrier semaphores. Data moves between devices by JAX's collectives and lax.ppermute only.
A program may use at most 128 MiB of HBM per device.

v0:
```python
import functools

import jax
import jax.numpy as jnp
from jax import lax
from jax.experimental import pallas as pl
from jax.experimental.pallas import tpu as pltpu
from jax.sharding import PartitionSpec as P

EPSILON = 1e-05
OWNERS = ("section", "tensor")
EVERY = ("section", "dp", "tensor")
BF16, F16, F32 = jnp.bfloat16, jnp.float16, jnp.float32
MIB = 1 << 20
LIFT = 16.0

LINKS = {
    "core": lambda s, y, c: (s, y, 1 - c),
    "a": lambda s, y, c: (s, y ^ 1, c),
    "b": lambda s, y, c: (s, 3 - y, c),
    "z": lambda s, y, c: (1 - s, y, c),
}
WEIGHT = {"a": 4, "b": 2, "z": 1}
ORDERS = (("a", "b", "z"), ("b", "z", "a"), ("z", "a", "b"))
TILE = 256
CUTS = (0, 3, 6, 8)


def swap(x, link):
    pairs = []
    for s in range(2):
        for y in range(4):
            for c in range(2):
                s2, y2, c2 = LINKS[link](s, y, c)
                pairs.append((s * 8 + y * 2 + c, s2 * 8 + y2 * 2 + c2))
    return lax.ppermute(x, OWNERS, pairs)


def places(order):
    w = [WEIGHT[link] for link in order]
    return [(q >> 2 & 1) * w[0] + (q >> 1 & 1) * w[1] + (q & 1) * w[2] for q in range(8)]


def lower(shape):
    return lax.broadcasted_iota(jnp.int32, shape, len(shape) - 2) % 8 < 4


def norm_kernel(act, gain, shift, out, twice):
    x = act[...].astype(F32)
    twice[0:4, :] = x
    twice[4:8, :] = x
    x = twice[...]
    center = x - jnp.mean(x, axis=1, keepdims=True)
    inverse = lax.rsqrt(jnp.mean(center * center, axis=1, keepdims=True) + EPSILON)
    twice[...] = center * inverse * gain[...] + shift[...]
    low = lower((8, 128))
    for g in range(16):
        cols = [twice[:, g * 512 + k * 128 : g * 512 + (k + 1) * 128] for k in range(4)]
        piece = jnp.concatenate([jnp.where(low, cols[0], cols[1]), jnp.where(low, cols[2], cols[3])], axis=0)
        piece = piece.astype(BF16)
        for d in range(8):
            out[g // 8, d, g % 8] = piece


def norm_messages(act, gain, shift):
    return pl.pallas_call(
        norm_kernel,
        out_shape=jax.ShapeDtypeStruct((2, 8, 8, 16, 128), BF16),
        scratch_shapes=[pltpu.VMEM((8, 8192), F32)],
        name="norm_messages",
    )(act, gain.reshape(1, -1), shift.reshape(1, -1))


def rows_kernel(x, out):
    even = x[:, 0].astype(F32)
    odd = x[:, 1].astype(F32)
    low = lower((64, 8, 128))
    for k in range(4):
        tile = slice(k // 2 * 8, k // 2 * 8 + 8)
        e, o = even[:, tile], odd[:, tile]
        if k % 2 == 0:
            col = jnp.where(low, e, pltpu.roll(o, 4, 1))
        else:
            col = jnp.where(low, pltpu.roll(e, 4, 1), o)
        out[:, k * 128 : (k + 1) * 128] = col.reshape(512, 128).astype(BF16)


def to_rows(x):
    return pl.pallas_call(
        rows_kernel, out_shape=jax.ShapeDtypeStruct((512, 512), BF16), name="token_rows"
    )(x.reshape(64, 2, 16, 128))


def part_kernel(rel, contract, at, x, x_other, w, w_other, keep, send, lhs):
    @pl.when(pl.program_id(0) == 0)
    def _():
        for q in range(8):
            src = pl.multiple_of(jnp.bitwise_xor(at[0], rel[q]) * 64, 64)
            lhs[0, q * 64 : (q + 1) * 64, :] = x[pl.ds(src, 64), :]
            lhs[1, q * 64 : (q + 1) * 64, :] = x_other[pl.ds(src, 64), :]

    dims = (((1,), (contract,)), ((), ()))
    total = lax.dot_general(lhs[0], w[...], dims, preferred_element_type=F32)
    total = (total + lax.dot_general(lhs[1], w_other[...], dims, preferred_element_type=F32)) * LIFT
    keep[...] = total[:256]
    send[...] = total[256:]


def part_sum(at, x, x_other, w, w_other, part, contract):
    first, tiles = CUTS[part], CUTS[part + 1] - CUTS[part]
    whole = pl.BlockSpec((512, 512), lambda i, at: (0, 0))
    if contract == 1:
        weight = pl.BlockSpec((TILE, 512), lambda i, at: (at[1] * 8 + first + i, 0))
    else:
        weight = pl.BlockSpec((512, TILE), lambda i, at: (0, at[1] * 8 + first + i))
    out = pl.BlockSpec((256, TILE), lambda i, at: (0, i))
    return pl.pallas_call(
        functools.partial(part_kernel, places(ORDERS[part]), contract),
        grid_spec=pltpu.PrefetchScalarGridSpec(
            num_scalar_prefetch=1,
            grid=(tiles,),
            in_specs=[whole, whole, weight, weight],
            out_specs=[out, out],
            scratch_shapes=[pltpu.VMEM((2, 512, 512), BF16)],
        ),
        out_shape=[jax.ShapeDtypeStruct((256, tiles * TILE), F32)] * 2,
        compiler_params=pltpu.CompilerParams(vmem_limit_bytes=16 * MIB),
        cost_estimate=pl.CostEstimate(flops=2 * 512 * 1024 * tiles * TILE, bytes_accessed=4 * MIB, transcendentals=0),
        name="up_part" if contract else "pre_part",
    )(at, x, x_other, w, w_other)


def reduce_blocks(keep, send, order):
    send = send.astype(F16)
    for step, link in enumerate(order):
        came = swap(send, link).astype(F32)
        total = keep + came
        if step == 2:
            return total
        rows = total.shape[0] // 2
        keep, send = total[:rows], total[rows:].astype(F16)


def gather_blocks(x, order):
    x = jnp.concatenate([x, swap(x, order[0])], axis=0)
    x = jnp.concatenate([x, swap(x, order[1])], axis=0)
    return x, swap(x, order[2])


def assemble(at, pieces, whole):
    for h in range(2):
        base = at[1] * 2048 if h == 0 else (1 - at[1]) * 2048
        for p in range(3):
            rel = places(ORDERS[p][::-1])
            first, last = CUTS[p] * TILE, CUTS[p + 1] * TILE
            cols = pl.ds(pl.multiple_of(base + first, TILE), last - first)
            for q in range(8):
                dst = pl.multiple_of(jnp.bitwise_xor(at[0], rel[q]) * 64, 64)
                src = pieces[h * 6 + p * 2 + q // 4]
                whole[pl.ds(dst, 64), cols] = src[q % 4 * 64 : (q % 4 + 1) * 64, :]


def back_kernel(at, *refs):
    pieces, w, whole, out = refs[:12], refs[12], refs[13], refs[14]
    assemble(at, pieces, whole)
    total = jnp.zeros((512, 512), F32)
    for k in range(8):
        cols = slice(k * 512, (k + 1) * 512)
        total += lax.dot_general(whole[:, cols], w[:, cols], (((1,), (1,)), ((), ())), preferred_element_type=F32)
    low = lower((64, 8, 128))
    c = [total[:, k * 128 : (k + 1) * 128].reshape(64, 8, 128) for k in range(4)]
    r = [pltpu.roll(v, 4, 1) for v in c]
    for t in range(2):
        tile = slice(t * 8, t * 8 + 8)
        out[:, 0, tile] = jnp.where(low, c[2 * t], r[2 * t + 1]).astype(BF16)
        out[:, 1, tile] = jnp.where(low, r[2 * t], c[2 * t + 1]).astype(BF16)


SCALARS = pl.BlockSpec(memory_space=pltpu.SMEM)


def back_messages(at, pieces, w_in):
    return pl.pallas_call(
        back_kernel,
        in_specs=[SCALARS] + [pl.BlockSpec(memory_space=pltpu.VMEM)] * 13,
        out_shape=[jax.ShapeDtypeStruct((512, 4096), BF16), jax.ShapeDtypeStruct((64, 2, 16, 128), BF16)],
        compiler_params=pltpu.CompilerParams(vmem_limit_bytes=24 * MIB),
        cost_estimate=pl.CostEstimate(flops=2 * 512 * 512 * 4096, bytes_accessed=12 * MIB, transcendentals=0),
        name="back_messages",
    )(at, *pieces, w_in)


def grad_in_kernel(x, g, out):
    out[...] = jnp.dot(x[...], g[...], preferred_element_type=F32)


def grad_in_of(x_t, g):
    return pl.pallas_call(
        grad_in_kernel,
        grid=(8,),
        in_specs=[pl.BlockSpec((512, 512), lambda i: (0, 0)), pl.BlockSpec((512, 512), lambda i: (0, i))],
        out_specs=pl.BlockSpec((512, 512), lambda i: (0, i)),
        out_shape=jax.ShapeDtypeStruct((512, 4096), F32),
        compiler_params=pltpu.CompilerParams(vmem_limit_bytes=12 * MIB),
        cost_estimate=pl.CostEstimate(flops=2 * 512 * 512 * 4096, bytes_accessed=12 * MIB, transcendentals=0),
        name="grad_in",
    )(x_t, g)


def grad_out_kernel(at, *refs):
    pieces, cot, out, whole = refs[:12], refs[12], refs[13], refs[14]

    @pl.when(pl.program_id(0) == 0)
    def _():
        assemble(at, pieces, whole)

    cols = pl.ds(pl.multiple_of(pl.program_id(0) * 512, 512), 512)
    out[...] = lax.dot_general(whole[:, cols], cot[...], (((0,), (0,)), ((), ())), preferred_element_type=F32)


def grad_out_of(at, pieces, cot):
    return pl.pallas_call(
        grad_out_kernel,
        grid=(8,),
        in_specs=[SCALARS] + [pl.BlockSpec(p.shape, lambda i: (0, 0)) for p in pieces] + [pl.BlockSpec((512, 512), lambda i: (0, 0))],
        out_specs=pl.BlockSpec((512, 512), lambda i: (i, 0)),
        out_shape=jax.ShapeDtypeStruct((4096, 512), F32),
        scratch_shapes=[pltpu.VMEM((512, 4096), BF16)],
        compiler_params=pltpu.CompilerParams(vmem_limit_bytes=24 * MIB),
        cost_estimate=pl.CostEstimate(flops=2 * 512 * 512 * 4096, bytes_accessed=12 * MIB, transcendentals=0),
        name="grad_out",
    )(at, *pieces, cot)


def act_kernel(x, act, gain, out, twice, back):
    a = act[...].astype(F32)
    twice[0:4, :] = a
    twice[4:8, :] = a
    a = twice[...]
    center = a - jnp.mean(a, axis=1, keepdims=True)
    inverse = lax.rsqrt(jnp.mean(center * center, axis=1, keepdims=True) + EPSILON)
    scaled = center * inverse
    low = lower((8, 128))
    for g in range(16):
        total = x[g // 8, 0, g % 8].astype(F32)
        for d in range(1, 8):
            total += x[g // 8, d, g % 8].astype(F32)
        for t in range(2):
            tile = total[t * 8 : t * 8 + 8]
            turned = pltpu.roll(tile, 4, 0)
            at = g * 512 + t * 256
            back[:, at : at + 128] = jnp.where(low, tile, turned)
            back[:, at + 128 : at + 256] = jnp.where(low, turned, tile)
    dxhat = back[...] * gain[...]
    first = jnp.mean(dxhat, axis=1, keepdims=True)
    second = jnp.mean(dxhat * scaled, axis=1, keepdims=True)
    back[...] = inverse * (dxhat - first - scaled * second)
    out[...] = back[0:4, :]


def grad_act_of(x, act, gain):
    return pl.pallas_call(
        act_kernel,
        out_shape=jax.ShapeDtypeStruct((4, 8192), F32),
        scratch_shapes=[pltpu.VMEM((8, 8192), F32), pltpu.VMEM((8, 8192), F32)],
        name="grad_act",
    )(x.reshape(2, 8, 8, 16, 128), act, gain.reshape(1, -1))


def gelu_tanh(inner):
    return jax.nn.gelu(inner, approximate=True)


def activate(preact, upstream):
    value, pullback = jax.vjp(gelu_tanh, preact)
    return value.astype(BF16), pullback(upstream)[0].astype(BF16)


def local(act, gain, shift, w_in, w_out, cotangent):
    section, tensor = lax.axis_index("section"), lax.axis_index("tensor")
    core, ring = tensor % 2, tensor // 2
    bit_a = jnp.where((ring == 1) | (ring == 2), 1, 0)
    number = bit_a * 4 + ring // 2 * 2 + section
    at = jnp.stack([number, core]).astype(jnp.int32)

    out_other = swap(w_out, "core")
    cot_other = swap(cotangent, "core")
    in_other = swap(w_in, "core")

    mixed = lax.all_to_all(norm_messages(act, gain, shift).reshape(128, 16, 128), EVERY, 0, 0, tiled=True)
    mixed_other = swap(mixed, "core")

    ups = []
    for p, order in enumerate(ORDERS):
        ups.append(reduce_blocks(*part_sum(at, cotangent, cot_other, w_out, out_other, p, 1), order))

    tokens = to_rows(mixed)
    tokens_other = to_rows(mixed_other)
    pres = []
    for p, order in enumerate(ORDERS):
        pres.append(reduce_blocks(*part_sum(at, tokens, tokens_other, w_in, in_other, p, 0), order))

    hidden, pre_grad = [], []
    for p in range(3):
        h, g = activate(pres[p] * (1.0 / LIFT), ups[p] * (1.0 / LIFT))
        hidden.append(h)
        pre_grad.append(g)

    def both(parts):
        pieces = [half for x, order in zip(parts, ORDERS) for half in gather_blocks(x, order)]
        return pieces + [swap(piece, "core") for piece in pieces]

    pre_whole, share = back_messages(at, both(pre_grad), w_in)
    returned = lax.all_to_all(share.reshape(128, 16, 128), EVERY, 0, 0, tiled=True)
    grad_act = grad_act_of(returned, act, gain)
    grad_in = grad_in_of(tokens.T, pre_whole)
    grad_out = grad_out_of(at, both(hidden), cotangent)
    return (grad_in, grad_out, grad_act)


def solution(mesh):
    in_specs = (
        P(EVERY, None),
        P(),
        P(),
        P(OWNERS, "dp"),
        P("dp", OWNERS),
        P(None, OWNERS),
    )
    out_specs = (P(OWNERS, "dp"), P("dp", OWNERS), P(EVERY, None))
    return jax.shard_map(local, mesh=mesh, in_specs=in_specs, out_specs=out_specs, check_vma=False)
```

profile of v0, /device:TPU:1, one launch (start us, length us, event | category | flops | bytes accessed | tf_op | source)
XLA Modules:
  0.0 201.6 jit_solution(14153915135072554943)
XLA Ops:
  0.6 1.5 collective-permute-start.1
  2.2 2.1 %norm_messages.1 = bf16[2,8,8,16,128]{4,3,2,1,0:T(8,128)(2,1)} custom-call(bf16[4,8192]{1,0:T(4,128)(2,1)} %act.3, f32[1,8192]{1,0:T(1,128)} %bitcast.14, f32[1,8192]{1,0:T(1,128)} %bitcast.16), custom_call_target="tpu_custom_call" | custom-call | tf_op jit(solution)/shard_map/norm_messages/pallas_call | solution.py:66
  4.3 24.0 %all_to_all.10 = bf16[128,16,128]{2,1,0:T(8,128)(2,1)S(1)} all-to-all(bf16[128,16,128]{2,1,0:T(8,128)(2,1)} %bitcast.11), channel_id=1, replica_groups=mesh['section'=2,'dp'=8,'tensor'=8] {'section','dp','tensor'}, dimensions={0} | all-to-all | bytes 1048576 | tf_op jit(solution)/shard_map/all_to_all | solution.py:290
  29.5 2.0 %token_rows.2.x = bf16[512,512]{1,0:T(8,128)(2,1)} custom-call(bf16[64,2,16,128]{3,2,1,0:T(8,128)(2,1)} %bitcast.12), custom_call_target="tpu_custom_call" | custom-call | tf_op jit(solution)/shard_map/token_rows/pallas_call | solution.py:89
  32.4 2.0 %token_rows.3.x_other = bf16[512,512]{1,0:T(8,128)(2,1)} custom-call(bf16[64,2,16,128]{3,2,1,0:T(8,128)(2,1)} %bitcast.13), custom_call_target="tpu_custom_call" | custom-call | tf_op jit(solution)/shard_map/token_rows/pallas_call | solution.py:89
  34.5 2.2 %copy-done.1 = bf16[4096,512]{1,0:T(8,128)(2,1)S(1)} copy-done((bf16[4096,512]{1,0:T(8,128)(2,1)S(1)}, bf16[4096,512]{1,0:T(8,128)(2,1)}, u32[]{:S(2)}) %copy-start.1) | copy-done | bytes 4194328
  36.7 2.6 %up_part.5 = (f32[256,512]{1,0:T(8,128)S(1)}, f32[256,512]{1,0:T(8,128)S(1)}) custom-call(s32[2]{0:T(128)S(1)} %pad_add_fusion.at, bf16[512,512]{1,0:T(8,128)(2,1)S(1)} %copy-done.3, bf16[512,512]{1,0:T(8,128)(2,1)S(1)} %collective-permute-done.x_other, bf16[4096,512]{1,0:T(8,128)(2,1)S(1)} %copy-done.1, bf16[4096,512]{1,0:T(8,128)(2,1)} %collective-permute-done.1.w_other), custom_call_target="tpu_custom_call" | custom-call | flops 536870912 | bytes 4194304 | tf_op jit(solution)/shard_map/up_part/pallas_call | solution.py:117
  40.0 3.5 %up_part.4 = (f32[256,768]{1,0:T(8,128)S(1)}, f32[256,768]{1,0:T(8,128)S(1)}) custom-call(s32[2]{0:T(128)S(1)} %pad_add_fusion.at, bf16[512,512]{1,0:T(8,128)(2,1)S(1)} %copy-done.3, bf16[512,512]{1,0:T(8,128)(2,1)S(1)} %collective-permute-done.x_other, bf16[4096,512]{1,0:T(8,128)(2,1)S(1)} %copy-done.1, bf16[4096,512]{1,0:T(8,128)(2,1)} %collective-permute-done.1.w_other), custom_call_target="tpu_custom_call" | custom-call | flops 805306368 | bytes 4194304 | tf_op jit(solution)/shard_map/up_part/pallas_call | solution.py:117
  43.6 3.8 %up_part.3 = (f32[256,768]{1,0:T(8,128)S(1)}, f32[256,768]{1,0:T(8,128)S(1)}) custom-call(s32[2]{0:T(128)S(1)} %pad_add_fusion.at, bf16[512,512]{1,0:T(8,128)(2,1)S(1)} %copy-done.3, bf16[512,512]{1,0:T(8,128)(2,1)S(1)} %collective-permute-done.x_other, bf16[4096,512]{1,0:T(8,128)(2,1)S(1)} %copy-done.1, bf16[4096,512]{1,0:T(8,128)(2,1)} %collective-permute-done.1.w_other), custom_call_target="tpu_custom_call" | custom-call | flops 805306368 | bytes 4194304 | tf_op jit(solution)/shard_map/up_part/pallas_call | solution.py:117
  47.8 1.4 collective-permute-start.13
  49.2 2.6 %pre_part.5 = (f32[256,512]{1,0:T(8,128)S(1)}, f32[256,512]{1,0:T(8,128)S(1)}) custom-call(s32[2]{0:T(128)S(1)} %pad_add_fusion.at, bf16[512,512]{1,0:T(8,128)(2,1)S(1)} %copy-done.2, bf16[512,512]{1,0:T(8,128)(2,1)S(1)} %copy-done.4, bf16[512,4096]{1,0:T(8,128)(2,1)S(1)} %copy-done, bf16[512,4096]{1,0:T(8,128)(2,1)} %collective-permute-done.6.w_other), custom_call_target="tpu_custom_call" | custom-call | flops 536870912 | bytes 4194304 | tf_op jit(solution)/shard_map/pre_part/pallas_call | solution.py:117
  51.9 1.7 collective-permute-start.25
  53.6 3.6 %pre_part.4 = (f32[256,768]{1,0:T(8,128)S(1)}, f32[256,768]{1,0:T(8,128)S(1)}) custom-call(s32[2]{0:T(128)S(1)} %pad_add_fusion.at, bf16[512,512]{1,0:T(8,128)(2,1)S(1)} %copy-done.2, bf16[512,512]{1,0:T(8,128)(2,1)S(1)} %copy-done.4, bf16[512,4096]{1,0:T(8,128)(2,1)S(1)} %copy-done, bf16[512,4096]{1,0:T(8,128)(2,1)} %collective-permute-done.6.w_other), custom_call_target="tpu_custom_call" | custom-call | flops 805306368 | bytes 4194304 | tf_op jit(solution)/shard_map/pre_part/pallas_call | solution.py:117
  57.2 3.6 %pre_part.3 = (f32[256,768]{1,0:T(8,128)S(1)}, f32[256,768]{1,0:T(8,128)S(1)}) custom-call(s32[2]{0:T(128)S(1)} %pad_add_fusion.at, bf16[512,512]{1,0:T(8,128)(2,1)S(1)} %copy-done.2, bf16[512,512]{1,0:T(8,128)(2,1)S(1)} %copy-done.4, bf16[512,4096]{1,0:T(8,128)(2,1)S(1)} %copy-done, bf16[512,4096]{1,0:T(8,128)(2,1)} %collective-permute-done.6.w_other), custom_call_target="tpu_custom_call" | custom-call | flops 805306368 | bytes 4194304 | tf_op jit(solution)/shard_map/pre_part/pallas_call | solution.py:117
  61.6 2.1 %collective-permute-start.16 = (f16[256,768]{1,0:T(8,128)(2,1)S(1)}, f16[256,768]{1,0:T(8,128)(2,1)S(1)}, u32[]{:S(2)}, u32[]{:S(2)}) collective-permute-start(f16[256,768]{1,0:T(8,128)(2,1)S(1)} %convert_element_type.115), channel_id=1, source_target_pairs={{0,6},{1,7},{2,4},{3,5},{4,2},{5,3},{6,0},{7,1},{64,70},{65,71},{6... | collective-permute-start | bytes 1179656 | tf_op jit(solution)/shard_map/ppermute | solution.py:36
  64.1 8.8 %collective-permute-done.23 = f16[128,512]{1,0:T(8,128)(2,1)S(1)} collective-permute-done((f16[128,512]{1,0:T(8,128)(2,1)S(1)}, f16[128,512]{1,0:T(8,128)(2,1)S(1)}, u32[]{:S(2)}, u32[]{:S(2)}) %collective-permute-start.23) | collective-permute-done | bytes 131104 | tf_op jit(solution)/shard_map/ppermute | solution.py:36
  73.7 1.9 collective-permute-start.24
  78.2 1.4 collective-permute-start.27
  79.8 1.4 collective-permute-start.8
  81.3 1.6 collective-permute-done.27
  83.0 2.5 %collective-permute-start.43 = (bf16[64,512]{1,0:T(8,128)(2,1)S(1)}, bf16[64,512]{1,0:T(8,128)(2,1)S(1)}, u32[]{:S(2)}, u32[]{:S(2)}) collective-permute-start(bf16[64,512]{1,0:T(8,128)(2,1)S(1)} %get-tuple-element.35), channel_id=1, source_target_pairs={{0,64},{1,65},{2,66},{3,67},{4,68},{5,69},{6,70},{7,71},{64,0},{65... | collective-permute-start | bytes 196616 | tf_op jit(solution)/shard_map/ppermute | solution.py:36
  86.2 1.5 collective-permute-done.43
  87.7 2.4 %collective-permute-start.28 = (bf16[64,512]{1,0:T(8,128)(2,1)S(1)}, bf16[64,512]{1,0:T(8,128)(2,1)S(1)}, u32[]{:S(2)}, u32[]{:S(2)}) collective-permute-start(bf16[64,512]{1,0:T(8,128)(2,1)S(1)} %get-tuple-element.36), channel_id=1, source_target_pairs={{0,64},{1,65},{2,66},{3,67},{4,68},{5,69},{6,70},{7,71},{64,0},{65... | collective-permute-start | bytes 196616 | tf_op jit(solution)/shard_map/ppermute | solution.py:36
  90.2 2.2 %collective-permute-done.28 = bf16[64,512]{1,0:T(8,128)(2,1)S(1)} collective-permute-done((bf16[64,512]{1,0:T(8,128)(2,1)S(1)}, bf16[64,512]{1,0:T(8,128)(2,1)S(1)}, u32[]{:S(2)}, u32[]{:S(2)}) %collective-permute-start.28) | collective-permute-done | bytes 65568 | tf_op jit(solution)/shard_map/ppermute | solution.py:36
  94.0 3.3 %collective-permute-start.4 = (f16[64,768]{1,0:T(8,128)(2,1)S(1)}, f16[64,768]{1,0:T(8,128)(2,1)S(1)}, u32[]{:S(2)}, u32[]{:S(2)}) collective-permute-start(f16[64,768]{1,0:T(8,128)(2,1)S(1)} %slice_convert_fusion.9), channel_id=1, source_target_pairs={{0,64},{1,65},{2,66},{3,67},{4,68},{5,69},{6,70},{7,71},{64,0},{65... | collective-permute-start | bytes 294920 | tf_op jit(solution)/shard_map/ppermute | solution.py:36
  98.0 1.3 collective-permute-start.18
  99.3 10.0 %collective-permute-start.35 = (bf16[256,512]{1,0:T(8,128)(2,1)S(1)}, bf16[256,512]{1,0:T(8,128)(2,1)S(1)}, u32[]{:S(2)}, u32[]{:S(2)}) collective-permute-start(bf16[256,512]{1,0:T(8,128)(2,1)S(1)} %pad_maximum_fusion.4.refs_4_), channel_id=1, source_target_pairs={{0,1},{1,0},{2,3},{3,2},{4,5},{5,4},{6,7},{7,6},{64,65},{65,64},{6... | collective-permute-start | bytes 786440 | tf_op jit(solution)/shard_map/ppermute | solution.py:36
  111.4 1.8 collective-permute-start.37
  113.5 4.9 %collective-permute-done.10 = bf16[64,768]{1,0:T(8,128)(2,1)S(1)} collective-permute-done((bf16[64,768]{1,0:T(8,128)(2,1)S(1)}, bf16[64,768]{1,0:T(8,128)(2,1)S(1)}, u32[]{:S(2)}, u32[]{:S(2)}) %collective-permute-start.10) | collective-permute-done | bytes 98336 | tf_op jit(solution)/shard_map/ppermute | solution.py:36
  119.5 3.5 %collective-permute-done.19 = bf16[64,768]{1,0:T(8,128)(2,1)S(1)} collective-permute-done((bf16[64,768]{1,0:T(8,128)(2,1)S(1)}, bf16[64,768]{1,0:T(8,128)(2,1)S(1)}, u32[]{:S(2)}, u32[]{:S(2)}) %collective-permute-start.19) | collective-permute-done | bytes 98336 | tf_op jit(solution)/shard_map/ppermute | solution.py:36
  124.2 2.0 collective-permute-start.20
  126.2 2.6 %collective-permute-done.11 = bf16[128,768]{1,0:T(8,128)(2,1)S(1)} collective-permute-done((bf16[128,768]{1,0:T(8,128)(2,1)S(1)}, bf16[128,768]{1,0:T(8,128)(2,1)S(1)}, u32[]{:S(2)}, u32[]{:S(2)}) %collective-permute-start.11) | collective-permute-done | bytes 196640 | tf_op jit(solution)/shard_map/ppermute | solution.py:36
  130.3 1.6 collective-permute-start.38
  131.9 1.6 collective-permute-done.40
  133.5 4.3 %collective-permute-start.31 = (bf16[256,768]{1,0:T(8,128)(2,1)S(1)}, bf16[256,768]{1,0:T(8,128)(2,1)S(1)}, u32[]{:S(2)}, u32[]{:S(2)}) collective-permute-start(bf16[256,768]{1,0:T(8,128)(2,1)S(1)} %pad_maximum_fusion.refs_0_), channel_id=1, source_target_pairs={{0,1},{1,0},{2,3},{3,2},{4,5},{5,4},{6,7},{7,6},{64,65},{65,64},{6... | collective-permute-start | bytes 1179656 | tf_op jit(solution)/shard_map/ppermute | solution.py:36
  137.8 2.2 %collective-permute-start.12 = (bf16[256,768]{1,0:T(8,128)(2,1)S(1)}, bf16[256,768]{1,0:T(8,128)(2,1)S(1)}, u32[]{:S(2)}, u32[]{:S(2)}) collective-permute-start(bf16[256,768]{1,0:T(8,128)(2,1)S(1)} %pad_maximum_fusion.refs_0_), channel_id=1, source_target_pairs={{0,64},{1,65},{2,66},{3,67},{4,68},{5,69},{6,70},{7,71},{64,0},{65... | collective-permute-start | bytes 1179656 | tf_op jit(solution)/shard_map/ppermute | solution.py:36
  142.1 12.2 %collective-permute-done.41 = bf16[128,768]{1,0:T(8,128)(2,1)S(1)} collective-permute-done((bf16[128,768]{1,0:T(8,128)(2,1)S(1)}, bf16[128,768]{1,0:T(8,128)(2,1)S(1)}, u32[]{:S(2)}, u32[]{:S(2)}) %collective-permute-start.41) | collective-permute-done | bytes 196640 | tf_op jit(solution)/shard_map/ppermute | solution.py:36
  154.3 2.2 %collective-permute-start.39 = (bf16[256,768]{1,0:T(8,128)(2,1)S(1)}, bf16[256,768]{1,0:T(8,128)(2,1)S(1)}, u32[]{:S(2)}, u32[]{:S(2)}) collective-permute-start(bf16[256,768]{1,0:T(8,128)(2,1)S(1)} %pad_maximum_fusion.2.refs_0_), channel_id=1, source_target_pairs={{0,64},{1,65},{2,66},{3,67},{4,68},{5,69},{6,70},{7,71},{64,0},{65... | collective-permute-start | bytes 1179656 | tf_op jit(solution)/shard_map/ppermute | solution.py:36
  158.2 7.4 %collective-permute-done.39.refs_1_ = bf16[256,768]{1,0:T(8,128)(2,1)S(1)} collective-permute-done((bf16[256,768]{1,0:T(8,128)(2,1)S(1)}, bf16[256,768]{1,0:T(8,128)(2,1)S(1)}, u32[]{:S(2)}, u32[]{:S(2)}) %collective-permute-start.39) | collective-permute-done | bytes 393248 | tf_op jit(solution)/shard_map/ppermute | solution.py:36
  165.6 1.6 collective-permute-start.45
  167.2 2.0 collective-permute-start.46
  169.8 3.9 %back_messages.1 = (bf16[512,4096]{1,0:T(8,128)(2,1)S(1)}, bf16[64,2,16,128]{3,2,1,0:T(8,128)(2,1)}) custom-call(s32[2]{0:T(128)S(1)} %pad_add_fusion.at, bf16[256,768]{1,0:T(8,128)(2,1)S(1)} %pad_maximum_fusion.refs_0_, bf16[256,768]{1,0:T(8,128)(2,1)S(1)} %collective-permute-done.12.refs_1_, bf16[256,768]{1,0:T(8,128)(2,1)S(1)} %pad_maximum_fusion.1.refs_2_, ...), custom_call_target="tpu_custom_call" | custom-call | flops 2147483648 | bytes 12582912 | tf_op jit(solution)/shard_map/back_messages/pallas_call | solution.py:183
  173.7 2.0 copy-done.5
  175.7 5.4 %all-to-all-start.1 = ((bf16[128,16,128]{2,1,0:T(8,128)(2,1)}), bf16[128,16,128]{2,1,0:T(8,128)(2,1)}, u32[]{:S(2)}, u32[]{:S(2)}) async-start(bf16[128,16,128]{2,1,0:T(8,128)(2,1)} %bitcast.8), calls=%async_computation.1 | async-start | bytes 1048576 | tf_op jit(solution)/shard_map/all_to_all | solution.py:314
  182.6 2.2 %copy-done.6 = bf16[512,4096]{1,0:T(8,128)(2,1)S(1)} copy-done((bf16[512,4096]{1,0:T(8,128)(2,1)S(1)}, bf16[512,4096]{1,0:T(8,128)(2,1)}, u32[]{:S(2)}) %copy-start.6) | copy-done | bytes 4194328
  184.7 6.3 %grad_in.1 = f32[512,4096]{1,0:T(8,128)} custom-call(bf16[512,512]{1,0:T(8,128)(2,1)S(1)} %bitcast.10, bf16[512,4096]{1,0:T(8,128)(2,1)S(1)} %copy-done.6), custom_call_target="tpu_custom_call" | custom-call | flops 2147483648 | bytes 12582912 | tf_op jit(solution)/shard_map/grad_in/pallas_call | solution.py:198
  191.1 8.2 %grad_out.1 = f32[4096,512]{1,0:T(8,128)} custom-call(s32[2]{0:T(128)S(1)} %pad_add_fusion.at, bf16[256,768]{1,0:T(8,128)(2,1)S(1)} %pad_maximum_fusion.2.refs_0_, bf16[256,768]{1,0:T(8,128)(2,1)S(1)} %collective-permute-done.39.refs_1_, bf16[256,768]{1,0:T(8,128)(2,1)S(1)} %pad_maximum_fusion.3.refs_2_, ...), custom_call_target="tpu_custom_call" | custom-call | flops 2147483648 | bytes 12582912 | tf_op jit(solution)/shard_map/grad_out/pallas_call | solution.py:222
  199.3 2.3 %grad_act.1 = f32[4,8192]{1,0:T(4,128)} custom-call(bf16[2,8,8,16,128]{4,3,2,1,0:T(8,128)(2,1)} %bitcast.9.x, bf16[4,8192]{1,0:T(4,128)(2,1)} %act.3, f32[1,8192]{1,0:T(1,128)} %bitcast.15), custom_call_target="tpu_custom_call" | custom-call | tf_op jit(solution)/shard_map/grad_act/pallas_call | solution.py:262
  (141 shorter events, 23.2 us)
Async XLA Ops:
  0.6 33.8 %collective-permute-start.1 = (bf16[4096,512]{1,0:T(8,128)(2,1)}, bf16[4096,512]{1,0:T(8,128)(2,1)}, u32[]{:S(2)}, u32[]{:S(2)}) collective-permute-start(bf16[4096,512]{1,0:T(8,128)(2,1)} %w.10), channel_id=1, source_target_pairs={{0,1},{1,0},{2,3},{3,2},{4,5},{5,4},{6,7},{7,6},{64,65},{65,64},{6... | collective-permute-start | bytes 12582920 | tf_op jit(solution)/shard_map/ppermute | solution.py:36
  2.1 47.1 %collective-permute-start.6 = (bf16[512,4096]{1,0:T(8,128)(2,1)}, bf16[512,4096]{1,0:T(8,128)(2,1)}, u32[]{:S(2)}, u32[]{:S(2)}) collective-permute-start(bf16[512,4096]{1,0:T(8,128)(2,1)} %refs_12_.2), channel_id=1, source_target_pairs={{0,1},{1,0},{2,3},{3,2},{4,5},{5,4},{6,7},{7,6},{64,65},{65,64},{6... | collective-permute-start | bytes 12582920 | tf_op jit(solution)/shard_map/ppermute | solution.py:36
  29.4 5.1 %collective-permute-start = (bf16[512,512]{1,0:T(8,128)(2,1)}, bf16[512,512]{1,0:T(8,128)(2,1)S(1)}, u32[]{:S(2)}, u32[]{:S(2)}) collective-permute-start(bf16[512,512]{1,0:T(8,128)(2,1)} %refs_12_.3), channel_id=1, source_target_pairs={{0,1},{1,0},{2,3},{3,2},{4,5},{5,4},{6,7},{7,6},{64,65},{65,64},{6... | collective-permute-start | bytes 1572872 | tf_op jit(solution)/shard_map/ppermute | solution.py:36
  39.3 22.3 %collective-permute-start.22 = (f16[256,512]{1,0:T(8,128)(2,1)S(1)}, f16[256,512]{1,0:T(8,128)(2,1)S(1)}, u32[]{:S(2)}, u32[]{:S(2)}) collective-permute-start(f16[256,512]{1,0:T(8,128)(2,1)S(1)} %convert_element_type.120), channel_id=1, source_target_pairs={{0,64},{1,65},{2,66},{3,67},{4,68},{5,69},{6,70},{7,71},{64,0},{65... | collective-permute-start | bytes 786440 | tf_op jit(solution)/shard_map/ppermute | solution.py:36
  47.5 26.2 %collective-permute-start.2 = (f16[256,768]{1,0:T(8,128)(2,1)S(1)}, f16[256,768]{1,0:T(8,128)(2,1)S(1)}, u32[]{:S(2)}, u32[]{:S(2)}) collective-permute-start(f16[256,768]{1,0:T(8,128)(2,1)S(1)} %convert_element_type.102), channel_id=1, source_target_pairs={{0,2},{1,3},{2,0},{3,1},{4,6},{5,7},{6,4},{7,5},{64,66},{65,67},{6... | collective-permute-start | bytes 1179656 | tf_op jit(solution)/shard_map/ppermute | solution.py:36
  47.8 27.8 %collective-permute-start.13 = (f16[256,768]{1,0:T(8,128)(2,1)S(1)}, f16[256,768]{1,0:T(8,128)(2,1)S(1)}, u32[]{:S(2)}, u32[]{:S(2)}) collective-permute-start(f16[256,768]{1,0:T(8,128)(2,1)S(1)} %convert_element_type.111), channel_id=1, source_target_pairs={{0,6},{1,7},{2,4},{3,5},{4,2},{5,3},{6,0},{7,1},{64,70},{65,71},{6... | collective-permute-start | bytes 1179656 | tf_op jit(solution)/shard_map/ppermute | solution.py:36
  51.9 11.9 %collective-permute-start.25 = (f16[256,512]{1,0:T(8,128)(2,1)S(1)}, f16[256,512]{1,0:T(8,128)(2,1)S(1)}, u32[]{:S(2)}, u32[]{:S(2)}) collective-permute-start(f16[256,512]{1,0:T(8,128)(2,1)S(1)} %convert_element_type.124), channel_id=1, source_target_pairs={{0,64},{1,65},{2,66},{3,67},{4,68},{5,69},{6,70},{7,71},{64,0},{65... | collective-permute-start | bytes 786440 | tf_op jit(solution)/shard_map/ppermute | solution.py:36
  60.9 17.3 %collective-permute-start.7 = (f16[256,768]{1,0:T(8,128)(2,1)S(1)}, f16[256,768]{1,0:T(8,128)(2,1)S(1)}, u32[]{:S(2)}, u32[]{:S(2)}) collective-permute-start(f16[256,768]{1,0:T(8,128)(2,1)S(1)} %convert_element_type.106), channel_id=1, source_target_pairs={{0,2},{1,3},{2,0},{3,1},{4,6},{5,7},{6,4},{7,5},{64,66},{65,67},{6... | collective-permute-start | bytes 1179656 | tf_op jit(solution)/shard_map/ppermute | solution.py:36
  61.6 18.2 %collective-permute-start.16 = (f16[256,768]{1,0:T(8,128)(2,1)S(1)}, f16[256,768]{1,0:T(8,128)(2,1)S(1)}, u32[]{:S(2)}, u32[]{:S(2)}) collective-permute-start(f16[256,768]{1,0:T(8,128)(2,1)S(1)} %convert_element_type.115), channel_id=1, source_target_pairs={{0,6},{1,7},{2,4},{3,5},{4,2},{5,3},{6,0},{7,1},{64,70},{65,71},{6... | collective-permute-start | bytes 1179656 | tf_op jit(solution)/shard_map/ppermute | solution.py:36
  63.8 9.2 %collective-permute-start.23 = (f16[128,512]{1,0:T(8,128)(2,1)S(1)}, f16[128,512]{1,0:T(8,128)(2,1)S(1)}, u32[]{:S(2)}, u32[]{:S(2)}) collective-permute-start(f16[128,512]{1,0:T(8,128)(2,1)S(1)} %slice_convert_fusion.5), channel_id=1, source_target_pairs={{0,2},{1,3},{2,0},{3,1},{4,6},{5,7},{6,4},{7,5},{64,66},{65,67},{6... | collective-permute-start | bytes 393224 | tf_op jit(solution)/shard_map/ppermute | solution.py:36
  73.7 7.6 %collective-permute-start.24 = (f16[64,512]{1,0:T(8,128)(2,1)S(1)}, f16[64,512]{1,0:T(8,128)(2,1)S(1)}, u32[]{:S(2)}, u32[]{:S(2)}) collective-permute-start(f16[64,512]{1,0:T(8,128)(2,1)S(1)} %slice_convert_fusion.11), channel_id=1, source_target_pairs={{0,6},{1,7},{2,4},{3,5},{4,2},{5,3},{6,0},{7,1},{64,70},{65,71},{6... | collective-permute-start | bytes 196616 | tf_op jit(solution)/shard_map/ppermute | solution.py:36
  75.7 17.0 %collective-permute-start.3 = (f16[128,768]{1,0:T(8,128)(2,1)S(1)}, f16[128,768]{1,0:T(8,128)(2,1)S(1)}, u32[]{:S(2)}, u32[]{:S(2)}) collective-permute-start(f16[128,768]{1,0:T(8,128)(2,1)S(1)} %slice_convert_fusion.3), channel_id=1, source_target_pairs={{0,6},{1,7},{2,4},{3,5},{4,2},{5,3},{6,0},{7,1},{64,70},{65,71},{6... | collective-permute-start | bytes 589832 | tf_op jit(solution)/shard_map/ppermute | solution.py:36
  76.8 17.2 %collective-permute-start.14 = (f16[128,768]{1,0:T(8,128)(2,1)S(1)}, f16[128,768]{1,0:T(8,128)(2,1)S(1)}, u32[]{:S(2)}, u32[]{:S(2)}) collective-permute-start(f16[128,768]{1,0:T(8,128)(2,1)S(1)} %slice_convert_fusion.1), channel_id=1, source_target_pairs={{0,64},{1,65},{2,66},{3,67},{4,68},{5,69},{6,70},{7,71},{64,0},{65... | collective-permute-start | bytes 589832 | tf_op jit(solution)/shard_map/ppermute | solution.py:36
  78.2 4.7 %collective-permute-start.27 = (f16[64,512]{1,0:T(8,128)(2,1)S(1)}, f16[64,512]{1,0:T(8,128)(2,1)S(1)}, u32[]{:S(2)}, u32[]{:S(2)}) collective-permute-start(f16[64,512]{1,0:T(8,128)(2,1)S(1)} %slice_convert_fusion.10), channel_id=1, source_target_pairs={{0,6},{1,7},{2,4},{3,5},{4,2},{5,3},{6,0},{7,1},{64,70},{65,71},{6... | collective-permute-start | bytes 196616 | tf_op jit(solution)/shard_map/ppermute | solution.py:36
  79.8 17.6 %collective-permute-start.8 = (f16[128,768]{1,0:T(8,128)(2,1)S(1)}, f16[128,768]{1,0:T(8,128)(2,1)S(1)}, u32[]{:S(2)}, u32[]{:S(2)}) collective-permute-start(f16[128,768]{1,0:T(8,128)(2,1)S(1)} %slice_convert_fusion.2), channel_id=1, source_target_pairs={{0,6},{1,7},{2,4},{3,5},{4,2},{5,3},{6,0},{7,1},{64,70},{65,71},{6... | collective-permute-start | bytes 589832 | tf_op jit(solution)/shard_map/ppermute | solution.py:36
  83.0 4.7 %collective-permute-start.43 = (bf16[64,512]{1,0:T(8,128)(2,1)S(1)}, bf16[64,512]{1,0:T(8,128)(2,1)S(1)}, u32[]{:S(2)}, u32[]{:S(2)}) collective-permute-start(bf16[64,512]{1,0:T(8,128)(2,1)S(1)} %get-tuple-element.35), channel_id=1, source_target_pairs={{0,64},{1,65},{2,66},{3,67},{4,68},{5,69},{6,70},{7,71},{64,0},{65... | collective-permute-start | bytes 196616 | tf_op jit(solution)/shard_map/ppermute | solution.py:36
  85.6 12.0 %collective-permute-start.17 = (f16[128,768]{1,0:T(8,128)(2,1)S(1)}, f16[128,768]{1,0:T(8,128)(2,1)S(1)}, u32[]{:S(2)}, u32[]{:S(2)}) collective-permute-start(f16[128,768]{1,0:T(8,128)(2,1)S(1)} %slice_convert_fusion), channel_id=1, source_target_pairs={{0,64},{1,65},{2,66},{3,67},{4,68},{5,69},{6,70},{7,71},{64,0},{65... | collective-permute-start | bytes 589832 | tf_op jit(solution)/shard_map/ppermute | solution.py:36
  92.4 7.0 %collective-permute-start.44 = (bf16[128,512]{1,0:T(8,128)(2,1)S(1)}, bf16[128,512]{1,0:T(8,128)(2,1)S(1)}, u32[]{:S(2)}, u32[]{:S(2)}) collective-permute-start(bf16[128,512]{1,0:T(8,128)(2,1)S(1)} %pad_maximum_fusion.11), channel_id=1, source_target_pairs={{0,2},{1,3},{2,0},{3,1},{4,6},{5,7},{6,4},{7,5},{64,66},{65,67},{6... | collective-permute-start | bytes 393224 | tf_op jit(solution)/shard_map/ppermute | solution.py:36
  92.7 5.3 %collective-permute-start.29 = (bf16[128,512]{1,0:T(8,128)(2,1)S(1)}, bf16[128,512]{1,0:T(8,128)(2,1)S(1)}, u32[]{:S(2)}, u32[]{:S(2)}) collective-permute-start(bf16[128,512]{1,0:T(8,128)(2,1)S(1)} %pad_maximum_fusion.10), channel_id=1, source_target_pairs={{0,2},{1,3},{2,0},{3,1},{4,6},{5,7},{6,4},{7,5},{64,66},{65,67},{6... | collective-permute-start | bytes 393224 | tf_op jit(solution)/shard_map/ppermute | solution.py:36
  94.0 15.4 %collective-permute-start.4 = (f16[64,768]{1,0:T(8,128)(2,1)S(1)}, f16[64,768]{1,0:T(8,128)(2,1)S(1)}, u32[]{:S(2)}, u32[]{:S(2)}) collective-permute-start(f16[64,768]{1,0:T(8,128)(2,1)S(1)} %slice_convert_fusion.9), channel_id=1, source_target_pairs={{0,64},{1,65},{2,66},{3,67},{4,68},{5,69},{6,70},{7,71},{64,0},{65... | collective-permute-start | bytes 294920 | tf_op jit(solution)/shard_map/ppermute | solution.py:36
  97.4 13.9 %collective-permute-start.15 = (f16[64,768]{1,0:T(8,128)(2,1)S(1)}, f16[64,768]{1,0:T(8,128)(2,1)S(1)}, u32[]{:S(2)}, u32[]{:S(2)}) collective-permute-start(f16[64,768]{1,0:T(8,128)(2,1)S(1)} %slice_convert_fusion.7), channel_id=1, source_target_pairs={{0,2},{1,3},{2,0},{3,1},{4,6},{5,7},{6,4},{7,5},{64,66},{65,67},{6... | collective-permute-start | bytes 294920 | tf_op jit(solution)/shard_map/ppermute | solution.py:36
  97.6 13.1 %collective-permute-start.9 = (f16[64,768]{1,0:T(8,128)(2,1)S(1)}, f16[64,768]{1,0:T(8,128)(2,1)S(1)}, u32[]{:S(2)}, u32[]{:S(2)}) collective-permute-start(f16[64,768]{1,0:T(8,128)(2,1)S(1)} %slice_convert_fusion.8), channel_id=1, source_target_pairs={{0,64},{1,65},{2,66},{3,67},{4,68},{5,69},{6,70},{7,71},{64,0},{65... | collective-permute-start | bytes 294920 | tf_op jit(solution)/shard_map/ppermute | solution.py:36
  98.0 15.2 %collective-permute-start.18 = (f16[64,768]{1,0:T(8,128)(2,1)S(1)}, f16[64,768]{1,0:T(8,128)(2,1)S(1)}, u32[]{:S(2)}, u32[]{:S(2)}) collective-permute-start(f16[64,768]{1,0:T(8,128)(2,1)S(1)} %slice_convert_fusion.6), channel_id=1, source_target_pairs={{0,2},{1,3},{2,0},{3,1},{4,6},{5,7},{6,4},{7,5},{64,66},{65,67},{6... | collective-permute-start | bytes 294920 | tf_op jit(solution)/shard_map/ppermute | solution.py:36
  99.3 38.5 %collective-permute-start.35 = (bf16[256,512]{1,0:T(8,128)(2,1)S(1)}, bf16[256,512]{1,0:T(8,128)(2,1)S(1)}, u32[]{:S(2)}, u32[]{:S(2)}) collective-permute-start(bf16[256,512]{1,0:T(8,128)(2,1)S(1)} %pad_maximum_fusion.4.refs_4_), channel_id=1, source_target_pairs={{0,1},{1,0},{2,3},{3,2},{4,5},{5,4},{6,7},{7,6},{64,65},{65,64},{6... | collective-permute-start | bytes 786440 | tf_op jit(solution)/shard_map/ppermute | solution.py:36
  109.4 30.6 %collective-permute-start.30 = (bf16[256,512]{1,0:T(8,128)(2,1)S(1)}, bf16[256,512]{1,0:T(8,128)(2,1)S(1)}, u32[]{:S(2)}, u32[]{:S(2)}) collective-permute-start(bf16[256,512]{1,0:T(8,128)(2,1)S(1)} %pad_maximum_fusion.4.refs_4_), channel_id=1, source_target_pairs={{0,6},{1,7},{2,4},{3,5},{4,2},{5,3},{6,0},{7,1},{64,70},{65,71},{6... | collective-permute-start | bytes 786440 | tf_op jit(solution)/shard_map/ppermute | solution.py:36
  110.7 29.3 %collective-permute-start.50 = (bf16[256,512]{1,0:T(8,128)(2,1)S(1)}, bf16[256,512]{1,0:T(8,128)(2,1)S(1)}, u32[]{:S(2)}, u32[]{:S(2)}) collective-permute-start(bf16[256,512]{1,0:T(8,128)(2,1)S(1)} %pad_maximum_fusion.5.refs_4_), channel_id=1, source_target_pairs={{0,1},{1,0},{2,3},{3,2},{4,5},{5,4},{6,7},{7,6},{64,65},{65,64},{6... | collective-permute-start | bytes 786440 | tf_op jit(solution)/shard_map/ppermute | solution.py:36
  111.4 12.9 %collective-permute-start.37 = (bf16[64,768]{1,0:T(8,128)(2,1)S(1)}, bf16[64,768]{1,0:T(8,128)(2,1)S(1)}, u32[]{:S(2)}, u32[]{:S(2)}) collective-permute-start(bf16[64,768]{1,0:T(8,128)(2,1)S(1)} %get-tuple-element.33), channel_id=1, source_target_pairs={{0,2},{1,3},{2,0},{3,1},{4,6},{5,7},{6,4},{7,5},{64,66},{65,67},{6... | collective-permute-start | bytes 294920 | tf_op jit(solution)/shard_map/ppermute | solution.py:36
  113.2 5.2 %collective-permute-start.10 = (bf16[64,768]{1,0:T(8,128)(2,1)S(1)}, bf16[64,768]{1,0:T(8,128)(2,1)S(1)}, u32[]{:S(2)}, u32[]{:S(2)}) collective-permute-start(bf16[64,768]{1,0:T(8,128)(2,1)S(1)} %get-tuple-element.34), channel_id=1, source_target_pairs={{0,2},{1,3},{2,0},{3,1},{4,6},{5,7},{6,4},{7,5},{64,66},{65,67},{6... | collective-permute-start | bytes 294920 | tf_op jit(solution)/shard_map/ppermute | solution.py:36
  123.1 5.7 %collective-permute-start.11 = (bf16[128,768]{1,0:T(8,128)(2,1)S(1)}, bf16[128,768]{1,0:T(8,128)(2,1)S(1)}, u32[]{:S(2)}, u32[]{:S(2)}) collective-permute-start(bf16[128,768]{1,0:T(8,128)(2,1)S(1)} %pad_maximum_fusion.6), channel_id=1, source_target_pairs={{0,6},{1,7},{2,4},{3,5},{4,2},{5,3},{6,0},{7,1},{64,70},{65,71},{6... | collective-permute-start | bytes 589832 | tf_op jit(solution)/shard_map/ppermute | solution.py:36
  124.2 6.1 %collective-permute-start.20 = (bf16[128,768]{1,0:T(8,128)(2,1)S(1)}, bf16[128,768]{1,0:T(8,128)(2,1)S(1)}, u32[]{:S(2)}, u32[]{:S(2)}) collective-permute-start(bf16[128,768]{1,0:T(8,128)(2,1)S(1)} %pad_maximum_fusion.7), channel_id=1, source_target_pairs={{0,64},{1,65},{2,66},{3,67},{4,68},{5,69},{6,70},{7,71},{64,0},{65... | collective-permute-start | bytes 589832 | tf_op jit(solution)/shard_map/ppermute | solution.py:36
  130.3 11.2 %collective-permute-start.38 = (bf16[128,768]{1,0:T(8,128)(2,1)S(1)}, bf16[128,768]{1,0:T(8,128)(2,1)S(1)}, u32[]{:S(2)}, u32[]{:S(2)}) collective-permute-start(bf16[128,768]{1,0:T(8,128)(2,1)S(1)} %pad_maximum_fusion.8), channel_id=1, source_target_pairs={{0,6},{1,7},{2,4},{3,5},{4,2},{5,3},{6,0},{7,1},{64,70},{65,71},{6... | collective-permute-start | bytes 589832 | tf_op jit(solution)/shard_map/ppermute | solution.py:36
  133.5 24.1 %collective-permute-start.31 = (bf16[256,768]{1,0:T(8,128)(2,1)S(1)}, bf16[256,768]{1,0:T(8,128)(2,1)S(1)}, u32[]{:S(2)}, u32[]{:S(2)}) collective-permute-start(bf16[256,768]{1,0:T(8,128)(2,1)S(1)} %pad_maximum_fusion.refs_0_), channel_id=1, source_target_pairs={{0,1},{1,0},{2,3},{3,2},{4,5},{5,4},{6,7},{7,6},{64,65},{65,64},{6... | collective-permute-start | bytes 1179656 | tf_op jit(solution)/shard_map/ppermute | solution.py:36
  137.8 19.8 %collective-permute-start.12 = (bf16[256,768]{1,0:T(8,128)(2,1)S(1)}, bf16[256,768]{1,0:T(8,128)(2,1)S(1)}, u32[]{:S(2)}, u32[]{:S(2)}) collective-permute-start(bf16[256,768]{1,0:T(8,128)(2,1)S(1)} %pad_maximum_fusion.refs_0_), channel_id=1, source_target_pairs={{0,64},{1,65},{2,66},{3,67},{4,68},{5,69},{6,70},{7,71},{64,0},{65... | collective-permute-start | bytes 1179656 | tf_op jit(solution)/shard_map/ppermute | solution.py:36
  140.0 17.9 %collective-permute-start.21 = (bf16[256,768]{1,0:T(8,128)(2,1)S(1)}, bf16[256,768]{1,0:T(8,128)(2,1)S(1)}, u32[]{:S(2)}, u32[]{:S(2)}) collective-permute-start(bf16[256,768]{1,0:T(8,128)(2,1)S(1)} %pad_maximum_fusion.1.refs_2_), channel_id=1, source_target_pairs={{0,2},{1,3},{2,0},{3,1},{4,6},{5,7},{6,4},{7,5},{64,66},{65,67},{6... | collective-permute-start | bytes 1179656 | tf_op jit(solution)/shard_map/ppermute | solution.py:36
  140.7 13.6 %collective-permute-start.41 = (bf16[128,768]{1,0:T(8,128)(2,1)S(1)}, bf16[128,768]{1,0:T(8,128)(2,1)S(1)}, u32[]{:S(2)}, u32[]{:S(2)}) collective-permute-start(bf16[128,768]{1,0:T(8,128)(2,1)S(1)} %pad_maximum_fusion.9), channel_id=1, source_target_pairs={{0,64},{1,65},{2,66},{3,67},{4,68},{5,69},{6,70},{7,71},{64,0},{65... | collective-permute-start | bytes 589832 | tf_op jit(solution)/shard_map/ppermute | solution.py:36
  141.5 15.0 %collective-permute-start.36 = (bf16[256,512]{1,0:T(8,128)(2,1)S(1)}, bf16[256,512]{1,0:T(8,128)(2,1)S(1)}, u32[]{:S(2)}, u32[]{:S(2)}) collective-permute-start(bf16[256,512]{1,0:T(8,128)(2,1)S(1)} %collective-permute-done.30.refs_5_), channel_id=1, source_target_pairs={{0,1},{1,0},{2,3},{3,2},{4,5},{5,4},{6,7},{7,6},{64,65},{65,64},{6... | collective-permute-start | bytes 786440 | tf_op jit(solution)/shard_map/ppermute | solution.py:36
  154.3 11.4 %collective-permute-start.39 = (bf16[256,768]{1,0:T(8,128)(2,1)S(1)}, bf16[256,768]{1,0:T(8,128)(2,1)S(1)}, u32[]{:S(2)}, u32[]{:S(2)}) collective-permute-start(bf16[256,768]{1,0:T(8,128)(2,1)S(1)} %pad_maximum_fusion.2.refs_0_), channel_id=1, source_target_pairs={{0,64},{1,65},{2,66},{3,67},{4,68},{5,69},{6,70},{7,71},{64,0},{65... | collective-permute-start | bytes 1179656 | tf_op jit(solution)/shard_map/ppermute | solution.py:36
  156.5 10.7 %collective-permute-start.33 = (bf16[256,768]{1,0:T(8,128)(2,1)S(1)}, bf16[256,768]{1,0:T(8,128)(2,1)S(1)}, u32[]{:S(2)}, u32[]{:S(2)}) collective-permute-start(bf16[256,768]{1,0:T(8,128)(2,1)S(1)} %pad_maximum_fusion.1.refs_2_), channel_id=1, source_target_pairs={{0,1},{1,0},{2,3},{3,2},{4,5},{5,4},{6,7},{7,6},{64,65},{65,64},{6... | collective-permute-start | bytes 1179656 | tf_op jit(solution)/shard_map/ppermute | solution.py:36
  157.6 11.5 %collective-permute-start.42 = (bf16[256,768]{1,0:T(8,128)(2,1)S(1)}, bf16[256,768]{1,0:T(8,128)(2,1)S(1)}, u32[]{:S(2)}, u32[]{:S(2)}) collective-permute-start(bf16[256,768]{1,0:T(8,128)(2,1)S(1)} %pad_maximum_fusion.3.refs_2_), channel_id=1, source_target_pairs={{0,2},{1,3},{2,0},{3,1},{4,6},{5,7},{6,4},{7,5},{64,66},{65,67},{6... | collective-permute-start | bytes 1179656 | tf_op jit(solution)/shard_map/ppermute | solution.py:36
  157.7 11.6 %collective-permute-start.32 = (bf16[256,768]{1,0:T(8,128)(2,1)S(1)}, bf16[256,768]{1,0:T(8,128)(2,1)S(1)}, u32[]{:S(2)}, u32[]{:S(2)}) collective-permute-start(bf16[256,768]{1,0:T(8,128)(2,1)S(1)} %collective-permute-done.12.refs_1_), channel_id=1, source_target_pairs={{0,1},{1,0},{2,3},{3,2},{4,5},{5,4},{6,7},{7,6},{64,65},{65,64},{6... | collective-permute-start | bytes 1179656 | tf_op jit(solution)/shard_map/ppermute | solution.py:36
  157.8 11.8 %collective-permute-start.34 = (bf16[256,768]{1,0:T(8,128)(2,1)S(1)}, bf16[256,768]{1,0:T(8,128)(2,1)S(1)}, u32[]{:S(2)}, u32[]{:S(2)}) collective-permute-start(bf16[256,768]{1,0:T(8,128)(2,1)S(1)} %collective-permute-done.21.refs_3_), channel_id=1, source_target_pairs={{0,1},{1,0},{2,3},{3,2},{4,5},{5,4},{6,7},{7,6},{64,65},{65,64},{6... | collective-permute-start | bytes 1179656 | tf_op jit(solution)/shard_map/ppermute | solution.py:36
  165.6 15.5 %collective-permute-start.45 = (bf16[256,512]{1,0:T(8,128)(2,1)S(1)}, bf16[256,512]{1,0:T(8,128)(2,1)}, u32[]{:S(2)}, u32[]{:S(2)}) collective-permute-start(bf16[256,512]{1,0:T(8,128)(2,1)S(1)} %pad_maximum_fusion.5.refs_4_), channel_id=1, source_target_pairs={{0,6},{1,7},{2,4},{3,5},{4,2},{5,3},{6,0},{7,1},{64,70},{65,71},{6... | collective-permute-start | bytes 786440 | tf_op jit(solution)/shard_map/ppermute | solution.py:36
  167.2 23.8 %collective-permute-start.46 = (bf16[256,768]{1,0:T(8,128)(2,1)S(1)}, bf16[256,768]{1,0:T(8,128)(2,1)}, u32[]{:S(2)}, u32[]{:S(2)}) collective-permute-start(bf16[256,768]{1,0:T(8,128)(2,1)S(1)} %pad_maximum_fusion.2.refs_0_), channel_id=1, source_target_pairs={{0,1},{1,0},{2,3},{3,2},{4,5},{5,4},{6,7},{7,6},{64,65},{65,64},{6... | collective-permute-start | bytes 1179656 | tf_op jit(solution)/shard_map/ppermute | solution.py:36
  169.2 21.9 %collective-permute-start.48 = (bf16[256,768]{1,0:T(8,128)(2,1)S(1)}, bf16[256,768]{1,0:T(8,128)(2,1)}, u32[]{:S(2)}, u32[]{:S(2)}) collective-permute-start(bf16[256,768]{1,0:T(8,128)(2,1)S(1)} %pad_maximum_fusion.3.refs_2_), channel_id=1, source_target_pairs={{0,1},{1,0},{2,3},{3,2},{4,5},{5,4},{6,7},{7,6},{64,65},{65,64},{6... | collective-permute-start | bytes 1179656 | tf_op jit(solution)/shard_map/ppermute | solution.py:36
  169.2 21.8 %collective-permute-start.47 = (bf16[256,768]{1,0:T(8,128)(2,1)S(1)}, bf16[256,768]{1,0:T(8,128)(2,1)}, u32[]{:S(2)}, u32[]{:S(2)}) collective-permute-start(bf16[256,768]{1,0:T(8,128)(2,1)S(1)} %collective-permute-done.39.refs_1_), channel_id=1, source_target_pairs={{0,1},{1,0},{2,3},{3,2},{4,5},{5,4},{6,7},{7,6},{64,65},{65,64},{6... | collective-permute-start | bytes 1179656 | tf_op jit(solution)/shard_map/ppermute | solution.py:36
  169.7 21.4 %collective-permute-start.49 = (bf16[256,768]{1,0:T(8,128)(2,1)S(1)}, bf16[256,768]{1,0:T(8,128)(2,1)}, u32[]{:S(2)}, u32[]{:S(2)}) collective-permute-start(bf16[256,768]{1,0:T(8,128)(2,1)S(1)} %collective-permute-done.42.refs_3_), channel_id=1, source_target_pairs={{0,1},{1,0},{2,3},{3,2},{4,5},{5,4},{6,7},{7,6},{64,65},{65,64},{6... | collective-permute-start | bytes 1179656 | tf_op jit(solution)/shard_map/ppermute | solution.py:36
  175.7 23.6 %all-to-all-start.1 = ((bf16[128,16,128]{2,1,0:T(8,128)(2,1)}), bf16[128,16,128]{2,1,0:T(8,128)(2,1)}, u32[]{:S(2)}, u32[]{:S(2)}) async-start(bf16[128,16,128]{2,1,0:T(8,128)(2,1)} %bitcast.8), calls=%async_computation.1 | async-start | bytes 1048576 | tf_op jit(solution)/shard_map/all_to_all | solution.py:314
  181.1 9.9 %collective-permute-start.51 = (bf16[256,512]{1,0:T(8,128)(2,1)}, bf16[256,512]{1,0:T(8,128)(2,1)}, u32[]{:S(2)}, u32[]{:S(2)}) collective-permute-start(bf16[256,512]{1,0:T(8,128)(2,1)} %collective-permute-done.45.refs_5_), channel_id=1, source_target_pairs={{0,1},{1,0},{2,3},{3,2},{4,5},{5,4},{6,7},{7,6},{64,65},{65,64},{6... | collective-permute-start | bytes 786440 | tf_op jit(solution)/shard_map/ppermute | solution.py:36
  (16 other events, 87.2 us)
where the time goes:
time: 202 us
  starting transfers between devices  72.5 us (36%)
  waiting for transfers between devices  47.1 us (23%)
  Pallas kernels  46.6 us (23%)
  blocking collectives  24 us (12%)
  local copies, waits for them, and re-layouts  8.09 us (4%)
  other arithmetic  2.09 us (1%)
    ppermute x52, starting transfers between devices, swap(): return lax.ppermute(x, OWNERS, pairs)  67.2 us
    ppermute x52, waiting for transfers between devices, swap(): return lax.ppermute(x, OWNERS, pairs)  47.1 us
    all_to_all x1, blocking collectives, local(): lax.all_to_all(norm_messages(act, gain, shift).reshape(128, 16, 128), EVE...  24 us
    pallas_call x6, Pallas kernels, part_sum(): pl.pallas_call(functools.partial(part_kernel, places(ORDERS[part]), contr...  19.8 us
    pallas_call x1, Pallas kernels, grad_out_of(): pl.pallas_call(grad_out_kernel, grid=(8,), in_specs=[SCALARS] + [pl.Block...  8.23 us
    unnamed x22, local copies, waits for them, and re-layouts  7.88 us
    pallas_call x1, Pallas kernels, grad_in_of(): pl.pallas_call(grad_in_kernel, grid=(8,), in_specs=[pl.BlockSpec((512, 51...  6.29 us
    all_to_all x1, starting transfers between devices, local(): lax.all_to_all(share.reshape(128, 16, 128), EVERY, 0, 0, tiled=True)  5.37 us
  transfers between devices with their start and end apart: 53, of which 12 were waited for; matrix products, arithmetic and copies ran while one was open for 1% of the time, Pallas kernels for 22%

commit v1 on v0

v1 whole, which is shorter than its diff:
```python
import functools

import jax
import jax.numpy as jnp
from jax import lax
from jax.experimental import pallas as pl
from jax.experimental.pallas import tpu as pltpu
from jax.sharding import PartitionSpec as P

EPSILON = 1e-05
OWNERS = ("section", "tensor")
EVERY = ("section", "dp", "tensor")
BF16, F16, F32 = jnp.bfloat16, jnp.float16, jnp.float32
MIB = 1 << 20
LIFT = 16.0


def swap(x, link):
    pairs = []
    for s in range(2):
        for y in range(4):
            for c in range(2):
                if link == "core":
                    s2, y2, c2 = s, y, 1 - c
                else:
                    y2 = y ^ 1 if link & 4 else y
                    y2 = 3 - y2 if link & 2 else y2
                    s2, c2 = s ^ (link & 1), c
                pairs.append((s * 8 + y * 2 + c, s2 * 8 + y2 * 2 + c2))
    return lax.ppermute(x, OWNERS, pairs)


def lower(shape):
    return lax.broadcasted_iota(jnp.int32, shape, len(shape) - 2) % 8 < 4


SCALARS = pl.BlockSpec(memory_space=pltpu.SMEM)


def norm_kernel(act, gain, shift, out, twice):
    x = act[...].astype(F32)
    twice[0:4, :] = x
    twice[4:8, :] = x
    x = twice[...]
    center = x - jnp.mean(x, axis=1, keepdims=True)
    inverse = lax.rsqrt(jnp.mean(center * center, axis=1, keepdims=True) + EPSILON)
    twice[...] = center * inverse * gain[...] + shift[...]
    low = lower((8, 128))
    for g in range(16):
        cols = [twice[:, g * 512 + k * 128 : g * 512 + (k + 1) * 128] for k in range(4)]
        piece = jnp.concatenate([jnp.where(low, cols[0], cols[1]), jnp.where(low, cols[2], cols[3])], axis=0)
        piece = piece.astype(BF16)
        for d in range(8):
            out[g // 8, d, g % 8] = piece


def norm_messages(act, gain, shift):
    return pl.pallas_call(
        norm_kernel,
        out_shape=pltpu.HBM((2, 8, 8, 16, 128), BF16),
        scratch_shapes=[pltpu.VMEM((8, 8192), F32)],
        name="norm_messages",
    )(act, gain.reshape(1, -1), shift.reshape(1, -1))


def unfold(even, odd, k, low):
    tile = slice(k // 2 * 8, k // 2 * 8 + 8)
    e, o = even[:, tile], odd[:, tile]
    if k % 2 == 0:
        return jnp.where(low, e, pltpu.roll(o, 4, 1))
    return jnp.where(low, pltpu.roll(e, 4, 1), o)


def rows_kernel(x, out):
    even, odd = x[:, 0].astype(F32), x[:, 1].astype(F32)
    low = lower((64, 8, 128))
    for k in range(4):
        out[:, k * 128 : (k + 1) * 128] = unfold(even, odd, k, low).reshape(512, 128).astype(BF16)


ORDERS = ((4, 2, 1), (2, 1, 4), (1, 4, 2))
CUTS = (0, 768, 1536, 2048)


def places(order):
    return [sum(link for k, link in enumerate(order) if q >> (2 - k) & 1) for q in range(8)]


def multiply(step, contract, lhs, w, w_other, outs):
    dims = (((1,), (contract,)), ((), ()))
    total = lax.dot_general(lhs[0], w[...], dims, preferred_element_type=F32)
    total = (total + lax.dot_general(lhs[1], w_other[...], dims, preferred_element_type=F32)) * LIFT
    for p, order in enumerate(ORDERS):
        first, last = max(CUTS[p], step * 1024), min(CUTS[p + 1], step * 1024 + 1024)
        if first >= last:
            continue
        cols = slice(first - CUTS[p], last - CUTS[p])
        for q, j in enumerate(places(order)):
            block = total[j * 64 : (j + 1) * 64, first - step * 1024 : last - step * 1024]
            outs[p * 2 + q // 4][q % 4 * 64 : (q % 4 + 1) * 64, cols] = block


def up_kernel(at, x, x_other, w, w_other, *refs):
    outs, lhs = refs[-7:-1], refs[-1]

    @pl.when(pl.program_id(0) == 0)
    def _():
        for j in range(8):
            src = pl.multiple_of(jnp.bitwise_xor(at[0], j) * 64, 64)
            lhs[0, j * 64 : (j + 1) * 64, :] = x[pl.ds(src, 64), :]
            lhs[1, j * 64 : (j + 1) * 64, :] = x_other[pl.ds(src, 64), :]

    for step in range(2):
        pl.when(pl.program_id(0) == step)(functools.partial(multiply, step, 1, lhs, w, w_other, outs))


def pre_kernel(at, x, x_other, w, w_other, *refs):
    outs, lhs = refs[-7:-1], refs[-1]

    @pl.when(pl.program_id(0) == 0)
    def _():
        low = lower((8, 8, 128))
        for j in range(8):
            src = jnp.bitwise_xor(at[0], j) * 8
            for n, ref in enumerate((x, x_other)):
                even, odd = ref[pl.ds(src, 8), 0].astype(F32), ref[pl.ds(src, 8), 1].astype(F32)
                for k in range(4):
                    rows = unfold(even, odd, k, low).reshape(64, 128).astype(BF16)
                    lhs[n, j * 64 : (j + 1) * 64, k * 128 : (k + 1) * 128] = rows

    for step in range(2):
        pl.when(pl.program_id(0) == step)(functools.partial(multiply, step, 0, lhs, w, w_other, outs))


def chip_sum(at, x, x_other, w, w_other, after, up):
    shape = x.shape
    whole = pl.BlockSpec(shape, lambda i, at: (0,) * len(shape))
    if up:
        weight = pl.BlockSpec((1024, 512), lambda i, at: (at[1] * 2 + i, 0))
    else:
        weight = pl.BlockSpec((512, 1024), lambda i, at: (0, at[1] * 2 + i))
    shapes = [(256, CUTS[p + 1] - CUTS[p]) for p in range(3) for _ in range(2)]
    w, w_other = [pltpu.with_memory_space_constraint(v, pltpu.HBM) for v in (w, w_other)]
    outs = pl.pallas_call(
        up_kernel if up else pre_kernel,
        grid_spec=pltpu.PrefetchScalarGridSpec(
            num_scalar_prefetch=1,
            grid=(2,),
            in_specs=[whole, whole, weight, weight] + [pl.BlockSpec(memory_space=pl.ANY)] * len(after),
            out_specs=[pl.BlockSpec(shape, lambda i, at: (0, 0)) for shape in shapes],
            scratch_shapes=[pltpu.VMEM((2, 512, 512), BF16)],
        ),
        out_shape=[jax.ShapeDtypeStruct(shape, F32) for shape in shapes],
        compiler_params=pltpu.CompilerParams(vmem_limit_bytes=20 * MIB),
        cost_estimate=pl.CostEstimate(flops=2 * 512 * 1024 * 2048, bytes_accessed=9 * MIB, transcendentals=0),
        name="up_sum" if up else "pre_sum",
    )(at, x, x_other, w, w_other, *after)
    return [(outs[2 * p], outs[2 * p + 1].astype(F16)) for p in range(3)]


def halve(keep, send, link):
    total = keep + swap(send, link).astype(F32)
    rows = total.shape[0] // 2
    return total[:rows], total[rows:].astype(F16)


def reduce_pairs(up, pre, order):
    keep = jnp.stack([up[0], pre[0]])
    send = jnp.stack([up[1], pre[1]])
    total = keep + swap(send, order[1]).astype(F32)
    return total[:, :64] + swap(total[:, 64:].astype(F16), order[2]).astype(F32)


def gather_pairs(g, h, order):
    x = jnp.stack([g, h])
    x = jnp.stack([x, swap(x, order[0])])
    came = swap(x, order[1])
    return [jnp.concatenate([x[:, n], came[:, n]]).reshape(256, -1) for n in range(2)]


def assemble(at, pieces, whole):
    for h in range(2):
        base = at[1] * 2048 if h == 0 else (1 - at[1]) * 2048
        for p, order in enumerate(ORDERS):
            cols = pl.ds(pl.multiple_of(base + CUTS[p], 256), CUTS[p + 1] - CUTS[p])
            for q, j in enumerate(places(order[::-1])):
                dst = pl.multiple_of(jnp.bitwise_xor(at[0], j) * 64, 64)
                src = pieces[h * 6 + p * 2 + q // 4]
                whole[pl.ds(dst, 64), cols] = src[q % 4 * 64 : (q % 4 + 1) * 64, :]


def back_kernel(at, *refs):
    pieces, w, out, whole = refs[:12], refs[12], refs[16], refs[20]
    assemble(at, pieces, whole)
    total = jnp.zeros((512, 512), F32)
    for k in range(4):
        cols = slice(k * 1024, (k + 1) * 1024)
        total += lax.dot_general(whole[:, cols], w[:, cols], (((1,), (1,)), ((), ())), preferred_element_type=F32)
    low = lower((64, 8, 128))
    c = [total[:, k * 128 : (k + 1) * 128].reshape(64, 8, 128) for k in range(4)]
    r = [pltpu.roll(v, 4, 1) for v in c]
    for t in range(2):
        tile = slice(t * 8, t * 8 + 8)
        out[:, 0, tile] = jnp.where(low, c[2 * t], r[2 * t + 1]).astype(BF16)
        out[:, 1, tile] = jnp.where(low, r[2 * t], c[2 * t + 1]).astype(BF16)


def back_messages(at, pieces, w_in, later):
    anywhere = pl.BlockSpec(memory_space=pl.ANY)
    outs = pl.pallas_call(
        back_kernel,
        in_specs=[SCALARS] + [pl.BlockSpec(memory_space=pltpu.VMEM)] * 13 + [anywhere] * 3,
        out_specs=[pl.BlockSpec(memory_space=pltpu.VMEM)] + [anywhere] * 3,
        out_shape=[pltpu.HBM((64, 2, 16, 128), BF16)] + [jax.ShapeDtypeStruct(x.shape, x.dtype) for x in later],
        scratch_shapes=[pltpu.VMEM((512, 4096), BF16)],
        input_output_aliases={14 + k: 1 + k for k in range(3)},
        compiler_params=pltpu.CompilerParams(vmem_limit_bytes=20 * MIB),
        cost_estimate=pl.CostEstimate(flops=2 * 512 * 512 * 4096, bytes_accessed=8 * MIB, transcendentals=0),
        name="back_messages",
    )(at, *pieces, w_in, *later)
    return outs[0], outs[1:]


def grad_kernel(out_first, at, *refs):
    pieces, x, out, whole, rows = refs[:12], refs[12], refs[13], refs[14], refs[15]

    @pl.when(pl.program_id(0) == 0)
    def _():
        assemble(at, pieces, whole)
        if not out_first:
            rows_kernel(x, rows)

    cols = pl.ds(pl.multiple_of(pl.program_id(0) * 1024, 1024), 1024)
    dims = (((0,), (0,)), ((), ()))
    if out_first:
        out[...] = lax.dot_general(whole[:, cols], x[...], dims, preferred_element_type=F32)
    else:
        out[...] = lax.dot_general(rows[...], whole[:, cols], dims, preferred_element_type=F32)


def grad_of(at, pieces, x, out_first):
    block, shape = ((1024, 512), (4096, 512)) if out_first else ((512, 1024), (512, 4096))
    pieces = [pltpu.with_memory_space_constraint(p, pltpu.HBM) for p in pieces]
    return pl.pallas_call(
        functools.partial(grad_kernel, out_first),
        grid=(4,),
        in_specs=[SCALARS]
        + [pl.BlockSpec(p.shape, lambda i: (0, 0)) for p in pieces]
        + [pl.BlockSpec(x.shape, lambda i: (0,) * len(x.shape))],
        out_specs=pl.BlockSpec(block, lambda i: (i, 0) if out_first else (0, i)),
        out_shape=jax.ShapeDtypeStruct(shape, F32),
        scratch_shapes=[pltpu.VMEM((512, 4096), BF16), pltpu.VMEM((512, 512), BF16)],
        compiler_params=pltpu.CompilerParams(vmem_limit_bytes=22 * MIB),
        cost_estimate=pl.CostEstimate(flops=2 * 512 * 512 * 4096, bytes_accessed=12 * MIB, transcendentals=0),
        name="grad_out" if out_first else "grad_in",
    )(at, *pieces, x)


def act_kernel(x, act, gain, out, twice, back):
    a = act[...].astype(F32)
    twice[0:4, :] = a
    twice[4:8, :] = a
    a = twice[...]
    center = a - jnp.mean(a, axis=1, keepdims=True)
    inverse = lax.rsqrt(jnp.mean(center * center, axis=1, keepdims=True) + EPSILON)
    scaled = center * inverse
    low = lower((8, 128))
    for g in range(16):
        total = x[g // 8, 0, g % 8].astype(F32)
        for d in range(1, 8):
            total += x[g // 8, d, g % 8].astype(F32)
        for t in range(2):
            tile = total[t * 8 : t * 8 + 8]
            turned = pltpu.roll(tile, 4, 0)
            at = g * 512 + t * 256
            back[:, at : at + 128] = jnp.where(low, tile, turned)
            back[:, at + 128 : at + 256] = jnp.where(low, turned, tile)
    dxhat = back[...] * gain[...]
    first = jnp.mean(dxhat, axis=1, keepdims=True)
    second = jnp.mean(dxhat * scaled, axis=1, keepdims=True)
    back[...] = inverse * (dxhat - first - scaled * second)
    out[...] = back[0:4, :]


def grad_act_of(x, act, gain):
    return pl.pallas_call(
        act_kernel,
        out_shape=jax.ShapeDtypeStruct((4, 8192), F32),
        scratch_shapes=[pltpu.VMEM((8, 8192), F32), pltpu.VMEM((8, 8192), F32)],
        name="grad_act",
    )(x.reshape(2, 8, 8, 16, 128), act, gain.reshape(1, -1))


def gelu_tanh(inner):
    return jax.nn.gelu(inner, approximate=True)


def activate(preact, upstream):
    value, pullback = jax.vjp(gelu_tanh, preact)
    return value.astype(BF16), pullback(upstream)[0].astype(BF16)


def local(act, gain, shift, w_in, w_out, cotangent):
    section, tensor = lax.axis_index("section"), lax.axis_index("tensor")
    core, ring = lax.bitwise_and(tensor, 1), lax.shift_right_logical(tensor, 1)
    bit_a = jnp.where((ring == 1) | (ring == 2), 1, 0)
    number = bit_a * 4 + lax.bitwise_and(ring, 2) + section
    at = jnp.stack([number, core]).astype(jnp.int32)

    out_other = swap(w_out, "core")
    cot_other = swap(cotangent, "core")
    in_other = swap(w_in, "core")
    messages = norm_messages(act, gain, shift)
    mixed = lax.all_to_all(messages.reshape(128, 16, 128), EVERY, 0, 0, tiled=True).reshape(64, 2, 16, 128)
    up = chip_sum(at, cotangent, cot_other, w_out, out_other, [], True)
    up = [halve(*pair, order[0]) for pair, order in zip(up, ORDERS)]
    mixed_other = swap(mixed, "core")
    pre = chip_sum(at, mixed, mixed_other, w_in, in_other, [pair[0] for pair in up], False)
    pre = [halve(*pair, order[0]) for pair, order in zip(pre, ORDERS)]
    pre_grad, hidden = [], []
    for u, v, order in zip(up, pre, ORDERS):
        total = reduce_pairs(u, v, order) * (1.0 / LIFT)
        h, g = activate(total[1], total[0])
        g, h = gather_pairs(g, h, order)
        pre_grad += [g, swap(g, order[2])]
        hidden.append(h)

    def both(pieces):
        return pieces + [swap(p, "core") for p in pieces]

    pre_grad = both(pre_grad)
    share, hidden = back_messages(at, pre_grad, w_in, hidden)
    hidden = [p for h, order in zip(hidden, ORDERS) for p in (h, swap(h, order[2]))]
    returned = lax.all_to_all(share.reshape(128, 16, 128), EVERY, 0, 0, tiled=True)
    grad_act = grad_act_of(returned, act, gain)
    grad_in = grad_of(at, pre_grad, mixed, False)
    grad_out = grad_of(at, both(hidden), cotangent, True)
    return (grad_in, grad_out, grad_act)


def solution(mesh):
    in_specs = (
        P(EVERY, None),
        P(),
        P(),
        P(OWNERS, "dp"),
        P("dp", OWNERS),
        P(None, OWNERS),
    )
    out_specs = (P(OWNERS, "dp"), P("dp", OWNERS), P(EVERY, None))
    return jax.shard_map(local, mesh=mesh, in_specs=in_specs, out_specs=out_specs, check_vma=False)
```

time: 202 us -> 156 us (0.77)
  blocking collectives: 24 us -> 0 us
  Pallas kernels: 46.6 us -> 32.7 us
  starting transfers between devices: 72.5 us -> 61.7 us
  waiting for transfers between devices: 47.1 us -> 52.3 us
  local copies, waits for them, and re-layouts: 8.09 us -> 3.7 us
    all_to_all x1 -> x0, blocking collectives: 24 us -> none  [local(): lax.all_to_all(norm_messages(act, gain, shift).reshape(128, 16, 128), EVE...]
    ppermute x52 -> x40, starting transfers between devices: 67.2 us -> 45.6 us  [swap(): return lax.ppermute(x, OWNERS, pairs)]
    pallas_call x11 -> x5, Pallas kernels: 40.4 us -> 26.5 us  [the longest x2 15.1 us: grad_of(): pl.pallas_call(functools.partial(grad_kernel, out_first), grid=(4,), in_s...]
    all_to_all x0 -> x1, starting transfers between devices: none -> 10.2 us  [local(): lax.all_to_all(messages.reshape(128, 16, 128), EVERY, 0, 0, tiled=True)]
    unnamed x22 -> x48, local copies, waits for them, and re-layouts: 7.88 us -> 3.56 us
    all_to_all x0 -> x1, waiting for transfers between devices: none -> 2.67 us  [local(): lax.all_to_all(messages.reshape(128, 16, 128), EVERY, 0, 0, tiled=True)]
    ppermute x52 -> x40, waiting for transfers between devices: 47.1 us -> 48.3 us  [swap(): return lax.ppermute(x, OWNERS, pairs)]
  transfers between devices with their start and end apart: 53 -> 42, of which waited for: 12 -> 18; matrix products, arithmetic and copies ran while one was open for 1% -> 3% of each run, Pallas kernels for 22% -> 11%
where the time goes in v1:
time: 156 us
  starting transfers between devices  61.7 us (40%)
  waiting for transfers between devices  52.3 us (34%)
  Pallas kernels  32.7 us (21%)
  other arithmetic  3.78 us (2%)
  local copies, waits for them, and re-layouts  3.7 us (2%)
    ppermute x40, waiting for transfers between devices, swap(): return lax.ppermute(x, OWNERS, pairs)  48.3 us
    ppermute x40, starting transfers between devices, swap(): return lax.ppermute(x, OWNERS, pairs)  45.6 us
    pallas_call x2, Pallas kernels, grad_of(): pl.pallas_call(functools.partial(grad_kernel, out_first), grid=(4,), in_s...  15.1 us
    all_to_all x1, starting transfers between devices, local(): lax.all_to_all(messages.reshape(128, 16, 128), EVERY, 0, 0, tiled=True)  10.2 us
    pallas_call x2, Pallas kernels, chip_sum(): pl.pallas_call(up_kernel if up else pre_kernel, grid_spec=pltpu.PrefetchS...  9.41 us
    all_to_all x1, starting transfers between devices, local(): lax.all_to_all(share.reshape(128, 16, 128), EVERY, 0, 0, tiled=True)  5.81 us
    pallas_call x1, Pallas kernels, back_messages(): pl.pallas_call(back_kernel, in_specs=[SCALARS] + [pl.BlockSpec(memory_spa...  3.94 us
    unnamed x48, local copies, waits for them, and re-layouts  3.56 us
  transfers between devices with their start and end apart: 42, of which 18 were waited for; matrix products, arithmetic and copies ran while one was open for 3% of the time, Pallas kernels for 11%

profile of v1, /device:TPU:1, one launch (start us, length us, event | category | flops | bytes accessed | tf_op | source)
XLA Modules:
  0.0 155.5 jit_solution(9612606700167668955)
XLA Ops:
  0.6 1.5 collective-permute-start.1
  2.6 2.1 %norm_messages.1 = bf16[2,8,8,16,128]{4,3,2,1,0:T(8,128)(2,1)} custom-call(bf16[4,8192]{1,0:T(4,128)(2,1)} %act.3, f32[1,8192]{1,0:T(1,128)} %bitcast.101, f32[1,8192]{1,0:T(1,128)} %bitcast.103), custom_call_target="tpu_custom_call" | custom-call | tf_op jit(solution)/shard_map/norm_messages/pallas_call | solution.py:58
  4.7 10.2 %all-to-all-start = ((bf16[128,16,128]{2,1,0:T(8,128)(2,1)}), bf16[128,16,128]{2,1,0:T(8,128)(2,1)S(1)}, u32[]{:S(2)}, u32[]{:S(2)}) async-start(bf16[128,16,128]{2,1,0:T(8,128)(2,1)} %bitcast.89), calls=%async_computation | async-start | bytes 1048576 | tf_op jit(solution)/shard_map/all_to_all | solution.py:314
  15.0 1.0 copy-done.7
  16.1 4.7 %up_sum.1 = (f32[256,768]{1,0:T(8,128)S(1)}, f32[256,768]{1,0:T(8,128)S(1)}, f32[256,768]{1,0:T(8,128)S(1)}, f32[256,768]{1,0:T(8,128)S(1)}, f32[256,512]{1,0:T(8,128)S(1)}, /*index=5*/f32[256,512]{1,0:T(8,128)S(1)}) custom-call(s32[2]{0:T(128)S(1)} %pad_add_fusion.at, bf16[512,512]{1,0:T(8,128)(2,1)S(1)} %copy-done.7, ...), custom_call_target="tpu_custom_call" | custom-call | flops 2147483648 | bytes 9437184 | tf_op jit(solution)/shard_map/up_sum/pallas_call | solution.py:144
  20.8 0.8 copy-done.20
  21.6 0.8 copy-done.18
  22.5 3.3 %collective-permute-start.6 = (f16[256,512]{1,0:T(8,128)(2,1)S(1)}, f16[256,512]{1,0:T(8,128)(2,1)S(1)}, u32[]{:S(2)}, u32[]{:S(2)}) collective-permute-start(f16[256,512]{1,0:T(8,128)(2,1)S(1)} %convert_element_type.91), channel_id=1, source_target_pairs={{0,64},{1,65},{2,66},{3,67},{4,68},{5,69},{6,70},{7,71},{64,0},{65... | collective-permute-start | bytes 786440 | tf_op jit(solution)/shard_map/ppermute | solution.py:30
  25.8 2.7 %all-to-all-done = bf16[128,16,128]{2,1,0:T(8,128)(2,1)S(1)} async-done(((bf16[128,16,128]{2,1,0:T(8,128)(2,1)}), bf16[128,16,128]{2,1,0:T(8,128)(2,1)S(1)}, u32[]{:S(2)}, u32[]{:S(2)}) %all-to-all-start) | async-done | bytes 524320 | tf_op jit(solution)/shard_map/all_to_all | solution.py:314
  28.4 1.1 collective-permute-start.3
  29.9 2.6 %collective-permute-done.6 = f16[256,512]{1,0:T(8,128)(2,1)S(1)} collective-permute-done((f16[256,512]{1,0:T(8,128)(2,1)S(1)}, f16[256,512]{1,0:T(8,128)(2,1)S(1)}, u32[]{:S(2)}, u32[]{:S(2)}) %collective-permute-start.6) | collective-permute-done | bytes 262176 | tf_op jit(solution)/shard_map/ppermute | solution.py:30
  32.6 1.1 convert_add_fusion.5
  33.8 7.9 %collective-permute-done.5 = f16[256,768]{1,0:T(8,128)(2,1)S(1)} collective-permute-done((f16[256,768]{1,0:T(8,128)(2,1)S(1)}, f16[256,768]{1,0:T(8,128)(2,1)S(1)}, u32[]{:S(2)}, u32[]{:S(2)}) %collective-permute-start.5) | collective-permute-done | bytes 393248 | tf_op jit(solution)/shard_map/ppermute | solution.py:30
  42.0 4.7 %pre_sum.1 = (f32[256,768]{1,0:T(8,128)S(1)}, f32[256,768]{1,0:T(8,128)S(1)}, f32[256,768]{1,0:T(8,128)S(1)}, f32[256,768]{1,0:T(8,128)S(1)}, f32[256,512]{1,0:T(8,128)S(1)}, /*index=5*/f32[256,512]{1,0:T(8,128)S(1)}) custom-call(s32[2]{0:T(128)S(1)} %pad_add_fusion.at, bf16[64,2,16,128]{3,2,1,0:T(8,128)(2,1)S(1)} %bitcast.72, ...), custom_call_target="tpu_custom_call" | custom-call | flops 2147483648 | bytes 9437184 | tf_op jit(solution)/shard_map/pre_sum/pallas_call | solution.py:144
  47.1 1.4 collective-permute-start.13
  48.5 7.0 %collective-permute-done.19 = f16[256,512]{1,0:T(8,128)(2,1)S(1)} collective-permute-done((f16[256,512]{1,0:T(8,128)(2,1)S(1)}, f16[256,512]{1,0:T(8,128)(2,1)S(1)}, u32[]{:S(2)}, u32[]{:S(2)}) %collective-permute-start.19) | collective-permute-done | bytes 262176 | tf_op jit(solution)/shard_map/ppermute | solution.py:30
  55.7 2.0 %collective-permute-done.13 = f16[256,768]{1,0:T(8,128)(2,1)S(1)} collective-permute-done((f16[256,768]{1,0:T(8,128)(2,1)S(1)}, f16[256,768]{1,0:T(8,128)(2,1)S(1)}, u32[]{:S(2)}, u32[]{:S(2)}) %collective-permute-start.13) | collective-permute-done | bytes 393248 | tf_op jit(solution)/shard_map/ppermute | solution.py:30
  57.9 3.1 %collective-permute-start.14 = (f16[2,128,768]{2,1,0:T(8,128)(2,1)S(1)}, f16[2,128,768]{2,1,0:T(8,128)(2,1)S(1)}, u32[]{:S(2)}, u32[]{:S(2)}) collective-permute-start(f16[2,128,768]{2,1,0:T(8,128)(2,1)S(1)} %pad_maximum_fusion.4), channel_id=1, source_target_pairs={{0,64},{1,65},{2,66},{3,67},{4,68},{5,69},{6,70},{7,71},{64,0},{65... | collective-permute-start | bytes 1179656 | tf_op jit(solution)/shard_map/ppermute | solution.py:30
  61.2 2.9 %collective-permute-done.20 = f16[2,128,512]{2,1,0:T(8,128)(2,1)S(1)} collective-permute-done((f16[2,128,512]{2,1,0:T(8,128)(2,1)S(1)}, f16[2,128,512]{2,1,0:T(8,128)(2,1)S(1)}, u32[]{:S(2)}, u32[]{:S(2)}) %collective-permute-start.20) | collective-permute-done | bytes 262176 | tf_op jit(solution)/shard_map/ppermute | solution.py:30
  65.1 2.1 %collective-permute-start.8 = (f16[2,128,768]{2,1,0:T(8,128)(2,1)S(1)}, f16[2,128,768]{2,1,0:T(8,128)(2,1)S(1)}, u32[]{:S(2)}, u32[]{:S(2)}) collective-permute-start(f16[2,128,768]{2,1,0:T(8,128)(2,1)S(1)} %pad_maximum_fusion.2), channel_id=1, source_target_pairs={{0,6},{1,7},{2,4},{3,5},{4,2},{5,3},{6,0},{7,1},{64,70},{65,71},{6... | collective-permute-start | bytes 1179656 | tf_op jit(solution)/shard_map/ppermute | solution.py:30
  67.2 2.4 %collective-permute-done.21 = f16[2,64,512]{2,1,0:T(8,128)(2,1)S(1)} collective-permute-done((f16[2,64,512]{2,1,0:T(8,128)(2,1)S(1)}, f16[2,64,512]{2,1,0:T(8,128)(2,1)S(1)}, u32[]{:S(2)}, u32[]{:S(2)}) %collective-permute-start.21) | collective-permute-done | bytes 131104 | tf_op jit(solution)/shard_map/ppermute | solution.py:30
  69.8 1.4 collective-permute-start.22
  71.4 6.0 %collective-permute-done.8 = f16[2,128,768]{2,1,0:T(8,128)(2,1)S(1)} collective-permute-done((f16[2,128,768]{2,1,0:T(8,128)(2,1)S(1)}, f16[2,128,768]{2,1,0:T(8,128)(2,1)S(1)}, u32[]{:S(2)}, u32[]{:S(2)}) %collective-permute-start.8) | collective-permute-done | bytes 393248 | tf_op jit(solution)/shard_map/ppermute | solution.py:30
  77.5 2.2 %collective-permute-start.9 = (f16[2,64,768]{2,1,0:T(8,128)(2,1)S(1)}, f16[2,64,768]{2,1,0:T(8,128)(2,1)S(1)}, u32[]{:S(2)}, u32[]{:S(2)}) collective-permute-start(f16[2,64,768]{2,1,0:T(8,128)(2,1)S(1)} %slice_convert_fusion.3), channel_id=1, source_target_pairs={{0,64},{1,65},{2,66},{3,67},{4,68},{5,69},{6,70},{7,71},{64,0},{65... | collective-permute-start | bytes 589832 | tf_op jit(solution)/shard_map/ppermute | solution.py:30
  80.7 2.9 %collective-permute-done.9 = f16[2,64,768]{2,1,0:T(8,128)(2,1)S(1)} collective-permute-done((f16[2,64,768]{2,1,0:T(8,128)(2,1)S(1)}, f16[2,64,768]{2,1,0:T(8,128)(2,1)S(1)}, u32[]{:S(2)}, u32[]{:S(2)}) %collective-permute-start.9) | collective-permute-done | bytes 196640 | tf_op jit(solution)/shard_map/ppermute | solution.py:30
  84.1 2.0 %collective-permute-done.16 = bf16[2,64,768]{2,1,0:T(8,128)(2,1)S(1)} collective-permute-done((bf16[2,64,768]{2,1,0:T(8,128)(2,1)S(1)}, bf16[2,64,768]{2,1,0:T(8,128)(2,1)S(1)}, u32[]{:S(2)}, u32[]{:S(2)}) %collective-permute-start.16) | collective-permute-done | bytes 196640 | tf_op jit(solution)/shard_map/ppermute | solution.py:30
  86.9 1.2 collective-permute-start.23
  88.0 0.9 collective-permute-done.10
  89.0 1.8 %collective-permute-start.11 = (bf16[2,2,64,768]{3,2,0,1:T(8,128)(2,1)S(1)}, bf16[2,2,64,768]{3,2,0,1:T(8,128)(2,1)S(1)}, u32[]{:S(2)}, u32[]{:S(2)}) collective-permute-start(bf16[2,2,64,768]{3,2,0,1:T(8,128)(2,1)S(1)} %copy.12), channel_id=1, source_target_pairs={{0,6},{1,7},{2,4},{3,5},{4,2},{5,3},{6,0},{7,1},{64,70},{65,71},{6... | collective-permute-start | bytes 1179656 | tf_op jit(solution)/shard_map/ppermute | solution.py:30
  90.9 3.5 %collective-permute-done.17 = bf16[2,2,64,768]{3,2,0,1:T(8,128)(2,1)S(1)} collective-permute-done((bf16[2,2,64,768]{3,2,0,1:T(8,128)(2,1)S(1)}, bf16[2,2,64,768]{3,2,0,1:T(8,128)(2,1)S(1)}, u32[]{:S(2)}, u32[]{:S(2)}) %collective-permute-start.17) | collective-permute-done | bytes 393248 | tf_op jit(solution)/shard_map/ppermute | solution.py:30
  94.6 2.6 %collective-permute-done.11 = bf16[2,2,64,768]{3,2,0,1:T(8,128)(2,1)S(1)} collective-permute-done((bf16[2,2,64,768]{3,2,0,1:T(8,128)(2,1)S(1)}, bf16[2,2,64,768]{3,2,0,1:T(8,128)(2,1)S(1)}, u32[]{:S(2)}, u32[]{:S(2)}) %collective-permute-start.11) | collective-permute-done | bytes 393248 | tf_op jit(solution)/shard_map/ppermute | solution.py:30
  97.3 1.8 %collective-permute-start.12 = (bf16[256,768]{1,0:T(8,128)(2,1)S(1)}, bf16[256,768]{1,0:T(8,128)(2,1)S(1)}, u32[]{:S(2)}, u32[]{:S(2)}) collective-permute-start(bf16[256,768]{1,0:T(8,128)(2,1)S(1)} %bitcast.78), channel_id=1, source_target_pairs={{0,64},{1,65},{2,66},{3,67},{4,68},{5,69},{6,70},{7,71},{64,0},{65... | collective-permute-start | bytes 1179656 | tf_op jit(solution)/shard_map/ppermute | solution.py:30
  99.2 8.0 %collective-permute-start.29 = (bf16[256,512]{1,0:T(8,128)(2,1)S(1)}, bf16[256,512]{1,0:T(8,128)(2,1)S(1)}, u32[]{:S(2)}, u32[]{:S(2)}) collective-permute-start(bf16[256,512]{1,0:T(8,128)(2,1)S(1)} %bitcast.84), channel_id=1, source_target_pairs={{0,1},{1,0},{2,3},{3,2},{4,5},{5,4},{6,7},{7,6},{64,65},{65,64},{6... | collective-permute-start | bytes 786440 | tf_op jit(solution)/shard_map/ppermute | solution.py:30
  108.9 4.7 %collective-permute-start.26 = (bf16[256,768]{1,0:T(8,128)(2,1)S(1)}, bf16[256,768]{1,0:T(8,128)(2,1)S(1)}, u32[]{:S(2)}, u32[]{:S(2)}) collective-permute-start(bf16[256,768]{1,0:T(8,128)(2,1)S(1)} %collective-permute-done.12.refs_1_), channel_id=1, source_target_pairs={{0,1},{1,0},{2,3},{3,2},{4,5},{5,4},{6,7},{7,6},{64,65},{65,64},{6... | collective-permute-start | bytes 1179656 | tf_op jit(solution)/shard_map/ppermute | solution.py:30
  113.6 2.7 %collective-permute-done.24.refs_5_ = bf16[256,512]{1,0:T(8,128)(2,1)S(1)} collective-permute-done((bf16[256,512]{1,0:T(8,128)(2,1)S(1)}, bf16[256,512]{1,0:T(8,128)(2,1)S(1)}, u32[]{:S(2)}, u32[]{:S(2)}) %collective-permute-start.24) | collective-permute-done | bytes 262176 | tf_op jit(solution)/shard_map/ppermute | solution.py:30
  116.2 0.9 collective-permute-start.30
  117.2 1.0 collective-permute-done.30.refs_11_
  118.4 3.9 %back_messages.1 = (bf16[64,2,16,128]{3,2,1,0:T(8,128)(2,1)}, bf16[256,768]{1,0:T(8,128)(2,1)S(1)}, bf16[256,768]{1,0:T(8,128)(2,1)S(1)}, bf16[256,512]{1,0:T(8,128)(2,1)S(1)}) custom-call(s32[2]{0:T(128)S(1)} %pad_add_fusion.at, bf16[256,768]{1,0:T(8,128)(2,1)S(1)} %bitcast.80, ...), custom_call_target="tpu_custom_call", output_to_operand_aliasing={{1}: (14, {}), {2}: (15, {}), {3}: (16, {})} | custom-call | flops 2147483648 | bytes 8388608 | tf_op jit(solution)/shard_map/back_messages/pallas_call | solution.py:210
  123.7 1.9 %collective-permute-start.33 = (bf16[256,512]{1,0:T(8,128)(2,1)S(1)}, bf16[256,512]{1,0:T(8,128)(2,1)}, u32[]{:S(2)}, u32[]{:S(2)}) collective-permute-start(bf16[256,512]{1,0:T(8,128)(2,1)S(1)} %get-tuple-element.33.refs_4_), channel_id=1, source_target_pairs={{0,6},{1,7},{2,4},{3,5},{4,2},{5,3},{6,0},{7,1},{64,70},{65,71},{6... | collective-permute-start | bytes 786440 | tf_op jit(solution)/shard_map/ppermute | solution.py:30
  125.6 5.8 %all-to-all-start.1 = ((bf16[128,16,128]{2,1,0:T(8,128)(2,1)}), bf16[128,16,128]{2,1,0:T(8,128)(2,1)S(1)}, u32[]{:S(2)}, u32[]{:S(2)}) async-start(bf16[128,16,128]{2,1,0:T(8,128)(2,1)} %bitcast.100), calls=%async_computation.1 | async-start | bytes 1048576 | tf_op jit(solution)/shard_map/all_to_all | solution.py:334
  131.4 1.1 collective-permute-start.34
  132.7 1.7 %collective-permute-done.31.refs_1_ = bf16[256,768]{1,0:T(8,128)(2,1)S(1)} collective-permute-done((bf16[256,768]{1,0:T(8,128)(2,1)S(1)}, bf16[256,768]{1,0:T(8,128)(2,1)S(1)}, u32[]{:S(2)}, u32[]{:S(2)}) %collective-permute-start.31) | collective-permute-done | bytes 393248 | tf_op jit(solution)/shard_map/ppermute | solution.py:30
  134.3 1.2 collective-permute-start.35
  136.1 7.5 %grad_in.1 = f32[512,4096]{1,0:T(8,128)} custom-call(s32[2]{0:T(128)S(1)} %pad_add_fusion.at, bf16[256,768]{1,0:T(8,128)(2,1)} %bitcast.81, bf16[256,768]{1,0:T(8,128)(2,1)} %copy-done.10, bf16[256,768]{1,0:T(8,128)(2,1)} %bitcast.77, bf16[256,768]{1,0:T(8,128)(2,1)} %copy-done.9, bf16[256,512]{1,0:T(8,128)(2,1)} %bitcast.87, bf16[256,512]{1,0:T(8,128)(2,1)} %copy-done.16, ...), custom_call_target="tpu_custom_call" | custom-call | flops 2147483648 | bytes 12582912 | tf_op jit(solution)/shard_map/grad_in/pallas_call | solution.py:244
  143.6 1.3 all-to-all-done.1
  144.9 0.8 copy-done.21
  145.7 2.3 %grad_act.1 = f32[4,8192]{1,0:T(4,128)} custom-call(bf16[2,8,8,16,128]{4,3,2,1,0:T(8,128)(2,1)} %bitcast.90, bf16[4,8192]{1,0:T(4,128)(2,1)} %act.3, f32[1,8192]{1,0:T(1,128)} %bitcast.102), custom_call_target="tpu_custom_call" | custom-call | tf_op jit(solution)/shard_map/grad_act/pallas_call | solution.py:286
  148.0 7.5 %grad_out.1 = f32[4096,512]{1,0:T(8,128)} custom-call(s32[2]{0:T(128)S(1)} %pad_add_fusion.at, bf16[256,768]{1,0:T(8,128)(2,1)} %copy-done.4, bf16[256,768]{1,0:T(8,128)(2,1)} %copy-done.22, bf16[256,768]{1,0:T(8,128)(2,1)} %copy-done.3, bf16[256,768]{1,0:T(8,128)(2,1)} %copy-done.23, bf16[256,512]{1,0:T(8,128)(2,1)} %copy-done.6, ...), custom_call_target="tpu_custom_call" | custom-call | flops 2147483648 | bytes 12582912 | tf_op jit(solution)/shard_map/grad_out/pallas_call | solution.py:244
  (149 shorter events, 9.9 us)
Async XLA Ops:
  0.6 14.4 %collective-permute-start.1 = (bf16[4096,512]{1,0:T(8,128)(2,1)}, bf16[4096,512]{1,0:T(8,128)(2,1)}, u32[]{:S(2)}, u32[]{:S(2)}) collective-permute-start(bf16[4096,512]{1,0:T(8,128)(2,1)} %w.2), channel_id=1, source_target_pairs={{0,1},{1,0},{2,3},{3,2},{4,5},{5,4},{6,7},{7,6},{64,65},{65,64},{6... | collective-permute-start | bytes 12582920 | tf_op jit(solution)/shard_map/ppermute | solution.py:30
  2.1 39.9 %collective-permute-start.4 = (bf16[512,4096]{1,0:T(8,128)(2,1)}, bf16[512,4096]{1,0:T(8,128)(2,1)}, u32[]{:S(2)}, u32[]{:S(2)}) collective-permute-start(bf16[512,4096]{1,0:T(8,128)(2,1)} %refs_12_.2), channel_id=1, source_target_pairs={{0,1},{1,0},{2,3},{3,2},{4,5},{5,4},{6,7},{7,6},{64,65},{65,64},{6... | collective-permute-start | bytes 12582920 | tf_op jit(solution)/shard_map/ppermute | solution.py:30
  2.2 12.8 %collective-permute-start = (bf16[512,512]{1,0:T(8,128)(2,1)}, bf16[512,512]{1,0:T(8,128)(2,1)S(1)}, u32[]{:S(2)}, u32[]{:S(2)}) collective-permute-start(bf16[512,512]{1,0:T(8,128)(2,1)} %refs_12_.3), channel_id=1, source_target_pairs={{0,1},{1,0},{2,3},{3,2},{4,5},{5,4},{6,7},{7,6},{64,65},{65,64},{6... | collective-permute-start | bytes 1572872 | tf_op jit(solution)/shard_map/ppermute | solution.py:30
  4.7 23.7 %all-to-all-start = ((bf16[128,16,128]{2,1,0:T(8,128)(2,1)}), bf16[128,16,128]{2,1,0:T(8,128)(2,1)S(1)}, u32[]{:S(2)}, u32[]{:S(2)}) async-start(bf16[128,16,128]{2,1,0:T(8,128)(2,1)} %bitcast.89), calls=%async_computation | async-start | bytes 1048576 | tf_op jit(solution)/shard_map/all_to_all | solution.py:314
  22.5 10.1 %collective-permute-start.6 = (f16[256,512]{1,0:T(8,128)(2,1)S(1)}, f16[256,512]{1,0:T(8,128)(2,1)S(1)}, u32[]{:S(2)}, u32[]{:S(2)}) collective-permute-start(f16[256,512]{1,0:T(8,128)(2,1)S(1)} %convert_element_type.91), channel_id=1, source_target_pairs={{0,64},{1,65},{2,66},{3,67},{4,68},{5,69},{6,70},{7,71},{64,0},{65... | collective-permute-start | bytes 786440 | tf_op jit(solution)/shard_map/ppermute | solution.py:30
  28.4 13.6 %collective-permute-start.3 = (bf16[64,2,16,128]{3,2,1,0:T(8,128)(2,1)S(1)}, bf16[64,2,16,128]{3,2,1,0:T(8,128)(2,1)S(1)}, u32[]{:S(2)}, u32[]{:S(2)}) collective-permute-start(bf16[64,2,16,128]{3,2,1,0:T(8,128)(2,1)S(1)} %bitcast.71), channel_id=1, source_target_pairs={{0,1},{1,0},{2,3},{3,2},{4,5},{5,4},{6,7},{7,6},{64,65},{65,64},{6... | collective-permute-start | bytes 1572872 | tf_op jit(solution)/shard_map/ppermute | solution.py:30
  29.6 12.0 %collective-permute-start.5 = (f16[256,768]{1,0:T(8,128)(2,1)S(1)}, f16[256,768]{1,0:T(8,128)(2,1)S(1)}, u32[]{:S(2)}, u32[]{:S(2)}) collective-permute-start(f16[256,768]{1,0:T(8,128)(2,1)S(1)} %convert_element_type.89), channel_id=1, source_target_pairs={{0,6},{1,7},{2,4},{3,5},{4,2},{5,3},{6,0},{7,1},{64,70},{65,71},{6... | collective-permute-start | bytes 1179656 | tf_op jit(solution)/shard_map/ppermute | solution.py:30
  29.9 11.9 %collective-permute-start.2 = (f16[256,768]{1,0:T(8,128)(2,1)S(1)}, f16[256,768]{1,0:T(8,128)(2,1)S(1)}, u32[]{:S(2)}, u32[]{:S(2)}) collective-permute-start(f16[256,768]{1,0:T(8,128)(2,1)S(1)} %convert_element_type.87), channel_id=1, source_target_pairs={{0,2},{1,3},{2,0},{3,1},{4,6},{5,7},{6,4},{7,5},{64,66},{65,67},{6... | collective-permute-start | bytes 1179656 | tf_op jit(solution)/shard_map/ppermute | solution.py:30
  46.8 8.6 %collective-permute-start.19 = (f16[256,512]{1,0:T(8,128)(2,1)S(1)}, f16[256,512]{1,0:T(8,128)(2,1)S(1)}, u32[]{:S(2)}, u32[]{:S(2)}) collective-permute-start(f16[256,512]{1,0:T(8,128)(2,1)S(1)} %convert_element_type.105), channel_id=1, source_target_pairs={{0,64},{1,65},{2,66},{3,67},{4,68},{5,69},{6,70},{7,71},{64,0},{65... | collective-permute-start | bytes 786440 | tf_op jit(solution)/shard_map/ppermute | solution.py:30
  47.1 10.6 %collective-permute-start.13 = (f16[256,768]{1,0:T(8,128)(2,1)S(1)}, f16[256,768]{1,0:T(8,128)(2,1)S(1)}, u32[]{:S(2)}, u32[]{:S(2)}) collective-permute-start(f16[256,768]{1,0:T(8,128)(2,1)S(1)} %convert_element_type.99), channel_id=1, source_target_pairs={{0,6},{1,7},{2,4},{3,5},{4,2},{5,3},{6,0},{7,1},{64,70},{65,71},{6... | collective-permute-start | bytes 1179656 | tf_op jit(solution)/shard_map/ppermute | solution.py:30
  48.5 12.6 %collective-permute-start.7 = (f16[256,768]{1,0:T(8,128)(2,1)S(1)}, f16[256,768]{1,0:T(8,128)(2,1)S(1)}, u32[]{:S(2)}, u32[]{:S(2)}) collective-permute-start(f16[256,768]{1,0:T(8,128)(2,1)S(1)} %convert_element_type.93), channel_id=1, source_target_pairs={{0,2},{1,3},{2,0},{3,1},{4,6},{5,7},{6,4},{7,5},{64,66},{65,67},{6... | collective-permute-start | bytes 1179656 | tf_op jit(solution)/shard_map/ppermute | solution.py:30
  55.6 8.5 %collective-permute-start.20 = (f16[2,128,512]{2,1,0:T(8,128)(2,1)S(1)}, f16[2,128,512]{2,1,0:T(8,128)(2,1)S(1)}, u32[]{:S(2)}, u32[]{:S(2)}) collective-permute-start(f16[2,128,512]{2,1,0:T(8,128)(2,1)S(1)} %pad_maximum_fusion.9), channel_id=1, source_target_pairs={{0,2},{1,3},{2,0},{3,1},{4,6},{5,7},{6,4},{7,5},{64,66},{65,67},{6... | collective-permute-start | bytes 786440 | tf_op jit(solution)/shard_map/ppermute | solution.py:30
  57.9 13.2 %collective-permute-start.14 = (f16[2,128,768]{2,1,0:T(8,128)(2,1)S(1)}, f16[2,128,768]{2,1,0:T(8,128)(2,1)S(1)}, u32[]{:S(2)}, u32[]{:S(2)}) collective-permute-start(f16[2,128,768]{2,1,0:T(8,128)(2,1)S(1)} %pad_maximum_fusion.4), channel_id=1, source_target_pairs={{0,64},{1,65},{2,66},{3,67},{4,68},{5,69},{6,70},{7,71},{64,0},{65... | collective-permute-start | bytes 1179656 | tf_op jit(solution)/shard_map/ppermute | solution.py:30
  64.2 5.4 %collective-permute-start.21 = (f16[2,64,512]{2,1,0:T(8,128)(2,1)S(1)}, f16[2,64,512]{2,1,0:T(8,128)(2,1)S(1)}, u32[]{:S(2)}, u32[]{:S(2)}) collective-permute-start(f16[2,64,512]{2,1,0:T(8,128)(2,1)S(1)} %slice_convert_fusion.6), channel_id=1, source_target_pairs={{0,6},{1,7},{2,4},{3,5},{4,2},{5,3},{6,0},{7,1},{64,70},{65,71},{6... | collective-permute-start | bytes 393224 | tf_op jit(solution)/shard_map/ppermute | solution.py:30
  65.1 12.3 %collective-permute-start.8 = (f16[2,128,768]{2,1,0:T(8,128)(2,1)S(1)}, f16[2,128,768]{2,1,0:T(8,128)(2,1)S(1)}, u32[]{:S(2)}, u32[]{:S(2)}) collective-permute-start(f16[2,128,768]{2,1,0:T(8,128)(2,1)S(1)} %pad_maximum_fusion.2), channel_id=1, source_target_pairs={{0,6},{1,7},{2,4},{3,5},{4,2},{5,3},{6,0},{7,1},{64,70},{65,71},{6... | collective-permute-start | bytes 1179656 | tf_op jit(solution)/shard_map/ppermute | solution.py:30
  69.8 10.0 %collective-permute-start.22 = (bf16[2,64,512]{2,1,0:T(8,128)(2,1)S(1)}, bf16[2,64,512]{2,1,0:T(8,128)(2,1)S(1)}, u32[]{:S(2)}, u32[]{:S(2)}) collective-permute-start(bf16[2,64,512]{2,1,0:T(8,128)(2,1)S(1)} %get-tuple-element.67), channel_id=1, source_target_pairs={{0,64},{1,65},{2,66},{3,67},{4,68},{5,69},{6,70},{7,71},{64,0},{65... | collective-permute-start | bytes 393224 | tf_op jit(solution)/shard_map/ppermute | solution.py:30
  71.3 8.5 %collective-permute-start.15 = (f16[2,64,768]{2,1,0:T(8,128)(2,1)S(1)}, f16[2,64,768]{2,1,0:T(8,128)(2,1)S(1)}, u32[]{:S(2)}, u32[]{:S(2)}) collective-permute-start(f16[2,64,768]{2,1,0:T(8,128)(2,1)S(1)} %slice_convert_fusion), channel_id=1, source_target_pairs={{0,2},{1,3},{2,0},{3,1},{4,6},{5,7},{6,4},{7,5},{64,66},{65,67},{6... | collective-permute-start | bytes 589832 | tf_op jit(solution)/shard_map/ppermute | solution.py:30
  77.5 6.1 %collective-permute-start.9 = (f16[2,64,768]{2,1,0:T(8,128)(2,1)S(1)}, f16[2,64,768]{2,1,0:T(8,128)(2,1)S(1)}, u32[]{:S(2)}, u32[]{:S(2)}) collective-permute-start(f16[2,64,768]{2,1,0:T(8,128)(2,1)S(1)} %slice_convert_fusion.3), channel_id=1, source_target_pairs={{0,64},{1,65},{2,66},{3,67},{4,68},{5,69},{6,70},{7,71},{64,0},{65... | collective-permute-start | bytes 589832 | tf_op jit(solution)/shard_map/ppermute | solution.py:30
  80.1 6.1 %collective-permute-start.16 = (bf16[2,64,768]{2,1,0:T(8,128)(2,1)S(1)}, bf16[2,64,768]{2,1,0:T(8,128)(2,1)S(1)}, u32[]{:S(2)}, u32[]{:S(2)}) collective-permute-start(bf16[2,64,768]{2,1,0:T(8,128)(2,1)S(1)} %get-tuple-element.63), channel_id=1, source_target_pairs={{0,6},{1,7},{2,4},{3,5},{4,2},{5,3},{6,0},{7,1},{64,70},{65,71},{6... | collective-permute-start | bytes 589832 | tf_op jit(solution)/shard_map/ppermute | solution.py:30
  83.9 5.1 %collective-permute-start.10 = (bf16[2,64,768]{2,1,0:T(8,128)(2,1)S(1)}, bf16[2,64,768]{2,1,0:T(8,128)(2,1)S(1)}, u32[]{:S(2)}, u32[]{:S(2)}) collective-permute-start(bf16[2,64,768]{2,1,0:T(8,128)(2,1)S(1)} %get-tuple-element.65), channel_id=1, source_target_pairs={{0,2},{1,3},{2,0},{3,1},{4,6},{5,7},{6,4},{7,5},{64,66},{65,67},{6... | collective-permute-start | bytes 589832 | tf_op jit(solution)/shard_map/ppermute | solution.py:30
  86.2 8.2 %collective-permute-start.17 = (bf16[2,2,64,768]{3,2,0,1:T(8,128)(2,1)S(1)}, bf16[2,2,64,768]{3,2,0,1:T(8,128)(2,1)S(1)}, u32[]{:S(2)}, u32[]{:S(2)}) collective-permute-start(bf16[2,2,64,768]{3,2,0,1:T(8,128)(2,1)S(1)} %copy.14), channel_id=1, source_target_pairs={{0,64},{1,65},{2,66},{3,67},{4,68},{5,69},{6,70},{7,71},{64,0},{65... | collective-permute-start | bytes 1179656 | tf_op jit(solution)/shard_map/ppermute | solution.py:30
  86.9 12.2 %collective-permute-start.23 = (bf16[2,2,64,512]{3,2,0,1:T(8,128)(2,1)S(1)}, bf16[2,2,64,512]{3,2,0,1:T(8,128)(2,1)S(1)}, u32[]{:S(2)}, u32[]{:S(2)}) collective-permute-start(bf16[2,2,64,512]{3,2,0,1:T(8,128)(2,1)S(1)} %copy.16), channel_id=1, source_target_pairs={{0,2},{1,3},{2,0},{3,1},{4,6},{5,7},{6,4},{7,5},{64,66},{65,67},{6... | collective-permute-start | bytes 786440 | tf_op jit(solution)/shard_map/ppermute | solution.py:30
  89.0 8.2 %collective-permute-start.11 = (bf16[2,2,64,768]{3,2,0,1:T(8,128)(2,1)S(1)}, bf16[2,2,64,768]{3,2,0,1:T(8,128)(2,1)S(1)}, u32[]{:S(2)}, u32[]{:S(2)}) collective-permute-start(bf16[2,2,64,768]{3,2,0,1:T(8,128)(2,1)S(1)} %copy.12), channel_id=1, source_target_pairs={{0,6},{1,7},{2,4},{3,5},{4,2},{5,3},{6,0},{7,1},{64,70},{65,71},{6... | collective-permute-start | bytes 1179656 | tf_op jit(solution)/shard_map/ppermute | solution.py:30
  90.9 27.5 %copy-start = (bf16[512,4096]{1,0:T(8,128)(2,1)S(1)}, bf16[512,4096]{1,0:T(8,128)(2,1)}, u32[]{:S(2)}) copy-start(bf16[512,4096]{1,0:T(8,128)(2,1)} %refs_12_.2) | copy-start | bytes 12582916
  94.5 27.8 %copy-start.1 = (bf16[4,64,768]{2,1,0:T(8,128)(2,1)}, bf16[4,64,768]{2,1,0:T(8,128)(2,1)S(1)}, u32[]{:S(2)}) copy-start(bf16[4,64,768]{2,1,0:T(8,128)(2,1)S(1)} %pad_maximum_fusion.5) | copy-start | bytes 1179652
  94.5 14.2 %collective-permute-start.18 = (bf16[256,768]{1,0:T(8,128)(2,1)S(1)}, bf16[256,768]{1,0:T(8,128)(2,1)S(1)}, u32[]{:S(2)}, u32[]{:S(2)}) collective-permute-start(bf16[256,768]{1,0:T(8,128)(2,1)S(1)} %bitcast.74), channel_id=1, source_target_pairs={{0,2},{1,3},{2,0},{3,1},{4,6},{5,7},{6,4},{7,5},{64,66},{65,67},{6... | collective-permute-start | bytes 1179656 | tf_op jit(solution)/shard_map/ppermute | solution.py:30
  97.3 25.0 %copy-start.2 = (bf16[4,64,768]{2,1,0:T(8,128)(2,1)}, bf16[4,64,768]{2,1,0:T(8,128)(2,1)S(1)}, u32[]{:S(2)}) copy-start(bf16[4,64,768]{2,1,0:T(8,128)(2,1)S(1)} %pad_maximum_fusion.3) | copy-start | bytes 1179652
  97.3 11.5 %collective-permute-start.12 = (bf16[256,768]{1,0:T(8,128)(2,1)S(1)}, bf16[256,768]{1,0:T(8,128)(2,1)S(1)}, u32[]{:S(2)}, u32[]{:S(2)}) collective-permute-start(bf16[256,768]{1,0:T(8,128)(2,1)S(1)} %bitcast.78), channel_id=1, source_target_pairs={{0,64},{1,65},{2,66},{3,67},{4,68},{5,69},{6,70},{7,71},{64,0},{65... | collective-permute-start | bytes 1179656 | tf_op jit(solution)/shard_map/ppermute | solution.py:30
  99.2 23.1 %copy-start.5 = (bf16[4,64,512]{2,1,0:T(8,128)(2,1)}, bf16[4,64,512]{2,1,0:T(8,128)(2,1)S(1)}, u32[]{:S(2)}) copy-start(bf16[4,64,512]{2,1,0:T(8,128)(2,1)S(1)} %pad_maximum_fusion.10) | copy-start | bytes 786436
  99.2 9.1 %collective-permute-start.29 = (bf16[256,512]{1,0:T(8,128)(2,1)S(1)}, bf16[256,512]{1,0:T(8,128)(2,1)S(1)}, u32[]{:S(2)}, u32[]{:S(2)}) collective-permute-start(bf16[256,512]{1,0:T(8,128)(2,1)S(1)} %bitcast.84), channel_id=1, source_target_pairs={{0,1},{1,0},{2,3},{3,2},{4,5},{5,4},{6,7},{7,6},{64,65},{65,64},{6... | collective-permute-start | bytes 786440 | tf_op jit(solution)/shard_map/ppermute | solution.py:30
  107.2 9.1 %collective-permute-start.24 = (bf16[256,512]{1,0:T(8,128)(2,1)S(1)}, bf16[256,512]{1,0:T(8,128)(2,1)S(1)}, u32[]{:S(2)}, u32[]{:S(2)}) collective-permute-start(bf16[256,512]{1,0:T(8,128)(2,1)S(1)} %bitcast.85), channel_id=1, source_target_pairs={{0,6},{1,7},{2,4},{3,5},{4,2},{5,3},{6,0},{7,1},{64,70},{65,71},{6... | collective-permute-start | bytes 786440 | tf_op jit(solution)/shard_map/ppermute | solution.py:30
  107.8 10.5 %collective-permute-start.27 = (bf16[256,768]{1,0:T(8,128)(2,1)S(1)}, bf16[256,768]{1,0:T(8,128)(2,1)S(1)}, u32[]{:S(2)}, u32[]{:S(2)}) collective-permute-start(bf16[256,768]{1,0:T(8,128)(2,1)S(1)} %bitcast.75), channel_id=1, source_target_pairs={{0,1},{1,0},{2,3},{3,2},{4,5},{5,4},{6,7},{7,6},{64,65},{65,64},{6... | collective-permute-start | bytes 1179656 | tf_op jit(solution)/shard_map/ppermute | solution.py:30
  108.3 10.0 %collective-permute-start.25 = (bf16[256,768]{1,0:T(8,128)(2,1)S(1)}, bf16[256,768]{1,0:T(8,128)(2,1)S(1)}, u32[]{:S(2)}, u32[]{:S(2)}) collective-permute-start(bf16[256,768]{1,0:T(8,128)(2,1)S(1)} %bitcast.79), channel_id=1, source_target_pairs={{0,1},{1,0},{2,3},{3,2},{4,5},{5,4},{6,7},{7,6},{64,65},{65,64},{6... | collective-permute-start | bytes 1179656 | tf_op jit(solution)/shard_map/ppermute | solution.py:30
  108.7 9.6 %collective-permute-start.28 = (bf16[256,768]{1,0:T(8,128)(2,1)S(1)}, bf16[256,768]{1,0:T(8,128)(2,1)S(1)}, u32[]{:S(2)}, u32[]{:S(2)}) collective-permute-start(bf16[256,768]{1,0:T(8,128)(2,1)S(1)} %collective-permute-done.18.refs_3_), channel_id=1, source_target_pairs={{0,1},{1,0},{2,3},{3,2},{4,5},{5,4},{6,7},{7,6},{64,65},{65,64},{6... | collective-permute-start | bytes 1179656 | tf_op jit(solution)/shard_map/ppermute | solution.py:30
  108.9 9.5 %collective-permute-start.26 = (bf16[256,768]{1,0:T(8,128)(2,1)S(1)}, bf16[256,768]{1,0:T(8,128)(2,1)S(1)}, u32[]{:S(2)}, u32[]{:S(2)}) collective-permute-start(bf16[256,768]{1,0:T(8,128)(2,1)S(1)} %collective-permute-done.12.refs_1_), channel_id=1, source_target_pairs={{0,1},{1,0},{2,3},{3,2},{4,5},{5,4},{6,7},{7,6},{64,65},{65,64},{6... | collective-permute-start | bytes 1179656 | tf_op jit(solution)/shard_map/ppermute | solution.py:30
  116.2 2.0 %collective-permute-start.30 = (bf16[256,512]{1,0:T(8,128)(2,1)S(1)}, bf16[256,512]{1,0:T(8,128)(2,1)S(1)}, u32[]{:S(2)}, u32[]{:S(2)}) collective-permute-start(bf16[256,512]{1,0:T(8,128)(2,1)S(1)} %collective-permute-done.24.refs_5_), channel_id=1, source_target_pairs={{0,1},{1,0},{2,3},{3,2},{4,5},{5,4},{6,7},{7,6},{64,65},{65,64},{6... | collective-permute-start | bytes 786440 | tf_op jit(solution)/shard_map/ppermute | solution.py:30
  122.4 21.2 %copy-start.3 = (bf16[256,768]{1,0:T(8,128)(2,1)}, bf16[256,768]{1,0:T(8,128)(2,1)S(1)}, u32[]{:S(2)}) copy-start(bf16[256,768]{1,0:T(8,128)(2,1)S(1)} %get-tuple-element.32.refs_2_) | copy-start | bytes 1179652
  122.4 21.2 %copy-start.4 = (bf16[256,768]{1,0:T(8,128)(2,1)}, bf16[256,768]{1,0:T(8,128)(2,1)S(1)}, u32[]{:S(2)}) copy-start(bf16[256,768]{1,0:T(8,128)(2,1)S(1)} %get-tuple-element.31.refs_0_) | copy-start | bytes 1179652
  122.4 11.9 %collective-permute-start.31 = (bf16[256,768]{1,0:T(8,128)(2,1)S(1)}, bf16[256,768]{1,0:T(8,128)(2,1)S(1)}, u32[]{:S(2)}, u32[]{:S(2)}) collective-permute-start(bf16[256,768]{1,0:T(8,128)(2,1)S(1)} %get-tuple-element.31.refs_0_), channel_id=1, source_target_pairs={{0,64},{1,65},{2,66},{3,67},{4,68},{5,69},{6,70},{7,71},{64,0},{65... | collective-permute-start | bytes 1179656 | tf_op jit(solution)/shard_map/ppermute | solution.py:30
  123.0 12.5 %collective-permute-start.32 = (bf16[256,768]{1,0:T(8,128)(2,1)S(1)}, bf16[256,768]{1,0:T(8,128)(2,1)S(1)}, u32[]{:S(2)}, u32[]{:S(2)}) collective-permute-start(bf16[256,768]{1,0:T(8,128)(2,1)S(1)} %get-tuple-element.32.refs_2_), channel_id=1, source_target_pairs={{0,2},{1,3},{2,0},{3,1},{4,6},{5,7},{6,4},{7,5},{64,66},{65,67},{6... | collective-permute-start | bytes 1179656 | tf_op jit(solution)/shard_map/ppermute | solution.py:30
  123.0 9.5 %collective-permute-start.38 = (bf16[256,512]{1,0:T(8,128)(2,1)S(1)}, bf16[256,512]{1,0:T(8,128)(2,1)}, u32[]{:S(2)}, u32[]{:S(2)}) collective-permute-start(bf16[256,512]{1,0:T(8,128)(2,1)S(1)} %get-tuple-element.33.refs_4_), channel_id=1, source_target_pairs={{0,1},{1,0},{2,3},{3,2},{4,5},{5,4},{6,7},{7,6},{64,65},{65,64},{6... | collective-permute-start | bytes 786440 | tf_op jit(solution)/shard_map/ppermute | solution.py:30
  123.7 12.0 %collective-permute-start.33 = (bf16[256,512]{1,0:T(8,128)(2,1)S(1)}, bf16[256,512]{1,0:T(8,128)(2,1)}, u32[]{:S(2)}, u32[]{:S(2)}) collective-permute-start(bf16[256,512]{1,0:T(8,128)(2,1)S(1)} %get-tuple-element.33.refs_4_), channel_id=1, source_target_pairs={{0,6},{1,7},{2,4},{3,5},{4,2},{5,3},{6,0},{7,1},{64,70},{65,71},{6... | collective-permute-start | bytes 786440 | tf_op jit(solution)/shard_map/ppermute | solution.py:30
  125.6 19.3 %all-to-all-start.1 = ((bf16[128,16,128]{2,1,0:T(8,128)(2,1)}), bf16[128,16,128]{2,1,0:T(8,128)(2,1)S(1)}, u32[]{:S(2)}, u32[]{:S(2)}) async-start(bf16[128,16,128]{2,1,0:T(8,128)(2,1)} %bitcast.100), calls=%async_computation.1 | async-start | bytes 1048576 | tf_op jit(solution)/shard_map/all_to_all | solution.py:334
  131.4 16.6 %collective-permute-start.34 = (bf16[256,768]{1,0:T(8,128)(2,1)S(1)}, bf16[256,768]{1,0:T(8,128)(2,1)}, u32[]{:S(2)}, u32[]{:S(2)}) collective-permute-start(bf16[256,768]{1,0:T(8,128)(2,1)S(1)} %get-tuple-element.31.refs_0_), channel_id=1, source_target_pairs={{0,1},{1,0},{2,3},{3,2},{4,5},{5,4},{6,7},{7,6},{64,65},{65,64},{6... | collective-permute-start | bytes 1179656 | tf_op jit(solution)/shard_map/ppermute | solution.py:30
  132.6 15.4 %collective-permute-start.36 = (bf16[256,768]{1,0:T(8,128)(2,1)S(1)}, bf16[256,768]{1,0:T(8,128)(2,1)}, u32[]{:S(2)}, u32[]{:S(2)}) collective-permute-start(bf16[256,768]{1,0:T(8,128)(2,1)S(1)} %get-tuple-element.32.refs_2_), channel_id=1, source_target_pairs={{0,1},{1,0},{2,3},{3,2},{4,5},{5,4},{6,7},{7,6},{64,65},{65,64},{6... | collective-permute-start | bytes 1179656 | tf_op jit(solution)/shard_map/ppermute | solution.py:30
  134.3 13.6 %collective-permute-start.35 = (bf16[256,768]{1,0:T(8,128)(2,1)S(1)}, bf16[256,768]{1,0:T(8,128)(2,1)}, u32[]{:S(2)}, u32[]{:S(2)}) collective-permute-start(bf16[256,768]{1,0:T(8,128)(2,1)S(1)} %collective-permute-done.31.refs_1_), channel_id=1, source_target_pairs={{0,1},{1,0},{2,3},{3,2},{4,5},{5,4},{6,7},{7,6},{64,65},{65,64},{6... | collective-permute-start | bytes 1179656 | tf_op jit(solution)/shard_map/ppermute | solution.py:30
  135.5 12.4 %collective-permute-start.37 = (bf16[256,768]{1,0:T(8,128)(2,1)S(1)}, bf16[256,768]{1,0:T(8,128)(2,1)}, u32[]{:S(2)}, u32[]{:S(2)}) collective-permute-start(bf16[256,768]{1,0:T(8,128)(2,1)S(1)} %collective-permute-done.32.refs_3_), channel_id=1, source_target_pairs={{0,1},{1,0},{2,3},{3,2},{4,5},{5,4},{6,7},{7,6},{64,65},{65,64},{6... | collective-permute-start | bytes 1179656 | tf_op jit(solution)/shard_map/ppermute | solution.py:30
  135.6 12.3 %collective-permute-start.39 = (bf16[256,512]{1,0:T(8,128)(2,1)}, bf16[256,512]{1,0:T(8,128)(2,1)}, u32[]{:S(2)}, u32[]{:S(2)}) collective-permute-start(bf16[256,512]{1,0:T(8,128)(2,1)} %collective-permute-done.33.refs_5_), channel_id=1, source_target_pairs={{0,1},{1,0},{2,3},{3,2},{4,5},{5,4},{6,7},{7,6},{64,65},{65,64},{6... | collective-permute-start | bytes 786440 | tf_op jit(solution)/shard_map/ppermute | solution.py:30
  (18 other events, 139.4 us)

commit v2 on v1

--- a/solution.py
+++ b/solution.py
@@ -10,10 +10,8 @@
 EPSILON = 1e-05
 OWNERS = ("section", "tensor")
 EVERY = ("section", "dp", "tensor")
-BF16, F16, F32 = jnp.bfloat16, jnp.float16, jnp.float32
+BF16, F32 = jnp.bfloat16, jnp.float32
 MIB = 1 << 20
-LIFT = 16.0
-
 
 def swap(x, link):
     pairs = []
@@ -89,7 +87,7 @@
 def multiply(step, contract, lhs, w, w_other, outs):
     dims = (((1,), (contract,)), ((), ()))
     total = lax.dot_general(lhs[0], w[...], dims, preferred_element_type=F32)
-    total = (total + lax.dot_general(lhs[1], w_other[...], dims, preferred_element_type=F32)) * LIFT
+    total = total + lax.dot_general(lhs[1], w_other[...], dims, preferred_element_type=F32)
     for p, order in enumerate(ORDERS):
         first, last = max(CUTS[p], step * 1024), min(CUTS[p + 1], step * 1024 + 1024)
         if first >= last:
@@ -97,7 +95,7 @@
         cols = slice(first - CUTS[p], last - CUTS[p])
         for q, j in enumerate(places(order)):
             block = total[j * 64 : (j + 1) * 64, first - step * 1024 : last - step * 1024]
-            outs[p * 2 + q // 4][q % 4 * 64 : (q % 4 + 1) * 64, cols] = block
+            outs[p * 2 + q // 4][q % 4 * 64 : (q % 4 + 1) * 64, cols] = block.astype(outs[p * 2 + q // 4].dtype)
 
 
 def up_kernel(at, x, x_other, w, w_other, *refs):
@@ -150,32 +148,94 @@
             out_specs=[pl.BlockSpec(shape, lambda i, at: (0, 0)) for shape in shapes],
             scratch_shapes=[pltpu.VMEM((2, 512, 512), BF16)],
         ),
-        out_shape=[jax.ShapeDtypeStruct(shape, F32) for shape in shapes],
+        out_shape=[jax.ShapeDtypeStruct(shape, BF16 if k % 2 else F32) for k, shape in enumerate(shapes)],
         compiler_params=pltpu.CompilerParams(vmem_limit_bytes=20 * MIB),
         cost_estimate=pl.CostEstimate(flops=2 * 512 * 1024 * 2048, bytes_accessed=9 * MIB, transcendentals=0),
         name="up_sum" if up else "pre_sum",
     )(at, x, x_other, w, w_other, *after)
-    return [(outs[2 * p], outs[2 * p + 1].astype(F16)) for p in range(3)]
-
-
-def halve(keep, send, link):
-    total = keep + swap(send, link).astype(F32)
-    rows = total.shape[0] // 2
-    return total[:rows], total[rows:].astype(F16)
-
-
-def reduce_pairs(up, pre, order):
-    keep = jnp.stack([up[0], pre[0]])
-    send = jnp.stack([up[1], pre[1]])
-    total = keep + swap(send, order[1]).astype(F32)
-    return total[:, :64] + swap(total[:, 64:].astype(F16), order[2]).astype(F32)
-
-
-def gather_pairs(g, h, order):
-    x = jnp.stack([g, h])
-    x = jnp.stack([x, swap(x, order[0])])
-    came = swap(x, order[1])
-    return [jnp.concatenate([x[:, n], came[:, n]]).reshape(256, -1) for n in range(2)]
+    return [(outs[2 * p], outs[2 * p + 1]) for p in range(3)]
+
+
+def first_kernel(*refs):
+    for p in range(3):
+        for n in range(2):
+            keep, came = refs[p * 4 + n * 2], refs[p * 4 + n * 2 + 1]
+            total = keep[...] + came[...].astype(F32)
+            refs[12 + p * 2][n] = total[:128]
+            refs[13 + p * 2][n] = total[128:].astype(BF16)
+
+
+def second_kernel(*refs):
+    for p in range(3):
+        total = refs[p * 2][...] + refs[p * 2 + 1][...].astype(F32)
+        refs[6 + p * 2][...] = total
+        refs[7 + p * 2][...] = total.astype(BF16)
+
+
+def third_kernel(*refs):
+    for p in range(3):
+        keep, came, out = refs[p * 2], refs[p * 2 + 1], refs[6 + p]
+        for block in range(2):
+            mine, theirs = slice(block * 64, block * 64 + 64), slice(64 - block * 64, 128 - block * 64)
+            for first in range(0, out.shape[2], 128):
+                cols = slice(first, first + 128)
+                up = keep[0, mine, cols] + came[0, theirs, cols].astype(F32)
+                v = keep[1, mine, cols] + came[1, theirs, cols].astype(F32)
+                square = v * v
+                t = jnp.tanh(SLOPE * v * (1.0 + CUBE * square))
+                half = 0.5 * (1.0 + t)
+                out[1, mine, cols] = (v * half).astype(BF16)
+                bend = 0.5 * SLOPE * v * (1.0 - t * t) * (1.0 + 3.0 * CUBE * square)
+                out[0, mine, cols] = (up * (half + bend)).astype(BF16)
+
+
+SLOPE, CUBE = 0.7978845608028654, 0.044715
+
+
+def joint(kernel, name, arrays, shapes):
+    outs = pl.pallas_call(
+        kernel,
+        in_specs=[pl.BlockSpec(memory_space=pltpu.VMEM)] * len(arrays),
+        out_specs=[pl.BlockSpec(memory_space=pltpu.VMEM)] * len(shapes),
+        out_shape=[jax.ShapeDtypeStruct(*shape) for shape in shapes],
+        compiler_params=pltpu.CompilerParams(vmem_limit_bytes=16 * MIB),
+        cost_estimate=pl.CostEstimate(flops=MIB, bytes_accessed=MIB, transcendentals=0),
+        name=name,
+    )(*arrays)
+    return list(outs)
+
+
+def exchange_sums(up, pre):
+    widths = [CUTS[p + 1] - CUTS[p] for p in range(3)]
+    arrays = []
+    for p, order in enumerate(ORDERS):
+        for keep, send in (up[p], pre[p]):
+            arrays += [keep, swap(send, order[0])]
+    pair = [((2, 128, width), dtype) for width in widths for dtype in (F32, BF16)]
+    left = joint(first_kernel, "first_sums", arrays, pair)
+    for p, order in enumerate(ORDERS):
+        left[p * 2 + 1] = swap(left[p * 2 + 1], order[1])
+    left = joint(second_kernel, "second_sums", left, pair)
+    for p, order in enumerate(ORDERS):
+        left[p * 2 + 1] = swap(left[p * 2 + 1], order[2])
+    return joint(third_kernel, "third_sums", left, [((2, 128, width), BF16) for width in widths])
+
+
+def fourth_kernel(*refs):
+    for p in range(3):
+        for k in range(2):
+            refs[6 + p][k] = refs[p * 2 + k][...]
+
+
+def gather(parts):
+    arrays = []
+    for x, order in zip(parts, ORDERS):
+        arrays += [x, swap(x, order[1])]
+    held = joint(fourth_kernel, "fourth_blocks", arrays, [((2, *x.shape), BF16) for x in parts])
+    pieces = []
+    for x, order in zip(held, ORDERS):
+        pieces += [x, swap(x, order[0])]
+    return pieces
 
 
 def assemble(at, pieces, whole):
@@ -183,14 +243,14 @@
         base = at[1] * 2048 if h == 0 else (1 - at[1]) * 2048
         for p, order in enumerate(ORDERS):
             cols = pl.ds(pl.multiple_of(base + CUTS[p], 256), CUTS[p + 1] - CUTS[p])
-            for q, j in enumerate(places(order[::-1])):
+            for q, j in enumerate(places(order)):
                 dst = pl.multiple_of(jnp.bitwise_xor(at[0], j) * 64, 64)
                 src = pieces[h * 6 + p * 2 + q // 4]
-                whole[pl.ds(dst, 64), cols] = src[q % 4 * 64 : (q % 4 + 1) * 64, :]
+                whole[pl.ds(dst, 64), cols] = src[q // 2 % 2, 0, q % 2 * 64 : q % 2 * 64 + 64, :]
 
 
 def back_kernel(at, *refs):
-    pieces, w, out, whole = refs[:12], refs[12], refs[16], refs[20]
+    pieces, w, out, whole = refs[:12], refs[12], refs[13], refs[14]
     assemble(at, pieces, whole)
     total = jnp.zeros((512, 512), F32)
     for k in range(4):
@@ -205,55 +265,85 @@
         out[:, 1, tile] = jnp.where(low, r[2 * t], c[2 * t + 1]).astype(BF16)
 
 
-def back_messages(at, pieces, w_in, later):
-    anywhere = pl.BlockSpec(memory_space=pl.ANY)
-    outs = pl.pallas_call(
+def back_messages(at, pieces, w_in):
+    return pl.pallas_call(
         back_kernel,
-        in_specs=[SCALARS] + [pl.BlockSpec(memory_space=pltpu.VMEM)] * 13 + [anywhere] * 3,
-        out_specs=[pl.BlockSpec(memory_space=pltpu.VMEM)] + [anywhere] * 3,
-        out_shape=[pltpu.HBM((64, 2, 16, 128), BF16)] + [jax.ShapeDtypeStruct(x.shape, x.dtype) for x in later],
+        in_specs=[SCALARS] + [pl.BlockSpec(memory_space=pltpu.VMEM)] * 13,
+        out_specs=pl.BlockSpec(memory_space=pltpu.VMEM),
+        out_shape=pltpu.HBM((64, 2, 16, 128), BF16),
         scratch_shapes=[pltpu.VMEM((512, 4096), BF16)],
-        input_output_aliases={14 + k: 1 + k for k in range(3)},
-        compiler_params=pltpu.CompilerParams(vmem_limit_bytes=20 * MIB),
+        compiler_params=pltpu.CompilerParams(vmem_limit_bytes=24 * MIB),
         cost_estimate=pl.CostEstimate(flops=2 * 512 * 512 * 4096, bytes_accessed=8 * MIB, transcendentals=0),
         name="back_messages",
-    )(at, *pieces, w_in, *later)
-    return outs[0], outs[1:]
-
-
-def grad_kernel(out_first, at, *refs):
-    pieces, x, out, whole, rows = refs[:12], refs[12], refs[13], refs[14], refs[15]
-
-    @pl.when(pl.program_id(0) == 0)
-    def _():
-        assemble(at, pieces, whole)
-        if not out_first:
-            rows_kernel(x, rows)
-
-    cols = pl.ds(pl.multiple_of(pl.program_id(0) * 1024, 1024), 1024)
+    )(at, *pieces, w_in)
+
+
+def grads_kernel(at, *refs):
+    pieces, (x, cot, grad_in, grad_out), scratch = refs[:12], refs[12:16], refs[16:]
+    held, rows, turned, wide_in, wide_out, loads, stores = scratch
+    todo = [(p, h) for p in range(3) for h in range(2)]
+    arrivals = {}
+    for p, h in todo:
+        for which in range(2):
+            for k in range(2):
+                n = h * 6 + p * 2 + k
+                target = held.at[which, h * 3 + p, k, :, :, 0 : CUTS[p + 1] - CUTS[p]]
+                copy = pltpu.make_async_copy(pieces[n].at[:, which], target, loads.at[which * 12 + n])
+                copy.start()
+                arrivals[which, h, p, k] = copy
+    rows_kernel(x, rows)
     dims = (((0,), (0,)), ((), ()))
-    if out_first:
-        out[...] = lax.dot_general(whole[:, cols], x[...], dims, preferred_element_type=F32)
-    else:
-        out[...] = lax.dot_general(rows[...], whole[:, cols], dims, preferred_element_type=F32)
-
-
-def grad_of(at, pieces, x, out_first):
-    block, shape = ((1024, 512), (4096, 512)) if out_first else ((512, 1024), (512, 4096))
+    leaving = []
+
+    def send(buffer, target):
+        leaving.append(pltpu.make_async_copy(buffer, target, stores.at[len(leaving)]))
+        leaving[-1].start()
+
+    for p, h in todo:
+        if h == 0:
+            for q, j in enumerate(places(ORDERS[p])):
+                src = pl.multiple_of(jnp.bitwise_xor(at[0], j) * 64, 64)
+                turned[0, q * 64 : (q + 1) * 64, :] = rows[pl.ds(src, 64), :]
+                turned[1, q * 64 : (q + 1) * 64, :] = cot[pl.ds(src, 64), :]
+        for which in range(2):
+            for k in range(2):
+                arrivals[which, h, p, k].wait()
+            for first in range(0, CUTS[p + 1] - CUTS[p], 256):
+                piece = held[which, h * 3 + p, :, :, :, first : first + 256].reshape(512, 256)
+                slot = (h * 2048 + CUTS[p] + first) // 256
+                base = (at[1] if h == 0 else 1 - at[1]) * 2048 + CUTS[p] + first
+                span = pl.ds(pl.multiple_of(base, 256), 256)
+                if which == 0:
+                    wide_in[slot] = lax.dot_general(turned[0], piece, dims, preferred_element_type=F32)
+                    send(wide_in.at[slot], grad_in.at[:, span])
+                else:
+                    wide_out[slot] = lax.dot_general(piece, turned[1], dims, preferred_element_type=F32)
+                    send(wide_out.at[slot], grad_out.at[span, :])
+    for copy in leaving:
+        copy.wait()
+
+
+def grads_of(at, pieces, x, cot):
+    anywhere, vmem = pl.BlockSpec(memory_space=pl.ANY), pl.BlockSpec(memory_space=pltpu.VMEM)
     pieces = [pltpu.with_memory_space_constraint(p, pltpu.HBM) for p in pieces]
     return pl.pallas_call(
-        functools.partial(grad_kernel, out_first),
-        grid=(4,),
-        in_specs=[SCALARS]
-        + [pl.BlockSpec(p.shape, lambda i: (0, 0)) for p in pieces]
-        + [pl.BlockSpec(x.shape, lambda i: (0,) * len(x.shape))],
-        out_specs=pl.BlockSpec(block, lambda i: (i, 0) if out_first else (0, i)),
-        out_shape=jax.ShapeDtypeStruct(shape, F32),
-        scratch_shapes=[pltpu.VMEM((512, 4096), BF16), pltpu.VMEM((512, 512), BF16)],
-        compiler_params=pltpu.CompilerParams(vmem_limit_bytes=22 * MIB),
-        cost_estimate=pl.CostEstimate(flops=2 * 512 * 512 * 4096, bytes_accessed=12 * MIB, transcendentals=0),
-        name="grad_out" if out_first else "grad_in",
-    )(at, *pieces, x)
+        grads_kernel,
+        in_specs=[SCALARS] + [anywhere] * 12 + [vmem] * 2,
+        out_specs=[anywhere] * 2,
+        out_shape=[pltpu.HBM((512, 4096), F32), pltpu.HBM((4096, 512), F32)],
+        scratch_shapes=[
+            pltpu.VMEM((2, 6, 2, 2, 128, 768), BF16),
+            pltpu.VMEM((512, 512), BF16),
+            pltpu.VMEM((2, 512, 512), BF16),
+            pltpu.VMEM((16, 512, 256), F32),
+            pltpu.VMEM((16, 256, 512), F32),
+            pltpu.SemaphoreType.DMA((24,)),
+            pltpu.SemaphoreType.DMA((32,)),
+        ],
+        compiler_params=pltpu.CompilerParams(vmem_limit_bytes=36 * MIB),
+        cost_estimate=pl.CostEstimate(flops=4 * 512 * 512 * 4096, bytes_accessed=24 * MIB, transcendentals=0),
+        name="grads",
+    )(at, *pieces, x, cot)
 
 
 def act_kernel(x, act, gain, out, twice, back):
@@ -291,15 +381,6 @@
     )(x.reshape(2, 8, 8, 16, 128), act, gain.reshape(1, -1))
 
 
-def gelu_tanh(inner):
-    return jax.nn.gelu(inner, approximate=True)
-
-
-def activate(preact, upstream):
-    value, pullback = jax.vjp(gelu_tanh, preact)
-    return value.astype(BF16), pullback(upstream)[0].astype(BF16)
-
-
 def local(act, gain, shift, w_in, w_out, cotangent):
     section, tensor = lax.axis_index("section"), lax.axis_index("tensor")
     core, ring = lax.bitwise_and(tensor, 1), lax.shift_right_logical(tensor, 1)
@@ -312,29 +393,16 @@
     in_other = swap(w_in, "core")
     messages = norm_messages(act, gain, shift)
     mixed = lax.all_to_all(messages.reshape(128, 16, 128), EVERY, 0, 0, tiled=True).reshape(64, 2, 16, 128)
+    mixed_other = swap(mixed, "core")
     up = chip_sum(at, cotangent, cot_other, w_out, out_other, [], True)
-    up = [halve(*pair, order[0]) for pair, order in zip(up, ORDERS)]
-    mixed_other = swap(mixed, "core")
-    pre = chip_sum(at, mixed, mixed_other, w_in, in_other, [pair[0] for pair in up], False)
-    pre = [halve(*pair, order[0]) for pair, order in zip(pre, ORDERS)]
-    pre_grad, hidden = [], []
-    for u, v, order in zip(up, pre, ORDERS):
-        total = reduce_pairs(u, v, order) * (1.0 / LIFT)
-        h, g = activate(total[1], total[0])
-        g, h = gather_pairs(g, h, order)
-        pre_grad += [g, swap(g, order[2])]
-        hidden.append(h)
-
-    def both(pieces):
-        return pieces + [swap(p, "core") for p in pieces]
-
-    pre_grad = both(pre_grad)
-    share, hidden = back_messages(at, pre_grad, w_in, hidden)
-    hidden = [p for h, order in zip(hidden, ORDERS) for p in (h, swap(h, order[2]))]
+    pre = chip_sum(at, mixed, mixed_other, w_in, in_other, [up[0][0]], False)
+    pieces = gather(exchange_sums(up, pre))
+    pieces += [swap(p, "core") for p in pieces]
+
+    share = back_messages(at, pieces, w_in)
     returned = lax.all_to_all(share.reshape(128, 16, 128), EVERY, 0, 0, tiled=True)
     grad_act = grad_act_of(returned, act, gain)
-    grad_in = grad_of(at, pre_grad, mixed, False)
-    grad_out = grad_of(at, both(hidden), cotangent, True)
+    grad_in, grad_out = grads_of(at, pieces, mixed, cotangent)
     return (grad_in, grad_out, grad_act)
 
 

time: 156 us -> 144 us (0.923)
  starting transfers between devices: 61.7 us -> 56.1 us
  other arithmetic: 3.78 us -> 0.07 us
  Pallas kernels: 32.7 us -> 30.2 us
  waiting for transfers between devices: 52.3 us -> 54.4 us
  local copies, waits for them, and re-layouts: 3.7 us -> 1.89 us
    all_to_all x1, waiting for transfers between devices: 2.67 us -> 12.4 us  [local(): lax.all_to_all(messages.reshape(128, 16, 128), EVERY, 0, 0, tiled=True)]
    ppermute x40 -> x28, waiting for transfers between devices: 48.3 us -> 39.5 us  [swap(): return lax.ppermute(x, OWNERS, pairs)]
    ppermute x40 -> x28, starting transfers between devices: 45.6 us -> 41.7 us  [swap(): return lax.ppermute(x, OWNERS, pairs)]
    pallas_call x2 -> x5, Pallas kernels: 15.1 us -> 12.5 us  [the longest x1 10.9 us: grads_of(): pl.pallas_call(grads_kernel, in_specs=[SCALARS] + [anywhere] * 12 + [vmem...]
    all_to_all x1, starting transfers between devices: 5.81 us -> 3.94 us  [local(): lax.all_to_all(share.reshape(128, 16, 128), EVERY, 0, 0, tiled=True)]
    add x9 -> x0, other arithmetic: 1.82 us -> none  [the longest x6 1.59 us: halve(): total = keep + swap(send, link).astype(F32)]
    unnamed x48 -> x32, local copies, waits for them, and re-layouts: 3.56 us -> 1.89 us
  transfers between devices with their start and end apart: 42 -> 30, of which waited for: 18 -> 14; matrix products, arithmetic and copies ran while one was open for 3% -> 0% of each run, Pallas kernels for 11% -> 16%
where the time goes in v2:
time: 144 us
  starting transfers between devices  56.1 us (39%)
  waiting for transfers between devices  54.4 us (38%)
  Pallas kernels  30.2 us (21%)
  local copies, waits for them, and re-layouts  1.89 us (1%)
    ppermute x28, starting transfers between devices, swap(): return lax.ppermute(x, OWNERS, pairs)  41.7 us
    ppermute x28, waiting for transfers between devices, swap(): return lax.ppermute(x, OWNERS, pairs)  39.5 us
    all_to_all x1, waiting for transfers between devices, local(): lax.all_to_all(messages.reshape(128, 16, 128), EVERY, 0, 0, tiled=True)  12.4 us
    pallas_call x1, Pallas kernels, grads_of(): pl.pallas_call(grads_kernel, in_specs=[SCALARS] + [anywhere] * 12 + [vmem...  10.9 us
    all_to_all x1, starting transfers between devices, local(): lax.all_to_all(messages.reshape(128, 16, 128), EVERY, 0, 0, tiled=True)  10.5 us
    pallas_call x2, Pallas kernels, chip_sum(): pl.pallas_call(up_kernel if up else pre_kernel, grid_spec=pltpu.PrefetchS...  9.41 us
    pallas_call x1, Pallas kernels, back_messages(): pl.pallas_call(back_kernel, in_specs=[SCALARS] + [pl.BlockSpec(memory_spa...  3.94 us
    all_to_all x1, starting transfers between devices, local(): lax.all_to_all(share.reshape(128, 16, 128), EVERY, 0, 0, tiled=True)  3.94 us
  transfers between devices with their start and end apart: 30, of which 14 were waited for; matrix products, arithmetic and copies ran while one was open for 0% of the time, Pallas kernels for 16%

profile of v2, /device:TPU:1, one launch (start us, length us, event | category | flops | bytes accessed | tf_op | source)
XLA Modules:
  0.0 143.6 jit_solution(9486003635921954075)
XLA Ops:
  0.6 1.5 %collective-permute-start.1 = (bf16[4096,512]{1,0:T(8,128)(2,1)}, bf16[4096,512]{1,0:T(8,128)(2,1)}, u32[]{:S(2)}, u32[]{:S(2)}) collective-permute-start(bf16[4096,512]{1,0:T(8,128)(2,1)} %w.2), channel_id=1, source_target_pairs={{0,1},{1,0},{2,3},{3,2},{4,5},{5,4},{6,7},{7,6},{64,65},{65,64},{6... | collective-permute-start | bytes 12582920 | tf_op jit(solution)/shard_map/ppermute | solution.py:28
  2.2 2.1 %norm_messages.1 = bf16[2,8,8,16,128]{4,3,2,1,0:T(8,128)(2,1)} custom-call(bf16[4,8192]{1,0:T(4,128)(2,1)} %act.3, f32[1,8192]{1,0:T(1,128)} %bitcast.14, f32[1,8192]{1,0:T(1,128)} %bitcast.16), custom_call_target="tpu_custom_call" | custom-call | tf_op jit(solution)/shard_map/norm_messages/pallas_call | solution.py:56
  4.3 10.5 %all-to-all-start = ((bf16[128,16,128]{2,1,0:T(8,128)(2,1)}), bf16[128,16,128]{2,1,0:T(8,128)(2,1)S(1)}, u32[]{:S(2)}, u32[]{:S(2)}) async-start(bf16[128,16,128]{2,1,0:T(8,128)(2,1)} %bitcast.12), calls=%async_computation | async-start | bytes 1048576 | tf_op jit(solution)/shard_map/all_to_all | solution.py:395
  14.8 1.1 collective-permute-start
  15.9 12.4 %all-to-all-done = bf16[128,16,128]{2,1,0:T(8,128)(2,1)S(1)} async-done(((bf16[128,16,128]{2,1,0:T(8,128)(2,1)}), bf16[128,16,128]{2,1,0:T(8,128)(2,1)S(1)}, u32[]{:S(2)}, u32[]{:S(2)}) %all-to-all-start) | async-done | bytes 524320 | tf_op jit(solution)/shard_map/all_to_all | solution.py:395
  28.3 1.1 collective-permute-start.3
  29.5 1.0 copy-done.9
  30.5 4.7 %up_sum.1 = (f32[256,768]{1,0:T(8,128)S(1)}, bf16[256,768]{1,0:T(8,128)(2,1)S(1)}, f32[256,768]{1,0:T(8,128)S(1)}, bf16[256,768]{1,0:T(8,128)(2,1)S(1)}, f32[256...) custom-call(s32[2]{0:T(128)S(1)} %pad_add_fusion.at, bf16[512,512]{1,0:T(8,128)(2,1)S(1)} %copy-done.9, ...), custom_call_target="tpu_custom_call" | custom-call | flops 2147483648 | bytes 9437184 | tf_op jit(solution)/shard_map/up_sum/pallas_call | solution.py:142
  35.2 0.2 collective-permute-start.2
  35.4 0.6 collective-permute-start.8
  36.0 4.7 %pre_sum.1 = (f32[256,768]{1,0:T(8,128)S(1)}, bf16[256,768]{1,0:T(8,128)(2,1)S(1)}, f32[256,768]{1,0:T(8,128)S(1)}, bf16[256,768]{1,0:T(8,128)(2,1)S(1)}, f32[25...) custom-call(s32[2]{0:T(128)S(1)} %pad_add_fusion.at, bf16[64,2,16,128]{3,2,1,0:T(8,128)(2,1)S(1)} %bitcast.9, ...), custom_call_target="tpu_custom_call" | custom-call | flops 2147483648 | bytes 9437184 | tf_op jit(solution)/shard_map/pre_sum/pallas_call | solution.py:142
  40.7 1.2 collective-permute-start.5
  41.9 1.1 collective-permute-start.6
  43.0 1.6 %collective-permute-start.7 = (bf16[256,768]{1,0:T(8,128)(2,1)S(1)}, bf16[256,768]{1,0:T(8,128)(2,1)S(1)}, u32[]{:S(2)}, u32[]{:S(2)}) collective-permute-start(bf16[256,768]{1,0:T(8,128)(2,1)S(1)} %get-tuple-element.42), channel_id=1, source_target_pairs={{0,6},{1,7},{2,4},{3,5},{4,2},{5,3},{6,0},{7,1},{64,70},{65,71},{6... | collective-permute-start | bytes 1179656 | tf_op jit(solution)/shard_map/ppermute | solution.py:28
  44.6 2.6 %collective-permute-start.9 = (bf16[256,512]{1,0:T(8,128)(2,1)S(1)}, bf16[256,512]{1,0:T(8,128)(2,1)S(1)}, u32[]{:S(2)}, u32[]{:S(2)}) collective-permute-start(bf16[256,512]{1,0:T(8,128)(2,1)S(1)} %get-tuple-element.46), channel_id=1, source_target_pairs={{0,64},{1,65},{2,66},{3,67},{4,68},{5,69},{6,70},{7,71},{64,0},{65... | collective-permute-start | bytes 786440 | tf_op jit(solution)/shard_map/ppermute | solution.py:28
  47.2 5.1 %collective-permute-done.9.refs_11_ = bf16[256,512]{1,0:T(8,128)(2,1)S(1)} collective-permute-done((bf16[256,512]{1,0:T(8,128)(2,1)S(1)}, bf16[256,512]{1,0:T(8,128)(2,1)S(1)}, u32[]{:S(2)}, u32[]{:S(2)}) %collective-permute-start.9) | collective-permute-done | bytes 262176 | tf_op jit(solution)/shard_map/ppermute | solution.py:28
  52.3 2.2 %collective-permute-done.5.refs_3_ = bf16[256,768]{1,0:T(8,128)(2,1)S(1)} collective-permute-done((bf16[256,768]{1,0:T(8,128)(2,1)S(1)}, bf16[256,768]{1,0:T(8,128)(2,1)S(1)}, u32[]{:S(2)}, u32[]{:S(2)}) %collective-permute-start.5) | collective-permute-done | bytes 393248 | tf_op jit(solution)/shard_map/ppermute | solution.py:28
  54.5 6.6 %collective-permute-done.7.refs_7_ = bf16[256,768]{1,0:T(8,128)(2,1)S(1)} collective-permute-done((bf16[256,768]{1,0:T(8,128)(2,1)S(1)}, bf16[256,768]{1,0:T(8,128)(2,1)S(1)}, u32[]{:S(2)}, u32[]{:S(2)}) %collective-permute-start.7) | collective-permute-done | bytes 393248 | tf_op jit(solution)/shard_map/ppermute | solution.py:28
  61.1 0.3 first_sums.1
  61.4 1.4 collective-permute-start.10
  62.8 1.6 %collective-permute-start.11 = (bf16[2,128,768]{2,1,0:T(8,128)(2,1)S(1)}, bf16[2,128,768]{2,1,0:T(8,128)(2,1)S(1)}, u32[]{:S(2)}, u32[]{:S(2)}) collective-permute-start(bf16[2,128,768]{2,1,0:T(8,128)(2,1)S(1)} %get-tuple-element.50), channel_id=1, source_target_pairs={{0,64},{1,65},{2,66},{3,67},{4,68},{5,69},{6,70},{7,71},{64,0},{65... | collective-permute-start | bytes 1179656 | tf_op jit(solution)/shard_map/ppermute | solution.py:28
  64.4 5.5 %collective-permute-done.12.refs_5_ = bf16[2,128,512]{2,1,0:T(8,128)(2,1)S(1)} collective-permute-done((bf16[2,128,512]{2,1,0:T(8,128)(2,1)S(1)}, bf16[2,128,512]{2,1,0:T(8,128)(2,1)S(1)}, u32[]{:S(2)}, u32[]{:S(2)}) %collective-permute-start.12) | collective-permute-done | bytes 262176 | tf_op jit(solution)/shard_map/ppermute | solution.py:28
  70.0 1.4 collective-permute-done.10.refs_1_
  71.4 1.5 %collective-permute-done.11.refs_3_ = bf16[2,128,768]{2,1,0:T(8,128)(2,1)S(1)} collective-permute-done((bf16[2,128,768]{2,1,0:T(8,128)(2,1)S(1)}, bf16[2,128,768]{2,1,0:T(8,128)(2,1)S(1)}, u32[]{:S(2)}, u32[]{:S(2)}) %collective-permute-start.11) | collective-permute-done | bytes 393248 | tf_op jit(solution)/shard_map/ppermute | solution.py:28
  72.9 0.3 second_sums.1
  73.2 1.6 %collective-permute-start.13 = (bf16[2,128,768]{2,1,0:T(8,128)(2,1)S(1)}, bf16[2,128,768]{2,1,0:T(8,128)(2,1)S(1)}, u32[]{:S(2)}, u32[]{:S(2)}) collective-permute-start(bf16[2,128,768]{2,1,0:T(8,128)(2,1)S(1)} %get-tuple-element.54), channel_id=1, source_target_pairs={{0,64},{1,65},{2,66},{3,67},{4,68},{5,69},{6,70},{7,71},{64,0},{65... | collective-permute-start | bytes 1179656 | tf_op jit(solution)/shard_map/ppermute | solution.py:28
  74.8 2.7 %collective-permute-start.15 = (bf16[2,128,512]{2,1,0:T(8,128)(2,1)S(1)}, bf16[2,128,512]{2,1,0:T(8,128)(2,1)S(1)}, u32[]{:S(2)}, u32[]{:S(2)}) collective-permute-start(bf16[2,128,512]{2,1,0:T(8,128)(2,1)S(1)} %get-tuple-element.58), channel_id=1, source_target_pairs={{0,6},{1,7},{2,4},{3,5},{4,2},{5,3},{6,0},{7,1},{64,70},{65,71},{6... | collective-permute-start | bytes 786440 | tf_op jit(solution)/shard_map/ppermute | solution.py:28
  77.5 4.1 %collective-permute-done.15.refs_5_ = bf16[2,128,512]{2,1,0:T(8,128)(2,1)S(1)} collective-permute-done((bf16[2,128,512]{2,1,0:T(8,128)(2,1)S(1)}, bf16[2,128,512]{2,1,0:T(8,128)(2,1)S(1)}, u32[]{:S(2)}, u32[]{:S(2)}) %collective-permute-start.15) | collective-permute-done | bytes 262176 | tf_op jit(solution)/shard_map/ppermute | solution.py:28
  81.5 0.9 collective-permute-done.13.refs_1_
  82.5 0.8 third_sums.1
  83.3 2.4 %collective-permute-start.16 = (bf16[2,128,768]{2,1,0:T(8,128)(2,1)S(1)}, bf16[2,128,768]{2,1,0:T(8,128)(2,1)S(1)}, u32[]{:S(2)}, u32[]{:S(2)}) collective-permute-start(bf16[2,128,768]{2,1,0:T(8,128)(2,1)S(1)} %get-tuple-element.59.refs_0_), channel_id=1, source_target_pairs={{0,6},{1,7},{2,4},{3,5},{4,2},{5,3},{6,0},{7,1},{64,70},{65,71},{6... | collective-permute-start | bytes 1179656 | tf_op jit(solution)/shard_map/ppermute | solution.py:28
  85.7 1.8 %collective-permute-start.17 = (bf16[2,128,768]{2,1,0:T(8,128)(2,1)S(1)}, bf16[2,128,768]{2,1,0:T(8,128)(2,1)S(1)}, u32[]{:S(2)}, u32[]{:S(2)}) collective-permute-start(bf16[2,128,768]{2,1,0:T(8,128)(2,1)S(1)} %get-tuple-element.60.refs_2_), channel_id=1, source_target_pairs={{0,64},{1,65},{2,66},{3,67},{4,68},{5,69},{6,70},{7,71},{64,0},{65... | collective-permute-start | bytes 1179656 | tf_op jit(solution)/shard_map/ppermute | solution.py:28
  87.5 5.5 %collective-permute-done.18.refs_5_ = bf16[2,128,512]{2,1,0:T(8,128)(2,1)S(1)} collective-permute-done((bf16[2,128,512]{2,1,0:T(8,128)(2,1)S(1)}, bf16[2,128,512]{2,1,0:T(8,128)(2,1)S(1)}, u32[]{:S(2)}, u32[]{:S(2)}) %collective-permute-start.18) | collective-permute-done | bytes 262176 | tf_op jit(solution)/shard_map/ppermute | solution.py:28
  93.0 0.8 collective-permute-done.17.refs_3_
  94.1 0.4 collective-permute-start.20
  94.5 2.1 %collective-permute-start.21 = (bf16[2,2,128,512]{3,2,1,0:T(8,128)(2,1)S(1)}, bf16[2,2,128,512]{3,2,1,0:T(8,128)(2,1)S(1)}, u32[]{:S(2)}, u32[]{:S(2)}) collective-permute-start(bf16[2,2,128,512]{3,2,1,0:T(8,128)(2,1)S(1)} %get-tuple-element.64.refs_4_), channel_id=1, source_target_pairs={{0,64},{1,65},{2,66},{3,67},{4,68},{5,69},{6,70},{7,71},{64,0},{65... | collective-permute-start | bytes 1572872 | tf_op jit(solution)/shard_map/ppermute | solution.py:28
  96.6 5.3 %collective-permute-start.26 = (bf16[2,2,128,512]{3,2,1,0:T(8,128)(2,1)S(1)}, bf16[2,2,128,512]{3,2,1,0:T(8,128)(2,1)S(1)}, u32[]{:S(2)}, u32[]{:S(2)}) collective-permute-start(bf16[2,2,128,512]{3,2,1,0:T(8,128)(2,1)S(1)} %get-tuple-element.64.refs_4_), channel_id=1, source_target_pairs={{0,1},{1,0},{2,3},{3,2},{4,5},{5,4},{6,7},{7,6},{64,65},{65,64},{6... | collective-permute-start | bytes 1572872 | tf_op jit(solution)/shard_map/ppermute | solution.py:28
  101.9 2.5 %collective-permute-done.21.refs_5_ = bf16[2,2,128,512]{3,2,1,0:T(8,128)(2,1)S(1)} collective-permute-done((bf16[2,2,128,512]{3,2,1,0:T(8,128)(2,1)S(1)}, bf16[2,2,128,512]{3,2,1,0:T(8,128)(2,1)S(1)}, u32[]{:S(2)}, u32[]{:S(2)}) %collective-permute-start.21) | collective-permute-done | bytes 524320 | tf_op jit(solution)/shard_map/ppermute | solution.py:28
  104.4 6.6 %collective-permute-start.24 = (bf16[2,2,128,768]{3,2,1,0:T(8,128)(2,1)S(1)}, bf16[2,2,128,768]{3,2,1,0:T(8,128)(2,1)S(1)}, u32[]{:S(2)}, u32[]{:S(2)}) collective-permute-start(bf16[2,2,128,768]{3,2,1,0:T(8,128)(2,1)S(1)} %get-tuple-element.63.refs_2_), channel_id=1, source_target_pairs={{0,1},{1,0},{2,3},{3,2},{4,5},{5,4},{6,7},{7,6},{64,65},{65,64},{6... | collective-permute-start | bytes 2359304 | tf_op jit(solution)/shard_map/ppermute | solution.py:28
  111.0 4.2 %collective-permute-start.23 = (bf16[2,2,128,768]{3,2,1,0:T(8,128)(2,1)S(1)}, bf16[2,2,128,768]{3,2,1,0:T(8,128)(2,1)S(1)}, u32[]{:S(2)}, u32[]{:S(2)}) collective-permute-start(bf16[2,2,128,768]{3,2,1,0:T(8,128)(2,1)S(1)} %collective-permute-done.19.refs_1_), channel_id=1, source_target_pairs={{0,1},{1,0},{2,3},{3,2},{4,5},{5,4},{6,7},{7,6},{64,65},{65,64},{6... | collective-permute-start | bytes 2359304 | tf_op jit(solution)/shard_map/ppermute | solution.py:28
  115.4 0.3 collective-permute-start.27
  115.7 3.2 %collective-permute-done.27.refs_11_ = bf16[2,2,128,512]{3,2,1,0:T(8,128)(2,1)S(1)} collective-permute-done((bf16[2,2,128,512]{3,2,1,0:T(8,128)(2,1)S(1)}, bf16[2,2,128,512]{3,2,1,0:T(8,128)(2,1)S(1)}, u32[]{:S(2)}, u32[]{:S(2)}) %collective-permute-start.27) | collective-permute-done | bytes 524320 | tf_op jit(solution)/shard_map/ppermute | solution.py:28
  119.0 3.9 %back_messages.1 = bf16[64,2,16,128]{3,2,1,0:T(8,128)(2,1)} custom-call(s32[2]{0:T(128)S(1)} %pad_add_fusion.at, bf16[2,2,128,768]{3,2,1,0:T(8,128)(2,1)S(1)} %get-tuple-element.62.refs_0_, bf16[2,2,128,768]{3,2,1,0:T(8,128)(2,1)S(1)} %collective-permute-done.19.refs_1_, bf16[2,2,128,768]{3,2,1,0:T(8,128)(2,1)S(1)} %get-tuple-element.63.refs_2_, ...), custom_call_target="tpu_custom_call" | custom-call | flops 2147483648 | bytes 8388608 | tf_op jit(solution)/shard_map/back_messages/pallas_call | solution.py:269
  123.0 3.9 %all-to-all-start.1 = ((bf16[128,16,128]{2,1,0:T(8,128)(2,1)}), bf16[128,16,128]{2,1,0:T(8,128)(2,1)S(1)}, u32[]{:S(2)}, u32[]{:S(2)}) async-start(bf16[128,16,128]{2,1,0:T(8,128)(2,1)} %bitcast.11), calls=%async_computation.1 | async-start | bytes 1048576 | tf_op jit(solution)/shard_map/all_to_all | solution.py:403
  127.0 10.9 %grads.1 = (f32[512,4096]{1,0:T(8,128)}, f32[4096,512]{1,0:T(8,128)}) custom-call(s32[2]{0:T(128)S(1)} %pad_add_fusion.at, bf16[2,2,128,768]{3,2,1,0:T(8,128)(2,1)} %copy-done.1, bf16[2,2,128,768]{3,2,1,0:T(8,128)(2,1)} %copy-done.3, bf16[2,2,128,768]{3,2,1,0:T(8,128)(2,1)} %copy-done.2, bf16[2,2,128,768]{3,2,1,0:T(8,128)(2,1)} %copy-done.4, ...), custom_call_target="tpu_custom_call" | custom-call | flops 4294967296 | bytes 25165824 | tf_op jit(solution)/shard_map/grads/pallas_call | solution.py:329
  137.9 2.6 %all-to-all-done.1 = bf16[128,16,128]{2,1,0:T(8,128)(2,1)S(1)} async-done(((bf16[128,16,128]{2,1,0:T(8,128)(2,1)}), bf16[128,16,128]{2,1,0:T(8,128)(2,1)S(1)}, u32[]{:S(2)}, u32[]{:S(2)}) %all-to-all-start.1) | async-done | bytes 524320 | tf_op jit(solution)/shard_map/all_to_all | solution.py:403
  140.5 0.8 copy-done.15
  141.3 2.3 %grad_act.1 = f32[4,8192]{1,0:T(4,128)} custom-call(bf16[2,8,8,16,128]{4,3,2,1,0:T(8,128)(2,1)} %bitcast.13, bf16[4,8192]{1,0:T(4,128)(2,1)} %act.3, f32[1,8192]{1,0:T(1,128)} %bitcast.15), custom_call_target="tpu_custom_call" | custom-call | tf_op jit(solution)/shard_map/grad_act/pallas_call | solution.py:376
  (55 shorter events, 0.7 us)
Async XLA Ops:
  0.6 28.8 %collective-permute-start.1 = (bf16[4096,512]{1,0:T(8,128)(2,1)}, bf16[4096,512]{1,0:T(8,128)(2,1)}, u32[]{:S(2)}, u32[]{:S(2)}) collective-permute-start(bf16[4096,512]{1,0:T(8,128)(2,1)} %w.2), channel_id=1, source_target_pairs={{0,1},{1,0},{2,3},{3,2},{4,5},{5,4},{6,7},{7,6},{64,65},{65,64},{6... | collective-permute-start | bytes 12582920 | tf_op jit(solution)/shard_map/ppermute | solution.py:28
  2.1 33.9 %collective-permute-start.4 = (bf16[512,4096]{1,0:T(8,128)(2,1)}, bf16[512,4096]{1,0:T(8,128)(2,1)}, u32[]{:S(2)}, u32[]{:S(2)}) collective-permute-start(bf16[512,4096]{1,0:T(8,128)(2,1)} %refs_12_.1), channel_id=1, source_target_pairs={{0,1},{1,0},{2,3},{3,2},{4,5},{5,4},{6,7},{7,6},{64,65},{65,64},{6... | collective-permute-start | bytes 12582920 | tf_op jit(solution)/shard_map/ppermute | solution.py:28
  4.3 24.0 %all-to-all-start = ((bf16[128,16,128]{2,1,0:T(8,128)(2,1)}), bf16[128,16,128]{2,1,0:T(8,128)(2,1)S(1)}, u32[]{:S(2)}, u32[]{:S(2)}) async-start(bf16[128,16,128]{2,1,0:T(8,128)(2,1)} %bitcast.12), calls=%async_computation | async-start | bytes 1048576 | tf_op jit(solution)/shard_map/all_to_all | solution.py:395
  14.8 14.7 %collective-permute-start = (bf16[512,512]{1,0:T(8,128)(2,1)}, bf16[512,512]{1,0:T(8,128)(2,1)S(1)}, u32[]{:S(2)}, u32[]{:S(2)}) collective-permute-start(bf16[512,512]{1,0:T(8,128)(2,1)} %refs_13_.1), channel_id=1, source_target_pairs={{0,1},{1,0},{2,3},{3,2},{4,5},{5,4},{6,7},{7,6},{64,65},{65,64},{6... | collective-permute-start | bytes 1572872 | tf_op jit(solution)/shard_map/ppermute | solution.py:28
  28.3 7.7 %collective-permute-start.3 = (bf16[64,2,16,128]{3,2,1,0:T(8,128)(2,1)S(1)}, bf16[64,2,16,128]{3,2,1,0:T(8,128)(2,1)S(1)}, u32[]{:S(2)}, u32[]{:S(2)}) collective-permute-start(bf16[64,2,16,128]{3,2,1,0:T(8,128)(2,1)S(1)} %bitcast.8), channel_id=1, source_target_pairs={{0,1},{1,0},{2,3},{3,2},{4,5},{5,4},{6,7},{7,6},{64,65},{65,64},{6... | collective-permute-start | bytes 1572872 | tf_op jit(solution)/shard_map/ppermute | solution.py:28
  29.4 1.0 copy-start.9
  35.2 17.1 %collective-permute-start.2 = (bf16[256,768]{1,0:T(8,128)(2,1)S(1)}, bf16[256,768]{1,0:T(8,128)(2,1)S(1)}, u32[]{:S(2)}, u32[]{:S(2)}) collective-permute-start(bf16[256,768]{1,0:T(8,128)(2,1)S(1)} %get-tuple-element.36), channel_id=1, source_target_pairs={{0,2},{1,3},{2,0},{3,1},{4,6},{5,7},{6,4},{7,5},{64,66},{65,67},{6... | collective-permute-start | bytes 1179656 | tf_op jit(solution)/shard_map/ppermute | solution.py:28
  35.4 9.1 %collective-permute-start.8 = (bf16[256,512]{1,0:T(8,128)(2,1)S(1)}, bf16[256,512]{1,0:T(8,128)(2,1)S(1)}, u32[]{:S(2)}, u32[]{:S(2)}) collective-permute-start(bf16[256,512]{1,0:T(8,128)(2,1)S(1)} %get-tuple-element.44), channel_id=1, source_target_pairs={{0,64},{1,65},{2,66},{3,67},{4,68},{5,69},{6,70},{7,71},{64,0},{65... | collective-permute-start | bytes 786440 | tf_op jit(solution)/shard_map/ppermute | solution.py:28
  40.7 13.8 %collective-permute-start.5 = (bf16[256,768]{1,0:T(8,128)(2,1)S(1)}, bf16[256,768]{1,0:T(8,128)(2,1)S(1)}, u32[]{:S(2)}, u32[]{:S(2)}) collective-permute-start(bf16[256,768]{1,0:T(8,128)(2,1)S(1)} %get-tuple-element.38), channel_id=1, source_target_pairs={{0,2},{1,3},{2,0},{3,1},{4,6},{5,7},{6,4},{7,5},{64,66},{65,67},{6... | collective-permute-start | bytes 1179656 | tf_op jit(solution)/shard_map/ppermute | solution.py:28
  41.9 12.6 %collective-permute-start.6 = (bf16[256,768]{1,0:T(8,128)(2,1)S(1)}, bf16[256,768]{1,0:T(8,128)(2,1)S(1)}, u32[]{:S(2)}, u32[]{:S(2)}) collective-permute-start(bf16[256,768]{1,0:T(8,128)(2,1)S(1)} %get-tuple-element.40), channel_id=1, source_target_pairs={{0,6},{1,7},{2,4},{3,5},{4,2},{5,3},{6,0},{7,1},{64,70},{65,71},{6... | collective-permute-start | bytes 1179656 | tf_op jit(solution)/shard_map/ppermute | solution.py:28
  43.0 18.1 %collective-permute-start.7 = (bf16[256,768]{1,0:T(8,128)(2,1)S(1)}, bf16[256,768]{1,0:T(8,128)(2,1)S(1)}, u32[]{:S(2)}, u32[]{:S(2)}) collective-permute-start(bf16[256,768]{1,0:T(8,128)(2,1)S(1)} %get-tuple-element.42), channel_id=1, source_target_pairs={{0,6},{1,7},{2,4},{3,5},{4,2},{5,3},{6,0},{7,1},{64,70},{65,71},{6... | collective-permute-start | bytes 1179656 | tf_op jit(solution)/shard_map/ppermute | solution.py:28
  44.6 7.7 %collective-permute-start.9 = (bf16[256,512]{1,0:T(8,128)(2,1)S(1)}, bf16[256,512]{1,0:T(8,128)(2,1)S(1)}, u32[]{:S(2)}, u32[]{:S(2)}) collective-permute-start(bf16[256,512]{1,0:T(8,128)(2,1)S(1)} %get-tuple-element.46), channel_id=1, source_target_pairs={{0,64},{1,65},{2,66},{3,67},{4,68},{5,69},{6,70},{7,71},{64,0},{65... | collective-permute-start | bytes 786440 | tf_op jit(solution)/shard_map/ppermute | solution.py:28
  61.4 9.9 %collective-permute-start.10 = (bf16[2,128,768]{2,1,0:T(8,128)(2,1)S(1)}, bf16[2,128,768]{2,1,0:T(8,128)(2,1)S(1)}, u32[]{:S(2)}, u32[]{:S(2)}) collective-permute-start(bf16[2,128,768]{2,1,0:T(8,128)(2,1)S(1)} %get-tuple-element.48), channel_id=1, source_target_pairs={{0,6},{1,7},{2,4},{3,5},{4,2},{5,3},{6,0},{7,1},{64,70},{65,71},{6... | collective-permute-start | bytes 1179656 | tf_op jit(solution)/shard_map/ppermute | solution.py:28
  62.8 10.1 %collective-permute-start.11 = (bf16[2,128,768]{2,1,0:T(8,128)(2,1)S(1)}, bf16[2,128,768]{2,1,0:T(8,128)(2,1)S(1)}, u32[]{:S(2)}, u32[]{:S(2)}) collective-permute-start(bf16[2,128,768]{2,1,0:T(8,128)(2,1)S(1)} %get-tuple-element.50), channel_id=1, source_target_pairs={{0,64},{1,65},{2,66},{3,67},{4,68},{5,69},{6,70},{7,71},{64,0},{65... | collective-permute-start | bytes 1179656 | tf_op jit(solution)/shard_map/ppermute | solution.py:28
  64.4 5.5 %collective-permute-start.12 = (bf16[2,128,512]{2,1,0:T(8,128)(2,1)S(1)}, bf16[2,128,512]{2,1,0:T(8,128)(2,1)S(1)}, u32[]{:S(2)}, u32[]{:S(2)}) collective-permute-start(bf16[2,128,512]{2,1,0:T(8,128)(2,1)S(1)} %get-tuple-element.52), channel_id=1, source_target_pairs={{0,2},{1,3},{2,0},{3,1},{4,6},{5,7},{6,4},{7,5},{64,66},{65,67},{6... | collective-permute-start | bytes 786440 | tf_op jit(solution)/shard_map/ppermute | solution.py:28
  72.9 46.1 %copy-start = (bf16[512,4096]{1,0:T(8,128)(2,1)S(1)}, bf16[512,4096]{1,0:T(8,128)(2,1)}, u32[]{:S(2)}) copy-start(bf16[512,4096]{1,0:T(8,128)(2,1)} %refs_12_.1) | copy-start | bytes 12582916
  73.2 9.3 %collective-permute-start.13 = (bf16[2,128,768]{2,1,0:T(8,128)(2,1)S(1)}, bf16[2,128,768]{2,1,0:T(8,128)(2,1)S(1)}, u32[]{:S(2)}, u32[]{:S(2)}) collective-permute-start(bf16[2,128,768]{2,1,0:T(8,128)(2,1)S(1)} %get-tuple-element.54), channel_id=1, source_target_pairs={{0,64},{1,65},{2,66},{3,67},{4,68},{5,69},{6,70},{7,71},{64,0},{65... | collective-permute-start | bytes 1179656 | tf_op jit(solution)/shard_map/ppermute | solution.py:28
  74.8 7.7 %collective-permute-start.14 = (bf16[2,128,768]{2,1,0:T(8,128)(2,1)S(1)}, bf16[2,128,768]{2,1,0:T(8,128)(2,1)S(1)}, u32[]{:S(2)}, u32[]{:S(2)}) collective-permute-start(bf16[2,128,768]{2,1,0:T(8,128)(2,1)S(1)} %get-tuple-element.56), channel_id=1, source_target_pairs={{0,2},{1,3},{2,0},{3,1},{4,6},{5,7},{6,4},{7,5},{64,66},{65,67},{6... | collective-permute-start | bytes 1179656 | tf_op jit(solution)/shard_map/ppermute | solution.py:28
  74.8 6.7 %collective-permute-start.15 = (bf16[2,128,512]{2,1,0:T(8,128)(2,1)S(1)}, bf16[2,128,512]{2,1,0:T(8,128)(2,1)S(1)}, u32[]{:S(2)}, u32[]{:S(2)}) collective-permute-start(bf16[2,128,512]{2,1,0:T(8,128)(2,1)S(1)} %get-tuple-element.58), channel_id=1, source_target_pairs={{0,6},{1,7},{2,4},{3,5},{4,2},{5,3},{6,0},{7,1},{64,70},{65,71},{6... | collective-permute-start | bytes 786440 | tf_op jit(solution)/shard_map/ppermute | solution.py:28
  83.3 9.8 %collective-permute-start.16 = (bf16[2,128,768]{2,1,0:T(8,128)(2,1)S(1)}, bf16[2,128,768]{2,1,0:T(8,128)(2,1)S(1)}, u32[]{:S(2)}, u32[]{:S(2)}) collective-permute-start(bf16[2,128,768]{2,1,0:T(8,128)(2,1)S(1)} %get-tuple-element.59.refs_0_), channel_id=1, source_target_pairs={{0,6},{1,7},{2,4},{3,5},{4,2},{5,3},{6,0},{7,1},{64,70},{65,71},{6... | collective-permute-start | bytes 1179656 | tf_op jit(solution)/shard_map/ppermute | solution.py:28
  85.7 8.1 %collective-permute-start.17 = (bf16[2,128,768]{2,1,0:T(8,128)(2,1)S(1)}, bf16[2,128,768]{2,1,0:T(8,128)(2,1)S(1)}, u32[]{:S(2)}, u32[]{:S(2)}) collective-permute-start(bf16[2,128,768]{2,1,0:T(8,128)(2,1)S(1)} %get-tuple-element.60.refs_2_), channel_id=1, source_target_pairs={{0,64},{1,65},{2,66},{3,67},{4,68},{5,69},{6,70},{7,71},{64,0},{65... | collective-permute-start | bytes 1179656 | tf_op jit(solution)/shard_map/ppermute | solution.py:28
  87.5 5.5 %collective-permute-start.18 = (bf16[2,128,512]{2,1,0:T(8,128)(2,1)S(1)}, bf16[2,128,512]{2,1,0:T(8,128)(2,1)S(1)}, u32[]{:S(2)}, u32[]{:S(2)}) collective-permute-start(bf16[2,128,512]{2,1,0:T(8,128)(2,1)S(1)} %get-tuple-element.61.refs_4_), channel_id=1, source_target_pairs={{0,2},{1,3},{2,0},{3,1},{4,6},{5,7},{6,4},{7,5},{64,66},{65,67},{6... | collective-permute-start | bytes 786440 | tf_op jit(solution)/shard_map/ppermute | solution.py:28
  94.0 28.9 %copy-start.1 = (bf16[2,2,128,768]{3,2,1,0:T(8,128)(2,1)}, bf16[2,2,128,768]{3,2,1,0:T(8,128)(2,1)S(1)}, u32[]{:S(2)}) copy-start(bf16[2,2,128,768]{3,2,1,0:T(8,128)(2,1)S(1)} %get-tuple-element.62.refs_0_) | copy-start | bytes 2359300
  94.0 28.9 %copy-start.2 = (bf16[2,2,128,768]{3,2,1,0:T(8,128)(2,1)}, bf16[2,2,128,768]{3,2,1,0:T(8,128)(2,1)S(1)}, u32[]{:S(2)}) copy-start(bf16[2,2,128,768]{3,2,1,0:T(8,128)(2,1)S(1)} %get-tuple-element.63.refs_2_) | copy-start | bytes 2359300
  94.0 28.9 %copy-start.11 = (bf16[2,2,128,512]{3,2,1,0:T(8,128)(2,1)}, bf16[2,2,128,512]{3,2,1,0:T(8,128)(2,1)S(1)}, u32[]{:S(2)}) copy-start(bf16[2,2,128,512]{3,2,1,0:T(8,128)(2,1)S(1)} %get-tuple-element.64.refs_4_) | copy-start | bytes 1572868
  94.0 17.0 %collective-permute-start.19 = (bf16[2,2,128,768]{3,2,1,0:T(8,128)(2,1)S(1)}, bf16[2,2,128,768]{3,2,1,0:T(8,128)(2,1)S(1)}, u32[]{:S(2)}, u32[]{:S(2)}) collective-permute-start(bf16[2,2,128,768]{3,2,1,0:T(8,128)(2,1)S(1)} %get-tuple-element.62.refs_0_), channel_id=1, source_target_pairs={{0,2},{1,3},{2,0},{3,1},{4,6},{5,7},{6,4},{7,5},{64,66},{65,67},{6... | collective-permute-start | bytes 2359304 | tf_op jit(solution)/shard_map/ppermute | solution.py:28
  94.1 21.1 %collective-permute-start.20 = (bf16[2,2,128,768]{3,2,1,0:T(8,128)(2,1)S(1)}, bf16[2,2,128,768]{3,2,1,0:T(8,128)(2,1)S(1)}, u32[]{:S(2)}, u32[]{:S(2)}) collective-permute-start(bf16[2,2,128,768]{3,2,1,0:T(8,128)(2,1)S(1)} %get-tuple-element.63.refs_2_), channel_id=1, source_target_pairs={{0,6},{1,7},{2,4},{3,5},{4,2},{5,3},{6,0},{7,1},{64,70},{65,71},{6... | collective-permute-start | bytes 2359304 | tf_op jit(solution)/shard_map/ppermute | solution.py:28
  94.5 32.5 %copy-start.10 = (bf16[512,512]{1,0:T(8,128)(2,1)S(1)}, bf16[512,512]{1,0:T(8,128)(2,1)}, u32[]{:S(2)}) copy-start(bf16[512,512]{1,0:T(8,128)(2,1)} %refs_13_.1) | copy-start | bytes 1572868
  94.5 9.9 %collective-permute-start.21 = (bf16[2,2,128,512]{3,2,1,0:T(8,128)(2,1)S(1)}, bf16[2,2,128,512]{3,2,1,0:T(8,128)(2,1)S(1)}, u32[]{:S(2)}, u32[]{:S(2)}) collective-permute-start(bf16[2,2,128,512]{3,2,1,0:T(8,128)(2,1)S(1)} %get-tuple-element.64.refs_4_), channel_id=1, source_target_pairs={{0,64},{1,65},{2,66},{3,67},{4,68},{5,69},{6,70},{7,71},{64,0},{65... | collective-permute-start | bytes 1572872 | tf_op jit(solution)/shard_map/ppermute | solution.py:28
  96.6 18.8 %collective-permute-start.26 = (bf16[2,2,128,512]{3,2,1,0:T(8,128)(2,1)S(1)}, bf16[2,2,128,512]{3,2,1,0:T(8,128)(2,1)S(1)}, u32[]{:S(2)}, u32[]{:S(2)}) collective-permute-start(bf16[2,2,128,512]{3,2,1,0:T(8,128)(2,1)S(1)} %get-tuple-element.64.refs_4_), channel_id=1, source_target_pairs={{0,1},{1,0},{2,3},{3,2},{4,5},{5,4},{6,7},{7,6},{64,65},{65,64},{6... | collective-permute-start | bytes 1572872 | tf_op jit(solution)/shard_map/ppermute | solution.py:28
  101.9 13.8 %collective-permute-start.22 = (bf16[2,2,128,768]{3,2,1,0:T(8,128)(2,1)S(1)}, bf16[2,2,128,768]{3,2,1,0:T(8,128)(2,1)S(1)}, u32[]{:S(2)}, u32[]{:S(2)}) collective-permute-start(bf16[2,2,128,768]{3,2,1,0:T(8,128)(2,1)S(1)} %get-tuple-element.62.refs_0_), channel_id=1, source_target_pairs={{0,1},{1,0},{2,3},{3,2},{4,5},{5,4},{6,7},{7,6},{64,65},{65,64},{6... | collective-permute-start | bytes 2359304 | tf_op jit(solution)/shard_map/ppermute | solution.py:28
  104.4 18.6 %copy-start.12 = (bf16[2,2,128,512]{3,2,1,0:T(8,128)(2,1)}, bf16[2,2,128,512]{3,2,1,0:T(8,128)(2,1)S(1)}, u32[]{:S(2)}) copy-start(bf16[2,2,128,512]{3,2,1,0:T(8,128)(2,1)S(1)} %collective-permute-done.21.refs_5_) | copy-start | bytes 1572868
  104.4 11.3 %collective-permute-start.24 = (bf16[2,2,128,768]{3,2,1,0:T(8,128)(2,1)S(1)}, bf16[2,2,128,768]{3,2,1,0:T(8,128)(2,1)S(1)}, u32[]{:S(2)}, u32[]{:S(2)}) collective-permute-start(bf16[2,2,128,768]{3,2,1,0:T(8,128)(2,1)S(1)} %get-tuple-element.63.refs_2_), channel_id=1, source_target_pairs={{0,1},{1,0},{2,3},{3,2},{4,5},{5,4},{6,7},{7,6},{64,65},{65,64},{6... | collective-permute-start | bytes 2359304 | tf_op jit(solution)/shard_map/ppermute | solution.py:28
  111.0 11.9 %copy-start.3 = (bf16[2,2,128,768]{3,2,1,0:T(8,128)(2,1)}, bf16[2,2,128,768]{3,2,1,0:T(8,128)(2,1)S(1)}, u32[]{:S(2)}) copy-start(bf16[2,2,128,768]{3,2,1,0:T(8,128)(2,1)S(1)} %collective-permute-done.19.refs_1_) | copy-start | bytes 2359300
  111.0 7.9 %collective-permute-start.23 = (bf16[2,2,128,768]{3,2,1,0:T(8,128)(2,1)S(1)}, bf16[2,2,128,768]{3,2,1,0:T(8,128)(2,1)S(1)}, u32[]{:S(2)}, u32[]{:S(2)}) collective-permute-start(bf16[2,2,128,768]{3,2,1,0:T(8,128)(2,1)S(1)} %collective-permute-done.19.refs_1_), channel_id=1, source_target_pairs={{0,1},{1,0},{2,3},{3,2},{4,5},{5,4},{6,7},{7,6},{64,65},{65,64},{6... | collective-permute-start | bytes 2359304 | tf_op jit(solution)/shard_map/ppermute | solution.py:28
  115.2 7.8 %copy-start.4 = (bf16[2,2,128,768]{3,2,1,0:T(8,128)(2,1)}, bf16[2,2,128,768]{3,2,1,0:T(8,128)(2,1)S(1)}, u32[]{:S(2)}) copy-start(bf16[2,2,128,768]{3,2,1,0:T(8,128)(2,1)S(1)} %collective-permute-done.20.refs_3_) | copy-start | bytes 2359300
  115.2 3.8 %collective-permute-start.25 = (bf16[2,2,128,768]{3,2,1,0:T(8,128)(2,1)S(1)}, bf16[2,2,128,768]{3,2,1,0:T(8,128)(2,1)S(1)}, u32[]{:S(2)}, u32[]{:S(2)}) collective-permute-start(bf16[2,2,128,768]{3,2,1,0:T(8,128)(2,1)S(1)} %collective-permute-done.20.refs_3_), channel_id=1, source_target_pairs={{0,1},{1,0},{2,3},{3,2},{4,5},{5,4},{6,7},{7,6},{64,65},{65,64},{6... | collective-permute-start | bytes 2359304 | tf_op jit(solution)/shard_map/ppermute | solution.py:28
  115.4 7.6 %copy-start.13 = (bf16[2,2,128,512]{3,2,1,0:T(8,128)(2,1)}, bf16[2,2,128,512]{3,2,1,0:T(8,128)(2,1)S(1)}, u32[]{:S(2)}) copy-start(bf16[2,2,128,512]{3,2,1,0:T(8,128)(2,1)S(1)} %collective-permute-done.26.refs_10_) | copy-start | bytes 1572868
  115.4 3.6 %collective-permute-start.27 = (bf16[2,2,128,512]{3,2,1,0:T(8,128)(2,1)S(1)}, bf16[2,2,128,512]{3,2,1,0:T(8,128)(2,1)S(1)}, u32[]{:S(2)}, u32[]{:S(2)}) collective-permute-start(bf16[2,2,128,512]{3,2,1,0:T(8,128)(2,1)S(1)} %collective-permute-done.21.refs_5_), channel_id=1, source_target_pairs={{0,1},{1,0},{2,3},{3,2},{4,5},{5,4},{6,7},{7,6},{64,65},{65,64},{6... | collective-permute-start | bytes 1572872 | tf_op jit(solution)/shard_map/ppermute | solution.py:28
  115.7 7.3 %copy-start.5 = (bf16[2,2,128,768]{3,2,1,0:T(8,128)(2,1)}, bf16[2,2,128,768]{3,2,1,0:T(8,128)(2,1)S(1)}, u32[]{:S(2)}) copy-start(bf16[2,2,128,768]{3,2,1,0:T(8,128)(2,1)S(1)} %collective-permute-done.22.refs_6_) | copy-start | bytes 2359300
  115.7 7.3 %copy-start.6 = (bf16[2,2,128,768]{3,2,1,0:T(8,128)(2,1)}, bf16[2,2,128,768]{3,2,1,0:T(8,128)(2,1)S(1)}, u32[]{:S(2)}) copy-start(bf16[2,2,128,768]{3,2,1,0:T(8,128)(2,1)S(1)} %collective-permute-done.24.refs_8_) | copy-start | bytes 2359300
  119.0 4.0 %copy-start.14 = (bf16[2,2,128,512]{3,2,1,0:T(8,128)(2,1)}, bf16[2,2,128,512]{3,2,1,0:T(8,128)(2,1)S(1)}, u32[]{:S(2)}) copy-start(bf16[2,2,128,512]{3,2,1,0:T(8,128)(2,1)S(1)} %collective-permute-done.27.refs_11_) | copy-start | bytes 1572868
  119.0 4.0 %copy-start.7 = (bf16[2,2,128,768]{3,2,1,0:T(8,128)(2,1)}, bf16[2,2,128,768]{3,2,1,0:T(8,128)(2,1)S(1)}, u32[]{:S(2)}) copy-start(bf16[2,2,128,768]{3,2,1,0:T(8,128)(2,1)S(1)} %collective-permute-done.23.refs_7_) | copy-start | bytes 2359300
  119.0 4.0 %copy-start.8 = (bf16[2,2,128,768]{3,2,1,0:T(8,128)(2,1)}, bf16[2,2,128,768]{3,2,1,0:T(8,128)(2,1)S(1)}, u32[]{:S(2)}) copy-start(bf16[2,2,128,768]{3,2,1,0:T(8,128)(2,1)S(1)} %collective-permute-done.25.refs_9_) | copy-start | bytes 2359300
  123.0 17.5 %all-to-all-start.1 = ((bf16[128,16,128]{2,1,0:T(8,128)(2,1)}), bf16[128,16,128]{2,1,0:T(8,128)(2,1)S(1)}, u32[]{:S(2)}, u32[]{:S(2)}) async-start(bf16[128,16,128]{2,1,0:T(8,128)(2,1)} %bitcast.11), calls=%async_computation.1 | async-start | bytes 1048576 | tf_op jit(solution)/shard_map/all_to_all | solution.py:403
  140.5 0.8 copy-start.15

commit v3 on v2

--- a/solution.py
+++ b/solution.py
@@ -57,6 +57,7 @@
         norm_kernel,
         out_shape=pltpu.HBM((2, 8, 8, 16, 128), BF16),
         scratch_shapes=[pltpu.VMEM((8, 8192), F32)],
+        compiler_params=pltpu.CompilerParams(vmem_limit_bytes=56 * MIB),
         name="norm_messages",
     )(act, gain.reshape(1, -1), shift.reshape(1, -1))
 
@@ -70,6 +71,7 @@
 
 
 def rows_kernel(x, out):
+    x = x[...].reshape(64, 2, 16, 128)
     even, odd = x[:, 0].astype(F32), x[:, 1].astype(F32)
     low = lower((64, 8, 128))
     for k in range(4):
@@ -84,76 +86,89 @@
     return [sum(link for k, link in enumerate(order) if q >> (2 - k) & 1) for q in range(8)]
 
 
-def multiply(step, contract, lhs, w, w_other, outs):
-    dims = (((1,), (contract,)), ((), ()))
-    total = lax.dot_general(lhs[0], w[...], dims, preferred_element_type=F32)
-    total = total + lax.dot_general(lhs[1], w_other[...], dims, preferred_element_type=F32)
+def split(total, first_column, outs):
+    last_column = first_column + total.shape[1]
     for p, order in enumerate(ORDERS):
-        first, last = max(CUTS[p], step * 1024), min(CUTS[p + 1], step * 1024 + 1024)
+        first, last = max(CUTS[p], first_column), min(CUTS[p + 1], last_column)
         if first >= last:
             continue
-        cols = slice(first - CUTS[p], last - CUTS[p])
         for q, j in enumerate(places(order)):
-            block = total[j * 64 : (j + 1) * 64, first - step * 1024 : last - step * 1024]
-            outs[p * 2 + q // 4][q % 4 * 64 : (q % 4 + 1) * 64, cols] = block.astype(outs[p * 2 + q // 4].dtype)
+            out = outs[p * 2 + q // 4]
+            block = total[j * 64 : (j + 1) * 64, first - first_column : last - first_column]
+            out[q % 4 * 64 : (q % 4 + 1) * 64, first - CUTS[p] : last - CUTS[p]] = block.astype(out.dtype)
 
 
 def up_kernel(at, x, x_other, w, w_other, *refs):
-    outs, lhs = refs[-7:-1], refs[-1]
-
-    @pl.when(pl.program_id(0) == 0)
-    def _():
+    outs, (lhs, weights, loads) = refs[:6], refs[6:]
+    span = pl.ds(pl.multiple_of(at[1] * 2048, 2048), 2048)
+    copies = []
+    for n, ref in enumerate((w, w_other)):
+        copies.append(pltpu.make_async_copy(ref.at[span, :], weights.at[:, n * 512 : n * 512 + 512], loads.at[n]))
+        copies[n].start()
+    for j in range(8):
+        src = pl.multiple_of(jnp.bitwise_xor(at[0], j) * 64, 64)
+        lhs[j * 64 : (j + 1) * 64, 0:512] = x[pl.ds(src, 64), :]
+        lhs[j * 64 : (j + 1) * 64, 512:1024] = x_other[pl.ds(src, 64), :]
+    for copy in copies:
+        copy.wait()
+    for first in (0, 1024):
+        dims = (((1,), (1,)), ((), ()))
+        split(lax.dot_general(lhs[...], weights[first : first + 1024], dims, preferred_element_type=F32), first, outs)
+
+
+def pre_kernel(at, x, x_other, w, w_other, *refs):
+    outs, (lhs, weights, tokens, loads, token_loads) = refs[:6], refs[6:]
+    copies = [pltpu.make_async_copy(ref, tokens.at[n], token_loads.at[n]) for n, ref in enumerate((x, x_other))]
+    for k in range(2):
+        for n, ref in enumerate((w, w_other)):
+            source = ref.at[:, pl.ds(pl.multiple_of(at[1] * 2048 + k * 1024, 1024), 1024)]
+            target = weights.at[n * 512 : n * 512 + 512, k * 1024 : k * 1024 + 1024]
+            copies.append(pltpu.make_async_copy(source, target, loads.at[k * 2 + n]))
+    for copy in copies:
+        copy.start()
+    low = lower((8, 8, 128))
+    for n in range(2):
+        copies[n].wait()
         for j in range(8):
-            src = pl.multiple_of(jnp.bitwise_xor(at[0], j) * 64, 64)
-            lhs[0, j * 64 : (j + 1) * 64, :] = x[pl.ds(src, 64), :]
-            lhs[1, j * 64 : (j + 1) * 64, :] = x_other[pl.ds(src, 64), :]
-
-    for step in range(2):
-        pl.when(pl.program_id(0) == step)(functools.partial(multiply, step, 1, lhs, w, w_other, outs))
-
-
-def pre_kernel(at, x, x_other, w, w_other, *refs):
-    outs, lhs = refs[-7:-1], refs[-1]
-
-    @pl.when(pl.program_id(0) == 0)
-    def _():
-        low = lower((8, 8, 128))
-        for j in range(8):
-            src = jnp.bitwise_xor(at[0], j) * 8
-            for n, ref in enumerate((x, x_other)):
-                even, odd = ref[pl.ds(src, 8), 0].astype(F32), ref[pl.ds(src, 8), 1].astype(F32)
-                for k in range(4):
-                    rows = unfold(even, odd, k, low).reshape(64, 128).astype(BF16)
-                    lhs[n, j * 64 : (j + 1) * 64, k * 128 : (k + 1) * 128] = rows
-
-    for step in range(2):
-        pl.when(pl.program_id(0) == step)(functools.partial(multiply, step, 0, lhs, w, w_other, outs))
-
-
-def chip_sum(at, x, x_other, w, w_other, after, up):
-    shape = x.shape
-    whole = pl.BlockSpec(shape, lambda i, at: (0,) * len(shape))
-    if up:
-        weight = pl.BlockSpec((1024, 512), lambda i, at: (at[1] * 2 + i, 0))
-    else:
-        weight = pl.BlockSpec((512, 1024), lambda i, at: (0, at[1] * 2 + i))
-    shapes = [(256, CUTS[p + 1] - CUTS[p]) for p in range(3) for _ in range(2)]
+            some = tokens[n, pl.ds(jnp.bitwise_xor(at[0], j) * 16, 16)].reshape(8, 2, 16, 128)
+            even, odd = some[:, 0].astype(F32), some[:, 1].astype(F32)
+            for k in range(4):
+                rows = unfold(even, odd, k, low).reshape(64, 128).astype(BF16)
+                lhs[j * 64 : (j + 1) * 64, n * 512 + k * 128 : n * 512 + (k + 1) * 128] = rows
+    for k in range(2):
+        copies[2 + 2 * k].wait()
+        copies[3 + 2 * k].wait()
+        split(jnp.dot(lhs[...], weights[:, k * 1024 : k * 1024 + 1024], preferred_element_type=F32), k * 1024, outs)
+
+
+HALVES = [
+    jax.ShapeDtypeStruct((256, CUTS[p + 1] - CUTS[p]), dtype) for p in range(3) for dtype in (F32, BF16)
+]
+VMEM_BLOCK, ANY_BLOCK = pl.BlockSpec(memory_space=pltpu.VMEM), pl.BlockSpec(memory_space=pl.ANY)
+
+
+def in_pairs(arrays):
+    return [(arrays[2 * p], arrays[2 * p + 1]) for p in range(3)]
+
+
+def chip_sum(at, x, x_other, w, w_other, up):
     w, w_other = [pltpu.with_memory_space_constraint(v, pltpu.HBM) for v in (w, w_other)]
+    scratch = [pltpu.VMEM((512, 1024), BF16), pltpu.VMEM((2048, 1024) if up else (1024, 2048), BF16)]
+    loads = [pltpu.SemaphoreType.DMA((2,))]
+    if not up:
+        scratch.append(pltpu.VMEM((2, 128, 16, 128), BF16))
+        loads.insert(0, pltpu.SemaphoreType.DMA((4,)))
     outs = pl.pallas_call(
         up_kernel if up else pre_kernel,
-        grid_spec=pltpu.PrefetchScalarGridSpec(
-            num_scalar_prefetch=1,
-            grid=(2,),
-            in_specs=[whole, whole, weight, weight] + [pl.BlockSpec(memory_space=pl.ANY)] * len(after),
-            out_specs=[pl.BlockSpec(shape, lambda i, at: (0, 0)) for shape in shapes],
-            scratch_shapes=[pltpu.VMEM((2, 512, 512), BF16)],
-        ),
-        out_shape=[jax.ShapeDtypeStruct(shape, BF16 if k % 2 else F32) for k, shape in enumerate(shapes)],
+        in_specs=[SCALARS] + [VMEM_BLOCK if up else ANY_BLOCK] * 2 + [ANY_BLOCK] * 2,
+        out_specs=[VMEM_BLOCK] * 6,
+        out_shape=HALVES,
+        scratch_shapes=scratch + loads,
         compiler_params=pltpu.CompilerParams(vmem_limit_bytes=20 * MIB),
-        cost_estimate=pl.CostEstimate(flops=2 * 512 * 1024 * 2048, bytes_accessed=9 * MIB, transcendentals=0),
+        cost_estimate=pl.CostEstimate(flops=MIB, bytes_accessed=MIB, transcendentals=0),
         name="up_sum" if up else "pre_sum",
-    )(at, x, x_other, w, w_other, *after)
-    return [(outs[2 * p], outs[2 * p + 1]) for p in range(3)]
+    )(at, x, x_other, w, w_other)
+    return in_pairs(outs)
 
 
 def first_kernel(*refs):
@@ -205,6 +220,24 @@
     return list(outs)
 
 
+def gate_kernel(x, after, out):
+    pass
+
+
+def gate(x, after):
+    anywhere = pl.BlockSpec(memory_space=pl.ANY)
+    return pl.pallas_call(
+        gate_kernel,
+        in_specs=[anywhere] * 2,
+        out_specs=anywhere,
+        out_shape=jax.ShapeDtypeStruct(x.shape, x.dtype),
+        input_output_aliases={0: 0},
+        cost_estimate=pl.CostEstimate(flops=MIB, bytes_accessed=MIB, transcendentals=0),
+        compiler_params=pltpu.CompilerParams(vmem_limit_bytes=MIB),
+        name="gate",
+    )(x, after)
+
+
 def exchange_sums(up, pre):
     widths = [CUTS[p + 1] - CUTS[p] for p in range(3)]
     arrays = []
@@ -238,24 +271,31 @@
     return pieces
 
 
-def assemble(at, pieces, whole):
-    for h in range(2):
-        base = at[1] * 2048 if h == 0 else (1 - at[1]) * 2048
-        for p, order in enumerate(ORDERS):
-            cols = pl.ds(pl.multiple_of(base + CUTS[p], 256), CUTS[p + 1] - CUTS[p])
-            for q, j in enumerate(places(order)):
-                dst = pl.multiple_of(jnp.bitwise_xor(at[0], j) * 64, 64)
-                src = pieces[h * 6 + p * 2 + q // 4]
-                whole[pl.ds(dst, 64), cols] = src[q // 2 % 2, 0, q % 2 * 64 : q % 2 * 64 + 64, :]
-
-
-def back_kernel(at, *refs):
-    pieces, w, out, whole = refs[:12], refs[12], refs[13], refs[14]
-    assemble(at, pieces, whole)
-    total = jnp.zeros((512, 512), F32)
-    for k in range(4):
-        cols = slice(k * 1024, (k + 1) * 1024)
-        total += lax.dot_general(whole[:, cols], w[:, cols], (((1,), (1,)), ((), ())), preferred_element_type=F32)
+def back_part(at, pieces, w, half, total):
+    for p, order in enumerate(ORDERS):
+        rows = None
+        width = CUTS[p + 1] - CUTS[p]
+        for h in range(2):
+            base = (at[1] if h == 0 else 1 - at[1]) * 2048 + CUTS[p]
+            piece = pieces[h * 3 + p][:, 0].reshape(256, width)
+            cols = w[:, pl.ds(pl.multiple_of(base, 256), width)]
+            part = lax.dot_general(piece, cols, (((1,), (1,)), ((), ())), preferred_element_type=F32)
+            rows = part if rows is None else rows + part
+        for q, j in enumerate(places(order)[half * 4 : half * 4 + 4]):
+            dst = pl.multiple_of(jnp.bitwise_xor(at[0], j) * 64, 64)
+            total[pl.ds(dst, 64), :] += rows[q * 64 : (q + 1) * 64]
+
+
+def held_kernel(at, *refs):
+    pieces, w, total = refs[:6], refs[6], refs[7]
+    total[...] = jnp.zeros_like(total)
+    back_part(at, pieces, w, 0, total)
+
+
+def came_kernel(at, *refs):
+    pieces, w, before, out, total = refs[:6], refs[6], refs[7], refs[8], refs[9]
+    total[...] = before[...]
+    back_part(at, pieces, w, 1, total)
     low = lower((64, 8, 128))
     c = [total[:, k * 128 : (k + 1) * 128].reshape(64, 8, 128) for k in range(4)]
     r = [pltpu.roll(v, 4, 1) for v in c]
@@ -266,16 +306,28 @@
 
 
 def back_messages(at, pieces, w_in):
+    vmem = pl.BlockSpec(memory_space=pltpu.VMEM)
+    settings = dict(
+        out_specs=vmem,
+        compiler_params=pltpu.CompilerParams(vmem_limit_bytes=20 * MIB),
+        cost_estimate=pl.CostEstimate(flops=512 * 512 * 4096, bytes_accessed=4 * MIB, transcendentals=0),
+    )
+    held, came = [[pieces[h * 6 + p * 2 + k] for h in range(2) for p in range(3)] for k in range(2)]
+    total = pl.pallas_call(
+        held_kernel,
+        in_specs=[SCALARS] + [vmem] * 7,
+        out_shape=jax.ShapeDtypeStruct((512, 512), F32),
+        name="back_held",
+        **settings,
+    )(at, *held, w_in)
     return pl.pallas_call(
-        back_kernel,
-        in_specs=[SCALARS] + [pl.BlockSpec(memory_space=pltpu.VMEM)] * 13,
-        out_specs=pl.BlockSpec(memory_space=pltpu.VMEM),
+        came_kernel,
+        in_specs=[SCALARS] + [vmem] * 8,
         out_shape=pltpu.HBM((64, 2, 16, 128), BF16),
-        scratch_shapes=[pltpu.VMEM((512, 4096), BF16)],
-        compiler_params=pltpu.CompilerParams(vmem_limit_bytes=24 * MIB),
-        cost_estimate=pl.CostEstimate(flops=2 * 512 * 512 * 4096, bytes_accessed=8 * MIB, transcendentals=0),
+        scratch_shapes=[pltpu.VMEM((512, 512), F32)],
         name="back_messages",
-    )(at, *pieces, w_in)
+        **settings,
+    )(at, *came, w_in, total)
 
 
 def grads_kernel(at, *refs):
@@ -356,9 +408,9 @@
     scaled = center * inverse
     low = lower((8, 128))
     for g in range(16):
-        total = x[g // 8, 0, g % 8].astype(F32)
+        total = x[g // 8 * 64 + g % 8].astype(F32)
         for d in range(1, 8):
-            total += x[g // 8, d, g % 8].astype(F32)
+            total += x[g // 8 * 64 + d * 8 + g % 8].astype(F32)
         for t in range(2):
             tile = total[t * 8 : t * 8 + 8]
             turned = pltpu.roll(tile, 4, 0)
@@ -375,10 +427,13 @@
 def grad_act_of(x, act, gain):
     return pl.pallas_call(
         act_kernel,
+        in_specs=[pl.BlockSpec(memory_space=pltpu.VMEM)] * 3,
+        out_specs=pl.BlockSpec(memory_space=pltpu.VMEM),
         out_shape=jax.ShapeDtypeStruct((4, 8192), F32),
         scratch_shapes=[pltpu.VMEM((8, 8192), F32), pltpu.VMEM((8, 8192), F32)],
+        compiler_params=pltpu.CompilerParams(vmem_limit_bytes=8 * MIB),
         name="grad_act",
-    )(x.reshape(2, 8, 8, 16, 128), act, gain.reshape(1, -1))
+    )(x, act, gain.reshape(1, -1))
 
 
 def local(act, gain, shift, w_in, w_out, cotangent):
@@ -392,10 +447,11 @@
     cot_other = swap(cotangent, "core")
     in_other = swap(w_in, "core")
     messages = norm_messages(act, gain, shift)
-    mixed = lax.all_to_all(messages.reshape(128, 16, 128), EVERY, 0, 0, tiled=True).reshape(64, 2, 16, 128)
+    mixed = lax.all_to_all(messages.reshape(128, 16, 128), EVERY, 0, 0, tiled=True)
+    up = chip_sum(at, cotangent, cot_other, w_out, out_other, True)
+    mixed = gate(mixed, up[0][0])
     mixed_other = swap(mixed, "core")
-    up = chip_sum(at, cotangent, cot_other, w_out, out_other, [], True)
-    pre = chip_sum(at, mixed, mixed_other, w_in, in_other, [up[0][0]], False)
+    pre = chip_sum(at, mixed, mixed_other, w_in, in_other, False)
     pieces = gather(exchange_sums(up, pre))
     pieces += [swap(p, "core") for p in pieces]
 

time: 144 us -> 132 us (0.917)
  waiting for transfers between devices: 54.4 us -> 45.4 us
  starting transfers between devices: 56.1 us -> 52.5 us
    all_to_all x1, waiting for transfers between devices: 12.4 us -> 5.7 us  [local(): lax.all_to_all(messages.reshape(128, 16, 128), EVERY, 0, 0, tiled=True)]
    ppermute x28, starting transfers between devices: 41.7 us -> 36 us  [swap(): return lax.ppermute(x, OWNERS, pairs)]
    all_to_all x1, starting transfers between devices: 3.94 us -> 6.31 us  [local(): lax.all_to_all(share.reshape(128, 16, 128), EVERY, 0, 0, tiled=True)]
    ppermute x28, waiting for transfers between devices: 39.5 us -> 37.2 us  [swap(): return lax.ppermute(x, OWNERS, pairs)]
    pallas_call x4 -> x6, Pallas kernels: 15.6 us -> 15.9 us  [the longest x2 9.87 us: chip_sum(): pl.pallas_call(up_kernel if up else pre_kernel, in_specs=[SCALARS] + [VME...]
  transfers between devices with their start and end apart: 30 -> 30, of which waited for: 14 -> 18; matrix products, arithmetic and copies ran while one was open for 0% -> 0% of each run, Pallas kernels for 16% -> 19%
where the time goes in v3:
time: 132 us
  starting transfers between devices  52.5 us (40%)
  waiting for transfers between devices  45.4 us (34%)
  Pallas kernels  30.5 us (23%)
  local copies, waits for them, and re-layouts  2.61 us (2%)
    ppermute x28, waiting for transfers between devices, swap(): return lax.ppermute(x, OWNERS, pairs)  37.2 us
    ppermute x28, starting transfers between devices, swap(): return lax.ppermute(x, OWNERS, pairs)  36 us
    pallas_call x1, Pallas kernels, grads_of(): pl.pallas_call(grads_kernel, in_specs=[SCALARS] + [anywhere] * 12 + [vmem...  10.9 us
    all_to_all x1, starting transfers between devices, local(): lax.all_to_all(messages.reshape(128, 16, 128), EVERY, 0, 0, tiled=True)  10.2 us
    pallas_call x2, Pallas kernels, chip_sum(): pl.pallas_call(up_kernel if up else pre_kernel, in_specs=[SCALARS] + [VME...  9.87 us
    all_to_all x1, starting transfers between devices, local(): lax.all_to_all(share.reshape(128, 16, 128), EVERY, 0, 0, tiled=True)  6.31 us
    all_to_all x1, waiting for transfers between devices, local(): lax.all_to_all(messages.reshape(128, 16, 128), EVERY, 0, 0, tiled=True)  5.7 us
    pallas_call x1, Pallas kernels, back_messages(): pl.pallas_call(came_kernel, in_specs=[SCALARS] + [vmem] * 8, out_shape=pl...  2.94 us
  transfers between devices with their start and end apart: 30, of which 18 were waited for; matrix products, arithmetic and copies ran while one was open for 0% of the time, Pallas kernels for 19%

profile of v3, /device:TPU:1, one launch (start us, length us, event | category | flops | bytes accessed | tf_op | source)
XLA Modules:
  0.0 132.1 jit_solution(7858564795044128079)
XLA Ops:
  0.6 1.5 %collective-permute-start.1 = (bf16[4096,512]{1,0:T(8,128)(2,1)}, bf16[4096,512]{1,0:T(8,128)(2,1)}, u32[]{:S(2)}, u32[]{:S(2)}) collective-permute-start(bf16[4096,512]{1,0:T(8,128)(2,1)} %w.2), channel_id=1, source_target_pairs={{0,1},{1,0},{2,3},{3,2},{4,5},{5,4},{6,7},{7,6},{64,65},{65,64},{6... | collective-permute-start | bytes 12582920 | tf_op jit(solution)/shard_map/ppermute | solution.py:28
  2.2 0.4 collective-permute-start
  2.6 2.1 %norm_messages.1 = bf16[2,8,8,16,128]{4,3,2,1,0:T(8,128)(2,1)} custom-call(bf16[4,8192]{1,0:T(4,128)(2,1)} %act.3, f32[1,8192]{1,0:T(1,128)} %bitcast.6, f32[1,8192]{1,0:T(1,128)} %bitcast.10), custom_call_target="tpu_custom_call" | custom-call | tf_op jit(solution)/shard_map/norm_messages/pallas_call | solution.py:56
  4.7 10.2 %all-to-all-start = ((bf16[128,16,128]{2,1,0:T(8,128)(2,1)}), bf16[128,16,128]{2,1,0:T(8,128)(2,1)S(1)}, u32[]{:S(2)}, u32[]{:S(2)}) async-start(bf16[128,16,128]{2,1,0:T(8,128)(2,1)} %bitcast.9), calls=%async_computation | async-start | bytes 1048576 | tf_op jit(solution)/shard_map/all_to_all | solution.py:450
  15.0 1.0 copy-done.9
  16.1 5.2 %up_sum.1 = (f32[256,768]{1,0:T(8,128)S(1)}, bf16[256,768]{1,0:T(8,128)(2,1)S(1)}, f32[256,768]{1,0:T(8,128)S(1)}, bf16[256,768]{1,0:T(8,128)(2,1)S(1)}, f32[256...) custom-call(s32[2]{0:T(128)S(1)} %pad_add_fusion.at, bf16[512,512]{1,0:T(8,128)(2,1)S(1)} %copy-done.9, ...), custom_call_target="tpu_custom_call" | custom-call | flops 1048576 | bytes 1048576 | tf_op jit(solution)/shard_map/up_sum/pallas_call | solution.py:161
  21.2 0.8 copy-done.17
  22.0 0.7 copy-done.18
  22.7 5.7 %all-to-all-done.x = bf16[128,16,128]{2,1,0:T(8,128)(2,1)S(1)} async-done(((bf16[128,16,128]{2,1,0:T(8,128)(2,1)}), bf16[128,16,128]{2,1,0:T(8,128)(2,1)S(1)}, u32[]{:S(2)}, u32[]{:S(2)}) %all-to-all-start) | async-done | bytes 524320 | tf_op jit(solution)/shard_map/all_to_all | solution.py:450
  28.4 1.1 collective-permute-start.3
  30.2 1.2 collective-permute-start.6
  31.4 4.7 %pre_sum.1 = (f32[256,768]{1,0:T(8,128)S(1)}, bf16[256,768]{1,0:T(8,128)(2,1)S(1)}, f32[256,768]{1,0:T(8,128)S(1)}, bf16[256,768]{1,0:T(8,128)(2,1)S(1)}, f32[25...) custom-call(s32[2]{0:T(128)S(1)} %pad_add_fusion.at, bf16[128,16,128]{2,1,0:T(8,128)(2,1)S(1)} %gate.1.x.refs_12_, ...), custom_call_target="tpu_custom_call" | custom-call | flops 1048576 | bytes 1048576 | tf_op jit(solution)/shard_map/pre_sum/pallas_call | solution.py:161
  36.2 0.4 collective-permute-start.5
  36.6 1.6 %collective-permute-start.7 = (bf16[256,768]{1,0:T(8,128)(2,1)S(1)}, bf16[256,768]{1,0:T(8,128)(2,1)S(1)}, u32[]{:S(2)}, u32[]{:S(2)}) collective-permute-start(bf16[256,768]{1,0:T(8,128)(2,1)S(1)} %get-tuple-element.42), channel_id=1, source_target_pairs={{0,6},{1,7},{2,4},{3,5},{4,2},{5,3},{6,0},{7,1},{64,70},{65,71},{6... | collective-permute-start | bytes 1179656 | tf_op jit(solution)/shard_map/ppermute | solution.py:28
  38.2 0.7 collective-permute-done.8.refs_9_
  38.9 1.9 %collective-permute-start.9 = (bf16[256,512]{1,0:T(8,128)(2,1)S(1)}, bf16[256,512]{1,0:T(8,128)(2,1)S(1)}, u32[]{:S(2)}, u32[]{:S(2)}) collective-permute-start(bf16[256,512]{1,0:T(8,128)(2,1)S(1)} %get-tuple-element.46), channel_id=1, source_target_pairs={{0,64},{1,65},{2,66},{3,67},{4,68},{5,69},{6,70},{7,71},{64,0},{65... | collective-permute-start | bytes 786440 | tf_op jit(solution)/shard_map/ppermute | solution.py:28
  40.8 0.8 collective-permute-done.6.refs_5_
  41.6 5.8 %collective-permute-done.9.refs_11_ = bf16[256,512]{1,0:T(8,128)(2,1)S(1)} collective-permute-done((bf16[256,512]{1,0:T(8,128)(2,1)S(1)}, bf16[256,512]{1,0:T(8,128)(2,1)S(1)}, u32[]{:S(2)}, u32[]{:S(2)}) %collective-permute-start.9) | collective-permute-done | bytes 262176 | tf_op jit(solution)/shard_map/ppermute | solution.py:28
  47.4 1.3 collective-permute-done.5.refs_3_
  48.7 1.4 %collective-permute-done.7.refs_7_ = bf16[256,768]{1,0:T(8,128)(2,1)S(1)} collective-permute-done((bf16[256,768]{1,0:T(8,128)(2,1)S(1)}, bf16[256,768]{1,0:T(8,128)(2,1)S(1)}, u32[]{:S(2)}, u32[]{:S(2)}) %collective-permute-start.7) | collective-permute-done | bytes 393248 | tf_op jit(solution)/shard_map/ppermute | solution.py:28
  50.1 0.4 first_sums.1
  50.5 1.2 collective-permute-start.10
  51.7 2.1 %collective-permute-start.11 = (bf16[2,128,768]{2,1,0:T(8,128)(2,1)S(1)}, bf16[2,128,768]{2,1,0:T(8,128)(2,1)S(1)}, u32[]{:S(2)}, u32[]{:S(2)}) collective-permute-start(bf16[2,128,768]{2,1,0:T(8,128)(2,1)S(1)} %get-tuple-element.50), channel_id=1, source_target_pairs={{0,64},{1,65},{2,66},{3,67},{4,68},{5,69},{6,70},{7,71},{64,0},{65... | collective-permute-start | bytes 1179656 | tf_op jit(solution)/shard_map/ppermute | solution.py:28
  53.7 6.0 %collective-permute-done.12.refs_5_ = bf16[2,128,512]{2,1,0:T(8,128)(2,1)S(1)} collective-permute-done((bf16[2,128,512]{2,1,0:T(8,128)(2,1)S(1)}, bf16[2,128,512]{2,1,0:T(8,128)(2,1)S(1)}, u32[]{:S(2)}, u32[]{:S(2)}) %collective-permute-start.12) | collective-permute-done | bytes 262176 | tf_op jit(solution)/shard_map/ppermute | solution.py:28
  59.7 1.2 collective-permute-done.10.refs_1_
  60.9 1.0 collective-permute-done.11.refs_3_
  62.2 2.5 %collective-permute-start.13 = (bf16[2,128,768]{2,1,0:T(8,128)(2,1)S(1)}, bf16[2,128,768]{2,1,0:T(8,128)(2,1)S(1)}, u32[]{:S(2)}, u32[]{:S(2)}) collective-permute-start(bf16[2,128,768]{2,1,0:T(8,128)(2,1)S(1)} %get-tuple-element.54), channel_id=1, source_target_pairs={{0,64},{1,65},{2,66},{3,67},{4,68},{5,69},{6,70},{7,71},{64,0},{65... | collective-permute-start | bytes 1179656 | tf_op jit(solution)/shard_map/ppermute | solution.py:28
  64.7 1.8 %collective-permute-start.15 = (bf16[2,128,512]{2,1,0:T(8,128)(2,1)S(1)}, bf16[2,128,512]{2,1,0:T(8,128)(2,1)S(1)}, u32[]{:S(2)}, u32[]{:S(2)}) collective-permute-start(bf16[2,128,512]{2,1,0:T(8,128)(2,1)S(1)} %get-tuple-element.58), channel_id=1, source_target_pairs={{0,6},{1,7},{2,4},{3,5},{4,2},{5,3},{6,0},{7,1},{64,70},{65,71},{6... | collective-permute-start | bytes 786440 | tf_op jit(solution)/shard_map/ppermute | solution.py:28
  66.5 4.9 %collective-permute-done.15.refs_5_ = bf16[2,128,512]{2,1,0:T(8,128)(2,1)S(1)} collective-permute-done((bf16[2,128,512]{2,1,0:T(8,128)(2,1)S(1)}, bf16[2,128,512]{2,1,0:T(8,128)(2,1)S(1)}, u32[]{:S(2)}, u32[]{:S(2)}) %collective-permute-start.15) | collective-permute-done | bytes 262176 | tf_op jit(solution)/shard_map/ppermute | solution.py:28
  71.5 1.1 collective-permute-done.14.refs_3_
  72.6 0.8 third_sums.1
  73.4 1.8 %collective-permute-start.16 = (bf16[2,128,768]{2,1,0:T(8,128)(2,1)S(1)}, bf16[2,128,768]{2,1,0:T(8,128)(2,1)S(1)}, u32[]{:S(2)}, u32[]{:S(2)}) collective-permute-start(bf16[2,128,768]{2,1,0:T(8,128)(2,1)S(1)} %get-tuple-element.59.refs_0_), channel_id=1, source_target_pairs={{0,6},{1,7},{2,4},{3,5},{4,2},{5,3},{6,0},{7,1},{64,70},{65,71},{6... | collective-permute-start | bytes 1179656 | tf_op jit(solution)/shard_map/ppermute | solution.py:28
  75.1 1.8 %collective-permute-start.17 = (bf16[2,128,768]{2,1,0:T(8,128)(2,1)S(1)}, bf16[2,128,768]{2,1,0:T(8,128)(2,1)S(1)}, u32[]{:S(2)}, u32[]{:S(2)}) collective-permute-start(bf16[2,128,768]{2,1,0:T(8,128)(2,1)S(1)} %get-tuple-element.60.refs_2_), channel_id=1, source_target_pairs={{0,64},{1,65},{2,66},{3,67},{4,68},{5,69},{6,70},{7,71},{64,0},{65... | collective-permute-start | bytes 1179656 | tf_op jit(solution)/shard_map/ppermute | solution.py:28
  76.9 5.5 %collective-permute-done.18.refs_5_ = bf16[2,128,512]{2,1,0:T(8,128)(2,1)S(1)} collective-permute-done((bf16[2,128,512]{2,1,0:T(8,128)(2,1)S(1)}, bf16[2,128,512]{2,1,0:T(8,128)(2,1)S(1)}, u32[]{:S(2)}, u32[]{:S(2)}) %collective-permute-start.18) | collective-permute-done | bytes 262176 | tf_op jit(solution)/shard_map/ppermute | solution.py:28
  82.5 0.8 collective-permute-done.17.refs_3_
  83.7 1.1 collective-permute-start.20
  84.8 5.4 %collective-permute-start.26 = (bf16[2,2,128,512]{3,2,1,0:T(8,128)(2,1)S(1)}, bf16[2,2,128,512]{3,2,1,0:T(8,128)(2,1)S(1)}, u32[]{:S(2)}, u32[]{:S(2)}) collective-permute-start(bf16[2,2,128,512]{3,2,1,0:T(8,128)(2,1)S(1)} %get-tuple-element.64.refs_4_.refs_2_), channel_id=1, source_target_pairs={{0,1},{1,0},{2,3},{3,2},{4,5},{5,4},{6,7},{7,6},{64,65},{65,64},{6... | collective-permute-start | bytes 1572872 | tf_op jit(solution)/shard_map/ppermute | solution.py:28
  90.2 1.6 %collective-permute-start.21 = (bf16[2,2,128,512]{3,2,1,0:T(8,128)(2,1)S(1)}, bf16[2,2,128,512]{3,2,1,0:T(8,128)(2,1)S(1)}, u32[]{:S(2)}, u32[]{:S(2)}) collective-permute-start(bf16[2,2,128,512]{3,2,1,0:T(8,128)(2,1)S(1)} %get-tuple-element.64.refs_4_.refs_2_), channel_id=1, source_target_pairs={{0,64},{1,65},{2,66},{3,67},{4,68},{5,69},{6,70},{7,71},{64,0},{65... | collective-permute-start | bytes 1572872 | tf_op jit(solution)/shard_map/ppermute | solution.py:28
  92.3 6.4 %collective-permute-done.19.refs_1_.refs_0_ = bf16[2,2,128,768]{3,2,1,0:T(8,128)(2,1)S(1)} collective-permute-done((bf16[2,2,128,768]{3,2,1,0:T(8,128)(2,1)S(1)}, bf16[2,2,128,768]{3,2,1,0:T(8,128)(2,1)S(1)}, u32[]{:S(2)}, u32[]{:S(2)}) %collective-permute-start.19) | collective-permute-done | bytes 786464 | tf_op jit(solution)/shard_map/ppermute | solution.py:28
  98.7 5.6 %collective-permute-start.23 = (bf16[2,2,128,768]{3,2,1,0:T(8,128)(2,1)S(1)}, bf16[2,2,128,768]{3,2,1,0:T(8,128)(2,1)S(1)}, u32[]{:S(2)}, u32[]{:S(2)}) collective-permute-start(bf16[2,2,128,768]{3,2,1,0:T(8,128)(2,1)S(1)} %collective-permute-done.19.refs_1_.refs_0_), channel_id=1, source_target_pairs={{0,1},{1,0},{2,3},{3,2},{4,5},{5,4},{6,7},{7,6},{64,65},{65,64},{6... | collective-permute-start | bytes 2359304 | tf_op jit(solution)/shard_map/ppermute | solution.py:28
  104.3 0.7 collective-permute-start.25
  105.2 0.8 collective-permute-start.27
  106.0 1.9 %back_held.1.refs_7_ = f32[512,512]{1,0:T(8,128)S(1)} custom-call(s32[2]{0:T(128)S(1)} %pad_add_fusion.at, bf16[2,2,128,768]{3,2,1,0:T(8,128)(2,1)S(1)} %get-tuple-element.62.refs_0_, bf16[2,2,128,768]{3,2,1,0:T(8,128)(2,1)S(1)} %get-tuple-element.63.refs_2_.refs_1_, bf16[2,2,128,512]{3,2,1,0:T(8,128)(2,1)S(1)} %get-tuple-element.64.refs_4_.refs_2_, ...), custom_call_target="tpu_custom_call" | custom-call | flops 1073741824 | bytes 4194304 | tf_op jit(solution)/shard_map/back_held/pallas_call | solution.py:316
  108.1 2.9 %back_messages.1 = bf16[64,2,16,128]{3,2,1,0:T(8,128)(2,1)} custom-call(s32[2]{0:T(128)S(1)} %pad_add_fusion.at, bf16[2,2,128,768]{3,2,1,0:T(8,128)(2,1)S(1)} %collective-permute-done.19.refs_1_.refs_0_, bf16[2,2,128,768]{3,2,1,0:T(8,128)(2,1)S(1)} %collective-permute-done.20.refs_3_.refs_1_, ...), custom_call_target="tpu_custom_call" | custom-call | flops 1073741824 | bytes 4194304 | tf_op jit(solution)/shard_map/back_messages/pallas_call | solution.py:323
  111.1 6.3 %all-to-all-start.1 = ((bf16[128,16,128]{2,1,0:T(8,128)(2,1)}), bf16[128,16,128]{2,1,0:T(8,128)(2,1)S(1)}, u32[]{:S(2)}, u32[]{:S(2)}) async-start(bf16[128,16,128]{2,1,0:T(8,128)(2,1)} %bitcast.8), calls=%async_computation.1 | async-start | bytes 1048576 | tf_op jit(solution)/shard_map/all_to_all | solution.py:459
  117.4 10.9 %grads.1 = (f32[512,4096]{1,0:T(8,128)}, f32[4096,512]{1,0:T(8,128)}) custom-call(s32[2]{0:T(128)S(1)} %pad_add_fusion.at, bf16[2,2,128,768]{3,2,1,0:T(8,128)(2,1)} %copy-done.1, bf16[2,2,128,768]{3,2,1,0:T(8,128)(2,1)} %copy-done.3, bf16[2,2,128,768]{3,2,1,0:T(8,128)(2,1)} %copy-done.2, bf16[2,2,128,768]{3,2,1,0:T(8,128)(2,1)} %copy-done.4, ...), custom_call_target="tpu_custom_call" | custom-call | flops 4294967296 | bytes 25165824 | tf_op jit(solution)/shard_map/grads/pallas_call | solution.py:381
  128.4 2.5 %all-to-all-done.1.x = bf16[128,16,128]{2,1,0:T(8,128)(2,1)S(1)} async-done(((bf16[128,16,128]{2,1,0:T(8,128)(2,1)}), bf16[128,16,128]{2,1,0:T(8,128)(2,1)S(1)}, u32[]{:S(2)}, u32[]{:S(2)}) %all-to-all-start.1) | async-done | bytes 524320 | tf_op jit(solution)/shard_map/all_to_all | solution.py:459
  130.9 1.2 grad_act.1
  (63 shorter events, 2.6 us)
Async XLA Ops:
  0.6 14.4 %collective-permute-start.1 = (bf16[4096,512]{1,0:T(8,128)(2,1)}, bf16[4096,512]{1,0:T(8,128)(2,1)}, u32[]{:S(2)}, u32[]{:S(2)}) collective-permute-start(bf16[4096,512]{1,0:T(8,128)(2,1)} %w.2), channel_id=1, source_target_pairs={{0,1},{1,0},{2,3},{3,2},{4,5},{5,4},{6,7},{7,6},{64,65},{65,64},{6... | collective-permute-start | bytes 12582920 | tf_op jit(solution)/shard_map/ppermute | solution.py:28
  2.1 29.3 %collective-permute-start.4 = (bf16[512,4096]{1,0:T(8,128)(2,1)}, bf16[512,4096]{1,0:T(8,128)(2,1)}, u32[]{:S(2)}, u32[]{:S(2)}) collective-permute-start(bf16[512,4096]{1,0:T(8,128)(2,1)} %refs_6_.3), channel_id=1, source_target_pairs={{0,1},{1,0},{2,3},{3,2},{4,5},{5,4},{6,7},{7,6},{64,65},{65,64},{6... | collective-permute-start | bytes 12582920 | tf_op jit(solution)/shard_map/ppermute | solution.py:28
  2.2 12.8 %collective-permute-start = (bf16[512,512]{1,0:T(8,128)(2,1)}, bf16[512,512]{1,0:T(8,128)(2,1)S(1)}, u32[]{:S(2)}, u32[]{:S(2)}) collective-permute-start(bf16[512,512]{1,0:T(8,128)(2,1)} %refs_13_.1), channel_id=1, source_target_pairs={{0,1},{1,0},{2,3},{3,2},{4,5},{5,4},{6,7},{7,6},{64,65},{65,64},{6... | collective-permute-start | bytes 1572872 | tf_op jit(solution)/shard_map/ppermute | solution.py:28
  4.7 23.7 %all-to-all-start = ((bf16[128,16,128]{2,1,0:T(8,128)(2,1)}), bf16[128,16,128]{2,1,0:T(8,128)(2,1)S(1)}, u32[]{:S(2)}, u32[]{:S(2)}) async-start(bf16[128,16,128]{2,1,0:T(8,128)(2,1)} %bitcast.9), calls=%async_computation | async-start | bytes 1048576 | tf_op jit(solution)/shard_map/all_to_all | solution.py:450
  15.0 1.0 copy-start.9
  21.2 0.8 copy-start.17
  28.4 3.0 %collective-permute-start.3 = (bf16[128,16,128]{2,1,0:T(8,128)(2,1)S(1)}, bf16[128,16,128]{2,1,0:T(8,128)(2,1)S(1)}, u32[]{:S(2)}, u32[]{:S(2)}) collective-permute-start(bf16[128,16,128]{2,1,0:T(8,128)(2,1)S(1)} %gate.1.x.refs_12_), channel_id=1, source_target_pairs={{0,1},{1,0},{2,3},{3,2},{4,5},{5,4},{6,7},{7,6},{64,65},{65,64},{6... | collective-permute-start | bytes 1572872 | tf_op jit(solution)/shard_map/ppermute | solution.py:28
  29.5 9.4 %collective-permute-start.8 = (bf16[256,512]{1,0:T(8,128)(2,1)S(1)}, bf16[256,512]{1,0:T(8,128)(2,1)S(1)}, u32[]{:S(2)}, u32[]{:S(2)}) collective-permute-start(bf16[256,512]{1,0:T(8,128)(2,1)S(1)} %get-tuple-element.44), channel_id=1, source_target_pairs={{0,64},{1,65},{2,66},{3,67},{4,68},{5,69},{6,70},{7,71},{64,0},{65... | collective-permute-start | bytes 786440 | tf_op jit(solution)/shard_map/ppermute | solution.py:28
  29.8 11.0 %collective-permute-start.2 = (bf16[256,768]{1,0:T(8,128)(2,1)}, bf16[256,768]{1,0:T(8,128)(2,1)S(1)}, u32[]{:S(2)}, u32[]{:S(2)}) collective-permute-start(bf16[256,768]{1,0:T(8,128)(2,1)} %copy-done.18), channel_id=1, source_target_pairs={{0,2},{1,3},{2,0},{3,1},{4,6},{5,7},{6,4},{7,5},{64,66},{65,67},{6... | collective-permute-start | bytes 1179656 | tf_op jit(solution)/shard_map/ppermute | solution.py:28
  30.2 11.4 %collective-permute-start.6 = (bf16[256,768]{1,0:T(8,128)(2,1)}, bf16[256,768]{1,0:T(8,128)(2,1)S(1)}, u32[]{:S(2)}, u32[]{:S(2)}) collective-permute-start(bf16[256,768]{1,0:T(8,128)(2,1)} %copy-done.17), channel_id=1, source_target_pairs={{0,6},{1,7},{2,4},{3,5},{4,2},{5,3},{6,0},{7,1},{64,70},{65,71},{6... | collective-permute-start | bytes 1179656 | tf_op jit(solution)/shard_map/ppermute | solution.py:28
  36.2 12.5 %collective-permute-start.5 = (bf16[256,768]{1,0:T(8,128)(2,1)S(1)}, bf16[256,768]{1,0:T(8,128)(2,1)S(1)}, u32[]{:S(2)}, u32[]{:S(2)}) collective-permute-start(bf16[256,768]{1,0:T(8,128)(2,1)S(1)} %get-tuple-element.38), channel_id=1, source_target_pairs={{0,2},{1,3},{2,0},{3,1},{4,6},{5,7},{6,4},{7,5},{64,66},{65,67},{6... | collective-permute-start | bytes 1179656 | tf_op jit(solution)/shard_map/ppermute | solution.py:28
  36.6 13.5 %collective-permute-start.7 = (bf16[256,768]{1,0:T(8,128)(2,1)S(1)}, bf16[256,768]{1,0:T(8,128)(2,1)S(1)}, u32[]{:S(2)}, u32[]{:S(2)}) collective-permute-start(bf16[256,768]{1,0:T(8,128)(2,1)S(1)} %get-tuple-element.42), channel_id=1, source_target_pairs={{0,6},{1,7},{2,4},{3,5},{4,2},{5,3},{6,0},{7,1},{64,70},{65,71},{6... | collective-permute-start | bytes 1179656 | tf_op jit(solution)/shard_map/ppermute | solution.py:28
  38.9 8.5 %collective-permute-start.9 = (bf16[256,512]{1,0:T(8,128)(2,1)S(1)}, bf16[256,512]{1,0:T(8,128)(2,1)S(1)}, u32[]{:S(2)}, u32[]{:S(2)}) collective-permute-start(bf16[256,512]{1,0:T(8,128)(2,1)S(1)} %get-tuple-element.46), channel_id=1, source_target_pairs={{0,64},{1,65},{2,66},{3,67},{4,68},{5,69},{6,70},{7,71},{64,0},{65... | collective-permute-start | bytes 786440 | tf_op jit(solution)/shard_map/ppermute | solution.py:28
  50.5 10.4 %collective-permute-start.10 = (bf16[2,128,768]{2,1,0:T(8,128)(2,1)S(1)}, bf16[2,128,768]{2,1,0:T(8,128)(2,1)S(1)}, u32[]{:S(2)}, u32[]{:S(2)}) collective-permute-start(bf16[2,128,768]{2,1,0:T(8,128)(2,1)S(1)} %get-tuple-element.48), channel_id=1, source_target_pairs={{0,6},{1,7},{2,4},{3,5},{4,2},{5,3},{6,0},{7,1},{64,70},{65,71},{6... | collective-permute-start | bytes 1179656 | tf_op jit(solution)/shard_map/ppermute | solution.py:28
  51.7 10.2 %collective-permute-start.11 = (bf16[2,128,768]{2,1,0:T(8,128)(2,1)S(1)}, bf16[2,128,768]{2,1,0:T(8,128)(2,1)S(1)}, u32[]{:S(2)}, u32[]{:S(2)}) collective-permute-start(bf16[2,128,768]{2,1,0:T(8,128)(2,1)S(1)} %get-tuple-element.50), channel_id=1, source_target_pairs={{0,64},{1,65},{2,66},{3,67},{4,68},{5,69},{6,70},{7,71},{64,0},{65... | collective-permute-start | bytes 1179656 | tf_op jit(solution)/shard_map/ppermute | solution.py:28
  53.7 6.0 %collective-permute-start.12 = (bf16[2,128,512]{2,1,0:T(8,128)(2,1)S(1)}, bf16[2,128,512]{2,1,0:T(8,128)(2,1)S(1)}, u32[]{:S(2)}, u32[]{:S(2)}) collective-permute-start(bf16[2,128,512]{2,1,0:T(8,128)(2,1)S(1)} %get-tuple-element.52), channel_id=1, source_target_pairs={{0,2},{1,3},{2,0},{3,1},{4,6},{5,7},{6,4},{7,5},{64,66},{65,67},{6... | collective-permute-start | bytes 786440 | tf_op jit(solution)/shard_map/ppermute | solution.py:28
  61.9 44.2 %copy-start = (bf16[512,4096]{1,0:T(8,128)(2,1)S(1)}, bf16[512,4096]{1,0:T(8,128)(2,1)}, u32[]{:S(2)}) copy-start(bf16[512,4096]{1,0:T(8,128)(2,1)} %refs_6_.3) | copy-start | bytes 12582916
  62.2 9.3 %collective-permute-start.13 = (bf16[2,128,768]{2,1,0:T(8,128)(2,1)S(1)}, bf16[2,128,768]{2,1,0:T(8,128)(2,1)S(1)}, u32[]{:S(2)}, u32[]{:S(2)}) collective-permute-start(bf16[2,128,768]{2,1,0:T(8,128)(2,1)S(1)} %get-tuple-element.54), channel_id=1, source_target_pairs={{0,64},{1,65},{2,66},{3,67},{4,68},{5,69},{6,70},{7,71},{64,0},{65... | collective-permute-start | bytes 1179656 | tf_op jit(solution)/shard_map/ppermute | solution.py:28
  64.7 7.9 %collective-permute-start.14 = (bf16[2,128,768]{2,1,0:T(8,128)(2,1)S(1)}, bf16[2,128,768]{2,1,0:T(8,128)(2,1)S(1)}, u32[]{:S(2)}, u32[]{:S(2)}) collective-permute-start(bf16[2,128,768]{2,1,0:T(8,128)(2,1)S(1)} %get-tuple-element.56), channel_id=1, source_target_pairs={{0,2},{1,3},{2,0},{3,1},{4,6},{5,7},{6,4},{7,5},{64,66},{65,67},{6... | collective-permute-start | bytes 1179656 | tf_op jit(solution)/shard_map/ppermute | solution.py:28
  64.7 6.7 %collective-permute-start.15 = (bf16[2,128,512]{2,1,0:T(8,128)(2,1)S(1)}, bf16[2,128,512]{2,1,0:T(8,128)(2,1)S(1)}, u32[]{:S(2)}, u32[]{:S(2)}) collective-permute-start(bf16[2,128,512]{2,1,0:T(8,128)(2,1)S(1)} %get-tuple-element.58), channel_id=1, source_target_pairs={{0,6},{1,7},{2,4},{3,5},{4,2},{5,3},{6,0},{7,1},{64,70},{65,71},{6... | collective-permute-start | bytes 786440 | tf_op jit(solution)/shard_map/ppermute | solution.py:28
  73.4 9.1 %collective-permute-start.16 = (bf16[2,128,768]{2,1,0:T(8,128)(2,1)S(1)}, bf16[2,128,768]{2,1,0:T(8,128)(2,1)S(1)}, u32[]{:S(2)}, u32[]{:S(2)}) collective-permute-start(bf16[2,128,768]{2,1,0:T(8,128)(2,1)S(1)} %get-tuple-element.59.refs_0_), channel_id=1, source_target_pairs={{0,6},{1,7},{2,4},{3,5},{4,2},{5,3},{6,0},{7,1},{64,70},{65,71},{6... | collective-permute-start | bytes 1179656 | tf_op jit(solution)/shard_map/ppermute | solution.py:28
  75.1 8.1 %collective-permute-start.17 = (bf16[2,128,768]{2,1,0:T(8,128)(2,1)S(1)}, bf16[2,128,768]{2,1,0:T(8,128)(2,1)S(1)}, u32[]{:S(2)}, u32[]{:S(2)}) collective-permute-start(bf16[2,128,768]{2,1,0:T(8,128)(2,1)S(1)} %get-tuple-element.60.refs_2_), channel_id=1, source_target_pairs={{0,64},{1,65},{2,66},{3,67},{4,68},{5,69},{6,70},{7,71},{64,0},{65... | collective-permute-start | bytes 1179656 | tf_op jit(solution)/shard_map/ppermute | solution.py:28
  76.9 5.5 %collective-permute-start.18 = (bf16[2,128,512]{2,1,0:T(8,128)(2,1)S(1)}, bf16[2,128,512]{2,1,0:T(8,128)(2,1)S(1)}, u32[]{:S(2)}, u32[]{:S(2)}) collective-permute-start(bf16[2,128,512]{2,1,0:T(8,128)(2,1)S(1)} %get-tuple-element.61.refs_4_), channel_id=1, source_target_pairs={{0,2},{1,3},{2,0},{3,1},{4,6},{5,7},{6,4},{7,5},{64,66},{65,67},{6... | collective-permute-start | bytes 786440 | tf_op jit(solution)/shard_map/ppermute | solution.py:28
  83.4 24.5 %copy-start.1 = (bf16[2,2,128,768]{3,2,1,0:T(8,128)(2,1)}, bf16[2,2,128,768]{3,2,1,0:T(8,128)(2,1)S(1)}, u32[]{:S(2)}) copy-start(bf16[2,2,128,768]{3,2,1,0:T(8,128)(2,1)S(1)} %get-tuple-element.62.refs_0_) | copy-start | bytes 2359300
  83.4 24.5 %copy-start.2 = (bf16[2,2,128,768]{3,2,1,0:T(8,128)(2,1)}, bf16[2,2,128,768]{3,2,1,0:T(8,128)(2,1)S(1)}, u32[]{:S(2)}) copy-start(bf16[2,2,128,768]{3,2,1,0:T(8,128)(2,1)S(1)} %get-tuple-element.63.refs_2_.refs_1_) | copy-start | bytes 2359300
  83.4 24.5 %copy-start.11 = (bf16[2,2,128,512]{3,2,1,0:T(8,128)(2,1)}, bf16[2,2,128,512]{3,2,1,0:T(8,128)(2,1)S(1)}, u32[]{:S(2)}) copy-start(bf16[2,2,128,512]{3,2,1,0:T(8,128)(2,1)S(1)} %get-tuple-element.64.refs_4_.refs_2_) | copy-start | bytes 1572868
  83.5 15.2 %collective-permute-start.19 = (bf16[2,2,128,768]{3,2,1,0:T(8,128)(2,1)S(1)}, bf16[2,2,128,768]{3,2,1,0:T(8,128)(2,1)S(1)}, u32[]{:S(2)}, u32[]{:S(2)}) collective-permute-start(bf16[2,2,128,768]{3,2,1,0:T(8,128)(2,1)S(1)} %get-tuple-element.62.refs_0_), channel_id=1, source_target_pairs={{0,2},{1,3},{2,0},{3,1},{4,6},{5,7},{6,4},{7,5},{64,66},{65,67},{6... | collective-permute-start | bytes 2359304 | tf_op jit(solution)/shard_map/ppermute | solution.py:28
  83.7 20.5 %collective-permute-start.20 = (bf16[2,2,128,768]{3,2,1,0:T(8,128)(2,1)S(1)}, bf16[2,2,128,768]{3,2,1,0:T(8,128)(2,1)S(1)}, u32[]{:S(2)}, u32[]{:S(2)}) collective-permute-start(bf16[2,2,128,768]{3,2,1,0:T(8,128)(2,1)S(1)} %get-tuple-element.63.refs_2_.refs_1_), channel_id=1, source_target_pairs={{0,6},{1,7},{2,4},{3,5},{4,2},{5,3},{6,0},{7,1},{64,70},{65,71},{6... | collective-permute-start | bytes 2359304 | tf_op jit(solution)/shard_map/ppermute | solution.py:28
  84.8 7.3 %collective-permute-start.26 = (bf16[2,2,128,512]{3,2,1,0:T(8,128)(2,1)S(1)}, bf16[2,2,128,512]{3,2,1,0:T(8,128)(2,1)S(1)}, u32[]{:S(2)}, u32[]{:S(2)}) collective-permute-start(bf16[2,2,128,512]{3,2,1,0:T(8,128)(2,1)S(1)} %get-tuple-element.64.refs_4_.refs_2_), channel_id=1, source_target_pairs={{0,1},{1,0},{2,3},{3,2},{4,5},{5,4},{6,7},{7,6},{64,65},{65,64},{6... | collective-permute-start | bytes 1572872 | tf_op jit(solution)/shard_map/ppermute | solution.py:28
  90.2 15.1 %collective-permute-start.21 = (bf16[2,2,128,512]{3,2,1,0:T(8,128)(2,1)S(1)}, bf16[2,2,128,512]{3,2,1,0:T(8,128)(2,1)S(1)}, u32[]{:S(2)}, u32[]{:S(2)}) collective-permute-start(bf16[2,2,128,512]{3,2,1,0:T(8,128)(2,1)S(1)} %get-tuple-element.64.refs_4_.refs_2_), channel_id=1, source_target_pairs={{0,64},{1,65},{2,66},{3,67},{4,68},{5,69},{6,70},{7,71},{64,0},{65... | collective-permute-start | bytes 1572872 | tf_op jit(solution)/shard_map/ppermute | solution.py:28
  91.8 14.2 %collective-permute-start.22 = (bf16[2,2,128,768]{3,2,1,0:T(8,128)(2,1)S(1)}, bf16[2,2,128,768]{3,2,1,0:T(8,128)(2,1)S(1)}, u32[]{:S(2)}, u32[]{:S(2)}) collective-permute-start(bf16[2,2,128,768]{3,2,1,0:T(8,128)(2,1)S(1)} %get-tuple-element.62.refs_0_), channel_id=1, source_target_pairs={{0,1},{1,0},{2,3},{3,2},{4,5},{5,4},{6,7},{7,6},{64,65},{65,64},{6... | collective-permute-start | bytes 2359304 | tf_op jit(solution)/shard_map/ppermute | solution.py:28
  92.1 15.9 %copy-start.12 = (bf16[2,2,128,512]{3,2,1,0:T(8,128)(2,1)}, bf16[2,2,128,512]{3,2,1,0:T(8,128)(2,1)S(1)}, u32[]{:S(2)}) copy-start(bf16[2,2,128,512]{3,2,1,0:T(8,128)(2,1)S(1)} %collective-permute-done.26.refs_10_.refs_5_) | copy-start | bytes 1572868
  92.1 14.0 %collective-permute-start.24 = (bf16[2,2,128,768]{3,2,1,0:T(8,128)(2,1)S(1)}, bf16[2,2,128,768]{3,2,1,0:T(8,128)(2,1)S(1)}, u32[]{:S(2)}, u32[]{:S(2)}) collective-permute-start(bf16[2,2,128,768]{3,2,1,0:T(8,128)(2,1)S(1)} %get-tuple-element.63.refs_2_.refs_1_), channel_id=1, source_target_pairs={{0,1},{1,0},{2,3},{3,2},{4,5},{5,4},{6,7},{7,6},{64,65},{65,64},{6... | collective-permute-start | bytes 2359304 | tf_op jit(solution)/shard_map/ppermute | solution.py:28
  98.7 9.4 %copy-start.3 = (bf16[2,2,128,768]{3,2,1,0:T(8,128)(2,1)}, bf16[2,2,128,768]{3,2,1,0:T(8,128)(2,1)S(1)}, u32[]{:S(2)}) copy-start(bf16[2,2,128,768]{3,2,1,0:T(8,128)(2,1)S(1)} %collective-permute-done.19.refs_1_.refs_0_) | copy-start | bytes 2359300
  98.7 9.4 %collective-permute-start.23 = (bf16[2,2,128,768]{3,2,1,0:T(8,128)(2,1)S(1)}, bf16[2,2,128,768]{3,2,1,0:T(8,128)(2,1)S(1)}, u32[]{:S(2)}, u32[]{:S(2)}) collective-permute-start(bf16[2,2,128,768]{3,2,1,0:T(8,128)(2,1)S(1)} %collective-permute-done.19.refs_1_.refs_0_), channel_id=1, source_target_pairs={{0,1},{1,0},{2,3},{3,2},{4,5},{5,4},{6,7},{7,6},{64,65},{65,64},{6... | collective-permute-start | bytes 2359304 | tf_op jit(solution)/shard_map/ppermute | solution.py:28
  104.3 3.8 %copy-start.4 = (bf16[2,2,128,768]{3,2,1,0:T(8,128)(2,1)}, bf16[2,2,128,768]{3,2,1,0:T(8,128)(2,1)S(1)}, u32[]{:S(2)}) copy-start(bf16[2,2,128,768]{3,2,1,0:T(8,128)(2,1)S(1)} %collective-permute-done.20.refs_3_.refs_1_) | copy-start | bytes 2359300
  104.3 3.8 %collective-permute-start.25 = (bf16[2,2,128,768]{3,2,1,0:T(8,128)(2,1)S(1)}, bf16[2,2,128,768]{3,2,1,0:T(8,128)(2,1)S(1)}, u32[]{:S(2)}, u32[]{:S(2)}) collective-permute-start(bf16[2,2,128,768]{3,2,1,0:T(8,128)(2,1)S(1)} %collective-permute-done.20.refs_3_.refs_1_), channel_id=1, source_target_pairs={{0,1},{1,0},{2,3},{3,2},{4,5},{5,4},{6,7},{7,6},{64,65},{65,64},{6... | collective-permute-start | bytes 2359304 | tf_op jit(solution)/shard_map/ppermute | solution.py:28
  105.2 2.9 %copy-start.13 = (bf16[2,2,128,512]{3,2,1,0:T(8,128)(2,1)}, bf16[2,2,128,512]{3,2,1,0:T(8,128)(2,1)S(1)}, u32[]{:S(2)}) copy-start(bf16[2,2,128,512]{3,2,1,0:T(8,128)(2,1)S(1)} %collective-permute-done.21.refs_5_.refs_2_) | copy-start | bytes 1572868
  105.2 2.8 %collective-permute-start.27 = (bf16[2,2,128,512]{3,2,1,0:T(8,128)(2,1)S(1)}, bf16[2,2,128,512]{3,2,1,0:T(8,128)(2,1)S(1)}, u32[]{:S(2)}, u32[]{:S(2)}) collective-permute-start(bf16[2,2,128,512]{3,2,1,0:T(8,128)(2,1)S(1)} %collective-permute-done.21.refs_5_.refs_2_), channel_id=1, source_target_pairs={{0,1},{1,0},{2,3},{3,2},{4,5},{5,4},{6,7},{7,6},{64,65},{65,64},{6... | collective-permute-start | bytes 1572872 | tf_op jit(solution)/shard_map/ppermute | solution.py:28
  106.0 1.9 %copy-start.5 = (bf16[2,2,128,768]{3,2,1,0:T(8,128)(2,1)}, bf16[2,2,128,768]{3,2,1,0:T(8,128)(2,1)S(1)}, u32[]{:S(2)}) copy-start(bf16[2,2,128,768]{3,2,1,0:T(8,128)(2,1)S(1)} %collective-permute-done.22.refs_6_.refs_3_) | copy-start | bytes 2359300
  106.0 1.9 %copy-start.6 = (bf16[2,2,128,768]{3,2,1,0:T(8,128)(2,1)}, bf16[2,2,128,768]{3,2,1,0:T(8,128)(2,1)S(1)}, u32[]{:S(2)}) copy-start(bf16[2,2,128,768]{3,2,1,0:T(8,128)(2,1)S(1)} %collective-permute-done.24.refs_8_.refs_4_) | copy-start | bytes 2359300
  108.1 3.0 %copy-start.14 = (bf16[2,2,128,512]{3,2,1,0:T(8,128)(2,1)}, bf16[2,2,128,512]{3,2,1,0:T(8,128)(2,1)S(1)}, u32[]{:S(2)}) copy-start(bf16[2,2,128,512]{3,2,1,0:T(8,128)(2,1)S(1)} %collective-permute-done.27.refs_11_.refs_5_) | copy-start | bytes 1572868
  108.1 9.3 %copy-start.10 = (bf16[512,512]{1,0:T(8,128)(2,1)S(1)}, bf16[512,512]{1,0:T(8,128)(2,1)}, u32[]{:S(2)}) copy-start(bf16[512,512]{1,0:T(8,128)(2,1)} %refs_13_.1) | copy-start | bytes 1572868
  108.1 3.0 %copy-start.7 = (bf16[2,2,128,768]{3,2,1,0:T(8,128)(2,1)}, bf16[2,2,128,768]{3,2,1,0:T(8,128)(2,1)S(1)}, u32[]{:S(2)}) copy-start(bf16[2,2,128,768]{3,2,1,0:T(8,128)(2,1)S(1)} %collective-permute-done.23.refs_7_.refs_3_) | copy-start | bytes 2359300
  108.1 3.0 %copy-start.8 = (bf16[2,2,128,768]{3,2,1,0:T(8,128)(2,1)}, bf16[2,2,128,768]{3,2,1,0:T(8,128)(2,1)S(1)}, u32[]{:S(2)}) copy-start(bf16[2,2,128,768]{3,2,1,0:T(8,128)(2,1)S(1)} %collective-permute-done.25.refs_9_.refs_4_) | copy-start | bytes 2359300
  111.1 19.8 %all-to-all-start.1 = ((bf16[128,16,128]{2,1,0:T(8,128)(2,1)}), bf16[128,16,128]{2,1,0:T(8,128)(2,1)S(1)}, u32[]{:S(2)}, u32[]{:S(2)}) async-start(bf16[128,16,128]{2,1,0:T(8,128)(2,1)} %bitcast.8), calls=%async_computation.1 | async-start | bytes 1048576 | tf_op jit(solution)/shard_map/all_to_all | solution.py:459
  117.4 13.5 %copy-start.15 = (bf16[4,8192]{1,0:T(4,128)(2,1)S(1)}, bf16[4,8192]{1,0:T(4,128)(2,1)}, u32[]{:S(2)}) copy-start(bf16[4,8192]{1,0:T(4,128)(2,1)} %act.3) | copy-start | bytes 196612
  117.4 13.5 %copy-start.16 = (f32[8192]{0:T(1024)S(1)}, f32[8192]{0:T(1024)}, u32[]{:S(2)}) copy-start(f32[8192]{0:T(1024)} %param.7) | copy-start | bytes 98308
  (1 other events, 0.7 us)

commit v4 on v3

--- a/solution.py
+++ b/solution.py
@@ -207,16 +207,25 @@
 SLOPE, CUBE = 0.7978845608028654, 0.044715
 
 
-def joint(kernel, name, arrays, shapes):
+def joint(kernel, name, arrays, shapes, step):
+    each = len(arrays) // 3
+    picked = [p * each + k for p in far_first(step) for k in range(each)]
+
+    def body(*refs):
+        inputs = [None] * len(picked)
+        for place, source in enumerate(picked):
+            inputs[source] = refs[place]
+        kernel(*inputs, *refs[len(picked) :])
+
     outs = pl.pallas_call(
-        kernel,
+        body,
         in_specs=[pl.BlockSpec(memory_space=pltpu.VMEM)] * len(arrays),
         out_specs=[pl.BlockSpec(memory_space=pltpu.VMEM)] * len(shapes),
         out_shape=[jax.ShapeDtypeStruct(*shape) for shape in shapes],
         compiler_params=pltpu.CompilerParams(vmem_limit_bytes=16 * MIB),
         cost_estimate=pl.CostEstimate(flops=MIB, bytes_accessed=MIB, transcendentals=0),
         name=name,
-    )(*arrays)
+    )(*[arrays[k] for k in picked])
     return list(outs)
 
 
@@ -238,20 +247,25 @@
     )(x, after)
 
 
+def far_first(step):
+    return sorted(range(3), key=lambda p: ORDERS[p][step] != 1)
+
+
 def exchange_sums(up, pre):
     widths = [CUTS[p + 1] - CUTS[p] for p in range(3)]
-    arrays = []
-    for p, order in enumerate(ORDERS):
-        for keep, send in (up[p], pre[p]):
-            arrays += [keep, swap(send, order[0])]
+    arrays = [None] * 12
+    for n, sums in enumerate((up, pre)):
+        for p in far_first(0):
+            keep, send = sums[p]
+            arrays[p * 4 + n * 2 : p * 4 + n * 2 + 2] = keep, swap(send, ORDERS[p][0])
     pair = [((2, 128, width), dtype) for width in widths for dtype in (F32, BF16)]
-    left = joint(first_kernel, "first_sums", arrays, pair)
-    for p, order in enumerate(ORDERS):
-        left[p * 2 + 1] = swap(left[p * 2 + 1], order[1])
-    left = joint(second_kernel, "second_sums", left, pair)
-    for p, order in enumerate(ORDERS):
-        left[p * 2 + 1] = swap(left[p * 2 + 1], order[2])
-    return joint(third_kernel, "third_sums", left, [((2, 128, width), BF16) for width in widths])
+    left = joint(first_kernel, "first_sums", arrays, pair, 0)
+    for p in far_first(1):
+        left[p * 2 + 1] = swap(left[p * 2 + 1], ORDERS[p][1])
+    left = joint(second_kernel, "second_sums", left, pair, 1)
+    for p in far_first(2):
+        left[p * 2 + 1] = swap(left[p * 2 + 1], ORDERS[p][2])
+    return joint(third_kernel, "third_sums", left, [((2, 128, width), BF16) for width in widths], 2)
 
 
 def fourth_kernel(*refs):
@@ -261,13 +275,13 @@
 
 
 def gather(parts):
-    arrays = []
-    for x, order in zip(parts, ORDERS):
-        arrays += [x, swap(x, order[1])]
-    held = joint(fourth_kernel, "fourth_blocks", arrays, [((2, *x.shape), BF16) for x in parts])
-    pieces = []
-    for x, order in zip(held, ORDERS):
-        pieces += [x, swap(x, order[0])]
+    arrays = [None] * 6
+    for p in far_first(1):
+        arrays[p * 2 : p * 2 + 2] = parts[p], swap(parts[p], ORDERS[p][1])
+    held = joint(fourth_kernel, "fourth_blocks", arrays, [((2, *x.shape), BF16) for x in parts], 1)
+    pieces = [None] * 6
+    for p in far_first(0):
+        pieces[p * 2 : p * 2 + 2] = held[p], swap(held[p], ORDERS[p][0])
     return pieces
 
 

time: 132 us -> 132 us (level)
  starting transfers between devices: 52.5 us -> 49 us
  waiting for transfers between devices: 45.4 us -> 48.6 us
    ppermute x28, starting transfers between devices: 36 us -> 32.7 us  [swap(): return lax.ppermute(x, OWNERS, pairs)]
    ppermute x28, waiting for transfers between devices: 37.2 us -> 40.4 us  [swap(): return lax.ppermute(x, OWNERS, pairs)]
  transfers between devices with their start and end apart: 30 -> 30, of which waited for: 18 -> 17; matrix products, arithmetic and copies ran while one was open for 0% -> 0% of each run, Pallas kernels for 19% -> 19%
where the time goes in v4:
time: 132 us
  starting transfers between devices  49 us (37%)
  waiting for transfers between devices  48.6 us (37%)
  Pallas kernels  30.5 us (23%)
  local copies, waits for them, and re-layouts  2.61 us (2%)
    ppermute x28, waiting for transfers between devices, swap(): return lax.ppermute(x, OWNERS, pairs)  40.4 us
    ppermute x28, starting transfers between devices, swap(): return lax.ppermute(x, OWNERS, pairs)  32.7 us
    pallas_call x1, Pallas kernels, grads_of(): pl.pallas_call(grads_kernel, in_specs=[SCALARS] + [anywhere] * 12 + [vmem...  10.9 us
    all_to_all x1, starting transfers between devices, local(): lax.all_to_all(messages.reshape(128, 16, 128), EVERY, 0, 0, tiled=True)  10.2 us
    pallas_call x2, Pallas kernels, chip_sum(): pl.pallas_call(up_kernel if up else pre_kernel, in_specs=[SCALARS] + [VME...  9.87 us
    all_to_all x1, starting transfers between devices, local(): lax.all_to_all(share.reshape(128, 16, 128), EVERY, 0, 0, tiled=True)  6.15 us
    all_to_all x1, waiting for transfers between devices, local(): lax.all_to_all(messages.reshape(128, 16, 128), EVERY, 0, 0, tiled=True)  5.7 us
    pallas_call x1, Pallas kernels, back_messages(): pl.pallas_call(came_kernel, in_specs=[SCALARS] + [vmem] * 8, out_shape=pl...  2.94 us
  transfers between devices with their start and end apart: 30, of which 17 were waited for; matrix products, arithmetic and copies ran while one was open for 0% of the time, Pallas kernels for 19%

profile of v4, /device:TPU:1, one launch (start us, length us, event | category | flops | bytes accessed | tf_op | source)
XLA Modules:
  0.0 131.8 jit_solution(17509915880651648957)
XLA Ops:
  0.6 1.5 %collective-permute-start.1 = (bf16[4096,512]{1,0:T(8,128)(2,1)}, bf16[4096,512]{1,0:T(8,128)(2,1)}, u32[]{:S(2)}, u32[]{:S(2)}) collective-permute-start(bf16[4096,512]{1,0:T(8,128)(2,1)} %w.2), channel_id=1, source_target_pairs={{0,1},{1,0},{2,3},{3,2},{4,5},{5,4},{6,7},{7,6},{64,65},{65,64},{6... | collective-permute-start | bytes 12582920 | tf_op jit(solution)/shard_map/ppermute | solution.py:28
  2.6 2.1 %norm_messages.1 = bf16[2,8,8,16,128]{4,3,2,1,0:T(8,128)(2,1)} custom-call(bf16[4,8192]{1,0:T(4,128)(2,1)} %act.3, f32[1,8192]{1,0:T(1,128)} %bitcast.6, f32[1,8192]{1,0:T(1,128)} %bitcast.10), custom_call_target="tpu_custom_call" | custom-call | tf_op jit(solution)/shard_map/norm_messages/pallas_call | solution.py:56
  4.7 10.2 %all-to-all-start = ((bf16[128,16,128]{2,1,0:T(8,128)(2,1)}), bf16[128,16,128]{2,1,0:T(8,128)(2,1)S(1)}, u32[]{:S(2)}, u32[]{:S(2)}) async-start(bf16[128,16,128]{2,1,0:T(8,128)(2,1)} %bitcast.9), calls=%async_computation | async-start | bytes 1048576 | tf_op jit(solution)/shard_map/all_to_all | solution.py:464
  15.0 1.0 copy-done.9
  16.1 5.2 %up_sum.1 = (f32[256,768]{1,0:T(8,128)S(1)}, bf16[256,768]{1,0:T(8,128)(2,1)S(1)}, f32[256,768]{1,0:T(8,128)S(1)}, bf16[256,768]{1,0:T(8,128)(2,1)S(1)}, f32[256...) custom-call(s32[2]{0:T(128)S(1)} %pad_add_fusion.at, bf16[512,512]{1,0:T(8,128)(2,1)S(1)} %copy-done.9, ...), custom_call_target="tpu_custom_call" | custom-call | flops 1048576 | bytes 1048576 | tf_op jit(solution)/shard_map/up_sum/pallas_call | solution.py:161
  21.2 0.8 copy-done.17
  22.0 0.7 copy-done.18
  22.7 5.7 %all-to-all-done.x = bf16[128,16,128]{2,1,0:T(8,128)(2,1)S(1)} async-done(((bf16[128,16,128]{2,1,0:T(8,128)(2,1)}), bf16[128,16,128]{2,1,0:T(8,128)(2,1)S(1)}, u32[]{:S(2)}, u32[]{:S(2)}) %all-to-all-start) | async-done | bytes 524320 | tf_op jit(solution)/shard_map/all_to_all | solution.py:464
  28.4 1.1 collective-permute-start.3
  30.2 1.2 collective-permute-start.8
  31.4 4.7 %pre_sum.1 = (f32[256,768]{1,0:T(8,128)S(1)}, bf16[256,768]{1,0:T(8,128)(2,1)S(1)}, f32[256,768]{1,0:T(8,128)S(1)}, bf16[256,768]{1,0:T(8,128)(2,1)S(1)}, f32[25...) custom-call(s32[2]{0:T(128)S(1)} %pad_add_fusion.at, bf16[128,16,128]{2,1,0:T(8,128)(2,1)S(1)} %gate.1.x.refs_12_, ...), custom_call_target="tpu_custom_call" | custom-call | flops 1048576 | bytes 1048576 | tf_op jit(solution)/shard_map/pre_sum/pallas_call | solution.py:161
  36.2 0.4 collective-permute-start.7
  36.6 1.6 %collective-permute-start.9 = (bf16[256,768]{1,0:T(8,128)(2,1)S(1)}, bf16[256,768]{1,0:T(8,128)(2,1)S(1)}, u32[]{:S(2)}, u32[]{:S(2)}) collective-permute-start(bf16[256,768]{1,0:T(8,128)(2,1)S(1)} %get-tuple-element.46), channel_id=1, source_target_pairs={{0,6},{1,7},{2,4},{3,5},{4,2},{5,3},{6,0},{7,1},{64,70},{65,71},{6... | collective-permute-start | bytes 1179656 | tf_op jit(solution)/shard_map/ppermute | solution.py:28
  38.2 0.7 collective-permute-done.2.refs_1_
  38.9 1.9 %collective-permute-start.5 = (bf16[256,512]{1,0:T(8,128)(2,1)S(1)}, bf16[256,512]{1,0:T(8,128)(2,1)S(1)}, u32[]{:S(2)}, u32[]{:S(2)}) collective-permute-start(bf16[256,512]{1,0:T(8,128)(2,1)S(1)} %get-tuple-element.39), channel_id=1, source_target_pairs={{0,64},{1,65},{2,66},{3,67},{4,68},{5,69},{6,70},{7,71},{64,0},{65... | collective-permute-start | bytes 786440 | tf_op jit(solution)/shard_map/ppermute | solution.py:28
  40.8 0.8 collective-permute-done.8.refs_9_
  41.6 5.8 %collective-permute-done.5.refs_3_ = bf16[256,512]{1,0:T(8,128)(2,1)S(1)} collective-permute-done((bf16[256,512]{1,0:T(8,128)(2,1)S(1)}, bf16[256,512]{1,0:T(8,128)(2,1)S(1)}, u32[]{:S(2)}, u32[]{:S(2)}) %collective-permute-start.5) | collective-permute-done | bytes 262176 | tf_op jit(solution)/shard_map/ppermute | solution.py:28
  47.4 1.3 collective-permute-done.7.refs_7_
  48.7 1.4 %collective-permute-done.9.refs_11_ = bf16[256,768]{1,0:T(8,128)(2,1)S(1)} collective-permute-done((bf16[256,768]{1,0:T(8,128)(2,1)S(1)}, bf16[256,768]{1,0:T(8,128)(2,1)S(1)}, u32[]{:S(2)}, u32[]{:S(2)}) %collective-permute-start.9) | collective-permute-done | bytes 393248 | tf_op jit(solution)/shard_map/ppermute | solution.py:28
  50.1 0.4 first_sums.1
  50.5 2.6 %collective-permute-start.10 = (bf16[2,128,768]{2,1,0:T(8,128)(2,1)S(1)}, bf16[2,128,768]{2,1,0:T(8,128)(2,1)S(1)}, u32[]{:S(2)}, u32[]{:S(2)}) collective-permute-start(bf16[2,128,768]{2,1,0:T(8,128)(2,1)S(1)} %get-tuple-element.48), channel_id=1, source_target_pairs={{0,64},{1,65},{2,66},{3,67},{4,68},{5,69},{6,70},{7,71},{64,0},{65... | collective-permute-start | bytes 1179656 | tf_op jit(solution)/shard_map/ppermute | solution.py:28
  53.1 0.7 collective-permute-start.11
  53.7 6.0 %collective-permute-done.12.refs_5_ = bf16[2,128,512]{2,1,0:T(8,128)(2,1)S(1)} collective-permute-done((bf16[2,128,512]{2,1,0:T(8,128)(2,1)S(1)}, bf16[2,128,512]{2,1,0:T(8,128)(2,1)S(1)}, u32[]{:S(2)}, u32[]{:S(2)}) %collective-permute-start.12) | collective-permute-done | bytes 262176 | tf_op jit(solution)/shard_map/ppermute | solution.py:28
  59.7 1.5 %collective-permute-done.10.refs_1_ = bf16[2,128,768]{2,1,0:T(8,128)(2,1)S(1)} collective-permute-done((bf16[2,128,768]{2,1,0:T(8,128)(2,1)S(1)}, bf16[2,128,768]{2,1,0:T(8,128)(2,1)S(1)}, u32[]{:S(2)}, u32[]{:S(2)}) %collective-permute-start.10) | collective-permute-done | bytes 393248 | tf_op jit(solution)/shard_map/ppermute | solution.py:28
  61.2 2.0 %collective-permute-done.11.refs_3_ = bf16[2,128,768]{2,1,0:T(8,128)(2,1)S(1)} collective-permute-done((bf16[2,128,768]{2,1,0:T(8,128)(2,1)S(1)}, bf16[2,128,768]{2,1,0:T(8,128)(2,1)S(1)}, u32[]{:S(2)}, u32[]{:S(2)}) %collective-permute-start.11) | collective-permute-done | bytes 393248 | tf_op jit(solution)/shard_map/ppermute | solution.py:28
  63.5 0.7 collective-permute-start.13
  64.3 0.8 collective-permute-start.15
  65.1 5.9 %collective-permute-done.15.refs_5_ = bf16[2,128,512]{2,1,0:T(8,128)(2,1)S(1)} collective-permute-done((bf16[2,128,512]{2,1,0:T(8,128)(2,1)S(1)}, bf16[2,128,512]{2,1,0:T(8,128)(2,1)S(1)}, u32[]{:S(2)}, u32[]{:S(2)}) %collective-permute-start.15) | collective-permute-done | bytes 262176 | tf_op jit(solution)/shard_map/ppermute | solution.py:28
  71.0 2.1 %collective-permute-done.13.refs_1_ = bf16[2,128,768]{2,1,0:T(8,128)(2,1)S(1)} collective-permute-done((bf16[2,128,768]{2,1,0:T(8,128)(2,1)S(1)}, bf16[2,128,768]{2,1,0:T(8,128)(2,1)S(1)}, u32[]{:S(2)}, u32[]{:S(2)}) %collective-permute-start.13) | collective-permute-done | bytes 393248 | tf_op jit(solution)/shard_map/ppermute | solution.py:28
  73.1 0.8 third_sums.1
  73.9 1.3 collective-permute-start.16
  75.1 1.0 collective-permute-start.17
  76.2 5.2 %collective-permute-done.18.refs_5_ = bf16[2,128,512]{2,1,0:T(8,128)(2,1)S(1)} collective-permute-done((bf16[2,128,512]{2,1,0:T(8,128)(2,1)S(1)}, bf16[2,128,512]{2,1,0:T(8,128)(2,1)S(1)}, u32[]{:S(2)}, u32[]{:S(2)}) %collective-permute-start.18) | collective-permute-done | bytes 262176 | tf_op jit(solution)/shard_map/ppermute | solution.py:28
  81.4 1.2 collective-permute-done.16.refs_1_
  82.5 0.7 collective-permute-done.17.refs_3_
  83.7 1.1 collective-permute-start.20
  84.8 5.3 %collective-permute-start.26 = (bf16[2,2,128,512]{3,2,1,0:T(8,128)(2,1)S(1)}, bf16[2,2,128,512]{3,2,1,0:T(8,128)(2,1)S(1)}, u32[]{:S(2)}, u32[]{:S(2)}) collective-permute-start(bf16[2,2,128,512]{3,2,1,0:T(8,128)(2,1)S(1)} %get-tuple-element.64.refs_4_.refs_2_), channel_id=1, source_target_pairs={{0,1},{1,0},{2,3},{3,2},{4,5},{5,4},{6,7},{7,6},{64,65},{65,64},{6... | collective-permute-start | bytes 1572872 | tf_op jit(solution)/shard_map/ppermute | solution.py:28
  90.1 1.4 %collective-permute-start.21 = (bf16[2,2,128,512]{3,2,1,0:T(8,128)(2,1)S(1)}, bf16[2,2,128,512]{3,2,1,0:T(8,128)(2,1)S(1)}, u32[]{:S(2)}, u32[]{:S(2)}) collective-permute-start(bf16[2,2,128,512]{3,2,1,0:T(8,128)(2,1)S(1)} %get-tuple-element.64.refs_4_.refs_2_), channel_id=1, source_target_pairs={{0,64},{1,65},{2,66},{3,67},{4,68},{5,69},{6,70},{7,71},{64,0},{65... | collective-permute-start | bytes 1572872 | tf_op jit(solution)/shard_map/ppermute | solution.py:28
  92.0 5.7 %collective-permute-done.19.refs_1_.refs_0_ = bf16[2,2,128,768]{3,2,1,0:T(8,128)(2,1)S(1)} collective-permute-done((bf16[2,2,128,768]{3,2,1,0:T(8,128)(2,1)S(1)}, bf16[2,2,128,768]{3,2,1,0:T(8,128)(2,1)S(1)}, u32[]{:S(2)}, u32[]{:S(2)}) %collective-permute-start.19) | collective-permute-done | bytes 786464 | tf_op jit(solution)/shard_map/ppermute | solution.py:28
  97.7 5.9 %collective-permute-start.23 = (bf16[2,2,128,768]{3,2,1,0:T(8,128)(2,1)S(1)}, bf16[2,2,128,768]{3,2,1,0:T(8,128)(2,1)S(1)}, u32[]{:S(2)}, u32[]{:S(2)}) collective-permute-start(bf16[2,2,128,768]{3,2,1,0:T(8,128)(2,1)S(1)} %collective-permute-done.19.refs_1_.refs_0_), channel_id=1, source_target_pairs={{0,1},{1,0},{2,3},{3,2},{4,5},{5,4},{6,7},{7,6},{64,65},{65,64},{6... | collective-permute-start | bytes 2359304 | tf_op jit(solution)/shard_map/ppermute | solution.py:28
  103.7 1.4 %collective-permute-start.25 = (bf16[2,2,128,768]{3,2,1,0:T(8,128)(2,1)S(1)}, bf16[2,2,128,768]{3,2,1,0:T(8,128)(2,1)S(1)}, u32[]{:S(2)}, u32[]{:S(2)}) collective-permute-start(bf16[2,2,128,768]{3,2,1,0:T(8,128)(2,1)S(1)} %collective-permute-done.20.refs_3_.refs_1_), channel_id=1, source_target_pairs={{0,1},{1,0},{2,3},{3,2},{4,5},{5,4},{6,7},{7,6},{64,65},{65,64},{6... | collective-permute-start | bytes 2359304 | tf_op jit(solution)/shard_map/ppermute | solution.py:28
  105.2 0.8 collective-permute-start.27
  106.0 1.9 %back_held.1.refs_7_ = f32[512,512]{1,0:T(8,128)S(1)} custom-call(s32[2]{0:T(128)S(1)} %pad_add_fusion.at, bf16[2,2,128,768]{3,2,1,0:T(8,128)(2,1)S(1)} %get-tuple-element.62.refs_0_, bf16[2,2,128,768]{3,2,1,0:T(8,128)(2,1)S(1)} %get-tuple-element.63.refs_2_.refs_1_, bf16[2,2,128,512]{3,2,1,0:T(8,128)(2,1)S(1)} %get-tuple-element.64.refs_4_.refs_2_, ...), custom_call_target="tpu_custom_call" | custom-call | flops 1073741824 | bytes 4194304 | tf_op jit(solution)/shard_map/back_held/pallas_call | solution.py:330
  108.0 2.9 %back_messages.1 = bf16[64,2,16,128]{3,2,1,0:T(8,128)(2,1)} custom-call(s32[2]{0:T(128)S(1)} %pad_add_fusion.at, bf16[2,2,128,768]{3,2,1,0:T(8,128)(2,1)S(1)} %collective-permute-done.19.refs_1_.refs_0_, bf16[2,2,128,768]{3,2,1,0:T(8,128)(2,1)S(1)} %collective-permute-done.20.refs_3_.refs_1_, ...), custom_call_target="tpu_custom_call" | custom-call | flops 1073741824 | bytes 4194304 | tf_op jit(solution)/shard_map/back_messages/pallas_call | solution.py:337
  111.0 6.1 %all-to-all-start.1 = ((bf16[128,16,128]{2,1,0:T(8,128)(2,1)}), bf16[128,16,128]{2,1,0:T(8,128)(2,1)S(1)}, u32[]{:S(2)}, u32[]{:S(2)}) async-start(bf16[128,16,128]{2,1,0:T(8,128)(2,1)} %bitcast.8), calls=%async_computation.1 | async-start | bytes 1048576 | tf_op jit(solution)/shard_map/all_to_all | solution.py:473
  117.1 10.9 %grads.1 = (f32[512,4096]{1,0:T(8,128)}, f32[4096,512]{1,0:T(8,128)}) custom-call(s32[2]{0:T(128)S(1)} %pad_add_fusion.at, bf16[2,2,128,768]{3,2,1,0:T(8,128)(2,1)} %copy-done.1, bf16[2,2,128,768]{3,2,1,0:T(8,128)(2,1)} %copy-done.3, bf16[2,2,128,768]{3,2,1,0:T(8,128)(2,1)} %copy-done.2, bf16[2,2,128,768]{3,2,1,0:T(8,128)(2,1)} %copy-done.4, ...), custom_call_target="tpu_custom_call" | custom-call | flops 4294967296 | bytes 25165824 | tf_op jit(solution)/shard_map/grads/pallas_call | solution.py:395
  128.1 2.5 %all-to-all-done.1.x = bf16[128,16,128]{2,1,0:T(8,128)(2,1)S(1)} async-done(((bf16[128,16,128]{2,1,0:T(8,128)(2,1)}), bf16[128,16,128]{2,1,0:T(8,128)(2,1)S(1)}, u32[]{:S(2)}, u32[]{:S(2)}) %all-to-all-start.1) | async-done | bytes 524320 | tf_op jit(solution)/shard_map/all_to_all | solution.py:473
  130.6 1.2 grad_act.1
  (63 shorter events, 2.8 us)
Async XLA Ops:
  0.6 14.4 %collective-permute-start.1 = (bf16[4096,512]{1,0:T(8,128)(2,1)}, bf16[4096,512]{1,0:T(8,128)(2,1)}, u32[]{:S(2)}, u32[]{:S(2)}) collective-permute-start(bf16[4096,512]{1,0:T(8,128)(2,1)} %w.2), channel_id=1, source_target_pairs={{0,1},{1,0},{2,3},{3,2},{4,5},{5,4},{6,7},{7,6},{64,65},{65,64},{6... | collective-permute-start | bytes 12582920 | tf_op jit(solution)/shard_map/ppermute | solution.py:28
  2.1 29.3 %collective-permute-start.4 = (bf16[512,4096]{1,0:T(8,128)(2,1)}, bf16[512,4096]{1,0:T(8,128)(2,1)}, u32[]{:S(2)}, u32[]{:S(2)}) collective-permute-start(bf16[512,4096]{1,0:T(8,128)(2,1)} %refs_6_.3), channel_id=1, source_target_pairs={{0,1},{1,0},{2,3},{3,2},{4,5},{5,4},{6,7},{7,6},{64,65},{65,64},{6... | collective-permute-start | bytes 12582920 | tf_op jit(solution)/shard_map/ppermute | solution.py:28
  2.2 12.8 %collective-permute-start = (bf16[512,512]{1,0:T(8,128)(2,1)}, bf16[512,512]{1,0:T(8,128)(2,1)S(1)}, u32[]{:S(2)}, u32[]{:S(2)}) collective-permute-start(bf16[512,512]{1,0:T(8,128)(2,1)} %refs_13_.1), channel_id=1, source_target_pairs={{0,1},{1,0},{2,3},{3,2},{4,5},{5,4},{6,7},{7,6},{64,65},{65,64},{6... | collective-permute-start | bytes 1572872 | tf_op jit(solution)/shard_map/ppermute | solution.py:28
  4.7 23.7 %all-to-all-start = ((bf16[128,16,128]{2,1,0:T(8,128)(2,1)}), bf16[128,16,128]{2,1,0:T(8,128)(2,1)S(1)}, u32[]{:S(2)}, u32[]{:S(2)}) async-start(bf16[128,16,128]{2,1,0:T(8,128)(2,1)} %bitcast.9), calls=%async_computation | async-start | bytes 1048576 | tf_op jit(solution)/shard_map/all_to_all | solution.py:464
  15.0 1.0 copy-start.9
  21.2 0.8 copy-start.17
  28.4 3.0 %collective-permute-start.3 = (bf16[128,16,128]{2,1,0:T(8,128)(2,1)S(1)}, bf16[128,16,128]{2,1,0:T(8,128)(2,1)S(1)}, u32[]{:S(2)}, u32[]{:S(2)}) collective-permute-start(bf16[128,16,128]{2,1,0:T(8,128)(2,1)S(1)} %gate.1.x.refs_12_), channel_id=1, source_target_pairs={{0,1},{1,0},{2,3},{3,2},{4,5},{5,4},{6,7},{7,6},{64,65},{65,64},{6... | collective-permute-start | bytes 1572872 | tf_op jit(solution)/shard_map/ppermute | solution.py:28
  29.5 9.4 %collective-permute-start.2 = (bf16[256,512]{1,0:T(8,128)(2,1)S(1)}, bf16[256,512]{1,0:T(8,128)(2,1)S(1)}, u32[]{:S(2)}, u32[]{:S(2)}) collective-permute-start(bf16[256,512]{1,0:T(8,128)(2,1)S(1)} %get-tuple-element.36), channel_id=1, source_target_pairs={{0,64},{1,65},{2,66},{3,67},{4,68},{5,69},{6,70},{7,71},{64,0},{65... | collective-permute-start | bytes 786440 | tf_op jit(solution)/shard_map/ppermute | solution.py:28
  29.8 11.0 %collective-permute-start.6 = (bf16[256,768]{1,0:T(8,128)(2,1)}, bf16[256,768]{1,0:T(8,128)(2,1)S(1)}, u32[]{:S(2)}, u32[]{:S(2)}) collective-permute-start(bf16[256,768]{1,0:T(8,128)(2,1)} %copy-done.18), channel_id=1, source_target_pairs={{0,2},{1,3},{2,0},{3,1},{4,6},{5,7},{6,4},{7,5},{64,66},{65,67},{6... | collective-permute-start | bytes 1179656 | tf_op jit(solution)/shard_map/ppermute | solution.py:28
  30.2 11.4 %collective-permute-start.8 = (bf16[256,768]{1,0:T(8,128)(2,1)}, bf16[256,768]{1,0:T(8,128)(2,1)S(1)}, u32[]{:S(2)}, u32[]{:S(2)}) collective-permute-start(bf16[256,768]{1,0:T(8,128)(2,1)} %copy-done.17), channel_id=1, source_target_pairs={{0,6},{1,7},{2,4},{3,5},{4,2},{5,3},{6,0},{7,1},{64,70},{65,71},{6... | collective-permute-start | bytes 1179656 | tf_op jit(solution)/shard_map/ppermute | solution.py:28
  36.2 12.5 %collective-permute-start.7 = (bf16[256,768]{1,0:T(8,128)(2,1)S(1)}, bf16[256,768]{1,0:T(8,128)(2,1)S(1)}, u32[]{:S(2)}, u32[]{:S(2)}) collective-permute-start(bf16[256,768]{1,0:T(8,128)(2,1)S(1)} %get-tuple-element.42), channel_id=1, source_target_pairs={{0,2},{1,3},{2,0},{3,1},{4,6},{5,7},{6,4},{7,5},{64,66},{65,67},{6... | collective-permute-start | bytes 1179656 | tf_op jit(solution)/shard_map/ppermute | solution.py:28
  36.6 13.5 %collective-permute-start.9 = (bf16[256,768]{1,0:T(8,128)(2,1)S(1)}, bf16[256,768]{1,0:T(8,128)(2,1)S(1)}, u32[]{:S(2)}, u32[]{:S(2)}) collective-permute-start(bf16[256,768]{1,0:T(8,128)(2,1)S(1)} %get-tuple-element.46), channel_id=1, source_target_pairs={{0,6},{1,7},{2,4},{3,5},{4,2},{5,3},{6,0},{7,1},{64,70},{65,71},{6... | collective-permute-start | bytes 1179656 | tf_op jit(solution)/shard_map/ppermute | solution.py:28
  38.9 8.5 %collective-permute-start.5 = (bf16[256,512]{1,0:T(8,128)(2,1)S(1)}, bf16[256,512]{1,0:T(8,128)(2,1)S(1)}, u32[]{:S(2)}, u32[]{:S(2)}) collective-permute-start(bf16[256,512]{1,0:T(8,128)(2,1)S(1)} %get-tuple-element.39), channel_id=1, source_target_pairs={{0,64},{1,65},{2,66},{3,67},{4,68},{5,69},{6,70},{7,71},{64,0},{65... | collective-permute-start | bytes 786440 | tf_op jit(solution)/shard_map/ppermute | solution.py:28
  50.5 10.7 %collective-permute-start.10 = (bf16[2,128,768]{2,1,0:T(8,128)(2,1)S(1)}, bf16[2,128,768]{2,1,0:T(8,128)(2,1)S(1)}, u32[]{:S(2)}, u32[]{:S(2)}) collective-permute-start(bf16[2,128,768]{2,1,0:T(8,128)(2,1)S(1)} %get-tuple-element.48), channel_id=1, source_target_pairs={{0,64},{1,65},{2,66},{3,67},{4,68},{5,69},{6,70},{7,71},{64,0},{65... | collective-permute-start | bytes 1179656 | tf_op jit(solution)/shard_map/ppermute | solution.py:28
  53.1 10.1 %collective-permute-start.11 = (bf16[2,128,768]{2,1,0:T(8,128)(2,1)S(1)}, bf16[2,128,768]{2,1,0:T(8,128)(2,1)S(1)}, u32[]{:S(2)}, u32[]{:S(2)}) collective-permute-start(bf16[2,128,768]{2,1,0:T(8,128)(2,1)S(1)} %get-tuple-element.50), channel_id=1, source_target_pairs={{0,6},{1,7},{2,4},{3,5},{4,2},{5,3},{6,0},{7,1},{64,70},{65,71},{6... | collective-permute-start | bytes 1179656 | tf_op jit(solution)/shard_map/ppermute | solution.py:28
  53.7 6.0 %collective-permute-start.12 = (bf16[2,128,512]{2,1,0:T(8,128)(2,1)S(1)}, bf16[2,128,512]{2,1,0:T(8,128)(2,1)S(1)}, u32[]{:S(2)}, u32[]{:S(2)}) collective-permute-start(bf16[2,128,512]{2,1,0:T(8,128)(2,1)S(1)} %get-tuple-element.52), channel_id=1, source_target_pairs={{0,2},{1,3},{2,0},{3,1},{4,6},{5,7},{6,4},{7,5},{64,66},{65,67},{6... | collective-permute-start | bytes 786440 | tf_op jit(solution)/shard_map/ppermute | solution.py:28
  63.2 42.7 %copy-start = (bf16[512,4096]{1,0:T(8,128)(2,1)S(1)}, bf16[512,4096]{1,0:T(8,128)(2,1)}, u32[]{:S(2)}) copy-start(bf16[512,4096]{1,0:T(8,128)(2,1)} %refs_6_.3) | copy-start | bytes 12582916
  63.5 9.6 %collective-permute-start.13 = (bf16[2,128,768]{2,1,0:T(8,128)(2,1)S(1)}, bf16[2,128,768]{2,1,0:T(8,128)(2,1)S(1)}, u32[]{:S(2)}, u32[]{:S(2)}) collective-permute-start(bf16[2,128,768]{2,1,0:T(8,128)(2,1)S(1)} %get-tuple-element.54), channel_id=1, source_target_pairs={{0,64},{1,65},{2,66},{3,67},{4,68},{5,69},{6,70},{7,71},{64,0},{65... | collective-permute-start | bytes 1179656 | tf_op jit(solution)/shard_map/ppermute | solution.py:28
  64.2 8.9 %collective-permute-start.14 = (bf16[2,128,768]{2,1,0:T(8,128)(2,1)S(1)}, bf16[2,128,768]{2,1,0:T(8,128)(2,1)S(1)}, u32[]{:S(2)}, u32[]{:S(2)}) collective-permute-start(bf16[2,128,768]{2,1,0:T(8,128)(2,1)S(1)} %get-tuple-element.56), channel_id=1, source_target_pairs={{0,2},{1,3},{2,0},{3,1},{4,6},{5,7},{6,4},{7,5},{64,66},{65,67},{6... | collective-permute-start | bytes 1179656 | tf_op jit(solution)/shard_map/ppermute | solution.py:28
  64.3 6.7 %collective-permute-start.15 = (bf16[2,128,512]{2,1,0:T(8,128)(2,1)S(1)}, bf16[2,128,512]{2,1,0:T(8,128)(2,1)S(1)}, u32[]{:S(2)}, u32[]{:S(2)}) collective-permute-start(bf16[2,128,512]{2,1,0:T(8,128)(2,1)S(1)} %get-tuple-element.58), channel_id=1, source_target_pairs={{0,6},{1,7},{2,4},{3,5},{4,2},{5,3},{6,0},{7,1},{64,70},{65,71},{6... | collective-permute-start | bytes 786440 | tf_op jit(solution)/shard_map/ppermute | solution.py:28
  73.9 8.6 %collective-permute-start.16 = (bf16[2,128,768]{2,1,0:T(8,128)(2,1)S(1)}, bf16[2,128,768]{2,1,0:T(8,128)(2,1)S(1)}, u32[]{:S(2)}, u32[]{:S(2)}) collective-permute-start(bf16[2,128,768]{2,1,0:T(8,128)(2,1)S(1)} %get-tuple-element.59.refs_0_), channel_id=1, source_target_pairs={{0,64},{1,65},{2,66},{3,67},{4,68},{5,69},{6,70},{7,71},{64,0},{65... | collective-permute-start | bytes 1179656 | tf_op jit(solution)/shard_map/ppermute | solution.py:28
  75.1 8.1 %collective-permute-start.17 = (bf16[2,128,768]{2,1,0:T(8,128)(2,1)S(1)}, bf16[2,128,768]{2,1,0:T(8,128)(2,1)S(1)}, u32[]{:S(2)}, u32[]{:S(2)}) collective-permute-start(bf16[2,128,768]{2,1,0:T(8,128)(2,1)S(1)} %get-tuple-element.60.refs_2_), channel_id=1, source_target_pairs={{0,6},{1,7},{2,4},{3,5},{4,2},{5,3},{6,0},{7,1},{64,70},{65,71},{6... | collective-permute-start | bytes 1179656 | tf_op jit(solution)/shard_map/ppermute | solution.py:28
  76.2 5.2 %collective-permute-start.18 = (bf16[2,128,512]{2,1,0:T(8,128)(2,1)S(1)}, bf16[2,128,512]{2,1,0:T(8,128)(2,1)S(1)}, u32[]{:S(2)}, u32[]{:S(2)}) collective-permute-start(bf16[2,128,512]{2,1,0:T(8,128)(2,1)S(1)} %get-tuple-element.61.refs_4_), channel_id=1, source_target_pairs={{0,2},{1,3},{2,0},{3,1},{4,6},{5,7},{6,4},{7,5},{64,66},{65,67},{6... | collective-permute-start | bytes 786440 | tf_op jit(solution)/shard_map/ppermute | solution.py:28
  83.4 24.4 %copy-start.1 = (bf16[2,2,128,768]{3,2,1,0:T(8,128)(2,1)}, bf16[2,2,128,768]{3,2,1,0:T(8,128)(2,1)S(1)}, u32[]{:S(2)}) copy-start(bf16[2,2,128,768]{3,2,1,0:T(8,128)(2,1)S(1)} %get-tuple-element.62.refs_0_) | copy-start | bytes 2359300
  83.4 24.4 %copy-start.2 = (bf16[2,2,128,768]{3,2,1,0:T(8,128)(2,1)}, bf16[2,2,128,768]{3,2,1,0:T(8,128)(2,1)S(1)}, u32[]{:S(2)}) copy-start(bf16[2,2,128,768]{3,2,1,0:T(8,128)(2,1)S(1)} %get-tuple-element.63.refs_2_.refs_1_) | copy-start | bytes 2359300
  83.4 24.4 %copy-start.11 = (bf16[2,2,128,512]{3,2,1,0:T(8,128)(2,1)}, bf16[2,2,128,512]{3,2,1,0:T(8,128)(2,1)S(1)}, u32[]{:S(2)}) copy-start(bf16[2,2,128,512]{3,2,1,0:T(8,128)(2,1)S(1)} %get-tuple-element.64.refs_4_.refs_2_) | copy-start | bytes 1572868
  83.5 14.3 %collective-permute-start.19 = (bf16[2,2,128,768]{3,2,1,0:T(8,128)(2,1)S(1)}, bf16[2,2,128,768]{3,2,1,0:T(8,128)(2,1)S(1)}, u32[]{:S(2)}, u32[]{:S(2)}) collective-permute-start(bf16[2,2,128,768]{3,2,1,0:T(8,128)(2,1)S(1)} %get-tuple-element.62.refs_0_), channel_id=1, source_target_pairs={{0,2},{1,3},{2,0},{3,1},{4,6},{5,7},{6,4},{7,5},{64,66},{65,67},{6... | collective-permute-start | bytes 2359304 | tf_op jit(solution)/shard_map/ppermute | solution.py:28
  83.7 19.9 %collective-permute-start.20 = (bf16[2,2,128,768]{3,2,1,0:T(8,128)(2,1)S(1)}, bf16[2,2,128,768]{3,2,1,0:T(8,128)(2,1)S(1)}, u32[]{:S(2)}, u32[]{:S(2)}) collective-permute-start(bf16[2,2,128,768]{3,2,1,0:T(8,128)(2,1)S(1)} %get-tuple-element.63.refs_2_.refs_1_), channel_id=1, source_target_pairs={{0,6},{1,7},{2,4},{3,5},{4,2},{5,3},{6,0},{7,1},{64,70},{65,71},{6... | collective-permute-start | bytes 2359304 | tf_op jit(solution)/shard_map/ppermute | solution.py:28
  84.8 7.0 %collective-permute-start.26 = (bf16[2,2,128,512]{3,2,1,0:T(8,128)(2,1)S(1)}, bf16[2,2,128,512]{3,2,1,0:T(8,128)(2,1)S(1)}, u32[]{:S(2)}, u32[]{:S(2)}) collective-permute-start(bf16[2,2,128,512]{3,2,1,0:T(8,128)(2,1)S(1)} %get-tuple-element.64.refs_4_.refs_2_), channel_id=1, source_target_pairs={{0,1},{1,0},{2,3},{3,2},{4,5},{5,4},{6,7},{7,6},{64,65},{65,64},{6... | collective-permute-start | bytes 1572872 | tf_op jit(solution)/shard_map/ppermute | solution.py:28
  90.1 15.1 %collective-permute-start.21 = (bf16[2,2,128,512]{3,2,1,0:T(8,128)(2,1)S(1)}, bf16[2,2,128,512]{3,2,1,0:T(8,128)(2,1)S(1)}, u32[]{:S(2)}, u32[]{:S(2)}) collective-permute-start(bf16[2,2,128,512]{3,2,1,0:T(8,128)(2,1)S(1)} %get-tuple-element.64.refs_4_.refs_2_), channel_id=1, source_target_pairs={{0,64},{1,65},{2,66},{3,67},{4,68},{5,69},{6,70},{7,71},{64,0},{65... | collective-permute-start | bytes 1572872 | tf_op jit(solution)/shard_map/ppermute | solution.py:28
  91.5 14.5 %collective-permute-start.22 = (bf16[2,2,128,768]{3,2,1,0:T(8,128)(2,1)S(1)}, bf16[2,2,128,768]{3,2,1,0:T(8,128)(2,1)S(1)}, u32[]{:S(2)}, u32[]{:S(2)}) collective-permute-start(bf16[2,2,128,768]{3,2,1,0:T(8,128)(2,1)S(1)} %get-tuple-element.62.refs_0_), channel_id=1, source_target_pairs={{0,1},{1,0},{2,3},{3,2},{4,5},{5,4},{6,7},{7,6},{64,65},{65,64},{6... | collective-permute-start | bytes 2359304 | tf_op jit(solution)/shard_map/ppermute | solution.py:28
  91.8 16.1 %copy-start.12 = (bf16[2,2,128,512]{3,2,1,0:T(8,128)(2,1)}, bf16[2,2,128,512]{3,2,1,0:T(8,128)(2,1)S(1)}, u32[]{:S(2)}) copy-start(bf16[2,2,128,512]{3,2,1,0:T(8,128)(2,1)S(1)} %collective-permute-done.26.refs_10_.refs_5_) | copy-start | bytes 1572868
  91.8 14.2 %collective-permute-start.24 = (bf16[2,2,128,768]{3,2,1,0:T(8,128)(2,1)S(1)}, bf16[2,2,128,768]{3,2,1,0:T(8,128)(2,1)S(1)}, u32[]{:S(2)}, u32[]{:S(2)}) collective-permute-start(bf16[2,2,128,768]{3,2,1,0:T(8,128)(2,1)S(1)} %get-tuple-element.63.refs_2_.refs_1_), channel_id=1, source_target_pairs={{0,1},{1,0},{2,3},{3,2},{4,5},{5,4},{6,7},{7,6},{64,65},{65,64},{6... | collective-permute-start | bytes 2359304 | tf_op jit(solution)/shard_map/ppermute | solution.py:28
  97.7 10.2 %copy-start.3 = (bf16[2,2,128,768]{3,2,1,0:T(8,128)(2,1)}, bf16[2,2,128,768]{3,2,1,0:T(8,128)(2,1)S(1)}, u32[]{:S(2)}) copy-start(bf16[2,2,128,768]{3,2,1,0:T(8,128)(2,1)S(1)} %collective-permute-done.19.refs_1_.refs_0_) | copy-start | bytes 2359300
  97.7 10.2 %collective-permute-start.23 = (bf16[2,2,128,768]{3,2,1,0:T(8,128)(2,1)S(1)}, bf16[2,2,128,768]{3,2,1,0:T(8,128)(2,1)S(1)}, u32[]{:S(2)}, u32[]{:S(2)}) collective-permute-start(bf16[2,2,128,768]{3,2,1,0:T(8,128)(2,1)S(1)} %collective-permute-done.19.refs_1_.refs_0_), channel_id=1, source_target_pairs={{0,1},{1,0},{2,3},{3,2},{4,5},{5,4},{6,7},{7,6},{64,65},{65,64},{6... | collective-permute-start | bytes 2359304 | tf_op jit(solution)/shard_map/ppermute | solution.py:28
  103.7 4.3 %copy-start.4 = (bf16[2,2,128,768]{3,2,1,0:T(8,128)(2,1)}, bf16[2,2,128,768]{3,2,1,0:T(8,128)(2,1)S(1)}, u32[]{:S(2)}) copy-start(bf16[2,2,128,768]{3,2,1,0:T(8,128)(2,1)S(1)} %collective-permute-done.20.refs_3_.refs_1_) | copy-start | bytes 2359300
  103.7 4.3 %collective-permute-start.25 = (bf16[2,2,128,768]{3,2,1,0:T(8,128)(2,1)S(1)}, bf16[2,2,128,768]{3,2,1,0:T(8,128)(2,1)S(1)}, u32[]{:S(2)}, u32[]{:S(2)}) collective-permute-start(bf16[2,2,128,768]{3,2,1,0:T(8,128)(2,1)S(1)} %collective-permute-done.20.refs_3_.refs_1_), channel_id=1, source_target_pairs={{0,1},{1,0},{2,3},{3,2},{4,5},{5,4},{6,7},{7,6},{64,65},{65,64},{6... | collective-permute-start | bytes 2359304 | tf_op jit(solution)/shard_map/ppermute | solution.py:28
  105.2 2.8 %copy-start.13 = (bf16[2,2,128,512]{3,2,1,0:T(8,128)(2,1)}, bf16[2,2,128,512]{3,2,1,0:T(8,128)(2,1)S(1)}, u32[]{:S(2)}) copy-start(bf16[2,2,128,512]{3,2,1,0:T(8,128)(2,1)S(1)} %collective-permute-done.21.refs_5_.refs_2_) | copy-start | bytes 1572868
  105.2 2.8 %collective-permute-start.27 = (bf16[2,2,128,512]{3,2,1,0:T(8,128)(2,1)S(1)}, bf16[2,2,128,512]{3,2,1,0:T(8,128)(2,1)S(1)}, u32[]{:S(2)}, u32[]{:S(2)}) collective-permute-start(bf16[2,2,128,512]{3,2,1,0:T(8,128)(2,1)S(1)} %collective-permute-done.21.refs_5_.refs_2_), channel_id=1, source_target_pairs={{0,1},{1,0},{2,3},{3,2},{4,5},{5,4},{6,7},{7,6},{64,65},{65,64},{6... | collective-permute-start | bytes 1572872 | tf_op jit(solution)/shard_map/ppermute | solution.py:28
  105.9 1.9 %copy-start.5 = (bf16[2,2,128,768]{3,2,1,0:T(8,128)(2,1)}, bf16[2,2,128,768]{3,2,1,0:T(8,128)(2,1)S(1)}, u32[]{:S(2)}) copy-start(bf16[2,2,128,768]{3,2,1,0:T(8,128)(2,1)S(1)} %collective-permute-done.22.refs_6_.refs_3_) | copy-start | bytes 2359300
  106.0 1.9 %copy-start.6 = (bf16[2,2,128,768]{3,2,1,0:T(8,128)(2,1)}, bf16[2,2,128,768]{3,2,1,0:T(8,128)(2,1)S(1)}, u32[]{:S(2)}) copy-start(bf16[2,2,128,768]{3,2,1,0:T(8,128)(2,1)S(1)} %collective-permute-done.24.refs_8_.refs_4_) | copy-start | bytes 2359300
  107.9 3.0 %copy-start.14 = (bf16[2,2,128,512]{3,2,1,0:T(8,128)(2,1)}, bf16[2,2,128,512]{3,2,1,0:T(8,128)(2,1)S(1)}, u32[]{:S(2)}) copy-start(bf16[2,2,128,512]{3,2,1,0:T(8,128)(2,1)S(1)} %collective-permute-done.27.refs_11_.refs_5_) | copy-start | bytes 1572868
  107.9 9.2 %copy-start.10 = (bf16[512,512]{1,0:T(8,128)(2,1)S(1)}, bf16[512,512]{1,0:T(8,128)(2,1)}, u32[]{:S(2)}) copy-start(bf16[512,512]{1,0:T(8,128)(2,1)} %refs_13_.1) | copy-start | bytes 1572868
  107.9 3.0 %copy-start.7 = (bf16[2,2,128,768]{3,2,1,0:T(8,128)(2,1)}, bf16[2,2,128,768]{3,2,1,0:T(8,128)(2,1)S(1)}, u32[]{:S(2)}) copy-start(bf16[2,2,128,768]{3,2,1,0:T(8,128)(2,1)S(1)} %collective-permute-done.23.refs_7_.refs_3_) | copy-start | bytes 2359300
  108.0 3.0 %copy-start.8 = (bf16[2,2,128,768]{3,2,1,0:T(8,128)(2,1)}, bf16[2,2,128,768]{3,2,1,0:T(8,128)(2,1)S(1)}, u32[]{:S(2)}) copy-start(bf16[2,2,128,768]{3,2,1,0:T(8,128)(2,1)S(1)} %collective-permute-done.25.refs_9_.refs_4_) | copy-start | bytes 2359300
  111.0 19.7 %all-to-all-start.1 = ((bf16[128,16,128]{2,1,0:T(8,128)(2,1)}), bf16[128,16,128]{2,1,0:T(8,128)(2,1)S(1)}, u32[]{:S(2)}, u32[]{:S(2)}) async-start(bf16[128,16,128]{2,1,0:T(8,128)(2,1)} %bitcast.8), calls=%async_computation.1 | async-start | bytes 1048576 | tf_op jit(solution)/shard_map/all_to_all | solution.py:473
  117.1 13.5 %copy-start.15 = (bf16[4,8192]{1,0:T(4,128)(2,1)S(1)}, bf16[4,8192]{1,0:T(4,128)(2,1)}, u32[]{:S(2)}) copy-start(bf16[4,8192]{1,0:T(4,128)(2,1)} %act.3) | copy-start | bytes 196612
  117.1 13.5 %copy-start.16 = (f32[8192]{0:T(1024)S(1)}, f32[8192]{0:T(1024)}, u32[]{:S(2)}) copy-start(f32[8192]{0:T(1024)} %param.7) | copy-start | bytes 98308
  (1 other events, 0.7 us)

commit v5 on v4

--- a/solution.py
+++ b/solution.py
@@ -227,24 +227,6 @@
         name=name,
     )(*[arrays[k] for k in picked])
     return list(outs)
-
-
-def gate_kernel(x, after, out):
-    pass
-
-
-def gate(x, after):
-    anywhere = pl.BlockSpec(memory_space=pl.ANY)
-    return pl.pallas_call(
-        gate_kernel,
-        in_specs=[anywhere] * 2,
-        out_specs=anywhere,
-        out_shape=jax.ShapeDtypeStruct(x.shape, x.dtype),
-        input_output_aliases={0: 0},
-        cost_estimate=pl.CostEstimate(flops=MIB, bytes_accessed=MIB, transcendentals=0),
-        compiler_params=pltpu.CompilerParams(vmem_limit_bytes=MIB),
-        name="gate",
-    )(x, after)
 
 
 def far_first(step):
@@ -463,7 +445,7 @@
     messages = norm_messages(act, gain, shift)
     mixed = lax.all_to_all(messages.reshape(128, 16, 128), EVERY, 0, 0, tiled=True)
     up = chip_sum(at, cotangent, cot_other, w_out, out_other, True)
-    mixed = gate(mixed, up[0][0])
+    mixed, _ = lax.optimization_barrier((mixed, up[0][0]))
     mixed_other = swap(mixed, "core")
     pre = chip_sum(at, mixed, mixed_other, w_in, in_other, False)
     pieces = gather(exchange_sums(up, pre))

time: 132 us -> 132 us (level)
  no operation moved by 1% of the time
where the time goes in v5:
time: 132 us
  starting transfers between devices  49 us (37%)
  waiting for transfers between devices  48.6 us (37%)
  Pallas kernels  30.5 us (23%)
  local copies, waits for them, and re-layouts  2.61 us (2%)
    ppermute x28, waiting for transfers between devices, swap(): return lax.ppermute(x, OWNERS, pairs)  40.4 us
    ppermute x28, starting transfers between devices, swap(): return lax.ppermute(x, OWNERS, pairs)  32.7 us
    pallas_call x1, Pallas kernels, grads_of(): pl.pallas_call(grads_kernel, in_specs=[SCALARS] + [anywhere] * 12 + [vmem...  10.9 us
    all_to_all x1, starting transfers between devices, local(): lax.all_to_all(messages.reshape(128, 16, 128), EVERY, 0, 0, tiled=True)  10.2 us
    pallas_call x2, Pallas kernels, chip_sum(): pl.pallas_call(up_kernel if up else pre_kernel, in_specs=[SCALARS] + [VME...  9.87 us
    all_to_all x1, starting transfers between devices, local(): lax.all_to_all(share.reshape(128, 16, 128), EVERY, 0, 0, tiled=True)  6.14 us
    all_to_all x1, waiting for transfers between devices, local(): lax.all_to_all(messages.reshape(128, 16, 128), EVERY, 0, 0, tiled=True)  5.7 us
    pallas_call x1, Pallas kernels, back_messages(): pl.pallas_call(came_kernel, in_specs=[SCALARS] + [vmem] * 8, out_shape=pl...  2.94 us
  transfers between devices with their start and end apart: 30, of which 17 were waited for; matrix products, arithmetic and copies ran while one was open for 0% of the time, Pallas kernels for 19%

profile of v5, /device:TPU:1, one launch (start us, length us, event | category | flops | bytes accessed | tf_op | source)
XLA Modules:
  0.0 131.8 jit_solution(8111548317085550118)
XLA Ops:
  0.6 1.5 %collective-permute-start.1 = (bf16[4096,512]{1,0:T(8,128)(2,1)}, bf16[4096,512]{1,0:T(8,128)(2,1)}, u32[]{:S(2)}, u32[]{:S(2)}) collective-permute-start(bf16[4096,512]{1,0:T(8,128)(2,1)} %w.2), channel_id=1, source_target_pairs={{0,1},{1,0},{2,3},{3,2},{4,5},{5,4},{6,7},{7,6},{64,65},{65,64},{6... | collective-permute-start | bytes 12582920 | tf_op jit(solution)/shard_map/ppermute | solution.py:28
  2.6 2.1 %norm_messages.1 = bf16[2,8,8,16,128]{4,3,2,1,0:T(8,128)(2,1)} custom-call(bf16[4,8192]{1,0:T(4,128)(2,1)} %act.3, f32[1,8192]{1,0:T(1,128)} %bitcast.6, f32[1,8192]{1,0:T(1,128)} %bitcast.10), custom_call_target="tpu_custom_call" | custom-call | tf_op jit(solution)/shard_map/norm_messages/pallas_call | solution.py:56
  4.7 10.2 %all-to-all-start = ((bf16[128,16,128]{2,1,0:T(8,128)(2,1)}), bf16[128,16,128]{2,1,0:T(8,128)(2,1)S(1)}, u32[]{:S(2)}, u32[]{:S(2)}) async-start(bf16[128,16,128]{2,1,0:T(8,128)(2,1)} %bitcast.9), calls=%async_computation | async-start | bytes 1048576 | tf_op jit(solution)/shard_map/all_to_all | solution.py:446
  15.0 1.0 copy-done.9
  16.1 5.2 %up_sum.1 = (f32[256,768]{1,0:T(8,128)S(1)}, bf16[256,768]{1,0:T(8,128)(2,1)S(1)}, f32[256,768]{1,0:T(8,128)S(1)}, bf16[256,768]{1,0:T(8,128)(2,1)S(1)}, f32[256...) custom-call(s32[2]{0:T(128)S(1)} %pad_add_fusion.at, bf16[512,512]{1,0:T(8,128)(2,1)S(1)} %copy-done.9, ...), custom_call_target="tpu_custom_call" | custom-call | flops 1048576 | bytes 1048576 | tf_op jit(solution)/shard_map/up_sum/pallas_call | solution.py:161
  21.2 0.8 copy-done.17
  22.0 0.7 copy-done.18
  22.7 5.7 %all-to-all-done.x.refs_12_ = bf16[128,16,128]{2,1,0:T(8,128)(2,1)S(1)} async-done(((bf16[128,16,128]{2,1,0:T(8,128)(2,1)}), bf16[128,16,128]{2,1,0:T(8,128)(2,1)S(1)}, u32[]{:S(2)}, u32[]{:S(2)}) %all-to-all-start) | async-done | bytes 524320 | tf_op jit(solution)/shard_map/all_to_all | solution.py:446
  28.4 1.1 collective-permute-start.3
  30.2 1.2 collective-permute-start.8
  31.4 4.7 %pre_sum.1 = (f32[256,768]{1,0:T(8,128)S(1)}, bf16[256,768]{1,0:T(8,128)(2,1)S(1)}, f32[256,768]{1,0:T(8,128)S(1)}, bf16[256,768]{1,0:T(8,128)(2,1)S(1)}, f32[25...) custom-call(s32[2]{0:T(128)S(1)} %pad_add_fusion.at, bf16[128,16,128]{2,1,0:T(8,128)(2,1)S(1)} %all-to-all-done.x.refs_12_, ...), custom_call_target="tpu_custom_call" | custom-call | flops 1048576 | bytes 1048576 | tf_op jit(solution)/shard_map/pre_sum/pallas_call | solution.py:161
  36.2 0.4 collective-permute-start.7
  36.6 1.6 %collective-permute-start.9 = (bf16[256,768]{1,0:T(8,128)(2,1)S(1)}, bf16[256,768]{1,0:T(8,128)(2,1)S(1)}, u32[]{:S(2)}, u32[]{:S(2)}) collective-permute-start(bf16[256,768]{1,0:T(8,128)(2,1)S(1)} %get-tuple-element.48), channel_id=1, source_target_pairs={{0,6},{1,7},{2,4},{3,5},{4,2},{5,3},{6,0},{7,1},{64,70},{65,71},{6... | collective-permute-start | bytes 1179656 | tf_op jit(solution)/shard_map/ppermute | solution.py:28
  38.2 0.7 collective-permute-done.2.refs_1_
  38.9 1.9 %collective-permute-start.5 = (bf16[256,512]{1,0:T(8,128)(2,1)S(1)}, bf16[256,512]{1,0:T(8,128)(2,1)S(1)}, u32[]{:S(2)}, u32[]{:S(2)}) collective-permute-start(bf16[256,512]{1,0:T(8,128)(2,1)S(1)} %get-tuple-element.41), channel_id=1, source_target_pairs={{0,64},{1,65},{2,66},{3,67},{4,68},{5,69},{6,70},{7,71},{64,0},{65... | collective-permute-start | bytes 786440 | tf_op jit(solution)/shard_map/ppermute | solution.py:28
  40.8 0.8 collective-permute-done.8.refs_9_
  41.6 5.8 %collective-permute-done.5.refs_3_ = bf16[256,512]{1,0:T(8,128)(2,1)S(1)} collective-permute-done((bf16[256,512]{1,0:T(8,128)(2,1)S(1)}, bf16[256,512]{1,0:T(8,128)(2,1)S(1)}, u32[]{:S(2)}, u32[]{:S(2)}) %collective-permute-start.5) | collective-permute-done | bytes 262176 | tf_op jit(solution)/shard_map/ppermute | solution.py:28
  47.4 1.3 collective-permute-done.7.refs_7_
  48.7 1.4 %collective-permute-done.9.refs_11_ = bf16[256,768]{1,0:T(8,128)(2,1)S(1)} collective-permute-done((bf16[256,768]{1,0:T(8,128)(2,1)S(1)}, bf16[256,768]{1,0:T(8,128)(2,1)S(1)}, u32[]{:S(2)}, u32[]{:S(2)}) %collective-permute-start.9) | collective-permute-done | bytes 393248 | tf_op jit(solution)/shard_map/ppermute | solution.py:28
  50.1 0.4 first_sums.1
  50.5 2.6 %collective-permute-start.10 = (bf16[2,128,768]{2,1,0:T(8,128)(2,1)S(1)}, bf16[2,128,768]{2,1,0:T(8,128)(2,1)S(1)}, u32[]{:S(2)}, u32[]{:S(2)}) collective-permute-start(bf16[2,128,768]{2,1,0:T(8,128)(2,1)S(1)} %get-tuple-element.50), channel_id=1, source_target_pairs={{0,64},{1,65},{2,66},{3,67},{4,68},{5,69},{6,70},{7,71},{64,0},{65... | collective-permute-start | bytes 1179656 | tf_op jit(solution)/shard_map/ppermute | solution.py:28
  53.1 0.7 collective-permute-start.11
  53.7 6.0 %collective-permute-done.12.refs_5_ = bf16[2,128,512]{2,1,0:T(8,128)(2,1)S(1)} collective-permute-done((bf16[2,128,512]{2,1,0:T(8,128)(2,1)S(1)}, bf16[2,128,512]{2,1,0:T(8,128)(2,1)S(1)}, u32[]{:S(2)}, u32[]{:S(2)}) %collective-permute-start.12) | collective-permute-done | bytes 262176 | tf_op jit(solution)/shard_map/ppermute | solution.py:28
  59.7 1.5 %collective-permute-done.10.refs_1_ = bf16[2,128,768]{2,1,0:T(8,128)(2,1)S(1)} collective-permute-done((bf16[2,128,768]{2,1,0:T(8,128)(2,1)S(1)}, bf16[2,128,768]{2,1,0:T(8,128)(2,1)S(1)}, u32[]{:S(2)}, u32[]{:S(2)}) %collective-permute-start.10) | collective-permute-done | bytes 393248 | tf_op jit(solution)/shard_map/ppermute | solution.py:28
  61.2 2.0 %collective-permute-done.11.refs_3_ = bf16[2,128,768]{2,1,0:T(8,128)(2,1)S(1)} collective-permute-done((bf16[2,128,768]{2,1,0:T(8,128)(2,1)S(1)}, bf16[2,128,768]{2,1,0:T(8,128)(2,1)S(1)}, u32[]{:S(2)}, u32[]{:S(2)}) %collective-permute-start.11) | collective-permute-done | bytes 393248 | tf_op jit(solution)/shard_map/ppermute | solution.py:28
  63.5 0.7 collective-permute-start.13
  64.3 0.8 collective-permute-start.15
  65.1 5.9 %collective-permute-done.15.refs_5_ = bf16[2,128,512]{2,1,0:T(8,128)(2,1)S(1)} collective-permute-done((bf16[2,128,512]{2,1,0:T(8,128)(2,1)S(1)}, bf16[2,128,512]{2,1,0:T(8,128)(2,1)S(1)}, u32[]{:S(2)}, u32[]{:S(2)}) %collective-permute-start.15) | collective-permute-done | bytes 262176 | tf_op jit(solution)/shard_map/ppermute | solution.py:28
  71.0 2.1 %collective-permute-done.13.refs_1_ = bf16[2,128,768]{2,1,0:T(8,128)(2,1)S(1)} collective-permute-done((bf16[2,128,768]{2,1,0:T(8,128)(2,1)S(1)}, bf16[2,128,768]{2,1,0:T(8,128)(2,1)S(1)}, u32[]{:S(2)}, u32[]{:S(2)}) %collective-permute-start.13) | collective-permute-done | bytes 393248 | tf_op jit(solution)/shard_map/ppermute | solution.py:28
  73.1 0.8 third_sums.1
  73.9 1.3 collective-permute-start.16
  75.1 1.0 collective-permute-start.17
  76.2 5.2 %collective-permute-done.18.refs_5_ = bf16[2,128,512]{2,1,0:T(8,128)(2,1)S(1)} collective-permute-done((bf16[2,128,512]{2,1,0:T(8,128)(2,1)S(1)}, bf16[2,128,512]{2,1,0:T(8,128)(2,1)S(1)}, u32[]{:S(2)}, u32[]{:S(2)}) %collective-permute-start.18) | collective-permute-done | bytes 262176 | tf_op jit(solution)/shard_map/ppermute | solution.py:28
  81.4 1.2 collective-permute-done.16.refs_1_
  82.5 0.7 collective-permute-done.17.refs_3_
  83.7 1.1 collective-permute-start.20
  84.8 5.3 %collective-permute-start.26 = (bf16[2,2,128,512]{3,2,1,0:T(8,128)(2,1)S(1)}, bf16[2,2,128,512]{3,2,1,0:T(8,128)(2,1)S(1)}, u32[]{:S(2)}, u32[]{:S(2)}) collective-permute-start(bf16[2,2,128,512]{3,2,1,0:T(8,128)(2,1)S(1)} %get-tuple-element.66.refs_4_.refs_2_), channel_id=1, source_target_pairs={{0,1},{1,0},{2,3},{3,2},{4,5},{5,4},{6,7},{7,6},{64,65},{65,64},{6... | collective-permute-start | bytes 1572872 | tf_op jit(solution)/shard_map/ppermute | solution.py:28
  90.1 1.4 %collective-permute-start.21 = (bf16[2,2,128,512]{3,2,1,0:T(8,128)(2,1)S(1)}, bf16[2,2,128,512]{3,2,1,0:T(8,128)(2,1)S(1)}, u32[]{:S(2)}, u32[]{:S(2)}) collective-permute-start(bf16[2,2,128,512]{3,2,1,0:T(8,128)(2,1)S(1)} %get-tuple-element.66.refs_4_.refs_2_), channel_id=1, source_target_pairs={{0,64},{1,65},{2,66},{3,67},{4,68},{5,69},{6,70},{7,71},{64,0},{65... | collective-permute-start | bytes 1572872 | tf_op jit(solution)/shard_map/ppermute | solution.py:28
  92.0 5.7 %collective-permute-done.19.refs_1_.refs_0_ = bf16[2,2,128,768]{3,2,1,0:T(8,128)(2,1)S(1)} collective-permute-done((bf16[2,2,128,768]{3,2,1,0:T(8,128)(2,1)S(1)}, bf16[2,2,128,768]{3,2,1,0:T(8,128)(2,1)S(1)}, u32[]{:S(2)}, u32[]{:S(2)}) %collective-permute-start.19) | collective-permute-done | bytes 786464 | tf_op jit(solution)/shard_map/ppermute | solution.py:28
  97.7 5.9 %collective-permute-start.23 = (bf16[2,2,128,768]{3,2,1,0:T(8,128)(2,1)S(1)}, bf16[2,2,128,768]{3,2,1,0:T(8,128)(2,1)S(1)}, u32[]{:S(2)}, u32[]{:S(2)}) collective-permute-start(bf16[2,2,128,768]{3,2,1,0:T(8,128)(2,1)S(1)} %collective-permute-done.19.refs_1_.refs_0_), channel_id=1, source_target_pairs={{0,1},{1,0},{2,3},{3,2},{4,5},{5,4},{6,7},{7,6},{64,65},{65,64},{6... | collective-permute-start | bytes 2359304 | tf_op jit(solution)/shard_map/ppermute | solution.py:28
  103.7 1.4 %collective-permute-start.25 = (bf16[2,2,128,768]{3,2,1,0:T(8,128)(2,1)S(1)}, bf16[2,2,128,768]{3,2,1,0:T(8,128)(2,1)S(1)}, u32[]{:S(2)}, u32[]{:S(2)}) collective-permute-start(bf16[2,2,128,768]{3,2,1,0:T(8,128)(2,1)S(1)} %collective-permute-done.20.refs_3_.refs_1_), channel_id=1, source_target_pairs={{0,1},{1,0},{2,3},{3,2},{4,5},{5,4},{6,7},{7,6},{64,65},{65,64},{6... | collective-permute-start | bytes 2359304 | tf_op jit(solution)/shard_map/ppermute | solution.py:28
  105.2 0.8 collective-permute-start.27
  106.0 1.9 %back_held.1.refs_7_ = f32[512,512]{1,0:T(8,128)S(1)} custom-call(s32[2]{0:T(128)S(1)} %pad_add_fusion.at, bf16[2,2,128,768]{3,2,1,0:T(8,128)(2,1)S(1)} %get-tuple-element.64.refs_0_, bf16[2,2,128,768]{3,2,1,0:T(8,128)(2,1)S(1)} %get-tuple-element.65.refs_2_.refs_1_, bf16[2,2,128,512]{3,2,1,0:T(8,128)(2,1)S(1)} %get-tuple-element.66.refs_4_.refs_2_, ...), custom_call_target="tpu_custom_call" | custom-call | flops 1073741824 | bytes 4194304 | tf_op jit(solution)/shard_map/back_held/pallas_call | solution.py:312
  108.0 2.9 %back_messages.1 = bf16[64,2,16,128]{3,2,1,0:T(8,128)(2,1)} custom-call(s32[2]{0:T(128)S(1)} %pad_add_fusion.at, bf16[2,2,128,768]{3,2,1,0:T(8,128)(2,1)S(1)} %collective-permute-done.19.refs_1_.refs_0_, bf16[2,2,128,768]{3,2,1,0:T(8,128)(2,1)S(1)} %collective-permute-done.20.refs_3_.refs_1_, ...), custom_call_target="tpu_custom_call" | custom-call | flops 1073741824 | bytes 4194304 | tf_op jit(solution)/shard_map/back_messages/pallas_call | solution.py:319
  111.0 6.1 %all-to-all-start.1 = ((bf16[128,16,128]{2,1,0:T(8,128)(2,1)}), bf16[128,16,128]{2,1,0:T(8,128)(2,1)S(1)}, u32[]{:S(2)}, u32[]{:S(2)}) async-start(bf16[128,16,128]{2,1,0:T(8,128)(2,1)} %bitcast.8), calls=%async_computation.1 | async-start | bytes 1048576 | tf_op jit(solution)/shard_map/all_to_all | solution.py:455
  117.1 10.9 %grads.1 = (f32[512,4096]{1,0:T(8,128)}, f32[4096,512]{1,0:T(8,128)}) custom-call(s32[2]{0:T(128)S(1)} %pad_add_fusion.at, bf16[2,2,128,768]{3,2,1,0:T(8,128)(2,1)} %copy-done.1, bf16[2,2,128,768]{3,2,1,0:T(8,128)(2,1)} %copy-done.3, bf16[2,2,128,768]{3,2,1,0:T(8,128)(2,1)} %copy-done.2, bf16[2,2,128,768]{3,2,1,0:T(8,128)(2,1)} %copy-done.4, ...), custom_call_target="tpu_custom_call" | custom-call | flops 4294967296 | bytes 25165824 | tf_op jit(solution)/shard_map/grads/pallas_call | solution.py:377
  128.1 2.5 %all-to-all-done.1.x = bf16[128,16,128]{2,1,0:T(8,128)(2,1)S(1)} async-done(((bf16[128,16,128]{2,1,0:T(8,128)(2,1)}), bf16[128,16,128]{2,1,0:T(8,128)(2,1)S(1)}, u32[]{:S(2)}, u32[]{:S(2)}) %all-to-all-start.1) | async-done | bytes 524320 | tf_op jit(solution)/shard_map/all_to_all | solution.py:455
  130.6 1.2 grad_act.1
  (62 shorter events, 2.8 us)
Async XLA Ops:
  0.6 14.4 %collective-permute-start.1 = (bf16[4096,512]{1,0:T(8,128)(2,1)}, bf16[4096,512]{1,0:T(8,128)(2,1)}, u32[]{:S(2)}, u32[]{:S(2)}) collective-permute-start(bf16[4096,512]{1,0:T(8,128)(2,1)} %w.2), channel_id=1, source_target_pairs={{0,1},{1,0},{2,3},{3,2},{4,5},{5,4},{6,7},{7,6},{64,65},{65,64},{6... | collective-permute-start | bytes 12582920 | tf_op jit(solution)/shard_map/ppermute | solution.py:28
  2.1 29.3 %collective-permute-start.4 = (bf16[512,4096]{1,0:T(8,128)(2,1)}, bf16[512,4096]{1,0:T(8,128)(2,1)}, u32[]{:S(2)}, u32[]{:S(2)}) collective-permute-start(bf16[512,4096]{1,0:T(8,128)(2,1)} %refs_6_.3), channel_id=1, source_target_pairs={{0,1},{1,0},{2,3},{3,2},{4,5},{5,4},{6,7},{7,6},{64,65},{65,64},{6... | collective-permute-start | bytes 12582920 | tf_op jit(solution)/shard_map/ppermute | solution.py:28
  2.2 12.8 %collective-permute-start = (bf16[512,512]{1,0:T(8,128)(2,1)}, bf16[512,512]{1,0:T(8,128)(2,1)S(1)}, u32[]{:S(2)}, u32[]{:S(2)}) collective-permute-start(bf16[512,512]{1,0:T(8,128)(2,1)} %refs_13_.1), channel_id=1, source_target_pairs={{0,1},{1,0},{2,3},{3,2},{4,5},{5,4},{6,7},{7,6},{64,65},{65,64},{6... | collective-permute-start | bytes 1572872 | tf_op jit(solution)/shard_map/ppermute | solution.py:28
  4.7 23.7 %all-to-all-start = ((bf16[128,16,128]{2,1,0:T(8,128)(2,1)}), bf16[128,16,128]{2,1,0:T(8,128)(2,1)S(1)}, u32[]{:S(2)}, u32[]{:S(2)}) async-start(bf16[128,16,128]{2,1,0:T(8,128)(2,1)} %bitcast.9), calls=%async_computation | async-start | bytes 1048576 | tf_op jit(solution)/shard_map/all_to_all | solution.py:446
  15.0 1.0 copy-start.9
  21.2 0.8 copy-start.17
  28.4 3.0 %collective-permute-start.3 = (bf16[128,16,128]{2,1,0:T(8,128)(2,1)S(1)}, bf16[128,16,128]{2,1,0:T(8,128)(2,1)S(1)}, u32[]{:S(2)}, u32[]{:S(2)}) collective-permute-start(bf16[128,16,128]{2,1,0:T(8,128)(2,1)S(1)} %all-to-all-done.x.refs_12_), channel_id=1, source_target_pairs={{0,1},{1,0},{2,3},{3,2},{4,5},{5,4},{6,7},{7,6},{64,65},{65,64},{6... | collective-permute-start | bytes 1572872 | tf_op jit(solution)/shard_map/ppermute | solution.py:28
  29.5 9.4 %collective-permute-start.2 = (bf16[256,512]{1,0:T(8,128)(2,1)S(1)}, bf16[256,512]{1,0:T(8,128)(2,1)S(1)}, u32[]{:S(2)}, u32[]{:S(2)}) collective-permute-start(bf16[256,512]{1,0:T(8,128)(2,1)S(1)} %get-tuple-element.37), channel_id=1, source_target_pairs={{0,64},{1,65},{2,66},{3,67},{4,68},{5,69},{6,70},{7,71},{64,0},{65... | collective-permute-start | bytes 786440 | tf_op jit(solution)/shard_map/ppermute | solution.py:28
  29.8 11.0 %collective-permute-start.6 = (bf16[256,768]{1,0:T(8,128)(2,1)}, bf16[256,768]{1,0:T(8,128)(2,1)S(1)}, u32[]{:S(2)}, u32[]{:S(2)}) collective-permute-start(bf16[256,768]{1,0:T(8,128)(2,1)} %copy-done.18), channel_id=1, source_target_pairs={{0,2},{1,3},{2,0},{3,1},{4,6},{5,7},{6,4},{7,5},{64,66},{65,67},{6... | collective-permute-start | bytes 1179656 | tf_op jit(solution)/shard_map/ppermute | solution.py:28
  30.2 11.4 %collective-permute-start.8 = (bf16[256,768]{1,0:T(8,128)(2,1)}, bf16[256,768]{1,0:T(8,128)(2,1)S(1)}, u32[]{:S(2)}, u32[]{:S(2)}) collective-permute-start(bf16[256,768]{1,0:T(8,128)(2,1)} %copy-done.17), channel_id=1, source_target_pairs={{0,6},{1,7},{2,4},{3,5},{4,2},{5,3},{6,0},{7,1},{64,70},{65,71},{6... | collective-permute-start | bytes 1179656 | tf_op jit(solution)/shard_map/ppermute | solution.py:28
  36.2 12.5 %collective-permute-start.7 = (bf16[256,768]{1,0:T(8,128)(2,1)S(1)}, bf16[256,768]{1,0:T(8,128)(2,1)S(1)}, u32[]{:S(2)}, u32[]{:S(2)}) collective-permute-start(bf16[256,768]{1,0:T(8,128)(2,1)S(1)} %get-tuple-element.44), channel_id=1, source_target_pairs={{0,2},{1,3},{2,0},{3,1},{4,6},{5,7},{6,4},{7,5},{64,66},{65,67},{6... | collective-permute-start | bytes 1179656 | tf_op jit(solution)/shard_map/ppermute | solution.py:28
  36.6 13.5 %collective-permute-start.9 = (bf16[256,768]{1,0:T(8,128)(2,1)S(1)}, bf16[256,768]{1,0:T(8,128)(2,1)S(1)}, u32[]{:S(2)}, u32[]{:S(2)}) collective-permute-start(bf16[256,768]{1,0:T(8,128)(2,1)S(1)} %get-tuple-element.48), channel_id=1, source_target_pairs={{0,6},{1,7},{2,4},{3,5},{4,2},{5,3},{6,0},{7,1},{64,70},{65,71},{6... | collective-permute-start | bytes 1179656 | tf_op jit(solution)/shard_map/ppermute | solution.py:28
  38.9 8.5 %collective-permute-start.5 = (bf16[256,512]{1,0:T(8,128)(2,1)S(1)}, bf16[256,512]{1,0:T(8,128)(2,1)S(1)}, u32[]{:S(2)}, u32[]{:S(2)}) collective-permute-start(bf16[256,512]{1,0:T(8,128)(2,1)S(1)} %get-tuple-element.41), channel_id=1, source_target_pairs={{0,64},{1,65},{2,66},{3,67},{4,68},{5,69},{6,70},{7,71},{64,0},{65... | collective-permute-start | bytes 786440 | tf_op jit(solution)/shard_map/ppermute | solution.py:28
  50.5 10.7 %collective-permute-start.10 = (bf16[2,128,768]{2,1,0:T(8,128)(2,1)S(1)}, bf16[2,128,768]{2,1,0:T(8,128)(2,1)S(1)}, u32[]{:S(2)}, u32[]{:S(2)}) collective-permute-start(bf16[2,128,768]{2,1,0:T(8,128)(2,1)S(1)} %get-tuple-element.50), channel_id=1, source_target_pairs={{0,64},{1,65},{2,66},{3,67},{4,68},{5,69},{6,70},{7,71},{64,0},{65... | collective-permute-start | bytes 1179656 | tf_op jit(solution)/shard_map/ppermute | solution.py:28
  53.1 10.1 %collective-permute-start.11 = (bf16[2,128,768]{2,1,0:T(8,128)(2,1)S(1)}, bf16[2,128,768]{2,1,0:T(8,128)(2,1)S(1)}, u32[]{:S(2)}, u32[]{:S(2)}) collective-permute-start(bf16[2,128,768]{2,1,0:T(8,128)(2,1)S(1)} %get-tuple-element.52), channel_id=1, source_target_pairs={{0,6},{1,7},{2,4},{3,5},{4,2},{5,3},{6,0},{7,1},{64,70},{65,71},{6... | collective-permute-start | bytes 1179656 | tf_op jit(solution)/shard_map/ppermute | solution.py:28
  53.7 6.0 %collective-permute-start.12 = (bf16[2,128,512]{2,1,0:T(8,128)(2,1)S(1)}, bf16[2,128,512]{2,1,0:T(8,128)(2,1)S(1)}, u32[]{:S(2)}, u32[]{:S(2)}) collective-permute-start(bf16[2,128,512]{2,1,0:T(8,128)(2,1)S(1)} %get-tuple-element.54), channel_id=1, source_target_pairs={{0,2},{1,3},{2,0},{3,1},{4,6},{5,7},{6,4},{7,5},{64,66},{65,67},{6... | collective-permute-start | bytes 786440 | tf_op jit(solution)/shard_map/ppermute | solution.py:28
  63.2 42.7 %copy-start = (bf16[512,4096]{1,0:T(8,128)(2,1)S(1)}, bf16[512,4096]{1,0:T(8,128)(2,1)}, u32[]{:S(2)}) copy-start(bf16[512,4096]{1,0:T(8,128)(2,1)} %refs_6_.3) | copy-start | bytes 12582916
  63.5 9.6 %collective-permute-start.13 = (bf16[2,128,768]{2,1,0:T(8,128)(2,1)S(1)}, bf16[2,128,768]{2,1,0:T(8,128)(2,1)S(1)}, u32[]{:S(2)}, u32[]{:S(2)}) collective-permute-start(bf16[2,128,768]{2,1,0:T(8,128)(2,1)S(1)} %get-tuple-element.56), channel_id=1, source_target_pairs={{0,64},{1,65},{2,66},{3,67},{4,68},{5,69},{6,70},{7,71},{64,0},{65... | collective-permute-start | bytes 1179656 | tf_op jit(solution)/shard_map/ppermute | solution.py:28
  64.1 8.9 %collective-permute-start.14 = (bf16[2,128,768]{2,1,0:T(8,128)(2,1)S(1)}, bf16[2,128,768]{2,1,0:T(8,128)(2,1)S(1)}, u32[]{:S(2)}, u32[]{:S(2)}) collective-permute-start(bf16[2,128,768]{2,1,0:T(8,128)(2,1)S(1)} %get-tuple-element.58), channel_id=1, source_target_pairs={{0,2},{1,3},{2,0},{3,1},{4,6},{5,7},{6,4},{7,5},{64,66},{65,67},{6... | collective-permute-start | bytes 1179656 | tf_op jit(solution)/shard_map/ppermute | solution.py:28
  64.3 6.7 %collective-permute-start.15 = (bf16[2,128,512]{2,1,0:T(8,128)(2,1)S(1)}, bf16[2,128,512]{2,1,0:T(8,128)(2,1)S(1)}, u32[]{:S(2)}, u32[]{:S(2)}) collective-permute-start(bf16[2,128,512]{2,1,0:T(8,128)(2,1)S(1)} %get-tuple-element.60), channel_id=1, source_target_pairs={{0,6},{1,7},{2,4},{3,5},{4,2},{5,3},{6,0},{7,1},{64,70},{65,71},{6... | collective-permute-start | bytes 786440 | tf_op jit(solution)/shard_map/ppermute | solution.py:28
  73.9 8.6 %collective-permute-start.16 = (bf16[2,128,768]{2,1,0:T(8,128)(2,1)S(1)}, bf16[2,128,768]{2,1,0:T(8,128)(2,1)S(1)}, u32[]{:S(2)}, u32[]{:S(2)}) collective-permute-start(bf16[2,128,768]{2,1,0:T(8,128)(2,1)S(1)} %get-tuple-element.61.refs_0_), channel_id=1, source_target_pairs={{0,64},{1,65},{2,66},{3,67},{4,68},{5,69},{6,70},{7,71},{64,0},{65... | collective-permute-start | bytes 1179656 | tf_op jit(solution)/shard_map/ppermute | solution.py:28
  75.1 8.1 %collective-permute-start.17 = (bf16[2,128,768]{2,1,0:T(8,128)(2,1)S(1)}, bf16[2,128,768]{2,1,0:T(8,128)(2,1)S(1)}, u32[]{:S(2)}, u32[]{:S(2)}) collective-permute-start(bf16[2,128,768]{2,1,0:T(8,128)(2,1)S(1)} %get-tuple-element.62.refs_2_), channel_id=1, source_target_pairs={{0,6},{1,7},{2,4},{3,5},{4,2},{5,3},{6,0},{7,1},{64,70},{65,71},{6... | collective-permute-start | bytes 1179656 | tf_op jit(solution)/shard_map/ppermute | solution.py:28
  76.1 5.2 %collective-permute-start.18 = (bf16[2,128,512]{2,1,0:T(8,128)(2,1)S(1)}, bf16[2,128,512]{2,1,0:T(8,128)(2,1)S(1)}, u32[]{:S(2)}, u32[]{:S(2)}) collective-permute-start(bf16[2,128,512]{2,1,0:T(8,128)(2,1)S(1)} %get-tuple-element.63.refs_4_), channel_id=1, source_target_pairs={{0,2},{1,3},{2,0},{3,1},{4,6},{5,7},{6,4},{7,5},{64,66},{65,67},{6... | collective-permute-start | bytes 786440 | tf_op jit(solution)/shard_map/ppermute | solution.py:28
  83.4 24.4 %copy-start.1 = (bf16[2,2,128,768]{3,2,1,0:T(8,128)(2,1)}, bf16[2,2,128,768]{3,2,1,0:T(8,128)(2,1)S(1)}, u32[]{:S(2)}) copy-start(bf16[2,2,128,768]{3,2,1,0:T(8,128)(2,1)S(1)} %get-tuple-element.64.refs_0_) | copy-start | bytes 2359300
  83.4 24.4 %copy-start.2 = (bf16[2,2,128,768]{3,2,1,0:T(8,128)(2,1)}, bf16[2,2,128,768]{3,2,1,0:T(8,128)(2,1)S(1)}, u32[]{:S(2)}) copy-start(bf16[2,2,128,768]{3,2,1,0:T(8,128)(2,1)S(1)} %get-tuple-element.65.refs_2_.refs_1_) | copy-start | bytes 2359300
  83.4 24.4 %copy-start.11 = (bf16[2,2,128,512]{3,2,1,0:T(8,128)(2,1)}, bf16[2,2,128,512]{3,2,1,0:T(8,128)(2,1)S(1)}, u32[]{:S(2)}) copy-start(bf16[2,2,128,512]{3,2,1,0:T(8,128)(2,1)S(1)} %get-tuple-element.66.refs_4_.refs_2_) | copy-start | bytes 1572868
  83.5 14.3 %collective-permute-start.19 = (bf16[2,2,128,768]{3,2,1,0:T(8,128)(2,1)S(1)}, bf16[2,2,128,768]{3,2,1,0:T(8,128)(2,1)S(1)}, u32[]{:S(2)}, u32[]{:S(2)}) collective-permute-start(bf16[2,2,128,768]{3,2,1,0:T(8,128)(2,1)S(1)} %get-tuple-element.64.refs_0_), channel_id=1, source_target_pairs={{0,2},{1,3},{2,0},{3,1},{4,6},{5,7},{6,4},{7,5},{64,66},{65,67},{6... | collective-permute-start | bytes 2359304 | tf_op jit(solution)/shard_map/ppermute | solution.py:28
  83.7 19.9 %collective-permute-start.20 = (bf16[2,2,128,768]{3,2,1,0:T(8,128)(2,1)S(1)}, bf16[2,2,128,768]{3,2,1,0:T(8,128)(2,1)S(1)}, u32[]{:S(2)}, u32[]{:S(2)}) collective-permute-start(bf16[2,2,128,768]{3,2,1,0:T(8,128)(2,1)S(1)} %get-tuple-element.65.refs_2_.refs_1_), channel_id=1, source_target_pairs={{0,6},{1,7},{2,4},{3,5},{4,2},{5,3},{6,0},{7,1},{64,70},{65,71},{6... | collective-permute-start | bytes 2359304 | tf_op jit(solution)/shard_map/ppermute | solution.py:28
  84.8 7.0 %collective-permute-start.26 = (bf16[2,2,128,512]{3,2,1,0:T(8,128)(2,1)S(1)}, bf16[2,2,128,512]{3,2,1,0:T(8,128)(2,1)S(1)}, u32[]{:S(2)}, u32[]{:S(2)}) collective-permute-start(bf16[2,2,128,512]{3,2,1,0:T(8,128)(2,1)S(1)} %get-tuple-element.66.refs_4_.refs_2_), channel_id=1, source_target_pairs={{0,1},{1,0},{2,3},{3,2},{4,5},{5,4},{6,7},{7,6},{64,65},{65,64},{6... | collective-permute-start | bytes 1572872 | tf_op jit(solution)/shard_map/ppermute | solution.py:28
  90.1 15.1 %collective-permute-start.21 = (bf16[2,2,128,512]{3,2,1,0:T(8,128)(2,1)S(1)}, bf16[2,2,128,512]{3,2,1,0:T(8,128)(2,1)S(1)}, u32[]{:S(2)}, u32[]{:S(2)}) collective-permute-start(bf16[2,2,128,512]{3,2,1,0:T(8,128)(2,1)S(1)} %get-tuple-element.66.refs_4_.refs_2_), channel_id=1, source_target_pairs={{0,64},{1,65},{2,66},{3,67},{4,68},{5,69},{6,70},{7,71},{64,0},{65... | collective-permute-start | bytes 1572872 | tf_op jit(solution)/shard_map/ppermute | solution.py:28
  91.5 14.5 %collective-permute-start.22 = (bf16[2,2,128,768]{3,2,1,0:T(8,128)(2,1)S(1)}, bf16[2,2,128,768]{3,2,1,0:T(8,128)(2,1)S(1)}, u32[]{:S(2)}, u32[]{:S(2)}) collective-permute-start(bf16[2,2,128,768]{3,2,1,0:T(8,128)(2,1)S(1)} %get-tuple-element.64.refs_0_), channel_id=1, source_target_pairs={{0,1},{1,0},{2,3},{3,2},{4,5},{5,4},{6,7},{7,6},{64,65},{65,64},{6... | collective-permute-start | bytes 2359304 | tf_op jit(solution)/shard_map/ppermute | solution.py:28
  91.8 16.1 %copy-start.12 = (bf16[2,2,128,512]{3,2,1,0:T(8,128)(2,1)}, bf16[2,2,128,512]{3,2,1,0:T(8,128)(2,1)S(1)}, u32[]{:S(2)}) copy-start(bf16[2,2,128,512]{3,2,1,0:T(8,128)(2,1)S(1)} %collective-permute-done.26.refs_10_.refs_5_) | copy-start | bytes 1572868
  91.8 14.2 %collective-permute-start.24 = (bf16[2,2,128,768]{3,2,1,0:T(8,128)(2,1)S(1)}, bf16[2,2,128,768]{3,2,1,0:T(8,128)(2,1)S(1)}, u32[]{:S(2)}, u32[]{:S(2)}) collective-permute-start(bf16[2,2,128,768]{3,2,1,0:T(8,128)(2,1)S(1)} %get-tuple-element.65.refs_2_.refs_1_), channel_id=1, source_target_pairs={{0,1},{1,0},{2,3},{3,2},{4,5},{5,4},{6,7},{7,6},{64,65},{65,64},{6... | collective-permute-start | bytes 2359304 | tf_op jit(solution)/shard_map/ppermute | solution.py:28
  97.7 10.2 %copy-start.3 = (bf16[2,2,128,768]{3,2,1,0:T(8,128)(2,1)}, bf16[2,2,128,768]{3,2,1,0:T(8,128)(2,1)S(1)}, u32[]{:S(2)}) copy-start(bf16[2,2,128,768]{3,2,1,0:T(8,128)(2,1)S(1)} %collective-permute-done.19.refs_1_.refs_0_) | copy-start | bytes 2359300
  97.7 10.2 %collective-permute-start.23 = (bf16[2,2,128,768]{3,2,1,0:T(8,128)(2,1)S(1)}, bf16[2,2,128,768]{3,2,1,0:T(8,128)(2,1)S(1)}, u32[]{:S(2)}, u32[]{:S(2)}) collective-permute-start(bf16[2,2,128,768]{3,2,1,0:T(8,128)(2,1)S(1)} %collective-permute-done.19.refs_1_.refs_0_), channel_id=1, source_target_pairs={{0,1},{1,0},{2,3},{3,2},{4,5},{5,4},{6,7},{7,6},{64,65},{65,64},{6... | collective-permute-start | bytes 2359304 | tf_op jit(solution)/shard_map/ppermute | solution.py:28
  103.7 4.3 %copy-start.4 = (bf16[2,2,128,768]{3,2,1,0:T(8,128)(2,1)}, bf16[2,2,128,768]{3,2,1,0:T(8,128)(2,1)S(1)}, u32[]{:S(2)}) copy-start(bf16[2,2,128,768]{3,2,1,0:T(8,128)(2,1)S(1)} %collective-permute-done.20.refs_3_.refs_1_) | copy-start | bytes 2359300
  103.7 4.3 %collective-permute-start.25 = (bf16[2,2,128,768]{3,2,1,0:T(8,128)(2,1)S(1)}, bf16[2,2,128,768]{3,2,1,0:T(8,128)(2,1)S(1)}, u32[]{:S(2)}, u32[]{:S(2)}) collective-permute-start(bf16[2,2,128,768]{3,2,1,0:T(8,128)(2,1)S(1)} %collective-permute-done.20.refs_3_.refs_1_), channel_id=1, source_target_pairs={{0,1},{1,0},{2,3},{3,2},{4,5},{5,4},{6,7},{7,6},{64,65},{65,64},{6... | collective-permute-start | bytes 2359304 | tf_op jit(solution)/shard_map/ppermute | solution.py:28
  105.1 2.8 %copy-start.13 = (bf16[2,2,128,512]{3,2,1,0:T(8,128)(2,1)}, bf16[2,2,128,512]{3,2,1,0:T(8,128)(2,1)S(1)}, u32[]{:S(2)}) copy-start(bf16[2,2,128,512]{3,2,1,0:T(8,128)(2,1)S(1)} %collective-permute-done.21.refs_5_.refs_2_) | copy-start | bytes 1572868
  105.2 2.8 %collective-permute-start.27 = (bf16[2,2,128,512]{3,2,1,0:T(8,128)(2,1)S(1)}, bf16[2,2,128,512]{3,2,1,0:T(8,128)(2,1)S(1)}, u32[]{:S(2)}, u32[]{:S(2)}) collective-permute-start(bf16[2,2,128,512]{3,2,1,0:T(8,128)(2,1)S(1)} %collective-permute-done.21.refs_5_.refs_2_), channel_id=1, source_target_pairs={{0,1},{1,0},{2,3},{3,2},{4,5},{5,4},{6,7},{7,6},{64,65},{65,64},{6... | collective-permute-start | bytes 1572872 | tf_op jit(solution)/shard_map/ppermute | solution.py:28
  105.9 1.9 %copy-start.5 = (bf16[2,2,128,768]{3,2,1,0:T(8,128)(2,1)}, bf16[2,2,128,768]{3,2,1,0:T(8,128)(2,1)S(1)}, u32[]{:S(2)}) copy-start(bf16[2,2,128,768]{3,2,1,0:T(8,128)(2,1)S(1)} %collective-permute-done.22.refs_6_.refs_3_) | copy-start | bytes 2359300
  106.0 1.9 %copy-start.6 = (bf16[2,2,128,768]{3,2,1,0:T(8,128)(2,1)}, bf16[2,2,128,768]{3,2,1,0:T(8,128)(2,1)S(1)}, u32[]{:S(2)}) copy-start(bf16[2,2,128,768]{3,2,1,0:T(8,128)(2,1)S(1)} %collective-permute-done.24.refs_8_.refs_4_) | copy-start | bytes 2359300
  107.9 3.0 %copy-start.14 = (bf16[2,2,128,512]{3,2,1,0:T(8,128)(2,1)}, bf16[2,2,128,512]{3,2,1,0:T(8,128)(2,1)S(1)}, u32[]{:S(2)}) copy-start(bf16[2,2,128,512]{3,2,1,0:T(8,128)(2,1)S(1)} %collective-permute-done.27.refs_11_.refs_5_) | copy-start | bytes 1572868
  107.9 9.2 %copy-start.10 = (bf16[512,512]{1,0:T(8,128)(2,1)S(1)}, bf16[512,512]{1,0:T(8,128)(2,1)}, u32[]{:S(2)}) copy-start(bf16[512,512]{1,0:T(8,128)(2,1)} %refs_13_.1) | copy-start | bytes 1572868
  107.9 3.0 %copy-start.7 = (bf16[2,2,128,768]{3,2,1,0:T(8,128)(2,1)}, bf16[2,2,128,768]{3,2,1,0:T(8,128)(2,1)S(1)}, u32[]{:S(2)}) copy-start(bf16[2,2,128,768]{3,2,1,0:T(8,128)(2,1)S(1)} %collective-permute-done.23.refs_7_.refs_3_) | copy-start | bytes 2359300
  108.0 3.0 %copy-start.8 = (bf16[2,2,128,768]{3,2,1,0:T(8,128)(2,1)}, bf16[2,2,128,768]{3,2,1,0:T(8,128)(2,1)S(1)}, u32[]{:S(2)}) copy-start(bf16[2,2,128,768]{3,2,1,0:T(8,128)(2,1)S(1)} %collective-permute-done.25.refs_9_.refs_4_) | copy-start | bytes 2359300
  111.0 19.6 %all-to-all-start.1 = ((bf16[128,16,128]{2,1,0:T(8,128)(2,1)}), bf16[128,16,128]{2,1,0:T(8,128)(2,1)S(1)}, u32[]{:S(2)}, u32[]{:S(2)}) async-start(bf16[128,16,128]{2,1,0:T(8,128)(2,1)} %bitcast.8), calls=%async_computation.1 | async-start | bytes 1048576 | tf_op jit(solution)/shard_map/all_to_all | solution.py:455
  117.1 13.5 %copy-start.15 = (bf16[4,8192]{1,0:T(4,128)(2,1)S(1)}, bf16[4,8192]{1,0:T(4,128)(2,1)}, u32[]{:S(2)}) copy-start(bf16[4,8192]{1,0:T(4,128)(2,1)} %act.3) | copy-start | bytes 196612
  117.1 13.5 %copy-start.16 = (f32[8192]{0:T(1024)S(1)}, f32[8192]{0:T(1024)}, u32[]{:S(2)}) copy-start(f32[8192]{0:T(1024)} %param.7) | copy-start | bytes 98308
  (1 other events, 0.7 us)

commit v6 on v4

--- a/solution.py
+++ b/solution.py
@@ -78,7 +78,7 @@
         out[:, k * 128 : (k + 1) * 128] = unfold(even, odd, k, low).reshape(512, 128).astype(BF16)
 
 
-ORDERS = ((4, 2, 1), (2, 1, 4), (1, 4, 2))
+ORDERS = ((4, 1, 2), (2, 4, 1), (1, 2, 4))
 CUTS = (0, 768, 1536, 2048)
 
 

time: 132 us -> 132 us (level)
  no operation moved by 1% of the time
where the time goes in v6:
time: 132 us
  starting transfers between devices  48.8 us (37%)
  waiting for transfers between devices  48.8 us (37%)
  Pallas kernels  30.5 us (23%)
  local copies, waits for them, and re-layouts  2.61 us (2%)
    ppermute x28, waiting for transfers between devices, swap(): return lax.ppermute(x, OWNERS, pairs)  40.6 us
    ppermute x28, starting transfers between devices, swap(): return lax.ppermute(x, OWNERS, pairs)  32.3 us
    pallas_call x1, Pallas kernels, grads_of(): pl.pallas_call(grads_kernel, in_specs=[SCALARS] + [anywhere] * 12 + [vmem...  10.9 us
    all_to_all x1, starting transfers between devices, local(): lax.all_to_all(messages.reshape(128, 16, 128), EVERY, 0, 0, tiled=True)  10.2 us
    pallas_call x2, Pallas kernels, chip_sum(): pl.pallas_call(up_kernel if up else pre_kernel, in_specs=[SCALARS] + [VME...  9.87 us
    all_to_all x1, starting transfers between devices, local(): lax.all_to_all(share.reshape(128, 16, 128), EVERY, 0, 0, tiled=True)  6.34 us
    all_to_all x1, waiting for transfers between devices, local(): lax.all_to_all(messages.reshape(128, 16, 128), EVERY, 0, 0, tiled=True)  5.7 us
    pallas_call x1, Pallas kernels, back_messages(): pl.pallas_call(came_kernel, in_specs=[SCALARS] + [vmem] * 8, out_shape=pl...  2.94 us
  transfers between devices with their start and end apart: 30, of which 17 were waited for; matrix products, arithmetic and copies ran while one was open for 0% of the time, Pallas kernels for 19%

profile of v6, /device:TPU:1, one launch (start us, length us, event | category | flops | bytes accessed | tf_op | source)
XLA Modules:
  0.0 131.7 jit_solution(1137073911461629239)
XLA Ops:
  0.6 1.5 %collective-permute-start.1 = (bf16[4096,512]{1,0:T(8,128)(2,1)}, bf16[4096,512]{1,0:T(8,128)(2,1)}, u32[]{:S(2)}, u32[]{:S(2)}) collective-permute-start(bf16[4096,512]{1,0:T(8,128)(2,1)} %w.2), channel_id=1, source_target_pairs={{0,1},{1,0},{2,3},{3,2},{4,5},{5,4},{6,7},{7,6},{64,65},{65,64},{6... | collective-permute-start | bytes 12582920 | tf_op jit(solution)/shard_map/ppermute | solution.py:28
  2.6 2.1 %norm_messages.1 = bf16[2,8,8,16,128]{4,3,2,1,0:T(8,128)(2,1)} custom-call(bf16[4,8192]{1,0:T(4,128)(2,1)} %act.3, f32[1,8192]{1,0:T(1,128)} %bitcast.6, f32[1,8192]{1,0:T(1,128)} %bitcast.10), custom_call_target="tpu_custom_call" | custom-call | tf_op jit(solution)/shard_map/norm_messages/pallas_call | solution.py:56
  4.7 10.2 %all-to-all-start = ((bf16[128,16,128]{2,1,0:T(8,128)(2,1)}), bf16[128,16,128]{2,1,0:T(8,128)(2,1)S(1)}, u32[]{:S(2)}, u32[]{:S(2)}) async-start(bf16[128,16,128]{2,1,0:T(8,128)(2,1)} %bitcast.9), calls=%async_computation | async-start | bytes 1048576 | tf_op jit(solution)/shard_map/all_to_all | solution.py:464
  15.0 1.0 copy-done.9
  16.1 5.2 %up_sum.1 = (f32[256,768]{1,0:T(8,128)S(1)}, bf16[256,768]{1,0:T(8,128)(2,1)S(1)}, f32[256,768]{1,0:T(8,128)S(1)}, bf16[256,768]{1,0:T(8,128)(2,1)S(1)}, f32[256...) custom-call(s32[2]{0:T(128)S(1)} %pad_add_fusion.at, bf16[512,512]{1,0:T(8,128)(2,1)S(1)} %copy-done.9, ...), custom_call_target="tpu_custom_call" | custom-call | flops 1048576 | bytes 1048576 | tf_op jit(solution)/shard_map/up_sum/pallas_call | solution.py:161
  21.2 0.8 copy-done.17
  22.0 0.7 copy-done.18
  22.7 5.7 %all-to-all-done.x = bf16[128,16,128]{2,1,0:T(8,128)(2,1)S(1)} async-done(((bf16[128,16,128]{2,1,0:T(8,128)(2,1)}), bf16[128,16,128]{2,1,0:T(8,128)(2,1)S(1)}, u32[]{:S(2)}, u32[]{:S(2)}) %all-to-all-start) | async-done | bytes 524320 | tf_op jit(solution)/shard_map/all_to_all | solution.py:464
  28.4 1.1 collective-permute-start.3
  30.2 1.2 collective-permute-start.8
  31.4 4.7 %pre_sum.1 = (f32[256,768]{1,0:T(8,128)S(1)}, bf16[256,768]{1,0:T(8,128)(2,1)S(1)}, f32[256,768]{1,0:T(8,128)S(1)}, bf16[256,768]{1,0:T(8,128)(2,1)S(1)}, f32[25...) custom-call(s32[2]{0:T(128)S(1)} %pad_add_fusion.at, bf16[128,16,128]{2,1,0:T(8,128)(2,1)S(1)} %gate.1.x.refs_12_, ...), custom_call_target="tpu_custom_call" | custom-call | flops 1048576 | bytes 1048576 | tf_op jit(solution)/shard_map/pre_sum/pallas_call | solution.py:161
  36.2 0.4 collective-permute-start.7
  36.6 1.6 %collective-permute-start.9 = (bf16[256,768]{1,0:T(8,128)(2,1)S(1)}, bf16[256,768]{1,0:T(8,128)(2,1)S(1)}, u32[]{:S(2)}, u32[]{:S(2)}) collective-permute-start(bf16[256,768]{1,0:T(8,128)(2,1)S(1)} %get-tuple-element.46), channel_id=1, source_target_pairs={{0,6},{1,7},{2,4},{3,5},{4,2},{5,3},{6,0},{7,1},{64,70},{65,71},{6... | collective-permute-start | bytes 1179656 | tf_op jit(solution)/shard_map/ppermute | solution.py:28
  38.2 0.7 collective-permute-done.2.refs_1_
  38.9 1.9 %collective-permute-start.5 = (bf16[256,512]{1,0:T(8,128)(2,1)S(1)}, bf16[256,512]{1,0:T(8,128)(2,1)S(1)}, u32[]{:S(2)}, u32[]{:S(2)}) collective-permute-start(bf16[256,512]{1,0:T(8,128)(2,1)S(1)} %get-tuple-element.39), channel_id=1, source_target_pairs={{0,64},{1,65},{2,66},{3,67},{4,68},{5,69},{6,70},{7,71},{64,0},{65... | collective-permute-start | bytes 786440 | tf_op jit(solution)/shard_map/ppermute | solution.py:28
  40.8 0.8 collective-permute-done.8.refs_9_
  41.6 5.8 %collective-permute-done.5.refs_3_ = bf16[256,512]{1,0:T(8,128)(2,1)S(1)} collective-permute-done((bf16[256,512]{1,0:T(8,128)(2,1)S(1)}, bf16[256,512]{1,0:T(8,128)(2,1)S(1)}, u32[]{:S(2)}, u32[]{:S(2)}) %collective-permute-start.5) | collective-permute-done | bytes 262176 | tf_op jit(solution)/shard_map/ppermute | solution.py:28
  47.4 1.3 collective-permute-done.7.refs_7_
  48.7 1.4 %collective-permute-done.9.refs_11_ = bf16[256,768]{1,0:T(8,128)(2,1)S(1)} collective-permute-done((bf16[256,768]{1,0:T(8,128)(2,1)S(1)}, bf16[256,768]{1,0:T(8,128)(2,1)S(1)}, u32[]{:S(2)}, u32[]{:S(2)}) %collective-permute-start.9) | collective-permute-done | bytes 393248 | tf_op jit(solution)/shard_map/ppermute | solution.py:28
  50.5 2.6 %collective-permute-start.10 = (bf16[2,128,768]{2,1,0:T(8,128)(2,1)S(1)}, bf16[2,128,768]{2,1,0:T(8,128)(2,1)S(1)}, u32[]{:S(2)}, u32[]{:S(2)}) collective-permute-start(bf16[2,128,768]{2,1,0:T(8,128)(2,1)S(1)} %get-tuple-element.48), channel_id=1, source_target_pairs={{0,64},{1,65},{2,66},{3,67},{4,68},{5,69},{6,70},{7,71},{64,0},{65... | collective-permute-start | bytes 1179656 | tf_op jit(solution)/shard_map/ppermute | solution.py:28
  53.2 0.7 collective-permute-start.12
  53.9 6.3 %collective-permute-done.12.refs_5_ = bf16[2,128,512]{2,1,0:T(8,128)(2,1)S(1)} collective-permute-done((bf16[2,128,512]{2,1,0:T(8,128)(2,1)S(1)}, bf16[2,128,512]{2,1,0:T(8,128)(2,1)S(1)}, u32[]{:S(2)}, u32[]{:S(2)}) %collective-permute-start.12) | collective-permute-done | bytes 262176 | tf_op jit(solution)/shard_map/ppermute | solution.py:28
  60.2 1.0 collective-permute-done.10.refs_1_
  61.2 0.8 collective-permute-done.11.refs_3_
  62.3 1.9 %collective-permute-start.13 = (bf16[2,128,768]{2,1,0:T(8,128)(2,1)S(1)}, bf16[2,128,768]{2,1,0:T(8,128)(2,1)S(1)}, u32[]{:S(2)}, u32[]{:S(2)}) collective-permute-start(bf16[2,128,768]{2,1,0:T(8,128)(2,1)S(1)} %get-tuple-element.54), channel_id=1, source_target_pairs={{0,64},{1,65},{2,66},{3,67},{4,68},{5,69},{6,70},{7,71},{64,0},{65... | collective-permute-start | bytes 1179656 | tf_op jit(solution)/shard_map/ppermute | solution.py:28
  64.2 0.8 collective-permute-start.14
  65.0 5.5 %collective-permute-done.15.refs_5_ = bf16[2,128,512]{2,1,0:T(8,128)(2,1)S(1)} collective-permute-done((bf16[2,128,512]{2,1,0:T(8,128)(2,1)S(1)}, bf16[2,128,512]{2,1,0:T(8,128)(2,1)S(1)}, u32[]{:S(2)}, u32[]{:S(2)}) %collective-permute-start.15) | collective-permute-done | bytes 262176 | tf_op jit(solution)/shard_map/ppermute | solution.py:28
  70.5 1.4 %collective-permute-done.13.refs_1_ = bf16[2,128,768]{2,1,0:T(8,128)(2,1)S(1)} collective-permute-done((bf16[2,128,768]{2,1,0:T(8,128)(2,1)S(1)}, bf16[2,128,768]{2,1,0:T(8,128)(2,1)S(1)}, u32[]{:S(2)}, u32[]{:S(2)}) %collective-permute-start.13) | collective-permute-done | bytes 393248 | tf_op jit(solution)/shard_map/ppermute | solution.py:28
  71.9 1.5 %collective-permute-done.14.refs_3_ = bf16[2,128,768]{2,1,0:T(8,128)(2,1)S(1)} collective-permute-done((bf16[2,128,768]{2,1,0:T(8,128)(2,1)S(1)}, bf16[2,128,768]{2,1,0:T(8,128)(2,1)S(1)}, u32[]{:S(2)}, u32[]{:S(2)}) %collective-permute-start.14) | collective-permute-done | bytes 393248 | tf_op jit(solution)/shard_map/ppermute | solution.py:28
  73.3 0.8 third_sums.1
  74.2 1.0 collective-permute-start.16
  75.2 1.0 collective-permute-start.18
  76.2 5.4 %collective-permute-done.18.refs_5_ = bf16[2,128,512]{2,1,0:T(8,128)(2,1)S(1)} collective-permute-done((bf16[2,128,512]{2,1,0:T(8,128)(2,1)S(1)}, bf16[2,128,512]{2,1,0:T(8,128)(2,1)S(1)}, u32[]{:S(2)}, u32[]{:S(2)}) %collective-permute-start.18) | collective-permute-done | bytes 262176 | tf_op jit(solution)/shard_map/ppermute | solution.py:28
  81.6 1.2 collective-permute-done.16.refs_1_
  83.3 1.3 collective-permute-start.20
  84.5 4.7 %collective-permute-start.26 = (bf16[2,2,128,512]{3,2,1,0:T(8,128)(2,1)S(1)}, bf16[2,2,128,512]{3,2,1,0:T(8,128)(2,1)S(1)}, u32[]{:S(2)}, u32[]{:S(2)}) collective-permute-start(bf16[2,2,128,512]{3,2,1,0:T(8,128)(2,1)S(1)} %get-tuple-element.64.refs_4_.refs_2_), channel_id=1, source_target_pairs={{0,1},{1,0},{2,3},{3,2},{4,5},{5,4},{6,7},{7,6},{64,65},{65,64},{6... | collective-permute-start | bytes 1572872 | tf_op jit(solution)/shard_map/ppermute | solution.py:28
  89.2 2.3 %collective-permute-start.21 = (bf16[2,2,128,512]{3,2,1,0:T(8,128)(2,1)S(1)}, bf16[2,2,128,512]{3,2,1,0:T(8,128)(2,1)S(1)}, u32[]{:S(2)}, u32[]{:S(2)}) collective-permute-start(bf16[2,2,128,512]{3,2,1,0:T(8,128)(2,1)S(1)} %get-tuple-element.64.refs_4_.refs_2_), channel_id=1, source_target_pairs={{0,64},{1,65},{2,66},{3,67},{4,68},{5,69},{6,70},{7,71},{64,0},{65... | collective-permute-start | bytes 1572872 | tf_op jit(solution)/shard_map/ppermute | solution.py:28
  92.0 6.8 %collective-permute-done.19.refs_1_.refs_0_ = bf16[2,2,128,768]{3,2,1,0:T(8,128)(2,1)S(1)} collective-permute-done((bf16[2,2,128,768]{3,2,1,0:T(8,128)(2,1)S(1)}, bf16[2,2,128,768]{3,2,1,0:T(8,128)(2,1)S(1)}, u32[]{:S(2)}, u32[]{:S(2)}) %collective-permute-start.19) | collective-permute-done | bytes 786464 | tf_op jit(solution)/shard_map/ppermute | solution.py:28
  98.8 5.1 %collective-permute-start.23 = (bf16[2,2,128,768]{3,2,1,0:T(8,128)(2,1)S(1)}, bf16[2,2,128,768]{3,2,1,0:T(8,128)(2,1)S(1)}, u32[]{:S(2)}, u32[]{:S(2)}) collective-permute-start(bf16[2,2,128,768]{3,2,1,0:T(8,128)(2,1)S(1)} %collective-permute-done.19.refs_1_.refs_0_), channel_id=1, source_target_pairs={{0,1},{1,0},{2,3},{3,2},{4,5},{5,4},{6,7},{7,6},{64,65},{65,64},{6... | collective-permute-start | bytes 2359304 | tf_op jit(solution)/shard_map/ppermute | solution.py:28
  103.9 0.6 collective-permute-start.25
  104.5 0.5 collective-permute-start.27
  105.1 1.9 %back_held.1.refs_7_ = f32[512,512]{1,0:T(8,128)S(1)} custom-call(s32[2]{0:T(128)S(1)} %pad_add_fusion.at, bf16[2,2,128,768]{3,2,1,0:T(8,128)(2,1)S(1)} %get-tuple-element.62.refs_0_, bf16[2,2,128,768]{3,2,1,0:T(8,128)(2,1)S(1)} %get-tuple-element.63.refs_2_.refs_1_, bf16[2,2,128,512]{3,2,1,0:T(8,128)(2,1)S(1)} %get-tuple-element.64.refs_4_.refs_2_, ...), custom_call_target="tpu_custom_call" | custom-call | flops 1073741824 | bytes 4194304 | tf_op jit(solution)/shard_map/back_held/pallas_call | solution.py:330
  107.0 0.7 collective-permute-done.27.refs_11_.refs_5_
  107.7 2.9 %back_messages.1 = bf16[64,2,16,128]{3,2,1,0:T(8,128)(2,1)} custom-call(s32[2]{0:T(128)S(1)} %pad_add_fusion.at, bf16[2,2,128,768]{3,2,1,0:T(8,128)(2,1)S(1)} %collective-permute-done.19.refs_1_.refs_0_, bf16[2,2,128,768]{3,2,1,0:T(8,128)(2,1)S(1)} %collective-permute-done.20.refs_3_.refs_1_, ...), custom_call_target="tpu_custom_call" | custom-call | flops 1073741824 | bytes 4194304 | tf_op jit(solution)/shard_map/back_messages/pallas_call | solution.py:337
  110.7 6.3 %all-to-all-start.1 = ((bf16[128,16,128]{2,1,0:T(8,128)(2,1)}), bf16[128,16,128]{2,1,0:T(8,128)(2,1)S(1)}, u32[]{:S(2)}, u32[]{:S(2)}) async-start(bf16[128,16,128]{2,1,0:T(8,128)(2,1)} %bitcast.8), calls=%async_computation.1 | async-start | bytes 1048576 | tf_op jit(solution)/shard_map/all_to_all | solution.py:473
  117.1 10.9 %grads.1 = (f32[512,4096]{1,0:T(8,128)}, f32[4096,512]{1,0:T(8,128)}) custom-call(s32[2]{0:T(128)S(1)} %pad_add_fusion.at, bf16[2,2,128,768]{3,2,1,0:T(8,128)(2,1)} %copy-done.1, bf16[2,2,128,768]{3,2,1,0:T(8,128)(2,1)} %copy-done.3, bf16[2,2,128,768]{3,2,1,0:T(8,128)(2,1)} %copy-done.2, bf16[2,2,128,768]{3,2,1,0:T(8,128)(2,1)} %copy-done.4, ...), custom_call_target="tpu_custom_call" | custom-call | flops 4294967296 | bytes 25165824 | tf_op jit(solution)/shard_map/grads/pallas_call | solution.py:395
  128.0 2.5 %all-to-all-done.1.x = bf16[128,16,128]{2,1,0:T(8,128)(2,1)S(1)} async-done(((bf16[128,16,128]{2,1,0:T(8,128)(2,1)}), bf16[128,16,128]{2,1,0:T(8,128)(2,1)S(1)}, u32[]{:S(2)}, u32[]{:S(2)}) %all-to-all-start.1) | async-done | bytes 524320 | tf_op jit(solution)/shard_map/all_to_all | solution.py:473
  130.5 1.2 grad_act.1
  (63 shorter events, 3.1 us)
Async XLA Ops:
  0.6 14.4 %collective-permute-start.1 = (bf16[4096,512]{1,0:T(8,128)(2,1)}, bf16[4096,512]{1,0:T(8,128)(2,1)}, u32[]{:S(2)}, u32[]{:S(2)}) collective-permute-start(bf16[4096,512]{1,0:T(8,128)(2,1)} %w.2), channel_id=1, source_target_pairs={{0,1},{1,0},{2,3},{3,2},{4,5},{5,4},{6,7},{7,6},{64,65},{65,64},{6... | collective-permute-start | bytes 12582920 | tf_op jit(solution)/shard_map/ppermute | solution.py:28
  2.1 29.3 %collective-permute-start.4 = (bf16[512,4096]{1,0:T(8,128)(2,1)}, bf16[512,4096]{1,0:T(8,128)(2,1)}, u32[]{:S(2)}, u32[]{:S(2)}) collective-permute-start(bf16[512,4096]{1,0:T(8,128)(2,1)} %refs_6_.3), channel_id=1, source_target_pairs={{0,1},{1,0},{2,3},{3,2},{4,5},{5,4},{6,7},{7,6},{64,65},{65,64},{6... | collective-permute-start | bytes 12582920 | tf_op jit(solution)/shard_map/ppermute | solution.py:28
  2.2 12.8 %collective-permute-start = (bf16[512,512]{1,0:T(8,128)(2,1)}, bf16[512,512]{1,0:T(8,128)(2,1)S(1)}, u32[]{:S(2)}, u32[]{:S(2)}) collective-permute-start(bf16[512,512]{1,0:T(8,128)(2,1)} %refs_13_.1), channel_id=1, source_target_pairs={{0,1},{1,0},{2,3},{3,2},{4,5},{5,4},{6,7},{7,6},{64,65},{65,64},{6... | collective-permute-start | bytes 1572872 | tf_op jit(solution)/shard_map/ppermute | solution.py:28
  4.7 23.7 %all-to-all-start = ((bf16[128,16,128]{2,1,0:T(8,128)(2,1)}), bf16[128,16,128]{2,1,0:T(8,128)(2,1)S(1)}, u32[]{:S(2)}, u32[]{:S(2)}) async-start(bf16[128,16,128]{2,1,0:T(8,128)(2,1)} %bitcast.9), calls=%async_computation | async-start | bytes 1048576 | tf_op jit(solution)/shard_map/all_to_all | solution.py:464
  15.0 1.0 copy-start.9
  21.2 0.8 copy-start.17
  28.4 3.0 %collective-permute-start.3 = (bf16[128,16,128]{2,1,0:T(8,128)(2,1)S(1)}, bf16[128,16,128]{2,1,0:T(8,128)(2,1)S(1)}, u32[]{:S(2)}, u32[]{:S(2)}) collective-permute-start(bf16[128,16,128]{2,1,0:T(8,128)(2,1)S(1)} %gate.1.x.refs_12_), channel_id=1, source_target_pairs={{0,1},{1,0},{2,3},{3,2},{4,5},{5,4},{6,7},{7,6},{64,65},{65,64},{6... | collective-permute-start | bytes 1572872 | tf_op jit(solution)/shard_map/ppermute | solution.py:28
  29.5 9.4 %collective-permute-start.2 = (bf16[256,512]{1,0:T(8,128)(2,1)S(1)}, bf16[256,512]{1,0:T(8,128)(2,1)S(1)}, u32[]{:S(2)}, u32[]{:S(2)}) collective-permute-start(bf16[256,512]{1,0:T(8,128)(2,1)S(1)} %get-tuple-element.36), channel_id=1, source_target_pairs={{0,64},{1,65},{2,66},{3,67},{4,68},{5,69},{6,70},{7,71},{64,0},{65... | collective-permute-start | bytes 786440 | tf_op jit(solution)/shard_map/ppermute | solution.py:28
  29.8 11.0 %collective-permute-start.6 = (bf16[256,768]{1,0:T(8,128)(2,1)}, bf16[256,768]{1,0:T(8,128)(2,1)S(1)}, u32[]{:S(2)}, u32[]{:S(2)}) collective-permute-start(bf16[256,768]{1,0:T(8,128)(2,1)} %copy-done.18), channel_id=1, source_target_pairs={{0,2},{1,3},{2,0},{3,1},{4,6},{5,7},{6,4},{7,5},{64,66},{65,67},{6... | collective-permute-start | bytes 1179656 | tf_op jit(solution)/shard_map/ppermute | solution.py:28
  30.2 11.4 %collective-permute-start.8 = (bf16[256,768]{1,0:T(8,128)(2,1)}, bf16[256,768]{1,0:T(8,128)(2,1)S(1)}, u32[]{:S(2)}, u32[]{:S(2)}) collective-permute-start(bf16[256,768]{1,0:T(8,128)(2,1)} %copy-done.17), channel_id=1, source_target_pairs={{0,6},{1,7},{2,4},{3,5},{4,2},{5,3},{6,0},{7,1},{64,70},{65,71},{6... | collective-permute-start | bytes 1179656 | tf_op jit(solution)/shard_map/ppermute | solution.py:28
  36.2 12.5 %collective-permute-start.7 = (bf16[256,768]{1,0:T(8,128)(2,1)S(1)}, bf16[256,768]{1,0:T(8,128)(2,1)S(1)}, u32[]{:S(2)}, u32[]{:S(2)}) collective-permute-start(bf16[256,768]{1,0:T(8,128)(2,1)S(1)} %get-tuple-element.42), channel_id=1, source_target_pairs={{0,2},{1,3},{2,0},{3,1},{4,6},{5,7},{6,4},{7,5},{64,66},{65,67},{6... | collective-permute-start | bytes 1179656 | tf_op jit(solution)/shard_map/ppermute | solution.py:28
  36.6 13.5 %collective-permute-start.9 = (bf16[256,768]{1,0:T(8,128)(2,1)S(1)}, bf16[256,768]{1,0:T(8,128)(2,1)S(1)}, u32[]{:S(2)}, u32[]{:S(2)}) collective-permute-start(bf16[256,768]{1,0:T(8,128)(2,1)S(1)} %get-tuple-element.46), channel_id=1, source_target_pairs={{0,6},{1,7},{2,4},{3,5},{4,2},{5,3},{6,0},{7,1},{64,70},{65,71},{6... | collective-permute-start | bytes 1179656 | tf_op jit(solution)/shard_map/ppermute | solution.py:28
  38.9 8.5 %collective-permute-start.5 = (bf16[256,512]{1,0:T(8,128)(2,1)S(1)}, bf16[256,512]{1,0:T(8,128)(2,1)S(1)}, u32[]{:S(2)}, u32[]{:S(2)}) collective-permute-start(bf16[256,512]{1,0:T(8,128)(2,1)S(1)} %get-tuple-element.39), channel_id=1, source_target_pairs={{0,64},{1,65},{2,66},{3,67},{4,68},{5,69},{6,70},{7,71},{64,0},{65... | collective-permute-start | bytes 786440 | tf_op jit(solution)/shard_map/ppermute | solution.py:28
  50.5 10.7 %collective-permute-start.10 = (bf16[2,128,768]{2,1,0:T(8,128)(2,1)S(1)}, bf16[2,128,768]{2,1,0:T(8,128)(2,1)S(1)}, u32[]{:S(2)}, u32[]{:S(2)}) collective-permute-start(bf16[2,128,768]{2,1,0:T(8,128)(2,1)S(1)} %get-tuple-element.48), channel_id=1, source_target_pairs={{0,64},{1,65},{2,66},{3,67},{4,68},{5,69},{6,70},{7,71},{64,0},{65... | collective-permute-start | bytes 1179656 | tf_op jit(solution)/shard_map/ppermute | solution.py:28
  53.1 8.9 %collective-permute-start.11 = (bf16[2,128,768]{2,1,0:T(8,128)(2,1)S(1)}, bf16[2,128,768]{2,1,0:T(8,128)(2,1)S(1)}, u32[]{:S(2)}, u32[]{:S(2)}) collective-permute-start(bf16[2,128,768]{2,1,0:T(8,128)(2,1)S(1)} %get-tuple-element.50), channel_id=1, source_target_pairs={{0,2},{1,3},{2,0},{3,1},{4,6},{5,7},{6,4},{7,5},{64,66},{65,67},{6... | collective-permute-start | bytes 1179656 | tf_op jit(solution)/shard_map/ppermute | solution.py:28
  53.2 7.0 %collective-permute-start.12 = (bf16[2,128,512]{2,1,0:T(8,128)(2,1)S(1)}, bf16[2,128,512]{2,1,0:T(8,128)(2,1)S(1)}, u32[]{:S(2)}, u32[]{:S(2)}) collective-permute-start(bf16[2,128,512]{2,1,0:T(8,128)(2,1)S(1)} %get-tuple-element.52), channel_id=1, source_target_pairs={{0,6},{1,7},{2,4},{3,5},{4,2},{5,3},{6,0},{7,1},{64,70},{65,71},{6... | collective-permute-start | bytes 786440 | tf_op jit(solution)/shard_map/ppermute | solution.py:28
  62.0 43.1 %copy-start = (bf16[512,4096]{1,0:T(8,128)(2,1)S(1)}, bf16[512,4096]{1,0:T(8,128)(2,1)}, u32[]{:S(2)}) copy-start(bf16[512,4096]{1,0:T(8,128)(2,1)} %refs_6_.3) | copy-start | bytes 12582916
  62.3 9.6 %collective-permute-start.13 = (bf16[2,128,768]{2,1,0:T(8,128)(2,1)S(1)}, bf16[2,128,768]{2,1,0:T(8,128)(2,1)S(1)}, u32[]{:S(2)}, u32[]{:S(2)}) collective-permute-start(bf16[2,128,768]{2,1,0:T(8,128)(2,1)S(1)} %get-tuple-element.54), channel_id=1, source_target_pairs={{0,64},{1,65},{2,66},{3,67},{4,68},{5,69},{6,70},{7,71},{64,0},{65... | collective-permute-start | bytes 1179656 | tf_op jit(solution)/shard_map/ppermute | solution.py:28
  64.2 9.2 %collective-permute-start.14 = (bf16[2,128,768]{2,1,0:T(8,128)(2,1)S(1)}, bf16[2,128,768]{2,1,0:T(8,128)(2,1)S(1)}, u32[]{:S(2)}, u32[]{:S(2)}) collective-permute-start(bf16[2,128,768]{2,1,0:T(8,128)(2,1)S(1)} %get-tuple-element.56), channel_id=1, source_target_pairs={{0,6},{1,7},{2,4},{3,5},{4,2},{5,3},{6,0},{7,1},{64,70},{65,71},{6... | collective-permute-start | bytes 1179656 | tf_op jit(solution)/shard_map/ppermute | solution.py:28
  65.0 5.5 %collective-permute-start.15 = (bf16[2,128,512]{2,1,0:T(8,128)(2,1)S(1)}, bf16[2,128,512]{2,1,0:T(8,128)(2,1)S(1)}, u32[]{:S(2)}, u32[]{:S(2)}) collective-permute-start(bf16[2,128,512]{2,1,0:T(8,128)(2,1)S(1)} %get-tuple-element.58), channel_id=1, source_target_pairs={{0,2},{1,3},{2,0},{3,1},{4,6},{5,7},{6,4},{7,5},{64,66},{65,67},{6... | collective-permute-start | bytes 786440 | tf_op jit(solution)/shard_map/ppermute | solution.py:28
  74.2 8.6 %collective-permute-start.16 = (bf16[2,128,768]{2,1,0:T(8,128)(2,1)S(1)}, bf16[2,128,768]{2,1,0:T(8,128)(2,1)S(1)}, u32[]{:S(2)}, u32[]{:S(2)}) collective-permute-start(bf16[2,128,768]{2,1,0:T(8,128)(2,1)S(1)} %get-tuple-element.59.refs_0_), channel_id=1, source_target_pairs={{0,64},{1,65},{2,66},{3,67},{4,68},{5,69},{6,70},{7,71},{64,0},{65... | collective-permute-start | bytes 1179656 | tf_op jit(solution)/shard_map/ppermute | solution.py:28
  75.1 7.7 %collective-permute-start.17 = (bf16[2,128,768]{2,1,0:T(8,128)(2,1)S(1)}, bf16[2,128,768]{2,1,0:T(8,128)(2,1)S(1)}, u32[]{:S(2)}, u32[]{:S(2)}) collective-permute-start(bf16[2,128,768]{2,1,0:T(8,128)(2,1)S(1)} %get-tuple-element.60.refs_2_), channel_id=1, source_target_pairs={{0,2},{1,3},{2,0},{3,1},{4,6},{5,7},{6,4},{7,5},{64,66},{65,67},{6... | collective-permute-start | bytes 1179656 | tf_op jit(solution)/shard_map/ppermute | solution.py:28
  75.2 6.4 %collective-permute-start.18 = (bf16[2,128,512]{2,1,0:T(8,128)(2,1)S(1)}, bf16[2,128,512]{2,1,0:T(8,128)(2,1)S(1)}, u32[]{:S(2)}, u32[]{:S(2)}) collective-permute-start(bf16[2,128,512]{2,1,0:T(8,128)(2,1)S(1)} %get-tuple-element.61.refs_4_), channel_id=1, source_target_pairs={{0,6},{1,7},{2,4},{3,5},{4,2},{5,3},{6,0},{7,1},{64,70},{65,71},{6... | collective-permute-start | bytes 786440 | tf_op jit(solution)/shard_map/ppermute | solution.py:28
  83.0 24.0 %copy-start.1 = (bf16[2,2,128,768]{3,2,1,0:T(8,128)(2,1)}, bf16[2,2,128,768]{3,2,1,0:T(8,128)(2,1)S(1)}, u32[]{:S(2)}) copy-start(bf16[2,2,128,768]{3,2,1,0:T(8,128)(2,1)S(1)} %get-tuple-element.62.refs_0_) | copy-start | bytes 2359300
  83.0 24.0 %copy-start.2 = (bf16[2,2,128,768]{3,2,1,0:T(8,128)(2,1)}, bf16[2,2,128,768]{3,2,1,0:T(8,128)(2,1)S(1)}, u32[]{:S(2)}) copy-start(bf16[2,2,128,768]{3,2,1,0:T(8,128)(2,1)S(1)} %get-tuple-element.63.refs_2_.refs_1_) | copy-start | bytes 2359300
  83.0 24.0 %copy-start.11 = (bf16[2,2,128,512]{3,2,1,0:T(8,128)(2,1)}, bf16[2,2,128,512]{3,2,1,0:T(8,128)(2,1)S(1)}, u32[]{:S(2)}) copy-start(bf16[2,2,128,512]{3,2,1,0:T(8,128)(2,1)S(1)} %get-tuple-element.64.refs_4_.refs_2_) | copy-start | bytes 1572868
  83.0 15.8 %collective-permute-start.19 = (bf16[2,2,128,768]{3,2,1,0:T(8,128)(2,1)S(1)}, bf16[2,2,128,768]{3,2,1,0:T(8,128)(2,1)S(1)}, u32[]{:S(2)}, u32[]{:S(2)}) collective-permute-start(bf16[2,2,128,768]{3,2,1,0:T(8,128)(2,1)S(1)} %get-tuple-element.62.refs_0_), channel_id=1, source_target_pairs={{0,2},{1,3},{2,0},{3,1},{4,6},{5,7},{6,4},{7,5},{64,66},{65,67},{6... | collective-permute-start | bytes 2359304 | tf_op jit(solution)/shard_map/ppermute | solution.py:28
  83.3 20.6 %collective-permute-start.20 = (bf16[2,2,128,768]{3,2,1,0:T(8,128)(2,1)S(1)}, bf16[2,2,128,768]{3,2,1,0:T(8,128)(2,1)S(1)}, u32[]{:S(2)}, u32[]{:S(2)}) collective-permute-start(bf16[2,2,128,768]{3,2,1,0:T(8,128)(2,1)S(1)} %get-tuple-element.63.refs_2_.refs_1_), channel_id=1, source_target_pairs={{0,6},{1,7},{2,4},{3,5},{4,2},{5,3},{6,0},{7,1},{64,70},{65,71},{6... | collective-permute-start | bytes 2359304 | tf_op jit(solution)/shard_map/ppermute | solution.py:28
  84.5 7.3 %collective-permute-start.26 = (bf16[2,2,128,512]{3,2,1,0:T(8,128)(2,1)S(1)}, bf16[2,2,128,512]{3,2,1,0:T(8,128)(2,1)S(1)}, u32[]{:S(2)}, u32[]{:S(2)}) collective-permute-start(bf16[2,2,128,512]{3,2,1,0:T(8,128)(2,1)S(1)} %get-tuple-element.64.refs_4_.refs_2_), channel_id=1, source_target_pairs={{0,1},{1,0},{2,3},{3,2},{4,5},{5,4},{6,7},{7,6},{64,65},{65,64},{6... | collective-permute-start | bytes 1572872 | tf_op jit(solution)/shard_map/ppermute | solution.py:28
  89.2 15.3 %collective-permute-start.21 = (bf16[2,2,128,512]{3,2,1,0:T(8,128)(2,1)S(1)}, bf16[2,2,128,512]{3,2,1,0:T(8,128)(2,1)S(1)}, u32[]{:S(2)}, u32[]{:S(2)}) collective-permute-start(bf16[2,2,128,512]{3,2,1,0:T(8,128)(2,1)S(1)} %get-tuple-element.64.refs_4_.refs_2_), channel_id=1, source_target_pairs={{0,64},{1,65},{2,66},{3,67},{4,68},{5,69},{6,70},{7,71},{64,0},{65... | collective-permute-start | bytes 1572872 | tf_op jit(solution)/shard_map/ppermute | solution.py:28
  91.5 13.5 %collective-permute-start.22 = (bf16[2,2,128,768]{3,2,1,0:T(8,128)(2,1)S(1)}, bf16[2,2,128,768]{3,2,1,0:T(8,128)(2,1)S(1)}, u32[]{:S(2)}, u32[]{:S(2)}) collective-permute-start(bf16[2,2,128,768]{3,2,1,0:T(8,128)(2,1)S(1)} %get-tuple-element.62.refs_0_), channel_id=1, source_target_pairs={{0,1},{1,0},{2,3},{3,2},{4,5},{5,4},{6,7},{7,6},{64,65},{65,64},{6... | collective-permute-start | bytes 2359304 | tf_op jit(solution)/shard_map/ppermute | solution.py:28
  91.8 15.2 %copy-start.12 = (bf16[2,2,128,512]{3,2,1,0:T(8,128)(2,1)}, bf16[2,2,128,512]{3,2,1,0:T(8,128)(2,1)S(1)}, u32[]{:S(2)}) copy-start(bf16[2,2,128,512]{3,2,1,0:T(8,128)(2,1)S(1)} %collective-permute-done.26.refs_10_.refs_5_) | copy-start | bytes 1572868
  91.8 13.2 %collective-permute-start.24 = (bf16[2,2,128,768]{3,2,1,0:T(8,128)(2,1)S(1)}, bf16[2,2,128,768]{3,2,1,0:T(8,128)(2,1)S(1)}, u32[]{:S(2)}, u32[]{:S(2)}) collective-permute-start(bf16[2,2,128,768]{3,2,1,0:T(8,128)(2,1)S(1)} %get-tuple-element.63.refs_2_.refs_1_), channel_id=1, source_target_pairs={{0,1},{1,0},{2,3},{3,2},{4,5},{5,4},{6,7},{7,6},{64,65},{65,64},{6... | collective-permute-start | bytes 2359304 | tf_op jit(solution)/shard_map/ppermute | solution.py:28
  98.8 8.9 %copy-start.3 = (bf16[2,2,128,768]{3,2,1,0:T(8,128)(2,1)}, bf16[2,2,128,768]{3,2,1,0:T(8,128)(2,1)S(1)}, u32[]{:S(2)}) copy-start(bf16[2,2,128,768]{3,2,1,0:T(8,128)(2,1)S(1)} %collective-permute-done.19.refs_1_.refs_0_) | copy-start | bytes 2359300
  98.8 8.9 %collective-permute-start.23 = (bf16[2,2,128,768]{3,2,1,0:T(8,128)(2,1)S(1)}, bf16[2,2,128,768]{3,2,1,0:T(8,128)(2,1)S(1)}, u32[]{:S(2)}, u32[]{:S(2)}) collective-permute-start(bf16[2,2,128,768]{3,2,1,0:T(8,128)(2,1)S(1)} %collective-permute-done.19.refs_1_.refs_0_), channel_id=1, source_target_pairs={{0,1},{1,0},{2,3},{3,2},{4,5},{5,4},{6,7},{7,6},{64,65},{65,64},{6... | collective-permute-start | bytes 2359304 | tf_op jit(solution)/shard_map/ppermute | solution.py:28
  103.9 3.8 %copy-start.4 = (bf16[2,2,128,768]{3,2,1,0:T(8,128)(2,1)}, bf16[2,2,128,768]{3,2,1,0:T(8,128)(2,1)S(1)}, u32[]{:S(2)}) copy-start(bf16[2,2,128,768]{3,2,1,0:T(8,128)(2,1)S(1)} %collective-permute-done.20.refs_3_.refs_1_) | copy-start | bytes 2359300
  103.9 3.8 %collective-permute-start.25 = (bf16[2,2,128,768]{3,2,1,0:T(8,128)(2,1)S(1)}, bf16[2,2,128,768]{3,2,1,0:T(8,128)(2,1)S(1)}, u32[]{:S(2)}, u32[]{:S(2)}) collective-permute-start(bf16[2,2,128,768]{3,2,1,0:T(8,128)(2,1)S(1)} %collective-permute-done.20.refs_3_.refs_1_), channel_id=1, source_target_pairs={{0,1},{1,0},{2,3},{3,2},{4,5},{5,4},{6,7},{7,6},{64,65},{65,64},{6... | collective-permute-start | bytes 2359304 | tf_op jit(solution)/shard_map/ppermute | solution.py:28
  104.5 3.2 %copy-start.13 = (bf16[2,2,128,512]{3,2,1,0:T(8,128)(2,1)}, bf16[2,2,128,512]{3,2,1,0:T(8,128)(2,1)S(1)}, u32[]{:S(2)}) copy-start(bf16[2,2,128,512]{3,2,1,0:T(8,128)(2,1)S(1)} %collective-permute-done.21.refs_5_.refs_2_) | copy-start | bytes 1572868
  104.5 3.2 %collective-permute-start.27 = (bf16[2,2,128,512]{3,2,1,0:T(8,128)(2,1)S(1)}, bf16[2,2,128,512]{3,2,1,0:T(8,128)(2,1)S(1)}, u32[]{:S(2)}, u32[]{:S(2)}) collective-permute-start(bf16[2,2,128,512]{3,2,1,0:T(8,128)(2,1)S(1)} %collective-permute-done.21.refs_5_.refs_2_), channel_id=1, source_target_pairs={{0,1},{1,0},{2,3},{3,2},{4,5},{5,4},{6,7},{7,6},{64,65},{65,64},{6... | collective-permute-start | bytes 1572872 | tf_op jit(solution)/shard_map/ppermute | solution.py:28
  105.1 1.9 %copy-start.5 = (bf16[2,2,128,768]{3,2,1,0:T(8,128)(2,1)}, bf16[2,2,128,768]{3,2,1,0:T(8,128)(2,1)S(1)}, u32[]{:S(2)}) copy-start(bf16[2,2,128,768]{3,2,1,0:T(8,128)(2,1)S(1)} %collective-permute-done.22.refs_6_.refs_3_) | copy-start | bytes 2359300
  105.1 1.9 %copy-start.6 = (bf16[2,2,128,768]{3,2,1,0:T(8,128)(2,1)}, bf16[2,2,128,768]{3,2,1,0:T(8,128)(2,1)S(1)}, u32[]{:S(2)}) copy-start(bf16[2,2,128,768]{3,2,1,0:T(8,128)(2,1)S(1)} %collective-permute-done.24.refs_8_.refs_4_) | copy-start | bytes 2359300
  107.7 3.0 %copy-start.14 = (bf16[2,2,128,512]{3,2,1,0:T(8,128)(2,1)}, bf16[2,2,128,512]{3,2,1,0:T(8,128)(2,1)S(1)}, u32[]{:S(2)}) copy-start(bf16[2,2,128,512]{3,2,1,0:T(8,128)(2,1)S(1)} %collective-permute-done.27.refs_11_.refs_5_) | copy-start | bytes 1572868
  107.7 9.4 %copy-start.10 = (bf16[512,512]{1,0:T(8,128)(2,1)S(1)}, bf16[512,512]{1,0:T(8,128)(2,1)}, u32[]{:S(2)}) copy-start(bf16[512,512]{1,0:T(8,128)(2,1)} %refs_13_.1) | copy-start | bytes 1572868
  107.7 3.0 %copy-start.7 = (bf16[2,2,128,768]{3,2,1,0:T(8,128)(2,1)}, bf16[2,2,128,768]{3,2,1,0:T(8,128)(2,1)S(1)}, u32[]{:S(2)}) copy-start(bf16[2,2,128,768]{3,2,1,0:T(8,128)(2,1)S(1)} %collective-permute-done.23.refs_7_.refs_3_) | copy-start | bytes 2359300
  107.7 3.0 %copy-start.8 = (bf16[2,2,128,768]{3,2,1,0:T(8,128)(2,1)}, bf16[2,2,128,768]{3,2,1,0:T(8,128)(2,1)S(1)}, u32[]{:S(2)}) copy-start(bf16[2,2,128,768]{3,2,1,0:T(8,128)(2,1)S(1)} %collective-permute-done.25.refs_9_.refs_4_) | copy-start | bytes 2359300
  110.7 19.8 %all-to-all-start.1 = ((bf16[128,16,128]{2,1,0:T(8,128)(2,1)}), bf16[128,16,128]{2,1,0:T(8,128)(2,1)S(1)}, u32[]{:S(2)}, u32[]{:S(2)}) async-start(bf16[128,16,128]{2,1,0:T(8,128)(2,1)} %bitcast.8), calls=%async_computation.1 | async-start | bytes 1048576 | tf_op jit(solution)/shard_map/all_to_all | solution.py:473
  117.0 13.5 %copy-start.15 = (bf16[4,8192]{1,0:T(4,128)(2,1)S(1)}, bf16[4,8192]{1,0:T(4,128)(2,1)}, u32[]{:S(2)}) copy-start(bf16[4,8192]{1,0:T(4,128)(2,1)} %act.3) | copy-start | bytes 196612
  117.0 13.5 %copy-start.16 = (f32[8192]{0:T(1024)S(1)}, f32[8192]{0:T(1024)}, u32[]{:S(2)}) copy-start(f32[8192]{0:T(1024)} %param.7) | copy-start | bytes 98308
  (1 other events, 0.7 us)
